TPU v7x, 32 devices: a whole 2x2x4 slice. The times are simulated.
32 devices in a mesh: dp: 8 (over y, x, core), code: 4 (over z).
Axes of the slice: x: 2, y: 2, z: 4, core: 2. Of those that a mesh axis runs over, the one named last changes fastest.
Arguments:
- patches: bfloat16 [8, 496, 256], P('dp'), may hold values from -6 to 6
- lengths: int32 [8], P('dp'), may hold values from 248 to 496, as said below
- patch_masks: int32 [8, 496], P('dp'), may hold values from 0 to 1, as said below
- targets: int32 [8, 496], P('dp'), may hold values from 0 to 1023
- codebook: bfloat16 [1024, 256], P('code'), may hold values from -0.47851562 to 0.47851562
- params: float32 [19296256], P(('dp', 'code')), as said below
- first_moment: float32 [19296256], P(('dp', 'code')), may hold values from -7.581117e-07 to 7.581117e-07
- second_moment: float32 [19296256], P(('dp', 'code')), may hold values from 6.478701e-16 to 1.03659214e-14
- step_count: int32 [1], replicated, may hold values from 1 to 20
Outputs:
- new_params: float32 [19296256], P(('dp', 'code'))
- new_first: float32 [19296256], P(('dp', 'code'))
- new_second: float32 [19296256], P(('dp', 'code'))
- params_low: bfloat16 [19296256], P(('dp', 'code'))
- mean_loss: float32 [], replicated
- grad_norm: float32 [], replicated
- rel_grad: float32 [320, 12], replicated
Inputs may be any that keep to these rules, and one draw needn't show every extreme that they name: `lengths`: each length is 248 or 496, and both occur. `patch_masks`: in each clip exactly 3 / 4 of its first length positions are 1, all others 0. `targets`: read only where patch_masks is 1. `params`: entries past 19293992 are zero.
All inputs are finite; a program needn't handle non-finite values.
Results may differ from a plain program's by a relative error of at most 0.024.
Values may be sent and summed in bfloat16 or wider, within the bound.
No kernel may reach another device: no remote copies, remote signals or barrier semaphores. Data moves between devices by JAX's collectives and lax.ppermute only.
A program may use at most 448 MiB of HBM per device.

v0:
```python
import math

import jax
import jax.numpy as jnp
import numpy as np
from jax import lax
from jax.sharding import PartitionSpec as P

D = 768
HEADS = 12
HEAD_DIM = 64
FF = 3072
PATCH_IN = 256
PROJ = 256
KERNEL = 128
GROUPS = 16
BUCKETS = 320
MAX_DIST = 800
LAYERS = 2
LONG = 496
VISIBLE = 124


NORM_EPSILON = 1e-05
UNIT_EPSILON = 1e-06
DEEP_ALPHA = 2.2133638394006434
LOGIT_SCALE = 25.0
CLIP_NORM = 0.005
LEARN_RATE = 0.02
BETA_ONE = 0.9
BETA_TWO = 0.999
ADAM_EPSILON = 1e-10
WEIGHT_DECAY = 0.01
MASK_FILL = -1000000000.0
HIGHEST = lax.Precision.HIGHEST
LAYER_KEYS = ("w_qkv", "w_out", "w_up", "w_down", "layer_vec", "gate_proj", "gate_scale")


def combined_all(part, axis, combine):
    gathered = jax.tree.map(lambda a: lax.all_gather(a, axis), part)

    def take(source):
        return jax.tree.map(lambda a: lax.dynamic_index_in_dim(a, source, 0, False), gathered)

    return lax.fori_loop(
        1, lax.axis_size(axis), lambda source, state: combine(state, take(source)), take(0)
    )


def layout():
    return [
        ("w_patch", (PATCH_IN, D)),
        ("glob_vec", (4, D)),
        ("conv_w", (KERNEL, D // GROUPS, D)),
        ("w_qkv", (LAYERS, D, 3 * D)),
        ("w_out", (LAYERS, D, D)),
        ("w_up", (LAYERS, D, FF)),
        ("w_down", (LAYERS, FF, D)),
        ("layer_vec", (LAYERS, 8 * D + FF)),
        ("gate_proj", (LAYERS, HEAD_DIM + 1, 8)),
        ("gate_scale", (LAYERS, HEADS)),
        ("rel_table", (BUCKETS, HEADS)),
        ("w_head", (D, PROJ)),
    ]


def unpack(flat_vals):
    pieces = {}
    offset = 0
    for seg_name, extent in layout():
        amount = math.prod(extent)
        pieces[seg_name] = flat_vals[offset : offset + amount].reshape(extent)
        offset += amount
    return pieces


def bucket_onehot():
    offsets = np.arange(-(LONG - 1), LONG)
    half_count = BUCKETS // 2
    exact_count = half_count // 2
    distance = np.abs(offsets)
    scaled = (
        np.log(np.maximum(distance, 1) / exact_count)
        / np.log(MAX_DIST / exact_count)
        * (half_count - exact_count)
    )
    larger = np.minimum(exact_count + np.maximum(scaled, 0.0).astype(np.int64), half_count - 1)
    bucket = (offsets > 0) * half_count + np.where(distance < exact_count, distance, larger)
    return (bucket[:, None] == np.arange(BUCKETS)[None, :]).astype(np.float32)


def clip_layout(lengths, patch_masks):
    places = jnp.arange(LONG, dtype=jnp.int32)
    live_slot = places[None, :] < lengths[:, None]
    visible = live_slot & (patch_masks == 0)
    sort_order = jnp.argsort(jnp.where(visible, 0, 1).astype(jnp.int32), axis=1, stable=True)
    inverse = jnp.argsort(sort_order, axis=1, stable=True)
    seen_place = sort_order[:, :VISIBLE]
    seen_valid = places[None, :VISIBLE] < (lengths // 4)[:, None]
    rank_place = jnp.minimum(inverse, VISIBLE - 1)
    return (live_slot, visible, seen_place, seen_valid, rank_place)


def position_bias(rel_offsets, positions):
    offset_idx = positions[:, None, :] - positions[:, :, None] + (LONG - 1)
    head_table = jnp.transpose(rel_offsets)
    return jnp.transpose(jnp.take(head_table, offset_idx, axis=1), (1, 0, 2, 3))


def norm_forward(before, norm_gain, norm_shift):
    centred = before - jnp.mean(before, axis=-1, keepdims=True)
    inv_std = lax.rsqrt(jnp.mean(centred * centred, axis=-1, keepdims=True) + NORM_EPSILON)
    normed = centred * inv_std
    return (normed * norm_gain + norm_shift, normed, inv_std)


def norm_backward(upstream, normed, inv_std, norm_gain):
    scaled = upstream * norm_gain
    centred_grad = (
        scaled
        - jnp.mean(scaled, axis=-1, keepdims=True)
        - normed * jnp.mean(scaled * normed, axis=-1, keepdims=True)
    )
    return (
        centred_grad * inv_std,
        jnp.sum(upstream * normed, axis=(0, 1)),
        jnp.sum(upstream, axis=(0, 1)),
    )


def gelu_grad(pre_act):
    return (
        0.5 * (1.0 + jax.scipy.special.erf(pre_act * 0.7071067811865476))
        + pre_act * jnp.exp(-0.5 * pre_act * pre_act) * 0.3989422804014327
    )


def vec_part(vector, slot_index):
    return vector[slot_index * D : (slot_index + 1) * D]


def layer_weights(pieces, layer_index):
    return {seg_name: pieces[seg_name][layer_index] for seg_name in LAYER_KEYS}


def conv_forward(conv_in, conv_weight):
    return lax.conv_general_dilated(
        conv_in,
        conv_weight,
        (1,),
        [(KERNEL // 2, KERNEL // 2 - 1)],
        dimension_numbers=("NWC", "WIO", "NWC"),
        feature_group_count=GROUPS,
        preferred_element_type=jnp.float32,
    )


def conv_backward(conv_in, conv_weight, grad_low):
    group_width = D // GROUPS
    turned = jnp.transpose(
        conv_weight.reshape(KERNEL, group_width, GROUPS, group_width), (0, 3, 2, 1)
    ).reshape(KERNEL, group_width, D)[::-1]
    grad_input = lax.conv_general_dilated(
        grad_low,
        turned,
        (1,),
        [(KERNEL // 2 - 1, KERNEL // 2)],
        dimension_numbers=("NWC", "WIO", "NWC"),
        feature_group_count=GROUPS,
        preferred_element_type=jnp.float32,
    )
    grad_kernel = lax.conv_general_dilated(
        conv_in,
        grad_low,
        (1,),
        [(KERNEL // 2, KERNEL // 2 - 1)],
        dimension_numbers=("CWN", "IWO", "NWC"),
        batch_group_count=GROUPS,
        preferred_element_type=jnp.float32,
    )
    return (grad_input, jnp.transpose(grad_kernel, (1, 0, 2)))


def gate_forward(in_low, weights):
    batch_size, length = (in_low.shape[0], in_low.shape[1])
    heads_in = in_low.reshape(batch_size, length, HEADS, HEAD_DIM)
    gate_weight = weights["gate_proj"]
    gate_logit = jnp.einsum(
        "blhd,de->blhe", heads_in, gate_weight[:HEAD_DIM], preferred_element_type=jnp.float32
    ) + gate_weight[HEAD_DIM].astype(jnp.float32)
    gate_pair = jax.nn.sigmoid(
        jnp.sum(gate_logit.reshape(batch_size, length, HEADS, 2, 4), axis=-1)
    )
    gate_vals = (
        gate_pair[..., 0] * (gate_pair[..., 1] * weights["gate_scale"].astype(jnp.float32) - 1.0)
        + 2.0
    )
    return (gate_vals, gate_pair)


def gate_backward(grad_gate, gate_pair, in_low, weights):
    batch_size, length = (in_low.shape[0], in_low.shape[1])
    first_gate = gate_pair[..., 0]
    second_gate = gate_pair[..., 1]
    scale_vec = weights["gate_scale"].astype(jnp.float32)
    grad_first = grad_gate * (second_gate * scale_vec - 1.0)
    grad_second = grad_gate * first_gate * scale_vec
    grad_scale = jnp.sum(grad_gate * first_gate * second_gate, axis=(0, 1))
    grad_pair = jnp.stack(
        [
            grad_first * first_gate * (1.0 - first_gate),
            grad_second * second_gate * (1.0 - second_gate),
        ],
        axis=-1,
    )
    grad_logit = jnp.broadcast_to(grad_pair[..., None], (batch_size, length, HEADS, 2, 4)).reshape(
        batch_size, length, HEADS, 8
    )
    heads_in = in_low.astype(jnp.float32).reshape(batch_size, length, HEADS, HEAD_DIM)
    gate_weight = weights["gate_proj"].astype(jnp.float32)
    grad_proj = jnp.einsum("blhd,blhe->de", heads_in, grad_logit, precision=HIGHEST)
    grad_bias = jnp.sum(grad_logit, axis=(0, 1, 2))
    grad_heads = jnp.einsum(
        "blhe,de->blhd", grad_logit, gate_weight[:HEAD_DIM], precision=HIGHEST
    ).reshape(batch_size, length, D)
    return (grad_heads, jnp.concatenate([grad_proj, grad_bias[None, :]], axis=0), grad_scale)


def attention_scores(query_low, key_low, gate_vals, pos_bias, key_valid):
    raw_scores = jnp.einsum(
        "bqhd,bkhd->bhqk", query_low, key_low, preferred_element_type=jnp.float32
    )
    raw_scores = raw_scores + jnp.transpose(gate_vals, (0, 2, 1))[..., None] * pos_bias
    return raw_scores + jnp.where(key_valid, 0.0, MASK_FILL)[:, None, None, :]


def layer_forward(hidden, positions, key_valid, weights, rel_offsets):
    batch_size, length = (hidden.shape[0], hidden.shape[1])
    vector = weights["layer_vec"].astype(jnp.float32)
    in_low = hidden.astype(jnp.bfloat16)
    qkv_proj = jnp.einsum(
        "bld,de->ble", in_low, weights["w_qkv"], preferred_element_type=jnp.float32
    )
    query_low = (
        ((qkv_proj[..., :D] + vec_part(vector, 0)) * HEAD_DIM ** (-0.5))
        .astype(jnp.bfloat16)
        .reshape(batch_size, length, HEADS, HEAD_DIM)
    )
    key_low = (
        qkv_proj[..., D : 2 * D].astype(jnp.bfloat16).reshape(batch_size, length, HEADS, HEAD_DIM)
    )
    value_low = (
        (qkv_proj[..., 2 * D :] + vec_part(vector, 1))
        .astype(jnp.bfloat16)
        .reshape(batch_size, length, HEADS, HEAD_DIM)
    )
    gate_vals, gate_pair = gate_forward(in_low, weights)
    pos_bias = position_bias(rel_offsets, positions)
    scores = attention_scores(query_low, key_low, gate_vals, pos_bias, key_valid)
    log_total = jax.scipy.special.logsumexp(scores, axis=-1)
    probs_low = jnp.exp(scores - log_total[..., None]).astype(jnp.bfloat16)
    attended = (
        jnp.einsum("bhqk,bkhd->bqhd", probs_low, value_low, preferred_element_type=jnp.float32)
        .reshape(batch_size, length, D)
        .astype(jnp.bfloat16)
    )
    attn_out = jnp.einsum(
        "bld,de->ble", attended, weights["w_out"], preferred_element_type=jnp.float32
    ) + vec_part(vector, 2)
    mid_rows, normed_one, inv_one = norm_forward(
        DEEP_ALPHA * hidden + attn_out, vec_part(vector, 3), vec_part(vector, 4)
    )
    mid_low = mid_rows.astype(jnp.bfloat16)
    pre_act = (
        jnp.einsum("bld,df->blf", mid_low, weights["w_up"], preferred_element_type=jnp.float32)
        + vector[8 * D :]
    )
    act_low = jax.nn.gelu(pre_act, approximate=False).astype(jnp.bfloat16)
    ffn_out = jnp.einsum(
        "blf,fd->bld", act_low, weights["w_down"], preferred_element_type=jnp.float32
    ) + vec_part(vector, 5)
    final_rows, normed_two, inv_two = norm_forward(
        DEEP_ALPHA * mid_rows + ffn_out, vec_part(vector, 6), vec_part(vector, 7)
    )
    kept_vals = (
        in_low,
        query_low,
        key_low,
        value_low,
        gate_vals,
        gate_pair,
        log_total,
        attended,
        mid_low,
        pre_act,
        act_low,
        normed_one,
        inv_one,
        normed_two,
        inv_two,
    )
    return (final_rows, kept_vals)


def attention_backward(
    query_low, key_low, value_low, gate_vals, log_total, grad_att, rel_offsets, positions, key_valid
):

    def one_clip(clip_part):
        query_one, key_one, value_one, gate_one, total_one, grad_one, place_one, valid_one = (
            clip_part
        )
        query_one, key_one, value_one, gate_one = (
            query_one[None],
            key_one[None],
            value_one[None],
            gate_one[None],
        )
        grad_one, place_one, valid_one = (grad_one[None], place_one[None], valid_one[None])
        pos_bias = position_bias(rel_offsets, place_one)
        scores = attention_scores(query_one, key_one, gate_one, pos_bias, valid_one)
        attn_probs = jnp.exp(scores - total_one[None][..., None])
        grad_probs = jnp.einsum(
            "bqhd,bkhd->bhqk", grad_one, value_one, preferred_element_type=jnp.float32
        )
        grad_value = jnp.einsum(
            "bhqk,bqhd->bkhd",
            attn_probs.astype(jnp.bfloat16),
            grad_one,
            preferred_element_type=jnp.float32,
        )
        grad_scores = attn_probs * (
            grad_probs - jnp.sum(attn_probs * grad_probs, axis=-1, keepdims=True)
        )
        grad_gate = jnp.transpose(jnp.sum(grad_scores * pos_bias, axis=-1), (0, 2, 1))
        grad_bias = grad_scores * jnp.transpose(gate_one, (0, 2, 1))[..., None]
        _, bias_pull = jax.vjp(lambda rel_tab: position_bias(rel_tab, place_one), rel_offsets)
        (grad_rel,) = bias_pull(grad_bias)
        scores_low = grad_scores.astype(jnp.bfloat16)
        grad_query = jnp.einsum(
            "bhqk,bkhd->bqhd", scores_low, key_one, preferred_element_type=jnp.float32
        ) * HEAD_DIM ** (-0.5)
        grad_key = jnp.einsum(
            "bhqk,bqhd->bkhd", scores_low, query_one, preferred_element_type=jnp.float32
        )
        return (grad_query[0], grad_key[0], grad_value[0], grad_gate[0], grad_rel)

    results = lax.map(
        one_clip,
        (query_low, key_low, value_low, gate_vals, log_total, grad_att, positions, key_valid),
    )
    return (results[0], results[1], results[2], results[3], jnp.sum(results[4], axis=0))


def layer_backward(upstream, kept_vals, weights, rel_offsets, positions, key_valid):
    (
        in_low,
        query_low,
        key_low,
        value_low,
        gate_vals,
        gate_pair,
        log_total,
        attended,
        mid_low,
        pre_act,
        act_low,
        normed_one,
        inv_one,
        normed_two,
        inv_two,
    ) = kept_vals
    batch_size, length = (upstream.shape[0], upstream.shape[1])
    vector = weights["layer_vec"].astype(jnp.float32)
    grad_res_two, grad_gain_two, grad_shift_two = norm_backward(
        upstream, normed_two, inv_two, vec_part(vector, 6)
    )
    ffn_low = grad_res_two.astype(jnp.bfloat16)
    grad_down = jnp.einsum("blf,bld->fd", act_low, ffn_low, preferred_element_type=jnp.float32)
    grad_pre = jnp.einsum(
        "bld,fd->blf", ffn_low, weights["w_down"], preferred_element_type=jnp.float32
    ) * gelu_grad(pre_act)
    pre_low = grad_pre.astype(jnp.bfloat16)
    grad_up = jnp.einsum("bld,blf->df", mid_low, pre_low, preferred_element_type=jnp.float32)
    grad_mid = DEEP_ALPHA * grad_res_two + jnp.einsum(
        "blf,df->bld", pre_low, weights["w_up"], preferred_element_type=jnp.float32
    )
    grad_res_one, grad_gain_one, grad_shift_one = norm_backward(
        grad_mid, normed_one, inv_one, vec_part(vector, 3)
    )
    out_low = grad_res_one.astype(jnp.bfloat16)
    grad_out = jnp.einsum("bld,ble->de", attended, out_low, preferred_element_type=jnp.float32)
    grad_att = (
        jnp.einsum("ble,de->bld", out_low, weights["w_out"], preferred_element_type=jnp.float32)
        .astype(jnp.bfloat16)
        .reshape(batch_size, length, HEADS, HEAD_DIM)
    )
    grad_query, grad_key, grad_value, grad_gate, grad_rel = attention_backward(
        query_low,
        key_low,
        value_low,
        gate_vals,
        log_total,
        grad_att,
        rel_offsets,
        positions,
        key_valid,
    )
    grad_query = grad_query.reshape(batch_size, length, D)
    grad_key = grad_key.reshape(batch_size, length, D)
    grad_value = grad_value.reshape(batch_size, length, D)
    grad_heads, grad_gate_proj, grad_gate_scale = gate_backward(
        grad_gate, gate_pair, in_low, weights
    )
    proj_low = jnp.concatenate([grad_query, grad_key, grad_value], axis=-1).astype(jnp.bfloat16)
    grad_qkv = jnp.einsum("bld,ble->de", in_low, proj_low, preferred_element_type=jnp.float32)
    grad_hidden = (
        DEEP_ALPHA * grad_res_one
        + jnp.einsum("ble,de->bld", proj_low, weights["w_qkv"], preferred_element_type=jnp.float32)
        + grad_heads
    )
    grad_vec = jnp.concatenate(
        [
            jnp.sum(grad_query, axis=(0, 1)),
            jnp.sum(grad_value, axis=(0, 1)),
            jnp.sum(grad_res_one, axis=(0, 1)),
            grad_gain_one,
            grad_shift_one,
            jnp.sum(grad_res_two, axis=(0, 1)),
            grad_gain_two,
            grad_shift_two,
            jnp.sum(grad_pre, axis=(0, 1)),
        ]
    )
    grad_map = {
        "w_qkv": grad_qkv,
        "w_out": grad_out,
        "w_up": grad_up,
        "w_down": grad_down,
        "layer_vec": grad_vec,
        "gate_proj": grad_gate_proj,
        "gate_scale": grad_gate_scale,
    }
    return (grad_hidden, grad_map, grad_rel)


def merge_stats(first_part, second_part):
    new_top = jnp.maximum(first_part[0], second_part[0])
    new_total = first_part[1] * jnp.exp(first_part[0] - new_top) + second_part[1] * jnp.exp(
        second_part[0] - new_top
    )
    return (new_top, new_total, first_part[2] + second_part[2])


def head_pass(hidden, pieces, codebook, target_codes):
    row_low = hidden.reshape(-1, D).astype(jnp.bfloat16)
    projected = jnp.dot(row_low, pieces["w_head"], preferred_element_type=jnp.float32)
    inv_len = lax.rsqrt(jnp.sum(projected * projected, axis=-1, keepdims=True) + UNIT_EPSILON)
    unit_rows = projected * inv_len
    unit_low = unit_rows.astype(jnp.bfloat16)
    live_rows = (target_codes >= 0).astype(jnp.float32)
    local_count = codebook.shape[0]
    first_code = lax.axis_index("code") * local_count
    logits = LOGIT_SCALE * jnp.einsum(
        "rp,cp->rc", unit_low, codebook, preferred_element_type=jnp.float32
    )
    target_hits = (
        target_codes[:, None] - first_code == jnp.arange(local_count, dtype=jnp.int32)[None, :]
    ).astype(jnp.float32)
    local_top = jnp.max(logits, axis=1)
    local_total = jnp.sum(jnp.exp(logits - local_top[:, None]), axis=1)
    local_pick = jnp.sum(logits * target_hits, axis=1)
    top_all, total_all, pick_all = combined_all(
        (local_top, local_total, local_pick), "code", merge_stats
    )
    log_total = top_all + jnp.log(total_all)
    loss_local = jnp.sum((log_total - pick_all) * live_rows)
    grad_logits = (
        (jnp.exp(logits - log_total[:, None]) - target_hits) * live_rows[:, None] * LOGIT_SCALE
    ).astype(jnp.bfloat16)
    grad_terms = jnp.einsum("rc,cp->rp", grad_logits, codebook, preferred_element_type=jnp.float32)
    grad_unit = lax.psum(grad_terms, "code")
    grad_proj = (
        grad_unit - unit_rows * jnp.sum(unit_rows * grad_unit, axis=-1, keepdims=True)
    ) * inv_len
    proj_low = grad_proj.astype(jnp.bfloat16)
    grad_head = jnp.einsum("rd,rp->dp", row_low, proj_low, preferred_element_type=jnp.float32)
    grad_rows = jnp.einsum(
        "rp,dp->rd", proj_low, pieces["w_head"], preferred_element_type=jnp.float32
    )
    return (loss_local, grad_rows.reshape(hidden.shape), grad_head)


def local(
    patches,
    lengths,
    patch_masks,
    targets,
    codebook,
    params,
    first_moment,
    second_moment,
    step_count,
):
    own_low = params.astype(jnp.bfloat16)
    full_low = lax.all_gather(own_low, ("dp", "code"), axis=0, tiled=True)
    pieces = unpack(full_low)
    live_slot, visible, seen_place, seen_valid, rank_place = clip_layout(lengths, patch_masks)
    live_float = live_slot.astype(jnp.float32)[..., None]
    onehot = jnp.asarray(bucket_onehot())
    rel_offsets = jnp.dot(onehot, pieces["rel_table"].astype(jnp.float32), precision=HIGHEST)
    glob_vec = pieces["glob_vec"].astype(jnp.float32)
    embedded = jnp.einsum(
        "btp,pd->btd", patches, pieces["w_patch"], preferred_element_type=jnp.float32
    )
    normed_rows, normed_zero, inv_zero = norm_forward(embedded, glob_vec[0], glob_vec[1])
    start_rows = normed_rows * live_float
    conv_in = start_rows.astype(jnp.bfloat16)
    conv_pre = conv_forward(conv_in, pieces["conv_w"]) + glob_vec[2]
    full_rows = start_rows + jax.nn.gelu(conv_pre, approximate=False)
    seen_rows = jnp.take_along_axis(full_rows, seen_place[..., None], axis=1)
    encoded, kept_first = layer_forward(
        seen_rows, seen_place, seen_valid, layer_weights(pieces, 0), rel_offsets
    )
    placed = jnp.take_along_axis(encoded, rank_place[..., None], axis=1)
    hidden = jnp.where(visible[..., None], placed, glob_vec[3])
    positions = jnp.arange(LONG, dtype=jnp.int32)[None, :]
    layer_index = 1
    hidden, kept_vals = layer_forward(
        hidden, positions, live_slot, layer_weights(pieces, layer_index), rel_offsets
    )
    kept_rest = [kept_vals]
    target_codes = jnp.where(patch_masks == 1, targets, -1).reshape(-1)
    loss_local, upstream, grad_head = head_pass(hidden, pieces, codebook, target_codes)
    layer_grads = [None] * LAYERS
    rel_total = jnp.zeros_like(rel_offsets)
    layer_index = 1
    upstream, grad_map, grad_rel = layer_backward(
        upstream,
        kept_rest[layer_index - 1],
        layer_weights(pieces, layer_index),
        rel_offsets,
        positions,
        live_slot,
    )
    layer_grads[layer_index] = grad_map
    rel_total = rel_total + grad_rel
    grad_mask_emb = jnp.sum(jnp.where(visible[..., None], 0.0, upstream), axis=(0, 1))
    grad_encoded = jnp.take_along_axis(upstream, seen_place[..., None], axis=1) * seen_valid[
        ..., None
    ].astype(jnp.float32)
    grad_seen, grad_map, grad_rel = layer_backward(
        grad_encoded, kept_first, layer_weights(pieces, 0), rel_offsets, seen_place, seen_valid
    )
    layer_grads[0] = grad_map
    rel_total = rel_total + grad_rel
    grad_full = jnp.where(
        visible[..., None], jnp.take_along_axis(grad_seen, rank_place[..., None], axis=1), 0.0
    )
    grad_conv = grad_full * gelu_grad(conv_pre)
    grad_conv_in, grad_kernel = conv_backward(
        conv_in, pieces["conv_w"], grad_conv.astype(jnp.bfloat16)
    )
    grad_start = (grad_full + grad_conv_in) * live_float
    grad_embedded, grad_gain_zero, grad_shift_zero = norm_backward(
        grad_start, normed_zero, inv_zero, glob_vec[0]
    )
    grad_patch = jnp.einsum(
        "btp,btd->pd",
        patches,
        grad_embedded.astype(jnp.bfloat16),
        preferred_element_type=jnp.float32,
    )
    all_grads = {
        "w_patch": grad_patch,
        "glob_vec": jnp.stack(
            [grad_gain_zero, grad_shift_zero, jnp.sum(grad_conv, axis=(0, 1)), grad_mask_emb]
        ),
        "conv_w": grad_kernel,
        "rel_table": jnp.dot(jnp.transpose(onehot), rel_total, precision=HIGHEST),
        "w_head": grad_head,
    }
    for seg_name in LAYER_KEYS:
        all_grads[seg_name] = jnp.stack(
            [layer_grads[layer_index][seg_name] for layer_index in range(LAYERS)]
        )
    flat_grad = jnp.concatenate([all_grads[seg_name].reshape(-1) for seg_name, _ in layout()])
    flat_grad = jnp.pad(flat_grad, (0, full_low.shape[0] - flat_grad.shape[0]))
    dp_count = lax.axis_size("dp")
    code_count = lax.axis_size("code")
    shard_len = full_low.shape[0] // (dp_count * code_count)
    arranged = flat_grad.reshape(dp_count, code_count, shard_len)
    own_part = lax.dynamic_slice_in_dim(arranged, lax.axis_index("code"), 1, 1).reshape(-1)
    reduced = lax.psum_scatter(
        own_part.astype(jnp.bfloat16), "dp", scatter_dimension=0, tiled=True
    ).astype(jnp.float32)
    leader = (lax.axis_index("code") == 0).astype(jnp.float32)
    count_local = jnp.sum((target_codes >= 0).astype(jnp.float32))
    loss_all, squares_all, count_all, rel_all = lax.psum(
        (
            loss_local * leader,
            jnp.sum(reduced * reduced),
            count_local * leader,
            all_grads["rel_table"] * leader,
        ),
        ("dp", "code"),
    )
    grad_norm = jnp.sqrt(squares_all) / count_all
    clip_factor = jnp.minimum(1.0, CLIP_NORM / grad_norm)
    clipped = reduced / count_all * clip_factor
    rel_grad = rel_all / count_all * clip_factor
    step_value = step_count[0].astype(jnp.float32)
    new_first = BETA_ONE * first_moment + (1.0 - BETA_ONE) * clipped
    new_second = BETA_TWO * second_moment + (1.0 - BETA_TWO) * clipped * clipped
    first_hat = new_first / (1.0 - BETA_ONE**step_value)
    second_hat = new_second / (1.0 - BETA_TWO**step_value)
    new_params = params - LEARN_RATE * (
        first_hat / (jnp.sqrt(second_hat) + ADAM_EPSILON) + WEIGHT_DECAY * params
    )
    return (
        new_params,
        new_first,
        new_second,
        new_params.astype(jnp.bfloat16),
        loss_all / count_all,
        grad_norm,
        rel_grad,
    )


def solution(mesh):
    placed = (
        P("dp", None, None),
        P("dp"),
        P("dp", None),
        P("dp", None),
        P("code", None),
        P(("dp", "code")),
        P(("dp", "code")),
        P(("dp", "code")),
        P(),
    )
    return jax.shard_map(
        local,
        mesh=mesh,
        in_specs=placed,
        out_specs=(
            P(("dp", "code")),
            P(("dp", "code")),
            P(("dp", "code")),
            P(("dp", "code")),
            P(),
            P(),
            P(),
        ),
        check_vma=False,
    )
```

profile of v0, /device:TPU:0, one launch (start us, length us, event | category | flops | bytes accessed | tf_op | source)
XLA Modules:
  0.0 5969.0 jit_solution(11465249572701383800)
XLA Ops:
  9.1 14.5 reshape.2100
  43.8 388.3 %all-gather.6.cloned.1.call-done = bf16[32,1,603008]{2,1,0:T(2,128)(2,1)} async-done(((bf16[1,1,603008]{2,1,0:T(2,128)(2,1)}), bf16[32,1,603008]{2,1,0:T(2,128)(2,1)}) %all-gather.6.cloned.1.call-update) | async-done | bytes 38592528 | tf_op jit(solution)/shard_map/all_gather | solution.py:506
  432.1 208.8 %reduce.60 = bf16[32,603008]{1,0:T(8,128)(2,1)} reduce(bf16[32,1,603008]{2,1,0:T(2,128)(2,1)} %all-gather.6.cloned.1.call-done, bf16[]{:T(256)} %constant.469), dimensions={1}, to_apply=%all-gather.3.reduce_sub_computation | reduce | bytes 77185024 | tf_op jit(solution)/shard_map/all_gather | solution.py:506
  640.9 87.6 %reshape.2101 = bf16[19296256]{0:T(1024)(128)(2,1)} reshape(bf16[32,603008]{1,0:T(8,128)(2,1)} %reduce.60) | data formatting | bytes 77185024
  742.5 5.2 fusion.199
  747.8 9.1 slice.340
  756.9 13.8 fusion.196
  774.6 7.6 copy.177
  782.2 33.0 reshape.1955
  815.3 324.4 %fusion = f32[1,496,16,48]{3,0,2,1:T(1,128)} fusion(bf16[1,496,16,48]{3,0,2,1:T(2,128)(2,1)} %copy.177, bf16[128,48,16,48]{3,2,1,0:T(8,128)(2,1)} %reshape.1955), kind=kOutput, calls=%fused_computation.12 | convolution fusion | flops 4378853376 | bytes 11722752 | tf_op jit(solution)/shard_map/conv_general_dilated | solution.py:147
  1139.7 8.8 copy.179
  1151.1 5.0 fusion.46
  1167.5 8.0 squeeze.150
  1175.5 7.6 squeeze.156
  1183.1 29.5 gather_fusion.1
  1212.6 5.2 copy.189
  1221.7 9.5 squeeze.161
  1231.2 8.2 squeeze.160
  1239.5 9.2 squeeze.155
  1248.7 20.6 squeeze.154
  1276.0 5.8 fusion.32
  1295.8 494.8 %gather_fusion.3 = f32[246016,12]{1,0:T(8,128)} fusion(f32[12,991]{0,1:T(8,128)S(1)} %copy.188, s32[246784]{0:T(1024)} %pad_clamp_fusion), kind=kCustom, calls=%fused_computation.3.clone | custom fusion | bytes 24601600 | tf_op jit(solution)/shard_map/jit(_take)/gather | solution.py:107
  1790.6 71.8 %copy.201 = f32[496,496,12]{0,1,2:T(8,128)} copy(f32[496,496,12]{2,1,0:T(8,128)} %bitcast.55) | data formatting | bytes 23617536 | tf_op jit(solution)/shard_map/jit(_take)/gather | solution.py:107
  1862.4 6.3 fusion.209
  1876.7 19.4 fusion.6
  1903.0 17.0 all-reduce.6
  1929.7 39.7 copy.218
  1969.4 139.9 %rev.5 = bf16[128,48,768]{0,2,1:T(8,128)(2,1)} reverse(bf16[128,48,768]{0,2,1:T(8,128)(2,1)} %bitcast.558), dimensions={0} | reverse | bytes 18874368 | tf_op jit(solution)/shard_map/rev | solution.py:160
  2109.3 33.9 copy.220
  2150.1 7.7 fusion.213
  2161.4 5.0 convolution_bitcast_fusion.2
  2175.6 8.1 bitcast_convert_fusion
  2183.6 8.8 multiply_reduce_fusion.1
  2192.4 13.7 multiply_bitcast_fusion
  2206.2 11.2 multiply_reduce_fusion
  2217.4 7.5 fusion.78
  2233.8 5.6 fusion.61
  2242.3 4.9 fusion.214
  2326.4 5.3 reshape.1986
  2340.1 6.6 pad_maximum_fusion.2
  2346.8 14.0 reshape.1985
  2360.8 7.5 copy.219
  2368.3 664.7 %fusion.216 = bf16[48,128,16,48]{3,0,2,1:T(8,128)(2,1)} fusion(bf16[1,496,16,48]{3,0,2,1:T(2,128)(2,1)} %copy.177, bf16[1,496,16,48]{3,0,2,1:T(2,128)(2,1)} %copy.219), kind=kOutput, calls=%fused_computation.472 | convolution fusion | flops 4378853376 | bytes 10960896 | tf_op jit(solution)/shard_map/conv_general_dilated | solution.py:172
  3033.0 323.9 %fusion.215 = f32[1,496,16,48]{3,0,2,1:T(1,128)} fusion(bf16[1,496,16,48]{3,0,2,1:T(2,128)(2,1)S(1)} %copy-done.47, bf16[128,48,16,48]{3,1,2,0:T(8,128)(2,1)} %copy.220), kind=kOutput, calls=%fused_computation.471 | convolution fusion | flops 4378853376 | bytes 11722752 | tf_op jit(solution)/shard_map/conv_general_dilated | solution.py:163
  3357.0 10.3 copy.221
  3376.0 8.3 pad_maximum_fusion
  3384.3 9.8 copy.260
  3394.1 8.3 pad_maximum_fusion.1
  3402.4 16.9 reshape.1988
  3419.2 4.7 copy.234
  3423.9 30.5 copy.226
  3454.5 12.9 copy.227
  3467.3 16.8 reshape.1984
  3484.2 62.8 %copy.254 = f32[496,496,12]{2,1,0:T(8,128)} copy(f32[496,496,12]{0,1,2:T(8,128)} %get-tuple-element.341) | data formatting | bytes 23617536 | tf_op jit(solution)/shard_map/while/body/eval_jaxpr/transpose(jvp())/transpose | solution.py:107
  3547.0 85.5 %scatter_custom_fusion.1 = f32[12,991]{0,1:T(8,128)S(1)} fusion(s32[15376]{0:T(1024)} %reshape.2064, f32[15376,12]{1,0:T(8,128)} %copy.234, f32[]{:T(128)} %constant.169.clone.1), kind=kCustom, calls=%fused_computation.290 | custom fusion | flops 184512 | bytes 48080 | tf_op jit(solution)/shard_map/while/body/eval_jaxpr/transpose(jvp(jit(_take)))/scatter-add | solution.py:107
  3632.6 1309.0 %scatter_custom_fusion = f32[12,991]{0,1:T(8,128)} fusion(s32[246016]{0:T(1024)} %reshape.2056, f32[246016,12]{1,0:T(8,128)} %bitcast.154, f32[]{:T(128)} %constant.169.clone.1), kind=kCustom, calls=%fused_computation.292 | custom fusion | flops 2952192 | bytes 48080 | tf_op jit(solution)/shard_map/while/body/eval_jaxpr/transpose(jvp(jit(_take)))/scatter-add | solution.py:107
  4945.9 534.9 %concatenate.55 = bf16[19293992]{0:T(1024)(128)(2,1)} concatenate(bf16[196608]{0:T(1024)(128)(2,1)} %reshape.1982, bf16[3072]{0:T(1024)(128)(2,1)} %reshape.1983, bf16[4718592]{0:T(1024)(128)(2,1)} %reshape.1984, bf16[3538944]{0:T(1024)(128)(2,1)} %reshape.1985, bf16[1179648]{0:T(1024)(128)(2,1)S(1)} %copy-done.20, bf16[4718592]{0:T(1024)(128)(2,1)} %bitcast.557, ...), dimensions={0} | concatenate | bytes 77175968 | tf_op jit(solution)/shard_map/concatenate | solution.py:587
  5480.7 26.6 pad.4
  5507.3 76.6 %reshape.1995 = bf16[8,4,603008]{2,1,0:T(4,128)(2,1)} reshape(bf16[19296256]{0:T(1024)(128)(2,1)} %pad.4) | data formatting | bytes 77185024 | tf_op jit(solution)/shard_map/reshape | solution.py:592
  5583.9 162.0 %convert_reduce_fusion = bf16[8,603008]{1,0:T(8,128)(2,1)} fusion(bf16[8,4,603008]{2,1,0:T(4,128)(2,1)} %reshape.1995, s32[]{:T(128)S(6)} %select_n.195), kind=kLoop, calls=%fused_computation.14 | loop fusion | bytes 19296260 | tf_op jit(solution)/shard_map/convert_element_type | solution.py:595
  5745.8 21.9 convert_element_type.302
  5771.0 134.7 %all-reduce.12.cloned.1.call-done = bf16[4824064]{0:T(1024)(128)(2,1)} async-done(((bf16[4824064]{0:T(1024)(128)(2,1)}), bf16[4824064]{0:T(1024)(128)(2,1)}) %all-reduce.12.cloned.1.call-update) | async-done | bytes 9648144
  5908.3 40.0 all-reduce.5
  5952.9 7.1 fusion.184
  (691 shorter events, 236.3 us)
Async XLA Ops:
  7.2 765.2 %copy-start = (bf16[1,496,256]{2,1,0:T(8,128)(2,1)S(1)}, bf16[1,496,256]{2,1,0:T(8,128)(2,1)}, u32[]{:S(2)}) copy-start(bf16[1,496,256]{2,1,0:T(8,128)(2,1)} %param.20) | copy-start | bytes 761860
  7.2 425.0 %all-gather.6.cloned.1.call-start = ((), (), s32[]{:S(2)}) async-start(), calls=%async_computation.1 | async-start | bytes 79597056 | tf_op jit(solution)/shard_map/all_gather | solution.py:506
  23.6 2119.6 %all-reduce.10.cloned.1.call-start = ((), (), s32[]{:S(2)}) async-start(), calls=%async_computation | async-start | bytes 1015808 | tf_op jit(solution)/shard_map/psum | solution.py:482
  38.7 734.5 %copy-start.122 = (f32[496]{0:T(512)}, f32[496]{0:T(512)S(1)}, u32[]{:S(2)}) copy-start(f32[496]{0:T(512)S(1)} %fusion.170) | copy-start | bytes 5956
  1159.1 110.3 %copy-start.45 = (bf16[1,124,768]{2,1,0:T(8,128)(2,1)}, bf16[1,124,768]{2,1,0:T(8,128)(2,1)S(1)}, u32[]{:S(2)}) copy-start(bf16[1,124,768]{2,1,0:T(8,128)(2,1)S(1)} %fusion.126) | copy-start | bytes 571396
  1159.6 109.7 %copy-start.111 = (f32[1,124,12,2]{1,3,2,0:T(2,128)}, f32[1,124,12,2]{1,3,2,0:T(2,128)S(1)}, u32[]{:S(2)}) copy-start(f32[1,124,12,2]{1,3,2,0:T(2,128)S(1)} %fusion.286) | copy-start | bytes 35716
  1159.6 109.7 %copy-start.113 = (f32[124,12,2]{0,2,1:T(2,128)}, f32[124,12,2]{0,2,1:T(2,128)S(1)}, u32[]{:S(2)}) copy-start(f32[124,12,2]{0,2,1:T(2,128)S(1)} %add_divide_fusion) | copy-start | bytes 35716
  1159.8 127.7 %copy-start.94 = (bf16[64,8]{1,0:T(8,128)(2,1)}, bf16[64,8]{1,0:T(8,128)(2,1)S(1)}, u32[]{:S(2)}) copy-start(bf16[64,8]{1,0:T(8,128)(2,1)S(1)} %slice.305) | copy-start | bytes 3076
  1161.1 5.3 copy-start.44
  1167.4 107.7 %copy-start.15 = (bf16[768,768]{1,0:T(8,128)(2,1)}, bf16[768,768]{1,0:T(8,128)(2,1)S(1)}, u32[]{:S(2)}) copy-start(bf16[768,768]{1,0:T(8,128)(2,1)S(1)} %squeeze.153) | copy-start | bytes 3538948
  1175.5 7.7 copy-start.85
  1221.7 51.1 copy-start.29
  1248.7 20.6 copy-start.175
  1275.2 6.6 slice-start.5
  1275.7 6.1 copy-start.10
  1275.7 6.1 copy-start.131
  1275.9 5.9 copy-start.146
  1276.0 5.8 slice-start.6
  1276.0 5.8 copy-start.138
  1293.8 568.6 %copy-start.25 = (bf16[1,496,768]{1,2,0:T(8,128)(2,1)}, bf16[1,496,768]{1,2,0:T(8,128)(2,1)S(1)}, u32[]{:S(2)}) copy-start(bf16[1,496,768]{1,2,0:T(8,128)(2,1)S(1)} %copy.193) | copy-start | bytes 2285572
  1294.1 568.3 %copy-start.23 = (bf16[1,496,768]{1,2,0:T(8,128)(2,1)}, bf16[1,496,768]{1,2,0:T(8,128)(2,1)S(1)}, u32[]{:S(2)}) copy-start(bf16[1,496,768]{1,2,0:T(8,128)(2,1)S(1)} %copy.194) | copy-start | bytes 2285572
  1295.8 574.8 %copy-start.27 = (bf16[1,496,768]{1,2,0:T(8,128)(2,1)}, bf16[1,496,768]{1,2,0:T(8,128)(2,1)S(1)}, u32[]{:S(2)}) copy-start(bf16[1,496,768]{1,2,0:T(8,128)(2,1)S(1)} %copy.192) | copy-start | bytes 2285572
  1790.6 71.8 %copy-start.62 = (pred[496,496]{0,1:T(8,128)(4,1)S(1)}, pred[496,496]{0,1:T(8,128)(4,1)}, u32[]{:S(2)}) copy-start(pred[496,496]{0,1:T(8,128)(4,1)} %copy.198) | copy-start | bytes 738052
  1790.6 71.8 %copy-start.157 = (f32[496]{0:T(512)S(1)}, f32[496]{0:T(512)}, u32[]{:S(2)}) copy-start(f32[496]{0:T(512)} %fusion.169) | copy-start | bytes 5956
  1875.3 20.9 slice-start.9
  1876.3 19.8 copy-start.35
  1876.6 19.5 copy-start.158
  1876.7 19.4 slice-start.10
  1876.7 19.4 copy-start.181
  1900.0 20.5 copy-start.178
  1900.0 21.1 copy-start.156
  1901.6 20.7 copy-start.129
  1922.3 3983.4 %all-reduce.12.cloned.1.call-start = ((), (), s32[]{:S(2)}) async-start(), calls=%async_computation.2 | async-start | bytes 19296256
  1922.4 5.7 copy-start.13
  2109.3 33.9 copy-start.22
  2148.3 9.6 slice-start.7
  2150.1 7.7 copy-start.36
  2150.1 7.7 slice-start.8
  2150.1 7.7 copy-start.159
  2175.5 8.1 copy-start.28
  2175.6 16.9 slice-start
  2175.6 16.8 slice-start.1
  2183.6 8.8 slice-start.2
  2192.4 13.7 copy-start.63
  2206.1 11.2 copy-start.26
  2217.4 8.2 copy-start.2
  2217.4 8.3 copy-start.24
  2239.5 7.7 slice-start.3
  2257.0 6.8 copy-start.80
  2257.9 5.9 copy-start.59
  2257.9 5.9 copy-start.78
  2257.9 5.9 copy-start.79
  2279.2 6.9 copy-start.120
  2283.6 35.3 copy-start.46
  2283.6 35.3 copy-start.68
  2326.4 5.3 copy-start.144
  2368.3 664.7 %copy-start.47 = (bf16[1,496,16,48]{3,0,2,1:T(2,128)(2,1)S(1)}, bf16[1,496,16,48]{3,0,2,1:T(2,128)(2,1)}, u32[]{:S(2)}) copy-start(bf16[1,496,16,48]{3,0,2,1:T(2,128)(2,1)} %copy.219) | copy-start | bytes 2285572
  3402.4 16.9 copy-start.48
  3632.5 1313.3 %copy-start.20 = (bf16[1179648]{0:T(1024)(128)(2,1)S(1)}, bf16[1179648]{0:T(1024)(128)(2,1)}, u32[]{:S(2)}) copy-start(bf16[1179648]{0:T(1024)(128)(2,1)} %reshape.1986) | copy-start | bytes 7077892
  3632.5 1313.3 %copy-start.75 = (bf16[96,2,8,128]{3,1,2,0:T(2,128)(2,1)S(1)}, bf16[96,2,8,128]{3,1,2,0:T(2,128)(2,1)}, u32[]{:S(2)}) copy-start(bf16[96,2,8,128]{3,1,2,0:T(2,128)(2,1)} %copy.262) | copy-start | bytes 1179652
  3632.6 1313.3 %copy-start.96 = (bf16[1,72,2,128]{3,1,2,0:T(8,128)(2,1)S(1)}, bf16[1,72,2,128]{3,1,2,0:T(8,128)(2,1)}, u32[]{:S(2)}) copy-start(bf16[1,72,2,128]{3,1,2,0:T(8,128)(2,1)} %copy.261) | copy-start | bytes 110596
  3632.6 1313.3 %copy-start.140 = (bf16[1040]{0:T(1024)(128)(2,1)S(1)}, bf16[1040]{0:T(1024)(128)(2,1)}, u32[]{:S(2)}) copy-start(bf16[1040]{0:T(1024)(128)(2,1)} %reshape.1991) | copy-start | bytes 6244
  5767.7 140.6 %copy-start.100 = (f32[320,12]{0,1:T(8,128)S(1)}, f32[320,12]{0,1:T(8,128)}, u32[]{:S(2)}) copy-start(f32[320,12]{0,1:T(8,128)} %get-tuple-element.457) | copy-start | bytes 46084
  5767.7 185.2 %copy-start.19 = (f32[603008]{0:T(1024)S(1)}, f32[603008]{0:T(1024)}, u32[]{:S(2)}) copy-start(f32[603008]{0:T(1024)} %param.25) | copy-start | bytes 7236100
  (143 other events, 344.1 us)
Sparse Core Ops, SparseCore 0:
  23.8 408.3 all-gather.5
  1922.4 35.3 all-reduce.9
  5767.9 137.7 all-reduce.11
where the time goes:
time: 6080 us; the launch traced here: 5970 us
  local copies, waits for them, and re-layouts  2180 us (36%)
  other arithmetic  1720 us (28%)
  matrix products  1460 us (24%)
  waiting for transfers between devices  523 us (9%)
    scatter-add x2, other arithmetic, position_bias(): return jnp.transpose(jnp.take(head_table, offset_idx, axis=1), (1, 0, 2, 3))  1390 us
    conv_general_dilated x1, matrix products, conv_backward(): lax.conv_general_dilated(conv_in, grad_low, (1,), [(KERNEL // 2, KERNEL /...  665 us
    gather x6, local copies, waits for them, and re-layouts, position_bias(): return jnp.transpose(jnp.take(head_table, offset_idx, axis=1), (1, 0, 2, 3))  605 us
    concatenate x1, local copies, waits for them, and re-layouts, local(): jnp.concatenate([all_grads[seg_name].reshape(-1) for seg_name, _ in layou...  535 us
    all_gather x1, waiting for transfers between devices, local(): full_low = lax.all_gather(own_low, ('dp', 'code'), axis=0, tiled=True)  388 us
    conv_general_dilated x1, matrix products, conv_forward(): lax.conv_general_dilated(conv_in, conv_weight, (1,), [(KERNEL // 2, KERNE...  324 us
    conv_general_dilated x1, matrix products, conv_backward(): lax.conv_general_dilated(grad_low, turned, (1,), [(KERNEL // 2 - 1, KERNE...  324 us
    all_gather x1, other arithmetic, local(): full_low = lax.all_gather(own_low, ('dp', 'code'), axis=0, tiled=True)  209 us
  transfers between devices with their start and end apart: 3, of which 2 were waited for; matrix products, arithmetic and copies ran while one was open for 4% of the time, Pallas kernels for 0%

commit v1 on v0

v1 whole, which is shorter than its diff:
```python
import functools
import math

import jax
import jax.numpy as jnp
import numpy as np
from jax import lax
from jax.experimental import pallas as pl
from jax.experimental.pallas import tpu as pltpu
from jax.sharding import PartitionSpec as P

D = 768
HEADS = 12
HEAD_DIM = 64
FF = 3072
PATCH_IN = 256
PROJ = 256
KERNEL = 128
GROUPS = 16
WIDTH = D // GROUPS
BUCKETS = 320
MAX_DIST = 800
LAYERS = 2
LONG = 496
VISIBLE = 124
ROWS = 512
SEEN = 128
SPAN = 1024

NORM_EPSILON = 1e-05
UNIT_EPSILON = 1e-06
DEEP_ALPHA = 2.2133638394006434
LOGIT_SCALE = 25.0
CLIP_NORM = 0.005
LEARN_RATE = 0.02
BETA_ONE = 0.9
BETA_TWO = 0.999
ADAM_EPSILON = 1e-10
WEIGHT_DECAY = 0.01
MASK_FILL = -1000000000.0
HIGHEST = lax.Precision.HIGHEST
BF = jnp.bfloat16
F32 = jnp.float32
VMEM_LIMIT = 56 << 20


def layout():
    return [
        ("w_patch", (PATCH_IN, D)),
        ("glob_vec", (4, D)),
        ("conv_w", (KERNEL, WIDTH, D)),
        ("w_qkv", (LAYERS, D, 3 * D)),
        ("w_out", (LAYERS, D, D)),
        ("w_up", (LAYERS, D, FF)),
        ("w_down", (LAYERS, FF, D)),
        ("layer_vec", (LAYERS, 8 * D + FF)),
        ("gate_proj", (LAYERS, HEAD_DIM + 1, 8)),
        ("gate_scale", (LAYERS, HEADS)),
        ("rel_table", (BUCKETS, HEADS)),
        ("w_head", (D, PROJ)),
    ]


def starts():
    where = {}
    offset = 0
    for seg_name, extent in layout():
        where[seg_name] = offset
        offset += math.prod(extent)
    return where


def bucket_onehot():
    offsets = np.arange(-(LONG - 1), LONG)
    half_count = BUCKETS // 2
    exact_count = half_count // 2
    distance = np.abs(offsets)
    scaled = (
        np.log(np.maximum(distance, 1) / exact_count)
        / np.log(MAX_DIST / exact_count)
        * (half_count - exact_count)
    )
    larger = np.minimum(exact_count + np.maximum(scaled, 0.0).astype(np.int64), half_count - 1)
    bucket = (offsets > 0) * half_count + np.where(distance < exact_count, distance, larger)
    return (bucket[:, None] == np.arange(BUCKETS)[None, :]).astype(np.float32)


def span_onehot():
    shift = SPAN // 2 - (LONG - 1)
    table = np.zeros((SPAN, BUCKETS), np.float32)
    table[shift : shift + 2 * LONG - 1] = bucket_onehot()
    return table


def params_of(grid_rank=1):
    return pltpu.CompilerParams(
        dimension_semantics=("arbitrary",) * grid_rank, vmem_limit_bytes=VMEM_LIMIT
    )


def dot_nn(left, right):
    return lax.dot_general(left, right, (((1,), (0,)), ((), ())), preferred_element_type=F32)


def dot_nt(left, right):
    return lax.dot_general(left, right, (((1,), (1,)), ((), ())), preferred_element_type=F32)


def dot_tn(left, right):
    return lax.dot_general(left, right, (((0,), (0,)), ((), ())), preferred_element_type=F32)


TAPS = 16
SLOT = 256


def lane_masks(width):
    group = np.arange(width)[None, :] // WIDTH
    return (group == np.arange(width // WIDTH)[:, None]).astype(np.float32)


def shifted_taps(source_ref, target_ref, count):
    for tap in range(TAPS):
        target_ref[:, tap * SLOT : (tap + 1) * SLOT] = source_ref[tap : tap + count, :].astype(BF)


def conv_forward_kernel(in_ref, weight_ref, mask_ref, out_ref, taps_ref, block_ref):
    step = pl.program_id(0)
    width = weight_ref.shape[1]

    @pl.when(step == 0)
    def _():
        shifted_taps(in_ref, taps_ref, taps_ref.shape[0])
        block_ref[...] = jnp.zeros_like(block_ref)

    for tap in range(TAPS):
        piece = weight_ref[tap * WIDTH : (tap + 1) * WIDTH, :]
        for group in range(width // WIDTH):
            low = tap * SLOT + group * WIDTH
            block_ref[low : low + WIDTH, :] = piece * mask_ref[group : group + 1, :]
    begin = pl.multiple_of(step * TAPS, TAPS)
    term = dot_nn(taps_ref[pl.ds(begin, ROWS), :], block_ref[...])

    @pl.when(step == 0)
    def _():
        out_ref[...] = term

    @pl.when(step > 0)
    def _():
        out_ref[...] += term


def conv_input_kernel(in_ref, weight_ref, mask_ref, out_ref, taps_ref, block_ref):
    step = pl.program_id(0)
    width = weight_ref.shape[1]

    @pl.when(step == 0)
    def _():
        shifted_taps(in_ref, taps_ref, taps_ref.shape[0])
        block_ref[...] = jnp.zeros_like(block_ref)

    for tap in range(TAPS):
        piece = weight_ref[tap * WIDTH : (tap + 1) * WIDTH, :]
        low = (TAPS - 1 - tap) * SLOT
        for group in range(width // WIDTH):
            block_ref[group * WIDTH : (group + 1) * WIDTH, low : low + width] = (
                piece * mask_ref[group : group + 1, :]
            )
    begin = pl.multiple_of((pl.num_programs(0) - 1 - step) * TAPS, TAPS)
    term = dot_nt(taps_ref[pl.ds(begin, ROWS), :], block_ref[...])

    @pl.when(step == 0)
    def _():
        out_ref[...] = term

    @pl.when(step > 0)
    def _():
        out_ref[...] += term


def conv_call(kernel, conv_in, weight, front, nt):
    width = weight.shape[1]
    steps = KERNEL // TAPS
    count = ROWS + KERNEL - TAPS
    padded = jnp.pad(
        conv_in.astype(F32),
        ((front, count + TAPS - front - conv_in.shape[0]), (0, SLOT - width)),
    )
    block = (width, TAPS * SLOT) if nt else (TAPS * SLOT, width)
    return pl.pallas_call(
        kernel,
        grid=(steps,),
        in_specs=[
            pl.BlockSpec(padded.shape, lambda i: (0, 0)),
            pl.BlockSpec((TAPS * WIDTH, width), lambda i: (i, 0)),
            pl.BlockSpec((width // WIDTH, width), lambda i: (0, 0)),
        ],
        out_specs=pl.BlockSpec((ROWS, width), lambda i: (0, 0)),
        out_shape=jax.ShapeDtypeStruct((ROWS, width), F32),
        scratch_shapes=[pltpu.VMEM((count, TAPS * SLOT), BF), pltpu.VMEM(block, BF)],
        compiler_params=params_of(),
    )(padded, weight, jnp.asarray(lane_masks(width), BF))


def conv_weight_kernel(in_ref, grad_ref, mask_ref, out_ref, taps_ref):
    width = grad_ref.shape[2]

    @pl.when(pl.program_id(1) == 0)
    def _():
        shifted_taps(in_ref.at[0], taps_ref, taps_ref.shape[0])

    begin = pl.multiple_of(pl.program_id(1) * TAPS, TAPS)
    term = dot_tn(taps_ref[pl.ds(begin, ROWS), :], grad_ref[0])
    for tap in range(TAPS):
        total = None
        for group in range(width // WIDTH):
            low = tap * SLOT + group * WIDTH
            piece = term[low : low + WIDTH, :] * mask_ref[group : group + 1, :]
            total = piece if total is None else total + piece
        out_ref[0, tap * WIDTH : (tap + 1) * WIDTH, :] = total.astype(BF)


def conv_weight_grad(conv_in, grad_low):
    width = 4 * WIDTH
    parts = D // width
    count = ROWS + KERNEL - TAPS
    front = KERNEL // 2
    padded = jnp.pad(
        conv_in.astype(F32), ((front, count + TAPS - front - conv_in.shape[0]), (0, 0))
    )
    padded = jnp.pad(
        jnp.transpose(padded.reshape(-1, parts, width), (1, 0, 2)),
        ((0, 0), (0, 0), (0, SLOT - width)),
    )
    grads = jnp.transpose(grad_low.reshape(ROWS, parts, width), (1, 0, 2))
    out = pl.pallas_call(
        conv_weight_kernel,
        grid=(parts, KERNEL // TAPS),
        in_specs=[
            pl.BlockSpec((1,) + padded.shape[1:], lambda p, i: (p, 0, 0)),
            pl.BlockSpec((1, ROWS, width), lambda p, i: (p, 0, 0)),
            pl.BlockSpec((width // WIDTH, width), lambda p, i: (0, 0)),
        ],
        out_specs=pl.BlockSpec((1, TAPS * WIDTH, width), lambda p, i: (p, i, 0)),
        out_shape=jax.ShapeDtypeStruct((parts, KERNEL * WIDTH, width), BF),
        scratch_shapes=[pltpu.VMEM((count, TAPS * SLOT), BF)],
        compiler_params=params_of(2),
    )(padded, grads, jnp.asarray(lane_masks(width), F32))
    return jnp.transpose(out, (1, 0, 2)).reshape(KERNEL * WIDTH, D)


BLOCK = 128


def head_column(table, head):
    lane = lax.broadcasted_iota(jnp.int32, (1, BLOCK), 1)
    return jnp.sum(jnp.where(lane == head, table, 0.0), axis=1, keepdims=True)


def toeplitz(span_ref, head):
    row = jnp.broadcast_to(span_ref[pl.ds(head, 1), :], (BLOCK, SPAN))
    return pltpu.roll(row, 0, 1, stride=1, stride_axis=0)


def seen_bias(turned, select):
    rows = [turned[:, ROWS - low : SPAN - low] for low in range(0, ROWS, BLOCK)]
    table = jnp.concatenate(rows, axis=0).astype(BF)
    return dot_nt(dot_nn(select, table).astype(BF), select)


def attention_forward_kernel(*refs, picked):
    if picked:
        q_ref, k_ref, v_ref, gate_ref, span_ref, fill_ref, pick_ref, out_ref, lse_ref = refs
    else:
        q_ref, k_ref, v_ref, gate_ref, span_ref, fill_ref, out_ref, lse_ref = refs
    step = pl.program_id(0)
    length = q_ref.shape[0]
    lane = lax.broadcasted_iota(jnp.int32, (1, BLOCK), 1)

    @pl.when(step == 0)
    def _():
        lse_ref[...] = jnp.zeros_like(lse_ref)

    fill = fill_ref[0:1, :]
    for side in range(2):
        head = step * 2 + side
        cols = slice(side * HEAD_DIM, (side + 1) * HEAD_DIM)
        keys = k_ref[:, cols]
        vals = v_ref[:, cols]
        turned = toeplitz(span_ref, head)
        if picked:
            single = seen_bias(turned, pick_ref[...])
        for low in range(0, length, BLOCK):
            rows = slice(low, low + BLOCK)
            bias = single if picked else turned[:, ROWS - low : SPAN - low]
            gate = head_column(gate_ref[rows, :], head)
            scores = dot_nt(q_ref[rows, cols], keys) + gate * bias + fill
            top = jnp.max(scores, axis=1, keepdims=True)
            weights = jnp.exp(scores - top)
            total = jnp.sum(weights, axis=1, keepdims=True)
            probs = (weights * (1.0 / total)).astype(BF)
            out_ref[rows, cols] = dot_nn(probs, vals).astype(BF)
            lse_ref[rows, :] += jnp.where(lane == head, top + jnp.log(total), 0.0)


def pair_spec(length):
    return pl.BlockSpec((length, 2 * HEAD_DIM), lambda i: (0, i))


def whole_spec(shape):
    return pl.BlockSpec(shape, lambda i: (0,) * len(shape))


def attention_forward(query, keyv, value, gate, span, fill, pick):
    length = query.shape[0]
    args = [query, keyv, value, gate, span, fill] + ([] if pick is None else [pick])
    return pl.pallas_call(
        functools.partial(attention_forward_kernel, picked=pick is not None),
        grid=(HEADS // 2,),
        in_specs=[pair_spec(length)] * 3 + [whole_spec(a.shape) for a in args[3:]],
        out_specs=[pair_spec(length), whole_spec((length, BLOCK))],
        out_shape=[
            jax.ShapeDtypeStruct((length, D), BF),
            jax.ShapeDtypeStruct((length, BLOCK), F32),
        ],
        compiler_params=params_of(),
    )(*args)


def attention_backward_kernel(*refs, picked):
    if picked:
        (q_ref, k_ref, v_ref, up_ref, gate_ref, span_ref, fill_ref, lse_ref, pick_ref) = refs[:9]
    else:
        (q_ref, k_ref, v_ref, up_ref, gate_ref, span_ref, fill_ref, lse_ref) = refs[:8]
    out_ref, sum_ref, dgate_ref, dspan_ref, key_ref, val_ref, diag_ref = refs[-7:]
    step = pl.program_id(0)
    length = q_ref.shape[0]
    lane = lax.broadcasted_iota(jnp.int32, (1, BLOCK), 1)

    @pl.when(step == 0)
    def _():
        dgate_ref[...] = jnp.zeros_like(dgate_ref)
        dspan_ref[...] = jnp.zeros_like(dspan_ref)

    fill = fill_ref[0:1, :]
    for side in range(2):
        head = step * 2 + side
        cols = slice(side * HEAD_DIM, (side + 1) * HEAD_DIM)
        keys = k_ref[:, cols]
        vals = v_ref[:, cols]
        turned = toeplitz(span_ref, head)
        if picked:
            single = seen_bias(turned, pick_ref[...])
        query_sum = jnp.zeros((1, HEAD_DIM), F32)
        diag_ref[...] = jnp.zeros_like(diag_ref)
        for low in range(0, length, BLOCK):
            rows = slice(low, low + BLOCK)
            query = q_ref[rows, cols]
            upstream = up_ref[rows, cols]
            bias = single if picked else turned[:, ROWS - low : SPAN - low]
            gate = head_column(gate_ref[rows, :], head)
            lse = head_column(lse_ref[rows, :], head)
            probs = jnp.exp(dot_nt(query, keys) + gate * bias + fill - lse)
            grad_probs = dot_nt(upstream, vals)
            grad_scores = probs * (
                grad_probs - jnp.sum(probs * grad_probs, axis=1, keepdims=True)
            )
            dgate = jnp.sum(grad_scores * bias, axis=1, keepdims=True)
            dgate_ref[rows, :] += jnp.where(lane == head, dgate, 0.0)
            grad_bias = grad_scores * gate
            if picked:
                select = pick_ref[...]
                high = grad_bias.astype(BF)
                rest = (grad_bias - high.astype(F32)).astype(BF)
                table = dot_tn(select, dot_nn(high, select).astype(BF)) + dot_tn(
                    select, dot_nn(rest, select).astype(BF)
                )
                for base in range(0, ROWS, BLOCK):
                    diag_ref[:, ROWS - base : SPAN - base] += table[base : base + BLOCK, :]
            else:
                diag_ref[:, ROWS - low : SPAN - low] += grad_bias
            low_scores = grad_scores.astype(BF)
            grad_query = dot_nn(low_scores, keys) * HEAD_DIM ** (-0.5)
            query_sum += jnp.sum(grad_query, axis=0, keepdims=True)
            out_ref[0, rows, cols] = grad_query.astype(BF)
            key_term = dot_tn(low_scores, query)
            val_term = dot_tn(probs.astype(BF), upstream)
            if low == 0:
                key_ref[...] = key_term
                val_ref[...] = val_term
            else:
                key_ref[...] += key_term
                val_ref[...] += val_term
        out_ref[1, :, cols] = key_ref[...].astype(BF)
        out_ref[2, :, cols] = val_ref[...].astype(BF)
        sum_ref[0:1, cols] = query_sum
        sum_ref[1:2, cols] = jnp.sum(val_ref[...], axis=0, keepdims=True)
        turn = diag_ref[...]
        half = BLOCK // 2
        while half:
            turn = turn[:half, :] + pltpu.roll(turn[half:, :], SPAN - half, 1)
            half //= 2
        dspan_ref[pl.ds(head, 1), :] = turn


def attention_backward(query, keyv, value, upstream, gate, span, fill, lse, pick):
    length = query.shape[0]
    args = [query, keyv, value, upstream, gate, span, fill, lse]
    args = args + ([] if pick is None else [pick])
    return pl.pallas_call(
        functools.partial(attention_backward_kernel, picked=pick is not None),
        grid=(HEADS // 2,),
        in_specs=[pair_spec(length)] * 4 + [whole_spec(a.shape) for a in args[4:]],
        out_specs=[
            pl.BlockSpec((3, length, 2 * HEAD_DIM), lambda i: (0, 0, i)),
            pl.BlockSpec((8, 2 * HEAD_DIM), lambda i: (0, i)),
            whole_spec((length, BLOCK)),
            whole_spec((16, SPAN)),
        ],
        out_shape=[
            jax.ShapeDtypeStruct((3, length, D), BF),
            jax.ShapeDtypeStruct((8, D), F32),
            jax.ShapeDtypeStruct((length, BLOCK), F32),
            jax.ShapeDtypeStruct((16, SPAN), F32),
        ],
        scratch_shapes=[
            pltpu.VMEM((length, HEAD_DIM), F32),
            pltpu.VMEM((length, HEAD_DIM), F32),
            pltpu.VMEM((BLOCK, SPAN), F32),
        ],
        compiler_params=params_of(),
    )(*args)


def weight_grad_kernel(left_ref, right_ref, out_ref, turn_ref):
    rows = left_ref.shape[1]
    strips = right_ref.shape[1] // 128
    grad = dot_tn(left_ref[...], right_ref[...])
    for strip in range(strips):
        turn_ref[pl.ds(strip, rows, stride=strips), :] = grad[:, strip * 128 : (strip + 1) * 128]
    out_ref[...] = turn_ref[...].astype(BF)


def weight_grad(left, right, rows=128):
    length, depth = left.shape
    strips = right.shape[1] // 128
    return pl.pallas_call(
        weight_grad_kernel,
        grid=(depth // rows,),
        in_specs=[
            pl.BlockSpec((length, rows), lambda i: (0, i)),
            pl.BlockSpec(right.shape, lambda i: (0, 0)),
        ],
        out_specs=pl.BlockSpec((rows * strips, 128), lambda i: (i, 0)),
        out_shape=jax.ShapeDtypeStruct((depth * strips, 128), BF),
        scratch_shapes=[pltpu.VMEM((rows * strips, 128), F32)],
        compiler_params=params_of(),
    )(left, right)


def norm_forward(before, norm_gain, norm_shift):
    centred = before - jnp.mean(before, axis=-1, keepdims=True)
    inv_std = lax.rsqrt(jnp.mean(centred * centred, axis=-1, keepdims=True) + NORM_EPSILON)
    normed = centred * inv_std
    return (normed * norm_gain + norm_shift, normed, inv_std)


def norm_backward(upstream, normed, inv_std, norm_gain):
    scaled = upstream * norm_gain
    centred_grad = (
        scaled
        - jnp.mean(scaled, axis=-1, keepdims=True)
        - normed * jnp.mean(scaled * normed, axis=-1, keepdims=True)
    )
    return (
        centred_grad * inv_std,
        jnp.sum(upstream * normed, axis=0),
        jnp.sum(upstream, axis=0),
    )


def gelu_grad(pre_act):
    return (
        0.5 * (1.0 + lax.erf(pre_act * 0.7071067811865476))
        + pre_act * jnp.exp(-0.5 * pre_act * pre_act) * 0.3989422804014327
    )


def vec_part(vector, slot_index):
    return vector[slot_index * D : (slot_index + 1) * D]


def head_spread():
    return (np.arange(D)[:, None] // HEAD_DIM == np.arange(HEADS)[None, :]).astype(np.float32)


def gate_forward(in_low, weights):
    gate_weight = weights["gate_proj"]
    spread = jnp.asarray(head_spread(), BF)
    columns = jnp.concatenate(
        [jnp.tile(gate_weight[:HEAD_DIM, e], HEADS)[:, None] * spread for e in range(8)], axis=1
    )
    logit = dot_nn(in_low, columns) + jnp.repeat(gate_weight[HEAD_DIM].astype(F32), HEADS)
    parts = [logit[:, e * HEADS : (e + 1) * HEADS] for e in range(8)]
    first = jax.nn.sigmoid(parts[0] + parts[1] + parts[2] + parts[3])
    second = jax.nn.sigmoid(parts[4] + parts[5] + parts[6] + parts[7])
    gate_vals = first * (second * weights["gate_scale"].astype(F32) - 1.0) + 2.0
    return (gate_vals, first, second)


def gate_backward(grad_gate, first, second, in_low, weights):
    scale_vec = weights["gate_scale"].astype(F32)
    grad_scale = jnp.sum(grad_gate * first * second, axis=0)
    grad_one = grad_gate * (second * scale_vec - 1.0) * first * (1.0 - first)
    grad_two = grad_gate * first * scale_vec * second * (1.0 - second)
    both = jnp.concatenate([grad_one, grad_two], axis=1)
    spread = jnp.asarray(head_spread())
    product = lax.dot_general(
        in_low.astype(F32), both, (((0,), (0,)), ((), ())), precision=HIGHEST
    )
    proj_one = jnp.sum((product[:, :HEADS] * spread).reshape(HEADS, HEAD_DIM, HEADS), axis=(0, 2))
    proj_two = jnp.sum((product[:, HEADS:] * spread).reshape(HEADS, HEAD_DIM, HEADS), axis=(0, 2))
    grad_proj = jnp.concatenate(
        [jnp.tile(proj_one[:, None], (1, 4)), jnp.tile(proj_two[:, None], (1, 4))], axis=1
    )
    grad_bias = jnp.concatenate(
        [jnp.full((4,), jnp.sum(grad_one)), jnp.full((4,), jnp.sum(grad_two))]
    )
    gate_weight = weights["gate_proj"][:HEAD_DIM].astype(F32)
    weight_one = jnp.tile(jnp.sum(gate_weight[:, :4], axis=1), HEADS)[:, None] * spread
    weight_two = jnp.tile(jnp.sum(gate_weight[:, 4:], axis=1), HEADS)[:, None] * spread
    grad_heads = lax.dot_general(
        both,
        jnp.concatenate([weight_one, weight_two], axis=1),
        (((1,), (1,)), ((), ())),
        precision=HIGHEST,
    )
    return (grad_heads, jnp.concatenate([grad_proj, grad_bias[None, :]], axis=0), grad_scale)


def layer_forward(hidden, fill, weights, span, pick):
    vector = weights["layer_vec"].astype(F32)
    in_low = hidden.astype(BF)
    qkv_proj = dot_nn(in_low, weights["w_qkv"])
    query_low = ((qkv_proj[:, :D] + vec_part(vector, 0)) * HEAD_DIM ** (-0.5)).astype(BF)
    key_low = qkv_proj[:, D : 2 * D].astype(BF)
    value_low = (qkv_proj[:, 2 * D :] + vec_part(vector, 1)).astype(BF)
    gate_vals, first, second = gate_forward(in_low, weights)
    gate_wide = jnp.pad(gate_vals, ((0, 0), (0, BLOCK - HEADS)))
    attended, lse = attention_forward(query_low, key_low, value_low, gate_wide, span, fill, pick)
    attn_out = dot_nn(attended, weights["w_out"]) + vec_part(vector, 2)
    mid_rows, normed_one, inv_one = norm_forward(
        DEEP_ALPHA * hidden + attn_out, vec_part(vector, 3), vec_part(vector, 4)
    )
    mid_low = mid_rows.astype(BF)
    pre_act = dot_nn(mid_low, weights["w_up"]) + vector[8 * D :]
    act_low = jax.nn.gelu(pre_act, approximate=False).astype(BF)
    ffn_out = dot_nn(act_low, weights["w_down"]) + vec_part(vector, 5)
    final_rows, normed_two, inv_two = norm_forward(
        DEEP_ALPHA * mid_rows + ffn_out, vec_part(vector, 6), vec_part(vector, 7)
    )
    kept = (in_low, query_low, key_low, value_low, gate_wide, first, second, lse, attended)
    kept += (mid_low, pre_act, act_low, normed_one, inv_one, normed_two, inv_two)
    return (final_rows, kept)


def layer_backward(upstream, kept, fill, weights, span, pick):
    in_low, query_low, key_low, value_low, gate_wide, first, second, lse, attended = kept[:9]
    mid_low, pre_act, act_low, normed_one, inv_one, normed_two, inv_two = kept[9:]
    vector = weights["layer_vec"].astype(F32)
    grad_res_two, grad_gain_two, grad_shift_two = norm_backward(
        upstream, normed_two, inv_two, vec_part(vector, 6)
    )
    ffn_low = grad_res_two.astype(BF)
    grad_down = weight_grad(act_low, ffn_low, 384)
    grad_pre = dot_nt(ffn_low, weights["w_down"]) * gelu_grad(pre_act)
    pre_low = grad_pre.astype(BF)
    grad_up = weight_grad(mid_low, pre_low)
    grad_mid = DEEP_ALPHA * grad_res_two + dot_nt(pre_low, weights["w_up"])
    grad_res_one, grad_gain_one, grad_shift_one = norm_backward(
        grad_mid, normed_one, inv_one, vec_part(vector, 3)
    )
    out_low = grad_res_one.astype(BF)
    grad_out = weight_grad(attended, out_low)
    grad_att = dot_nt(out_low, weights["w_out"]).astype(BF)
    parts, part_sums, grad_gate, grad_span = attention_backward(
        query_low, key_low, value_low, grad_att, gate_wide, span, fill, lse, pick
    )
    grad_heads, grad_gate_proj, grad_gate_scale = gate_backward(
        grad_gate[:, :HEADS], first, second, in_low, weights
    )
    proj_low = jnp.concatenate([parts[0], parts[1], parts[2]], axis=1)
    grad_qkv = weight_grad(in_low, proj_low)
    grad_hidden = DEEP_ALPHA * grad_res_one + dot_nt(proj_low, weights["w_qkv"]) + grad_heads
    grad_vec = jnp.concatenate(
        [
            part_sums[0],
            part_sums[1],
            jnp.sum(grad_res_one, axis=0),
            grad_gain_one,
            grad_shift_one,
            jnp.sum(grad_res_two, axis=0),
            grad_gain_two,
            grad_shift_two,
            jnp.sum(grad_pre, axis=0),
        ]
    )
    grad_map = {
        "w_qkv": grad_qkv,
        "w_out": grad_out,
        "w_up": grad_up,
        "w_down": grad_down,
        "layer_vec": grad_vec,
        "gate_proj": grad_gate_proj,
        "gate_scale": grad_gate_scale,
    }
    return (grad_hidden, grad_map, grad_span)


def head_pass(hidden, w_head, codebook, target_codes):
    row_low = hidden.astype(BF)
    projected = dot_nn(row_low, w_head)
    inv_len = lax.rsqrt(jnp.sum(projected * projected, axis=-1, keepdims=True) + UNIT_EPSILON)
    unit_rows = projected * inv_len
    live_rows = (target_codes >= 0).astype(F32)[:, None]
    logits = LOGIT_SCALE * dot_nt(unit_rows.astype(BF), codebook)
    codes = lax.broadcasted_iota(jnp.int32, (1, codebook.shape[0]), 1)
    hits = (target_codes[:, None] == codes).astype(F32)
    top = jnp.max(logits, axis=1, keepdims=True)
    log_total = top + jnp.log(jnp.sum(jnp.exp(logits - top), axis=1, keepdims=True))
    picked = jnp.sum(logits * hits, axis=1, keepdims=True)
    loss_local = jnp.sum((log_total - picked) * live_rows)
    grad_logits = ((jnp.exp(logits - log_total) - hits) * live_rows * LOGIT_SCALE).astype(BF)
    grad_unit = dot_nn(grad_logits, codebook)
    grad_proj = (
        grad_unit - unit_rows * jnp.sum(unit_rows * grad_unit, axis=-1, keepdims=True)
    ) * inv_len
    proj_low = grad_proj.astype(BF)
    grad_head = dot_tn(row_low, proj_low)
    grad_rows = dot_nt(proj_low, w_head)
    return (loss_local, grad_rows, grad_head)


def local(
    patches,
    lengths,
    patch_masks,
    targets,
    codebook,
    params,
    first_moment,
    second_moment,
    step_count,
):
    dp_count = lax.axis_size("dp")
    code_count = lax.axis_size("code")
    code_index = lax.axis_index("code")
    shard_len = params.shape[0]
    shard_rows = shard_len // 128
    own_low = params.astype(BF).reshape(shard_rows, 128)
    full_low = lax.all_gather(own_low, ("dp", "code"), axis=0, tiled=False)
    flat = full_low.reshape(-1, 128)
    all_codes = lax.all_gather(codebook, "code", axis=0, tiled=True)
    where = starts()

    def piece(seg_name, index=0, count=None):
        extent = dict(layout())[seg_name]
        if count is None:
            amount, shape = math.prod(extent), (-1, extent[-1])
        else:
            amount, shape = math.prod(extent[1:]), (-1, extent[-1])
        begin = where[seg_name] + index * amount
        return flat[begin // 128 : (begin + amount) // 128].reshape(shape)

    tail_row = where["gate_proj"] // 128
    tail = flat[tail_row : tail_row + 2048].reshape(-1)

    def tail_piece(seg_name):
        extent = dict(layout())[seg_name]
        begin = where[seg_name] - tail_row * 128
        return tail[begin : begin + math.prod(extent)].reshape(extent)

    w_patch = piece("w_patch")
    glob_vec = piece("glob_vec").astype(F32)
    gate_proj = tail_piece("gate_proj")
    gate_scale = tail_piece("gate_scale")
    rel_table = tail_piece("rel_table")
    w_head = tail_piece("w_head")
    vec_row = where["layer_vec"] // 128
    vec_len = 8 * D + FF
    layer_vec = flat[vec_row : vec_row + LAYERS * vec_len // 128].reshape(LAYERS, vec_len)
    weights = [
        {
            "w_qkv": piece("w_qkv", index, True),
            "w_out": piece("w_out", index, True),
            "w_up": piece("w_up", index, True),
            "w_down": piece("w_down", index, True),
            "layer_vec": layer_vec[index],
            "gate_proj": gate_proj[index],
            "gate_scale": gate_scale[index],
        }
        for index in range(LAYERS)
    ]

    places = jnp.arange(ROWS, dtype=jnp.int32)
    mask_row = jnp.pad(patch_masks[0], (0, ROWS - LONG))
    live_slot = places < jnp.minimum(lengths[0], LONG)
    visible = live_slot & (mask_row == 0)
    rank = jnp.cumsum(visible.astype(jnp.int32)) - 1
    pick = (
        visible[None, :] & (rank[None, :] == jnp.arange(SEEN, dtype=jnp.int32)[:, None])
    )
    pick_low = pick.astype(BF)
    pick_full = pick.astype(F32)
    seen_valid = jnp.arange(SEEN, dtype=jnp.int32) < lengths[0] // 4
    seen_fill = jnp.where(seen_valid, 0.0, MASK_FILL)[None, :]
    live_fill = jnp.where(live_slot, 0.0, MASK_FILL)[None, :]
    live_float = live_slot.astype(F32)[:, None]
    span_table = jnp.asarray(span_onehot())
    span = jnp.pad(
        lax.dot_general(
            rel_table.astype(F32), span_table, (((0,), (1,)), ((), ())), precision=HIGHEST
        ),
        ((0, 16 - HEADS), (0, 0)),
    )

    patch_rows = jnp.pad(patches[0], ((0, ROWS - LONG), (0, 0)))
    embedded = dot_nn(patch_rows, w_patch)
    normed_rows, normed_zero, inv_zero = norm_forward(embedded, glob_vec[0], glob_vec[1])
    start_rows = normed_rows * live_float
    conv_in = start_rows.astype(BF)
    width = D // code_count
    own_cols = code_index * width
    conv_weight = lax.dynamic_slice_in_dim(piece("conv_w"), own_cols, width, 1)
    own_in = lax.dynamic_slice_in_dim(conv_in, own_cols, width, 1)
    half = KERNEL // 2
    conv_own = conv_call(conv_forward_kernel, own_in[:LONG], conv_weight, half, False)
    seen_own = lax.dot_general(
        pick_full, conv_own, (((1,), (0,)), ((), ())), precision=HIGHEST
    )
    seen_raw = jnp.transpose(lax.all_gather(seen_own, "code", axis=0), (1, 0, 2)).reshape(SEEN, D)
    seen_pre = seen_raw + glob_vec[2]
    seen_start = lax.dot_general(
        pick_full, start_rows, (((1,), (0,)), ((), ())), precision=HIGHEST
    )
    seen_rows = seen_start + jax.nn.gelu(seen_pre, approximate=False)
    encoded, kept_first = layer_forward(seen_rows, seen_fill, weights[0], span, pick_low)
    placed = lax.dot_general(
        pick_full, encoded, (((0,), (0,)), ((), ())), precision=HIGHEST
    )
    hidden = jnp.where(visible[:, None], placed, glob_vec[3])
    final, kept_second = layer_forward(hidden, live_fill, weights[1], span, None)
    target_codes = jnp.where(mask_row == 1, jnp.pad(targets[0], (0, ROWS - LONG)), -1)
    loss_local, upstream, grad_head = head_pass(final, w_head, all_codes, target_codes)

    upstream, map_second, span_second = layer_backward(
        upstream, kept_second, live_fill, weights[1], span, None
    )
    grad_mask_emb = jnp.sum(jnp.where(visible[:, None], 0.0, upstream), axis=0)
    grad_encoded = lax.dot_general(
        pick_full, upstream, (((1,), (0,)), ((), ())), precision=HIGHEST
    )
    grad_seen, map_first, span_first = layer_backward(
        grad_encoded, kept_first, seen_fill, weights[0], span, pick_low
    )
    grad_seen = grad_seen * seen_valid[:, None].astype(F32)
    grad_conv_seen = grad_seen * gelu_grad(seen_pre)
    grad_conv = dot_tn(pick_low, grad_conv_seen.astype(BF)).astype(BF)
    grad_full = lax.dot_general(
        pick_full, grad_seen, (((0,), (0,)), ((), ())), precision=HIGHEST
    )
    grad_kernel = conv_weight_grad(conv_in[:LONG], grad_conv)
    own_grad = lax.dynamic_slice_in_dim(grad_conv, own_cols, width, 1)
    grad_in_own = conv_call(conv_input_kernel, own_grad[:LONG], conv_weight, half - 1, True)
    grad_conv_in = jnp.transpose(
        lax.all_gather(grad_in_own.astype(BF), "code", axis=0), (1, 0, 2)
    ).reshape(ROWS, D)
    grad_start = (grad_full + grad_conv_in.astype(F32)) * live_float
    grad_embedded, grad_gain_zero, grad_shift_zero = norm_backward(
        grad_start, normed_zero, inv_zero, glob_vec[0]
    )
    grad_patch = dot_tn(patch_rows, grad_embedded.astype(BF))
    grad_glob = jnp.stack(
        [grad_gain_zero, grad_shift_zero, jnp.sum(grad_conv_seen, axis=0), grad_mask_emb]
    )
    grad_rel = lax.dot_general(
        span_table, (span_first + span_second)[:HEADS], (((0,), (1,)), ((), ())), precision=HIGHEST
    )
    both = (map_first, map_second)
    pieces = [grad_patch.astype(BF).reshape(-1, 128), grad_glob.astype(BF).reshape(-1, 128)]
    pieces.append(grad_kernel.reshape(-1, 128))
    for seg_name in ("w_qkv", "w_out", "w_up", "w_down"):
        pieces += [layer_map[seg_name] for layer_map in both]
    tail_parts = []
    for seg_name in ("layer_vec", "gate_proj", "gate_scale"):
        tail_parts += [layer_map[seg_name].reshape(-1) for layer_map in both]
    tail_grad = jnp.concatenate(tail_parts + [grad_rel.reshape(-1), grad_head.reshape(-1)])
    tail_rows = shard_rows * dp_count * code_count - vec_row
    tail_grad = jnp.pad(tail_grad, (0, tail_rows * 128 - tail_grad.shape[0])).astype(BF)
    pieces.append(tail_grad.reshape(-1, 128))
    flat_grad = jnp.concatenate(pieces, axis=0)
    arranged = flat_grad.reshape(dp_count, code_count, shard_rows, 128)
    own_part = lax.dynamic_index_in_dim(arranged, code_index, 1, False)
    reduced = (
        lax.psum_scatter(own_part, "dp", scatter_dimension=0, tiled=False)
        .astype(F32)
        .reshape(shard_len)
    )
    leader = (code_index == 0).astype(F32)
    count_local = jnp.sum((target_codes >= 0).astype(F32))
    loss_all, squares_all, count_all, rel_all = lax.psum(
        (
            loss_local * leader,
            jnp.sum(reduced * reduced),
            count_local * leader,
            grad_rel * leader,
        ),
        ("dp", "code"),
    )
    grad_norm = jnp.sqrt(squares_all) / count_all
    clip_factor = jnp.minimum(1.0, CLIP_NORM / grad_norm)
    clipped = reduced / count_all * clip_factor
    rel_grad = rel_all / count_all * clip_factor
    step_value = step_count[0].astype(F32)
    new_first = BETA_ONE * first_moment + (1.0 - BETA_ONE) * clipped
    new_second = BETA_TWO * second_moment + (1.0 - BETA_TWO) * clipped * clipped
    first_hat = new_first / (1.0 - BETA_ONE**step_value)
    second_hat = new_second / (1.0 - BETA_TWO**step_value)
    new_params = params - LEARN_RATE * (
        first_hat / (jnp.sqrt(second_hat) + ADAM_EPSILON) + WEIGHT_DECAY * params
    )
    return (
        new_params,
        new_first,
        new_second,
        new_params.astype(BF),
        loss_all / count_all,
        grad_norm,
        rel_grad,
    )


def solution(mesh):
    placed = (
        P("dp", None, None),
        P("dp"),
        P("dp", None),
        P("dp", None),
        P("code", None),
        P(("dp", "code")),
        P(("dp", "code")),
        P(("dp", "code")),
        P(),
    )
    return jax.shard_map(
        local,
        mesh=mesh,
        in_specs=placed,
        out_specs=(
            P(("dp", "code")),
            P(("dp", "code")),
            P(("dp", "code")),
            P(("dp", "code")),
            P(),
            P(),
            P(),
        ),
        check_vma=False,
    )
```

time: 6080 us -> 1140 us (0.19); the launches traced: 5970 us -> 1120 us
  local copies, waits for them, and re-layouts: 2180 us -> 335 us
  other arithmetic: 1720 us -> 56 us
  matrix products: 1460 us -> 89.4 us
  waiting for transfers between devices: 523 us -> 292 us
  Pallas kernels: 0 us -> 222 us
    scatter-add x2 -> x0, other arithmetic: 1390 us -> none  [position_bias(): return jnp.transpose(jnp.take(head_table, offset_idx, axis=1), (1, 0, 2, 3))]
    conv_general_dilated x3 -> x0, matrix products: 1310 us -> none  [the longest x1 665 us: conv_backward(): lax.conv_general_dilated(conv_in, grad_low, (1,), [(KERNEL // 2, KERNEL /...]
    gather x10 -> x0, local copies, waits for them, and re-layouts: 613 us -> none  [the longest x6 605 us: position_bias(): return jnp.transpose(jnp.take(head_table, offset_idx, axis=1), (1, 0, 2, 3))]
    concatenate x3 -> x6, local copies, waits for them, and re-layouts: 537 us -> 6.58 us  [the longest x1 4.42 us: local(): jnp.concatenate(tail_parts + [grad_rel.reshape(-1), grad_head.reshape(-1)])]
    pallas_call x0 -> x15, Pallas kernels: none -> 222 us  [the longest x2 54.4 us: attention_backward(): pl.pallas_call(functools.partial(attention_backward_kernel, picked=pick i...]
    all_gather x1 -> x0, other arithmetic: 209 us -> none  [local(): full_low = lax.all_gather(own_low, ('dp', 'code'), axis=0, tiled=True)]
    convert_element_type x14 -> x5, local copies, waits for them, and re-layouts: 205 us -> 4.13 us  [the longest x2 2.27 us: local(): grad_start = (grad_full + grad_conv_in.astype(F32)) * live_float]
    all_gather x1, waiting for transfers between devices: 388 us -> 200 us  [local(): full_low = lax.all_gather(own_low, ('dp', 'code'), axis=0, tiled=False)]
  transfers between devices with their start and end apart: 3 -> 2, of which waited for: 2 -> 2; matrix products, arithmetic and copies ran while one was open for 4% -> 0% of each run, Pallas kernels for 0% -> 0%
where the time goes in v1:
time: 1140 us; the launch traced here: 1120 us
  local copies, waits for them, and re-layouts  335 us (29%)
  waiting for transfers between devices  292 us (26%)
  Pallas kernels  222 us (19%)
  blocking collectives  96.6 us (8%)
  matrix products  89.4 us (8%)
  other arithmetic  56 us (5%)
  between operations  25.1 us (2%)
    all_gather x1, waiting for transfers between devices, local(): full_low = lax.all_gather(own_low, ('dp', 'code'), axis=0, tiled=False)  200 us
    unnamed x3, waiting for transfers between devices  91.6 us
    reshape x10, local copies, waits for them, and re-layouts, piece(): return flat[begin // 128:(begin + amount) // 128].reshape(shape)  68.2 us
    pallas_call x2, Pallas kernels, attention_backward(): pl.pallas_call(functools.partial(attention_backward_kernel, picked=pick i...  54.4 us
    pallas_call x8, Pallas kernels, weight_grad(): pl.pallas_call(weight_grad_kernel, grid=(depth // rows,), in_specs=[pl.Bl...  53.4 us
    pallas_call x1, Pallas kernels, conv_weight_grad(): pl.pallas_call(conv_weight_kernel, grid=(parts, KERNEL // TAPS), in_specs...  50.1 us
    dot_general x13, matrix products, dot_nn(): lax.dot_general(left, right, (((1,), (0,)), ((), ())), preferred_element_...  42.2 us
    unnamed x435, local copies, waits for them, and re-layouts  42 us
  transfers between devices with their start and end apart: 2, of which 2 were waited for; matrix products, arithmetic and copies ran while one was open for 0% of the time, Pallas kernels for 0%

profile of v1, /device:TPU:0, one launch (start us, length us, event | category | flops | bytes accessed | tf_op | source)
XLA Modules:
  0.0 1116.6 jit_solution(18105928453087355878)
XLA Ops:
  7.2 2.9 convert_bitcast_fusion
  13.7 21.9 %all_gather.21 = bf16[1024,256]{1,0:T(8,128)(2,1)} all-gather(bf16[256,256]{1,0:T(8,128)(2,1)S(1)} %copy-done.70), channel_id=1, replica_groups=mesh['dp'=8,'code'=4] {'code'}, dimensions={0}, use_global_device_ids=true | all-gather | bytes 655360 | tf_op jit(solution)/shard_map/all_gather | solution.py:663
  36.4 200.4 %all-gather.4.cloned.1.call-done = bf16[32,4711,128]{2,1,0:T(8,128)(2,1)} async-done(((bf16[1,4711,128]{2,1,0:T(8,128)(2,1)}), bf16[32,4711,128]{2,1,0:T(8,128)(2,1)}) %all-gather.4.cloned.1.call-update) | async-done | bytes 38592528 | tf_op jit(solution)/shard_map/all_gather | solution.py:661
  236.8 40.7 %reshape.446 = bf16[150752,128]{1,0:T(8,128)(2,1)} reshape(bf16[32,4711,128]{2,1,0:T(8,128)(2,1)} %all-gather.4.cloned.1.call-done) | data formatting | bytes 77185024 | tf_op jit(solution)/shard_map/reshape | solution.py:662
  280.2 9.2 slice.576
  289.4 5.2 fusion.165
  297.7 2.8 fusion.164
  300.5 13.8 %fusion.163 = (bf16[18432,128]{1,0:T(8,128)(2,1)}, bf16[18432,128]{1,0:T(8,128)(2,1)}, bf16[18432,128]{1,0:T(8,128)(2,1)}, bf16[18432,128]{1,0:T(8,128)(2,1)}) fusion(bf16[150752,128]{1,0:T(8,128)(2,1)} %reshape.446), kind=kLoop, calls=%fused_computation.433 | loop fusion | bytes 37748736 | tf_op jit(solution)/shard_map/slice | solution.py:673
  315.2 10.1 slice.464
  325.4 2.3 slice_reduce_fusion.4
  334.7 16.9 %reshape.448 = bf16[6144,768]{1,0:T(8,128)(2,1)} reshape(bf16[36864,128]{1,0:T(8,128)(2,1)} %slice.576) | data formatting | bytes 18874368 | tf_op jit(solution)/shard_map/reshape | solution.py:673
  351.6 5.7 constant_dynamic-slice_fusion.1.weight_ref
  357.3 14.1 %shard_map.216 = f32[512,192]{1,0:T(8,128)} custom-call(f32[640,256]{1,0:T(8,128)} %pad_convert_fusion.2.in_ref, bf16[6144,192]{1,0:T(8,128)(2,1)} %constant_dynamic-slice_fusion.1.weight_ref, bf16[4,192]{1,0:T(4,128)(2,1)} %constant.132.clone.mask_ref), custom_call_target="tpu_custom_call" | custom-call | tf_op jit(solution)/shard_map/pallas_call | solution.py:190
  373.1 15.3 %all-gather = f32[512,192]{0,1:T(8,128)S(1)} all-gather(f32[128,192]{0,1:T(8,128)S(1)} %fusion.92), channel_id=2, replica_groups=mesh['dp'=8,'code'=4] {'code'}, dimensions={0}, use_global_device_ids=true | all-gather | bytes 491520 | tf_op jit(solution)/shard_map/all_gather | solution.py:741
  388.7 7.7 reshape.450
  396.5 2.6 fusion.170
  409.1 2.4 fusion.62
  411.5 10.0 shard_map.217
  423.1 8.2 reshape.454
  431.3 9.4 reshape.455
  441.0 7.7 fusion.21
  451.2 5.2 reshape.456
  458.3 4.3 fusion.177
  470.9 3.3 fusion.26
  474.2 25.1 %shard_map.218 = (bf16[512,768]{1,0:T(8,128)(2,1)}, f32[512,128]{1,0:T(8,128)}) custom-call(bf16[512,768]{1,0:T(8,128)(2,1)} %get-tuple-element.136.refs_0_, bf16[512,768]{1,0:T(8,128)(2,1)} %slice.842.refs_1_, bf16[512,768]{1,0:T(8,128)(2,1)} %get-tuple-element.135.refs_2_, f32[512,128]{1,0:T(8,128)} %pad.61.refs_3_.refs_4_, ...), custom_call_target="tpu_custom_call" | custom-call | tf_op jit(solution)/shard_map/pallas_call | solution.py:317
  501.7 8.2 reshape.458
  509.9 9.2 reshape.459
  519.9 18.7 %fusion.2 = (bf16[512,3072]{1,0:T(8,128)(2,1)S(1)}, f32[512,3072]{1,0:T(8,128)}) fusion(f32[3072]{0:T(1024)S(1)} %copy-done.135, bf16[512,768]{1,0:T(8,128)(2,1)S(1)} %fusion.36.left_ref, bf16[768,3072]{1,0:T(8,128)(2,1)} %reshape.458), kind=kOutput, calls=%fused_computation.5 | convolution fusion | flops 2519728128 | bytes 14954496 | tf_op jit(solution)/shard_map/dot_general | solution.py:102
  538.7 2.8 fusion.175
  561.8 7.2 fusion.167
  569.1 3.7 multiply_reduce_fusion.2
  576.9 35.5 %shard_map.219 = (bf16[3,512,768]{2,1,0:T(8,128)(2,1)}, f32[8,768]{1,0:T(8,128)}, f32[512,128]{1,0:T(8,128)}, f32[16,1024]{1,0:T(8,128)}) custom-call(bf16[512,768]{1,0:T(8,128)(2,1)} %get-tuple-element.136.refs_0_, bf16[512,768]{1,0:T(8,128)(2,1)} %slice.842.refs_1_, bf16[512,768]{1,0:T(8,128)(2,1)} %get-tuple-element.135.refs_2_, ...), custom_call_target="tpu_custom_call" | custom-call | tf_op jit(solution)/shard_map/pallas_call | solution.py:410
  620.0 2.2 select_reduce_fusion.1
  624.6 2.3 fusion.168
  626.9 2.4 multiply_reduce_fusion.16
  632.1 18.9 %shard_map.220 = (bf16[3,128,768]{2,1,0:T(8,128)(2,1)}, f32[8,768]{1,0:T(8,128)}, f32[128,128]{1,0:T(8,128)}, f32[16,1024]{1,0:T(8,128)}) custom-call(bf16[128,768]{1,0:T(8,128)(2,1)} %get-tuple-element.143.refs_0_, bf16[128,768]{1,0:T(8,128)(2,1)} %slice.843.refs_1_, bf16[128,768]{1,0:T(8,128)(2,1)} %get-tuple-element.142.refs_2_, ...), custom_call_target="tpu_custom_call" | custom-call | tf_op jit(solution)/shard_map/pallas_call | solution.py:410
  653.0 2.2 fusion.151
  664.5 2.6 convolution_add_fusion.3
  675.1 4.7 shard_map.225
  679.7 5.5 shard_map.226
  685.2 6.2 shard_map.227
  691.4 8.0 shard_map.228
  699.4 7.2 shard_map.229
  706.6 8.8 shard_map.230
  717.5 15.0 %shard_map.221 = f32[512,192]{1,0:T(8,128)} custom-call(f32[640,256]{1,0:T(8,128)} %pad_convert_fusion.1.in_ref, bf16[6144,192]{1,0:T(8,128)(2,1)} %constant_dynamic-slice_fusion.1.weight_ref, bf16[4,192]{1,0:T(4,128)(2,1)} %constant.132.clone.mask_ref), custom_call_target="tpu_custom_call" | custom-call | tf_op jit(solution)/shard_map/pallas_call | solution.py:190
  733.6 19.5 %all-gather.1 = bf16[2048,192]{1,0:T(8,128)(2,1)S(1)} all-gather(bf16[512,192]{1,0:T(8,128)(2,1)S(1)} %convert_element_type.253), channel_id=3, replica_groups=mesh['dp'=8,'code'=4] {'code'}, dimensions={0}, use_global_device_ids=true | all-gather | bytes 983040 | tf_op jit(solution)/shard_map/all_gather | solution.py:776
  755.4 3.0 multiply_reduce_fusion.3
  764.9 50.1 %shard_map.222 = bf16[4,6144,192]{2,1,0:T(8,128)(2,1)} custom-call(f32[4,640,256]{2,1,0:T(8,128)} %pad_convert_fusion.in_ref, bf16[4,512,192]{2,1,0:T(8,128)(2,1)} %bitcast.190, f32[4,192]{1,0:T(4,128)} %constant.135.clone.mask_ref), custom_call_target="tpu_custom_call" | custom-call | tf_op jit(solution)/shard_map/pallas_call | solution.py:236
  815.0 17.2 %copy.118 = bf16[6144,4,192]{2,1,0:T(4,128)(2,1)} copy(bf16[6144,4,192]{2,0,1:T(8,128)(2,1)} %bitcast.167) | data formatting | bytes 18874368 | tf_op jit(solution)/shard_map/transpose | solution.py:249
  832.3 24.6 %reshape_reshape.3 = bf16[36864,128]{1,0:T(8,128)(2,1)} reshape(bf16[6144,4,192]{2,1,0:T(4,128)(2,1)} %copy.118) | data formatting | bytes 18874368 | tf_op jit(solution)/shard_map/reshape;reshape | solution.py:791
  856.9 5.5 shard_map.223
  862.5 7.4 shard_map.224
  875.9 9.6 constant_dynamic-update-slice_fusion.8
  893.4 2.6 constant_dynamic-update-slice_fusion.3
  896.7 2.5 constant_dynamic-update-slice_fusion.2
  899.2 2.6 constant_dynamic-update-slice_fusion.1
  903.1 2.6 constant_dynamic-update-slice_fusion
  905.8 4.4 concatenate.67
  911.0 40.9 %reshape.469 = bf16[8,4,4711,128]{3,2,1,0:T(8,128)(2,1)} reshape(bf16[150752,128]{1,0:T(8,128)(2,1)} %bitcast_dynamic-update-slice_fusion) | data formatting | bytes 77185024 | tf_op jit(solution)/shard_map/reshape | solution.py:802
  952.0 8.0 dynamic-slice_bitcast_fusion
  962.1 91.6 %reduce-scatter.4.cloned.1.call-done = bf16[1,4711,128]{2,1,0:T(8,128)(2,1)} async-done(((bf16[8,4711,128]{2,1,0:T(8,128)(2,1)}), bf16[1,4711,128]{2,1,0:T(8,128)(2,1)}) %reduce-scatter.4.cloned.1.call-update) | async-done | bytes 1206032
  1053.7 2.5 fusion.17
  1056.2 40.0 %all-reduce.14 = (f32[]{:T(128)}, f32[]{:T(128)}, f32[]{:T(128)}, f32[320,12]{0,1:T(8,128)S(1)}) all-reduce(f32[]{:T(128)S(6)} %mul.1022, f32[]{:T(128)} %fusion.17, f32[]{:T(128)S(6)} %mul.1040, f32[320,12]{0,1:T(8,128)S(1)} %get-tuple-element.177), channel_id=1, replica_groups=mesh['dp'=8,'code'=4] {'dp','code'}, use_global_device_ids=true, to_apply=%region_64.65 | all-reduce | flops 3843 | bytes 30744 | tf_op jit(solution)/shard_map/psum | solution.py:811
  1100.5 6.8 fusion.146
  (664 shorter events, 131.4 us)
Async XLA Ops:
  7.2 229.6 %all-gather.4.cloned.1.call-start = ((), (), s32[]{:S(2)}) async-start(), calls=%async_computation.1 | async-start | bytes 39806976 | tf_op jit(solution)/shard_map/all_gather | solution.py:661
  10.1 1043.6 %reduce-scatter.4.cloned.1.call-start = ((), (), s32[]{:S(2)}) async-start(), calls=%async_computation.2 | async-start | bytes 10856448
  10.9 321.2 %copy-start.110 = (f32[512]{0:T(512)}, f32[512]{0:T(512)S(1)}, u32[]{:S(2)}) copy-start(f32[512]{0:T(512)S(1)} %get-tuple-element.244) | copy-start | bytes 6148
  10.9 360.6 %copy-start.98 = (pred[512]{0:T(512)(128)(4,1)}, pred[512]{0:T(512)(128)(4,1)S(1)}, u32[]{:S(2)}) copy-start(pred[512]{0:T(512)(128)(4,1)S(1)} %get-tuple-element.120) | copy-start | bytes 1540
  315.2 15.7 %slice-start = ((bf16[150752,128]{1,0:T(8,128)(2,1)}), bf16[1536,128]{1,0:T(8,128)(2,1)S(1)}, s32[]{:S(2)}) async-start(bf16[150752,128]{1,0:T(8,128)(2,1)} %reshape.446), calls=%async_computation.3 | async-start | bytes 786432 | tf_op jit(solution)/shard_map/slice | solution.py:673
  315.2 16.0 %copy-start.58 = (bf16[1,496,256]{2,1,0:T(8,128)(2,1)S(1)}, bf16[1,496,256]{2,1,0:T(8,128)(2,1)}, u32[]{:S(2)}) copy-start(bf16[1,496,256]{2,1,0:T(8,128)(2,1)} %param.17) | copy-start | bytes 761860
  330.9 65.5 %copy-start.80 = (f32[768]{0:T(1024)}, f32[768]{0:T(1024)S(1)}, u32[]{:S(2)}) copy-start(f32[768]{0:T(1024)S(1)} %get-tuple-element.198) | copy-start | bytes 9220
  331.7 64.7 %copy-start = (f32[512,768]{1,0:T(8,128)}, f32[512,768]{1,0:T(8,128)S(1)}, u32[]{:S(2)}) copy-start(f32[512,768]{1,0:T(8,128)S(1)} %get-tuple-element.200) | copy-start | bytes 4718596
  388.6 7.8 copy-start.47
  388.6 7.8 copy-start.85
  388.6 7.8 copy-start.96
  388.7 7.8 copy-start.99
  388.7 7.8 copy-start.111
  388.7 7.8 copy-start.126
  388.7 7.8 copy-start.129
  409.0 13.8 %copy-start.12 = (bf16[768,768]{1,0:T(8,128)(2,1)}, bf16[768,768]{1,0:T(8,128)(2,1)S(1)}, u32[]{:S(2)}) copy-start(bf16[768,768]{1,0:T(8,128)(2,1)S(1)} %reshape.453) | copy-start | bytes 3538948
  409.1 12.4 %copy-start.64 = (f32[128,768]{1,0:T(8,128)S(1)}, f32[128,768]{1,0:T(8,128)}, u32[]{:S(2)}) copy-start(f32[128,768]{1,0:T(8,128)} %get-tuple-element.202) | copy-start | bytes 1179652
  409.1 12.4 %copy-start.117 = (f32[768]{0:T(1024)S(1)}, f32[768]{0:T(1024)}, u32[]{:S(2)}) copy-start(f32[768]{0:T(1024)} %get-tuple-element.238) | copy-start | bytes 9220
  422.8 17.9 %copy-start.6 = (f32[128,768]{1,0:T(8,128)}, f32[128,768]{1,0:T(8,128)S(1)}, u32[]{:S(2)}) copy-start(f32[128,768]{1,0:T(8,128)S(1)} %get-tuple-element.204) | copy-start | bytes 1179652
  422.8 17.9 %copy-start.132 = (f32[128]{0:T(128)}, f32[128]{0:T(128)S(1)}, u32[]{:S(2)}) copy-start(f32[128]{0:T(128)S(1)} %broadcast_multiply_fusion.35) | copy-start | bytes 1540
  423.0 17.7 %copy-start.144 = (f32[128]{0:T(128)}, f32[128]{0:T(128)S(1)}, u32[]{:S(2)}) copy-start(f32[128]{0:T(128)S(1)} %add_rsqrt_fusion.5) | copy-start | bytes 1540
  431.3 9.5 copy-start.89
  431.3 9.6 copy-start.137
  440.7 7.9 slice-start.3
  440.9 7.8 copy-start.61
  440.9 7.7 slice-start.4
  440.9 7.7 copy-start.7
  440.9 7.7 copy-start.116
  440.9 7.7 copy-start.133
  441.0 7.7 copy-start.145
  458.3 8.3 copy-start.10
  474.2 25.1 %copy-start.52 = (bf16[768,768]{1,0:T(8,128)(2,1)S(1)}, bf16[768,768]{1,0:T(8,128)(2,1)}, u32[]{:S(2)}) copy-start(bf16[768,768]{1,0:T(8,128)(2,1)} %reshape.457) | copy-start | bytes 3538948
  474.2 25.1 %copy-start.163 = (f32[768]{0:T(1024)S(1)}, f32[768]{0:T(1024)}, u32[]{:S(2)}) copy-start(f32[768]{0:T(1024)} %get-tuple-element.166) | copy-start | bytes 9220
  501.4 37.3 %copy-start.90 = (f32[512]{0:T(512)}, f32[512]{0:T(512)S(1)}, u32[]{:S(2)}) copy-start(f32[512]{0:T(512)S(1)} %broadcast_multiply_fusion.28) | copy-start | bytes 6148
  501.7 37.0 %copy-start.106 = (f32[512]{0:T(512)}, f32[512]{0:T(512)S(1)}, u32[]{:S(2)}) copy-start(f32[512]{0:T(512)S(1)} %add_rsqrt_fusion.2) | copy-start | bytes 6148
  509.9 9.2 copy-start.87
  509.9 9.2 copy-start.113
  519.2 19.5 %slice-start.17 = ((s8[4718592]{0:T(1024)(128)(4,1)}), s8[4194304]{0:T(1024)(128)(4,1)S(1)}, s32[]{:S(2)}) async-start(s8[4718592]{0:T(1024)(128)(4,1)} %bitcast.186), calls=%async_computation.20 | async-start | bytes 8388608
  519.5 19.1 %copy-start.39 = (bf16[512,768]{1,0:T(8,128)(2,1)}, bf16[512,768]{1,0:T(8,128)(2,1)S(1)}, u32[]{:S(2)}) copy-start(bf16[512,768]{1,0:T(8,128)(2,1)S(1)} %fusion.36.left_ref) | copy-start | bytes 2359300
  519.9 18.8 %slice-start.18 = ((s8[4718592]{0:T(1024)(128)(4,1)}), s8[524288]{0:T(1024)(128)(4,1)S(1)}, s32[]{:S(2)}) async-start(s8[4718592]{0:T(1024)(128)(4,1)} %bitcast.186), calls=%async_computation.21 | async-start | bytes 1048576
  519.9 18.8 %copy-start.162 = (f32[768]{0:T(1024)S(1)}, f32[768]{0:T(1024)}, u32[]{:S(2)}) copy-start(f32[768]{0:T(1024)} %get-tuple-element.163) | copy-start | bytes 9220
  559.6 9.4 slice-start.15
  560.8 8.2 copy-start.40
  576.8 35.6 %copy-start.54 = (f32[512,12]{1,0:T(8,128)S(1)}, f32[512,12]{1,0:T(8,128)}, u32[]{:S(2)}) copy-start(f32[512,12]{1,0:T(8,128)} %get-tuple-element.114) | copy-start | bytes 73732
  576.8 35.6 %copy-start.55 = (f32[512,12]{1,0:T(8,128)S(1)}, f32[512,12]{1,0:T(8,128)}, u32[]{:S(2)}) copy-start(f32[512,12]{1,0:T(8,128)} %get-tuple-element.115) | copy-start | bytes 73732
  576.9 35.6 %copy-start.158 = (f32[12]{0:T(128)S(1)}, f32[12]{0:T(128)}, u32[]{:S(2)}) copy-start(f32[12]{0:T(128)} %get-tuple-element.152) | copy-start | bytes 148
  630.9 22.1 %copy-start.66 = (f32[128,12]{1,0:T(8,128)S(1)}, f32[128,12]{1,0:T(8,128)}, u32[]{:S(2)}) copy-start(f32[128,12]{1,0:T(8,128)} %get-tuple-element.117) | copy-start | bytes 18436
  630.9 22.1 %copy-start.67 = (f32[128,12]{1,0:T(8,128)S(1)}, f32[128,12]{1,0:T(8,128)}, u32[]{:S(2)}) copy-start(f32[128,12]{1,0:T(8,128)} %get-tuple-element.118) | copy-start | bytes 18436
  630.9 22.1 %copy-start.160 = (f32[12]{0:T(128)S(1)}, f32[12]{0:T(128)}, u32[]{:S(2)}) copy-start(f32[12]{0:T(128)} %get-tuple-element.153) | copy-start | bytes 148
  630.9 33.5 %copy-start.4 = (bf16[768,2304]{1,0:T(8,128)(2,1)S(1)}, bf16[768,2304]{1,0:T(8,128)(2,1)}, u32[]{:S(2)}) copy-start(bf16[768,2304]{1,0:T(8,128)(2,1)} %reshape.450) | copy-start | bytes 10616836
  632.1 25.5 %copy-start.150 = (f32[4,128]{1,0:T(4,128)S(1)}, f32[4,128]{1,0:T(4,128)}, u32[]{:S(2)}) copy-start(f32[4,128]{1,0:T(4,128)} %slice_convert_fusion.6) | copy-start | bytes 6148
  706.6 8.8 copy-start.18
  706.6 8.8 copy-start.57
  862.4 9.0 copy-start.123
  862.4 9.1 copy-start.122
  862.4 10.8 copy-start.121
  862.4 10.9 copy-start.120
  862.4 11.3 %copy-start.20 = (f32[1024,320]{1,0:T(8,128)S(1)}, f32[1024,320]{1,0:T(8,128)}, u32[]{:S(2)}) copy-start(f32[1024,320]{1,0:T(8,128)} %constant.131.clone) | copy-start | bytes 3932164
  862.4 11.3 %copy-start.82 = (f32[16,1024]{1,0:T(8,128)S(1)}, f32[16,1024]{1,0:T(8,128)}, u32[]{:S(2)}) copy-start(f32[16,1024]{1,0:T(8,128)} %get-tuple-element.30) | copy-start | bytes 196612
  862.5 11.3 %copy-start.83 = (f32[16,1024]{1,0:T(8,128)S(1)}, f32[16,1024]{1,0:T(8,128)}, u32[]{:S(2)}) copy-start(f32[16,1024]{1,0:T(8,128)} %get-tuple-element.29) | copy-start | bytes 196612
  875.9 9.6 copy-start.9
  875.9 11.5 %copy-start.5 = (bf16[13824,128]{1,0:T(8,128)(2,1)S(1)}, bf16[13824,128]{1,0:T(8,128)(2,1)}, u32[]{:S(2)}) copy-start(bf16[13824,128]{1,0:T(8,128)(2,1)} %shard_map.224) | copy-start | bytes 10616836
  885.5 7.9 slice-start.7
  960.0 140.5 %copy-start.16 = (f32[603008]{0:T(1024)S(1)}, f32[603008]{0:T(1024)}, u32[]{:S(2)}) copy-start(f32[603008]{0:T(1024)} %param.22) | copy-start | bytes 7236100
  (151 other events, 430.4 us)
Sparse Core Ops, SparseCore 0:
  11.5 225.1 all-gather.3
  960.1 93.4 reduce-scatter.3

commit v2 on v1

v2 whole, which is shorter than its diff:
```python
import functools
import math

import jax
import jax.numpy as jnp
import numpy as np
from jax import lax
from jax.experimental import pallas as pl
from jax.experimental.pallas import tpu as pltpu
from jax.sharding import PartitionSpec as P

D = 768
HEADS = 12
HEAD_DIM = 64
FF = 3072
PATCH_IN = 256
PROJ = 256
KERNEL = 128
GROUPS = 16
WIDTH = D // GROUPS
BUCKETS = 320
MAX_DIST = 800
LAYERS = 2
LONG = 496
VISIBLE = 124
ROWS = 512
SEEN = 128
SPAN = 1024

NORM_EPSILON = 1e-05
UNIT_EPSILON = 1e-06
DEEP_ALPHA = 2.2133638394006434
LOGIT_SCALE = 25.0
CLIP_NORM = 0.005
LEARN_RATE = 0.02
BETA_ONE = 0.9
BETA_TWO = 0.999
ADAM_EPSILON = 1e-10
WEIGHT_DECAY = 0.01
MASK_FILL = -1000000000.0
HIGHEST = lax.Precision.HIGHEST
BF = jnp.bfloat16
F32 = jnp.float32
VMEM_LIMIT = 56 << 20


def layout():
    return [
        ("w_patch", (PATCH_IN, D)),
        ("glob_vec", (4, D)),
        ("conv_w", (KERNEL, WIDTH, D)),
        ("w_qkv", (LAYERS, D, 3 * D)),
        ("w_out", (LAYERS, D, D)),
        ("w_up", (LAYERS, D, FF)),
        ("w_down", (LAYERS, FF, D)),
        ("layer_vec", (LAYERS, 8 * D + FF)),
        ("gate_proj", (LAYERS, HEAD_DIM + 1, 8)),
        ("gate_scale", (LAYERS, HEADS)),
        ("rel_table", (BUCKETS, HEADS)),
        ("w_head", (D, PROJ)),
    ]


def starts():
    where = {}
    offset = 0
    for seg_name, extent in layout():
        where[seg_name] = offset
        offset += math.prod(extent)
    return where


TILE = 16


class Geometry:
    def __init__(self, dp_count, code_count, shard_rows):
        self.dp_count, self.code_count, self.shard_rows = dp_count, code_count, shard_rows
        self.shards = dp_count * code_count
        self.phase = -(starts()["conv_w"] // 128) % TILE
        self.window = -(-(shard_rows + TILE - 1) // TILE) * TILE
        self.begins = [(shard_rows * s + self.phase) // TILE * TILE for s in range(self.shards)]
        self.offsets = [(shard_rows * s + self.phase) % TILE for s in range(self.shards)]

    def place(self, seg_name, index=0):
        extent = dict(layout())[seg_name]
        amount = math.prod(extent[1:]) if index else 0
        return (starts()[seg_name] + index * amount) // 128 + self.phase

    def pieces(self, low, high):
        main, edges = [], []
        row = low
        while row < high:
            shard = max(s for s in range(self.shards) if self.begins[s] <= row)
            begin = self.begins[shard]
            if row == begin and shard > 0 and self.offsets[shard]:
                main.append((shard - 1, row - self.begins[shard - 1], row - low, TILE))
                edges.append((shard, row - low))
                row += TILE
                continue
            stop = self.begins[shard + 1] if shard + 1 < self.shards else high
            count = min(stop, high) - row
            main.append((shard, row - begin, row - low, count))
            row += count
        merged = []
        for item in main:
            last = merged[-1] if merged else None
            if last and last[0] == item[0] and last[1] + last[3] == item[1]:
                merged[-1] = last[:3] + (last[3] + item[3],)
            else:
                merged.append(item)
        return merged, edges

    def exact(self, windows, low, high):
        parts = []
        row = low
        while row < high:
            shard = row // self.shard_rows
            stop = min(high, (shard + 1) * self.shard_rows)
            begin = self.offsets[shard] + row - shard * self.shard_rows
            parts.append(windows[shard, begin : begin + stop - row])
            row = stop
        return parts[0] if len(parts) == 1 else jnp.concatenate(parts, axis=0)


def bucket_onehot():
    offsets = np.arange(-(LONG - 1), LONG)
    half_count = BUCKETS // 2
    exact_count = half_count // 2
    distance = np.abs(offsets)
    scaled = (
        np.log(np.maximum(distance, 1) / exact_count)
        / np.log(MAX_DIST / exact_count)
        * (half_count - exact_count)
    )
    larger = np.minimum(exact_count + np.maximum(scaled, 0.0).astype(np.int64), half_count - 1)
    bucket = (offsets > 0) * half_count + np.where(distance < exact_count, distance, larger)
    return (bucket[:, None] == np.arange(BUCKETS)[None, :]).astype(np.float32)


def span_onehot():
    shift = SPAN // 2 - (LONG - 1)
    table = np.zeros((SPAN, BUCKETS), np.float32)
    table[shift : shift + 2 * LONG - 1] = bucket_onehot()[::-1]
    return table


def params_of(grid_rank=1):
    return pltpu.CompilerParams(
        dimension_semantics=("arbitrary",) * grid_rank, vmem_limit_bytes=VMEM_LIMIT
    )


def dot_nn(left, right):
    return lax.dot_general(left, right, (((1,), (0,)), ((), ())), preferred_element_type=F32)


def dot_nt(left, right):
    return lax.dot_general(left, right, (((1,), (1,)), ((), ())), preferred_element_type=F32)


def dot_tn(left, right):
    return lax.dot_general(left, right, (((0,), (0,)), ((), ())), preferred_element_type=F32)


TAPS = 16


def lane_masks(width):
    group = np.arange(width)[None, :] // WIDTH
    return (group == np.arange(width // WIDTH)[:, None]).astype(np.float32)


def shifted_taps(source_ref, target_ref, count):
    width = source_ref.shape[1]
    for tap in range(TAPS):
        target_ref[:, tap * width : (tap + 1) * width] = source_ref[tap : tap + count, :].astype(BF)


def conv_forward_kernel(in_ref, weight_ref, mask_ref, out_ref, taps_ref, block_ref):
    step = pl.program_id(0)
    width = weight_ref.shape[1]

    @pl.when(step == 0)
    def _():
        shifted_taps(in_ref, taps_ref, taps_ref.shape[0])
        block_ref[...] = jnp.zeros_like(block_ref)

    for tap in range(TAPS):
        piece = weight_ref[tap * WIDTH : (tap + 1) * WIDTH, :]
        for group in range(width // WIDTH):
            low = tap * width + group * WIDTH
            block_ref[low : low + WIDTH, :] = piece * mask_ref[group : group + 1, :]
    begin = pl.multiple_of(step * TAPS, TAPS)
    term = dot_nn(taps_ref[pl.ds(begin, ROWS), :], block_ref[...])

    @pl.when(step == 0)
    def _():
        out_ref[...] = term

    @pl.when(step > 0)
    def _():
        out_ref[...] += term


def conv_input_kernel(in_ref, weight_ref, mask_ref, out_ref, taps_ref, block_ref):
    step = pl.program_id(0)
    width = weight_ref.shape[1]

    @pl.when(step == 0)
    def _():
        shifted_taps(in_ref, taps_ref, taps_ref.shape[0])
        block_ref[...] = jnp.zeros_like(block_ref)

    for tap in range(TAPS):
        piece = weight_ref[tap * WIDTH : (tap + 1) * WIDTH, :]
        low = (TAPS - 1 - tap) * width
        for group in range(width // WIDTH):
            block_ref[group * WIDTH : (group + 1) * WIDTH, low : low + width] = (
                piece * mask_ref[group : group + 1, :]
            )
    begin = pl.multiple_of((pl.num_programs(0) - 1 - step) * TAPS, TAPS)
    term = dot_nt(taps_ref[pl.ds(begin, ROWS), :], block_ref[...])

    @pl.when(step == 0)
    def _():
        out_ref[...] = term

    @pl.when(step > 0)
    def _():
        out_ref[...] += term


def conv_call(kernel, conv_in, weight, front, nt):
    width = weight.shape[1]
    steps = KERNEL // TAPS
    count = ROWS + KERNEL - TAPS
    padded = jnp.pad(
        conv_in.astype(F32),
        ((front, count + TAPS - front - conv_in.shape[0]), (0, 0)),
    )
    block = (width, TAPS * width) if nt else (TAPS * width, width)
    return pl.pallas_call(
        kernel,
        grid=(steps,),
        in_specs=[
            pl.BlockSpec(padded.shape, lambda i: (0, 0)),
            pl.BlockSpec((TAPS * WIDTH, width), lambda i: (i, 0)),
            pl.BlockSpec((width // WIDTH, width), lambda i: (0, 0)),
        ],
        out_specs=pl.BlockSpec((ROWS, width), lambda i: (0, 0)),
        out_shape=jax.ShapeDtypeStruct((ROWS, width), F32),
        scratch_shapes=[pltpu.VMEM((count, TAPS * width), BF), pltpu.VMEM(block, BF)],
        compiler_params=params_of(),
    )(padded, weight, jnp.asarray(lane_masks(width), BF))


CHUNK = 6


def conv_weight_kernel(tap_ref, in_ref, grad_ref, mask_ref, out_ref, taps_ref, turn_ref):
    parts = in_ref.shape[0]
    begin = tap_ref[pl.program_id(0)]
    strips = D // 128
    rows = CHUNK * WIDTH
    for part in range(parts):
        turned = pltpu.roll(in_ref[part], in_ref.shape[2] - begin, 1)
        for tap in range(CHUNK):
            taps_ref[part, tap * PART : (tap + 1) * PART, :] = turned[:, tap : tap + ROWS].astype(
                BF
            )
    sums = []
    for part in range(parts):
        term = dot_nn(taps_ref[part], grad_ref[part])
        pieces = []
        for tap in range(CHUNK):
            total = None
            for group in range(mask_ref.shape[0]):
                low = tap * PART + group * WIDTH
                piece = term[low : low + WIDTH, :] * mask_ref[group : group + 1, :]
                total = piece if total is None else total + piece
            pieces.append(total)
        sums.append(jnp.concatenate(pieces, axis=0))
    for strip in range(strips):
        part, low = divmod(strip * 128, PART)
        columns = sums[part][:, low : min(low + 128, PART)]
        if low + 128 > PART:
            columns = jnp.concatenate([columns, sums[part + 1][:, : low + 128 - PART]], axis=1)
        turn_ref[pl.ds(strip, rows, stride=strips), :] = columns
    out_ref[...] = turn_ref[...].astype(BF)


PART = 4 * WIDTH


def conv_chunks(geometry):
    base, tap_rows = geometry.place("conv_w"), WIDTH * D // 128
    tables = []
    for slot in range(geometry.dp_count):
        needs = []
        for code in range(geometry.code_count):
            begin = geometry.begins[slot * geometry.code_count + code] - base
            low = max(begin // tap_rows, 0)
            high = min(-(-(begin + geometry.window) // tap_rows), KERNEL)
            needs.append((low, high))
        count = max(-(-(high - low) // CHUNK) for low, high in needs)
        for number in range(max(count, 0)):
            tables.append(
                [min(max(low, 0), KERNEL) + number * CHUNK for low, _ in needs]
            )
    clipped = [[min(tap, KERNEL - CHUNK) for tap in row] for row in tables]
    return [list(column) for column in zip(*clipped)]


def conv_weight_grad(conv_in, grad_low, geometry, code_index):
    parts = D // PART
    front = KERNEL // 2
    padded = jnp.pad(
        jnp.transpose(conv_in).astype(F32),
        ((0, 0), (front, ROWS + KERNEL - front - conv_in.shape[0])),
    ).reshape(parts, PART, ROWS + KERNEL)
    grads = jnp.transpose(grad_low.reshape(ROWS, parts, PART), (1, 0, 2))
    masks = jnp.asarray(lane_masks(PART), F32)
    chunks = conv_chunks(geometry)
    table = lax.dynamic_index_in_dim(jnp.asarray(chunks, jnp.int32), code_index, 0, False)
    rows = CHUNK * WIDTH * D // 128
    out = pl.pallas_call(
        conv_weight_kernel,
        grid_spec=pltpu.PrefetchScalarGridSpec(
            num_scalar_prefetch=1,
            grid=(len(chunks[0]),),
            in_specs=[
                pl.BlockSpec(padded.shape, lambda i, t: (0, 0, 0)),
                pl.BlockSpec(grads.shape, lambda i, t: (0, 0, 0)),
                pl.BlockSpec(masks.shape, lambda i, t: (0, 0)),
            ],
            out_specs=pl.BlockSpec((rows, 128), lambda i, t: (i, 0)),
            scratch_shapes=[
                pltpu.VMEM((parts, CHUNK * PART, ROWS), BF),
                pltpu.VMEM((rows, 128), F32),
            ],
        ),
        out_shape=jax.ShapeDtypeStruct((len(chunks[0]) * rows, 128), BF),
        compiler_params=params_of(),
    )(table, padded, grads, masks)
    return out, chunks


BLOCK = 128


def half_mask(side):
    lane = lax.broadcasted_iota(jnp.int32, (1, BLOCK), 1)
    return jnp.where(lane // HEAD_DIM == side, 1.0, 0.0).astype(BF)


def toeplitz(span_ref, head):
    row = jnp.broadcast_to(span_ref[pl.ds(head, 1), :], (BLOCK, SPAN))
    return pltpu.roll(row, 0, 1, stride=1, stride_axis=0)


def hop_columns(hop):
    return [hop[:, index : index + 1] for index in range(ROWS // BLOCK)]


def seen_biases(turned, pick, near, hop):
    moved = [dot_nn(near, item.astype(BF)) for item in turned]
    columns = [jnp.broadcast_to(column, (SEEN, ROWS)) for column in hop_columns(hop)]
    tables = []
    for item in moved:
        table = None
        for index, column in enumerate(columns):
            low = index * BLOCK
            part = column * item[:, ROWS - low : SPAN - low]
            table = part if table is None else table + part
        tables.append(table.astype(BF))
    return [dot_nt(table, pick) for table in tables]


def wide(column, length):
    return jnp.concatenate([column] * (length // BLOCK), axis=1)


def attention_forward_kernel(
    q_ref, k_ref, v_ref, gate_ref, span_ref, fill_ref, out_ref, lse_ref, score_ref, turn_ref
):
    step = pl.program_id(0)
    length = q_ref.shape[0]
    values = jnp.transpose(v_ref[...])
    sides = range(2)
    turned = [toeplitz(span_ref, step * 2 + side) for side in sides]
    for side in sides:
        score_ref[side] = dot_nt(k_ref[...] * half_mask(side), q_ref[...])
    tops = []
    for side in sides:
        gate = gate_ref[pl.ds(step * 2 + side, 1), :]
        top = None
        for low in range(0, length, BLOCK):
            rows = slice(low, low + BLOCK)
            bias = turned[side][:, ROWS - low : SPAN - low]
            scores = score_ref[side, rows, :] + gate * bias + wide(fill_ref[rows, :], length)
            score_ref[side, rows, :] = scores
            most = jnp.max(scores, axis=0, keepdims=True)
            top = most if top is None else jnp.maximum(top, most)
        tops.append(top)
    totals = []
    for side in sides:
        total = None
        for low in range(0, length, BLOCK):
            rows = slice(low, low + BLOCK)
            weights = jnp.exp(score_ref[side, rows, :] - tops[side])
            part = jnp.sum(weights, axis=0, keepdims=True)
            total = part if total is None else total + part
            turn_ref[side, rows, :] = weights.astype(BF)
        totals.append(total)
    mixed = []
    for side in sides:
        lse_ref[pl.ds(step * 2 + side, 1), :] = tops[side] + jnp.log(totals[side])
        part = dot_nn(values[side * HEAD_DIM : (side + 1) * HEAD_DIM, :], turn_ref[side])
        mixed.append(part * (1.0 / totals[side]))
    out_ref[...] = jnp.transpose(jnp.concatenate(mixed, axis=0)).astype(BF)


SEEN_HEADS = 12


def seen_forward_kernel(
    q_ref, k_ref, v_ref, gate_ref, span_ref, fill_ref, pick_ref, near_ref, hop_ref,
    out_ref, lse_ref, bias_ref,
):
    heads = range(SEEN_HEADS)
    base = pl.program_id(0) * SEEN_HEADS
    pick, near, hop = pick_ref[...], near_ref[...], hop_ref[...]
    pairs = range(SEEN_HEADS // 2)
    query = [q_ref[:, pair * BLOCK : (pair + 1) * BLOCK] for pair in pairs]
    keyv = [k_ref[:, pair * BLOCK : (pair + 1) * BLOCK] for pair in pairs]
    values = [jnp.transpose(v_ref[:, pair * BLOCK : (pair + 1) * BLOCK]) for pair in pairs]
    turned = [toeplitz(span_ref, base + head) for head in heads]
    bias = seen_biases(turned, pick, near, hop)
    scores = [dot_nt(keyv[head // 2] * half_mask(head % 2), query[head // 2]) for head in heads]
    for head in heads:
        bias_ref[head * BLOCK : (head + 1) * BLOCK, :] = bias[head].astype(BF)
    scores = [
        scores[head] + gate_ref[pl.ds(base + head, 1), :] * bias[head] + fill_ref[...]
        for head in heads
    ]
    tops = [jnp.max(item, axis=0, keepdims=True) for item in scores]
    weights = [jnp.exp(scores[head] - tops[head]) for head in heads]
    totals = [jnp.sum(item, axis=0, keepdims=True) for item in weights]
    mixed = []
    for head in heads:
        lse_ref[pl.ds(base + head, 1), :] = tops[head] + jnp.log(totals[head])
        low = (head % 2) * HEAD_DIM
        part = dot_nn(values[head // 2][low : low + HEAD_DIM, :], weights[head].astype(BF))
        mixed.append(part * (1.0 / totals[head]))
    for pair in pairs:
        both = jnp.concatenate(mixed[2 * pair : 2 * pair + 2], axis=0)
        out_ref[:, pair * BLOCK : (pair + 1) * BLOCK] = jnp.transpose(both).astype(BF)


def pair_spec(length):
    return pl.BlockSpec((length, 2 * HEAD_DIM), lambda i: (0, i))


def whole_spec(shape):
    return pl.BlockSpec(shape, lambda i: (0,) * len(shape))


def attention_forward(query, keyv, value, gate, span, fill, pick):
    length = query.shape[0]
    args = [query, keyv, value, gate, span, fill] + list(pick or ())
    shapes = [
        jax.ShapeDtypeStruct((length, D), BF),
        jax.ShapeDtypeStruct((16, length), F32),
    ]
    if pick is None:
        found = pl.pallas_call(
            attention_forward_kernel,
            grid=(HEADS // 2,),
            in_specs=[pair_spec(length)] * 3 + [whole_spec(a.shape) for a in args[3:]],
            out_specs=[pair_spec(length), whole_spec((16, length))],
            out_shape=shapes,
            scratch_shapes=[
                pltpu.VMEM((2, length, length), F32),
                pltpu.VMEM((2, length, length), BF),
            ],
            compiler_params=params_of(),
        )(*args)
        return found[0], found[1], None
    columns = pl.BlockSpec((length, SEEN_HEADS * HEAD_DIM), lambda i: (0, i))
    return pl.pallas_call(
        seen_forward_kernel,
        grid=(HEADS // SEEN_HEADS,),
        in_specs=[columns] * 3 + [whole_spec(a.shape) for a in args[3:]],
        out_specs=[
            columns,
            whole_spec((16, length)),
            pl.BlockSpec((SEEN_HEADS * BLOCK, BLOCK), lambda i: (i, 0)),
        ],
        out_shape=shapes + [jax.ShapeDtypeStruct((HEADS * BLOCK, BLOCK), BF)],
        compiler_params=params_of(),
    )(*args)


def diagonal_sums(turn):
    half = BLOCK // 2
    while half:
        turn = turn[:half, :] + pltpu.roll(turn[half:, :], SPAN - half, 1)
        half //= 2
    return turn


def attention_backward_kernel(
    q_ref, k_ref, v_ref, up_ref, gate_ref, span_ref, fill_ref, lse_ref,
    out_ref, sum_ref, dgate_ref, dspan_ref, prob_ref, grad_ref, turn_ref, low_ref, diag_ref,
):
    step = pl.program_id(0)
    length = q_ref.shape[0]
    sides = range(2)

    @pl.when(step == 0)
    def _():
        dspan_ref[...] = jnp.zeros_like(dspan_ref)
        dgate_ref[...] = jnp.zeros_like(dgate_ref)

    keys = jnp.transpose(k_ref[...])
    turned = [toeplitz(span_ref, step * 2 + side) for side in sides]
    for side in sides:
        prob_ref[side] = dot_nt(k_ref[...] * half_mask(side), q_ref[...])
        grad_ref[side] = dot_nt(v_ref[...] * half_mask(side), up_ref[...])
        diag_ref[side] = jnp.zeros_like(diag_ref[side])
    shared = []
    for side in sides:
        gate = gate_ref[pl.ds(step * 2 + side, 1), :]
        lse = lse_ref[pl.ds(step * 2 + side, 1), :]
        total = None
        for low in range(0, length, BLOCK):
            rows = slice(low, low + BLOCK)
            bias = turned[side][:, ROWS - low : SPAN - low]
            scores = prob_ref[side, rows, :] + gate * bias + wide(fill_ref[rows, :], length)
            probs = jnp.exp(scores - lse)
            prob_ref[side, rows, :] = probs
            low_ref[side, rows, :] = probs.astype(BF)
            part = jnp.sum(probs * grad_ref[side, rows, :], axis=0, keepdims=True)
            total = part if total is None else total + part
        shared.append(total)
    val_total = sum(dot_nn(low_ref[side], up_ref[...] * half_mask(side)) for side in sides)
    for side in sides:
        gate = gate_ref[pl.ds(step * 2 + side, 1), :]
        dgate = None
        for low in range(0, length, BLOCK):
            rows = slice(low, low + BLOCK)
            bias = turned[side][:, ROWS - low : SPAN - low]
            grad_scores = prob_ref[side, rows, :] * (grad_ref[side, rows, :] - shared[side])
            turn_ref[side, rows, :] = grad_scores.astype(BF)
            part = jnp.sum(grad_scores * bias, axis=0, keepdims=True)
            dgate = part if dgate is None else dgate + part
            diag_ref[side, :, ROWS - low : SPAN - low] += grad_scores * gate
        dgate_ref[pl.ds(step * 2 + side, 1), :] = dgate
    key_total = sum(dot_nn(turn_ref[side], q_ref[...] * half_mask(side)) for side in sides)
    halves = [
        dot_nn(keys[side * HEAD_DIM : (side + 1) * HEAD_DIM, :], turn_ref[side]) for side in sides
    ]
    for side in sides:
        dspan_ref[pl.ds(step * 2 + side, 1), :] = diagonal_sums(diag_ref[side])
    grad_query = jnp.transpose(jnp.concatenate(halves, axis=0)) * HEAD_DIM ** (-0.5)
    out_ref[0] = grad_query.astype(BF)
    out_ref[1] = key_total.astype(BF)
    out_ref[2] = val_total.astype(BF)
    sum_ref[0:1, :] = jnp.sum(grad_query, axis=0, keepdims=True)
    sum_ref[1:2, :] = jnp.sum(val_total, axis=0, keepdims=True)


def split_low(value):
    high = value.astype(BF)
    return high, (value - high.astype(F32)).astype(BF)


def seen_backward_kernel(
    q_ref, k_ref, v_ref, up_ref, gate_ref, fill_ref, lse_ref, pick_ref, hop_ref, flip_ref,
    bias_ref, out_ref, sum_ref, dgate_ref, dspan_ref, diag_ref,
):
    heads, pairs = range(SEEN_HEADS), range(SEEN_HEADS // 2)
    base = pl.program_id(0) * SEEN_HEADS

    @pl.when(base == 0)
    def _():
        dspan_ref[...] = jnp.zeros_like(dspan_ref)
        dgate_ref[...] = jnp.zeros_like(dgate_ref)

    def pair_of(ref):
        return [ref[:, pair * BLOCK : (pair + 1) * BLOCK] for pair in pairs]

    query, keyv, value, upstream = (pair_of(ref) for ref in (q_ref, k_ref, v_ref, up_ref))
    keys = [jnp.transpose(item) for item in keyv]
    gate = [gate_ref[pl.ds(base + head, 1), :] for head in heads]
    bias = [bias_ref[head * BLOCK : (head + 1) * BLOCK, :].astype(F32) for head in heads]
    scores = [dot_nt(keyv[head // 2] * half_mask(head % 2), query[head // 2]) for head in heads]
    grads = [dot_nt(value[head // 2] * half_mask(head % 2), upstream[head // 2]) for head in heads]
    probs = [
        jnp.exp(
            scores[head]
            + gate[head] * bias[head]
            + fill_ref[...]
            - lse_ref[pl.ds(base + head, 1), :]
        )
        for head in heads
    ]
    shared = [jnp.sum(probs[head] * grads[head], axis=0, keepdims=True) for head in heads]
    moves = [probs[head] * (grads[head] - shared[head]) for head in heads]
    val_terms = [
        dot_nn(probs[head].astype(BF), upstream[head // 2] * half_mask(head % 2)) for head in heads
    ]
    low = [item.astype(BF) for item in moves]
    key_terms = [dot_nn(low[head], query[head // 2] * half_mask(head % 2)) for head in heads]
    halves = [
        dot_nn(keys[head // 2][(head % 2) * HEAD_DIM : (head % 2 + 1) * HEAD_DIM, :], low[head])
        for head in heads
    ]
    for head in heads:
        dgate_ref[pl.ds(base + head, 1), :] = jnp.sum(
            moves[head] * bias[head], axis=0, keepdims=True
        )
    pieces = [jnp.concatenate(split_low(moves[head] * gate[head]), axis=0) for head in heads]
    placed = [dot_nn(piece, pick_ref[...]) for piece in pieces]
    columns = [jnp.broadcast_to(column, (SEEN, ROWS)) for column in hop_columns(hop_ref[...])]
    for head in heads:
        both = placed[head][:BLOCK, :] + placed[head][BLOCK:, :]
        diag_ref[head] = jnp.zeros_like(diag_ref[head])
        for index, column in enumerate(columns):
            begin = ROWS - index * BLOCK
            diag_ref[head, :, begin : begin + ROWS] += column * both
    turns = [
        dot_nn(flip_ref[...], jnp.concatenate(split_low(diag_ref[head]), axis=0)) for head in heads
    ]
    for head in heads:
        dspan_ref[pl.ds(base + head, 1), :] = diagonal_sums(turns[head])
    for pair in pairs:
        cols = slice(pair * BLOCK, (pair + 1) * BLOCK)
        grad_query = jnp.transpose(jnp.concatenate(halves[2 * pair : 2 * pair + 2], axis=0))
        grad_query = grad_query * HEAD_DIM ** (-0.5)
        val_total = val_terms[2 * pair] + val_terms[2 * pair + 1]
        out_ref[0, :, cols] = grad_query.astype(BF)
        out_ref[1, :, cols] = (key_terms[2 * pair] + key_terms[2 * pair + 1]).astype(BF)
        out_ref[2, :, cols] = val_total.astype(BF)
        sum_ref[0:1, cols] = jnp.sum(grad_query, axis=0, keepdims=True)
        sum_ref[1:2, cols] = jnp.sum(val_total, axis=0, keepdims=True)


def attention_backward(query, keyv, value, upstream, gate, span, fill, lse, pick, bias):
    length = query.shape[0]
    heads = 2 if pick is None else SEEN_HEADS
    columns = pl.BlockSpec((length, heads * HEAD_DIM), lambda i: (0, i))
    shapes = [
        jax.ShapeDtypeStruct((3, length, D), BF),
        jax.ShapeDtypeStruct((8, D), F32),
        jax.ShapeDtypeStruct((16, length), F32),
        jax.ShapeDtypeStruct((16, SPAN), F32),
    ]
    out_specs = [
        pl.BlockSpec((3, length, heads * HEAD_DIM), lambda i: (0, 0, i)),
        pl.BlockSpec((8, heads * HEAD_DIM), lambda i: (0, i)),
        whole_spec((16, length)),
        whole_spec((16, SPAN)),
    ]
    if pick is None:
        args = [query, keyv, value, upstream, gate, span, fill, lse]
        kernel, more = attention_backward_kernel, []
        scratch = [
            pltpu.VMEM((2, length, length), F32),
            pltpu.VMEM((2, length, length), F32),
            pltpu.VMEM((2, length, length), BF),
            pltpu.VMEM((2, length, length), BF),
            pltpu.VMEM((2, BLOCK, SPAN), F32),
        ]
    else:
        turned = jnp.transpose(pick[1])
        flip = jnp.concatenate([turned, turned], axis=1)
        args = [query, keyv, value, upstream, gate, fill, lse, pick[0], pick[2], flip, bias]
        kernel = seen_backward_kernel
        more = [pl.BlockSpec((heads * BLOCK, BLOCK), lambda i: (i, 0))]
        scratch = [pltpu.VMEM((heads, BLOCK, SPAN), F32)]
    return pl.pallas_call(
        kernel,
        grid=(HEADS // heads,),
        in_specs=[columns] * 4 + [whole_spec(a.shape) for a in args[4 : len(args) - len(more)]] + more,
        out_specs=out_specs,
        out_shape=shapes,
        scratch_shapes=scratch,
        compiler_params=params_of(),
    )(*args)


def weight_grad_kernel(left_ref, right_ref, out_ref, turn_ref):
    rows = left_ref.shape[1]
    strips = right_ref.shape[1] // 128
    grad = dot_tn(left_ref[...], right_ref[...])
    for strip in range(strips):
        turn_ref[pl.ds(strip, rows, stride=strips), :] = grad[:, strip * 128 : (strip + 1) * 128]
    out_ref[...] = turn_ref[...].astype(BF)


def weight_grad(left, right, rows=384):
    length, depth = left.shape
    strips = right.shape[1] // 128
    return pl.pallas_call(
        weight_grad_kernel,
        grid=(depth // rows,),
        in_specs=[
            pl.BlockSpec((length, rows), lambda i: (0, i)),
            pl.BlockSpec(right.shape, lambda i: (0, 0)),
        ],
        out_specs=pl.BlockSpec((rows * strips, 128), lambda i: (i, 0)),
        out_shape=jax.ShapeDtypeStruct((depth * strips, 128), BF),
        scratch_shapes=[pltpu.VMEM((rows * strips, 128), F32)],
        compiler_params=params_of(),
    )(left, right)


def unpack_jobs(geometry, specs):
    jobs = []
    for target, (base, depth, strips, rows) in enumerate(specs):
        for low in range(0, depth, rows):
            begin = base + low * strips
            jobs.append((target, low, rows, strips) + geometry.pieces(begin, begin + rows * strips))
    return jobs


def stream_jobs(jobs, source_ref, buffer_ref, edge_ref, sems, work):
    def copies(number):
        main, edges = jobs[number][4:6]
        slot = number % 2
        found = []
        for shard, begin, low, count in main:
            found.append(
                (source_ref.at[shard, pl.ds(begin, count)], buffer_ref.at[slot, pl.ds(low, count)])
            )
        for place, (shard, _) in enumerate(edges):
            found.append((source_ref.at[shard, pl.ds(0, TILE)], edge_ref.at[slot, place]))
        return [
            pltpu.make_async_copy(source, target, sems.at[slot, index])
            for index, (source, target) in enumerate(found)
        ]

    for copy in copies(0):
        copy.start()
    for number, job in enumerate(jobs):
        if number + 1 < len(jobs):
            for copy in copies(number + 1):
                copy.start()
        for copy in copies(number):
            copy.wait()
        slot = number % 2
        for place, (_, low) in enumerate(job[5]):
            buffer_ref[slot, low : low + TILE, :] += edge_ref[slot, place]
        work(number, job, slot)


def unpack_kernel(*refs, jobs, stages):
    source_ref = refs[0]
    targets = refs[1 : 1 + len(stages)]
    buffer_ref, edge_ref, turn_ref, sems, out_sems = refs[1 + len(stages) : 6 + len(stages)]
    stage_refs = refs[6 + len(stages) :]
    pending = {}

    def work(number, job, slot):
        target, low, rows, strips = job[:4]
        stage_ref, key = stage_refs[stages[target]], (stages[target], slot)
        if key in pending:
            pending.pop(key).wait()
        turn_ref[: rows * strips, :] = buffer_ref[slot, : rows * strips, :].astype(F32)
        for strip in range(strips):
            stage_ref[slot, :rows, strip * 128 : (strip + 1) * 128] = turn_ref[
                pl.ds(strip, rows, stride=strips), :
            ].astype(BF)
        copy = pltpu.make_async_copy(
            stage_ref.at[slot, pl.ds(0, rows)],
            targets[target].at[pl.ds(low, rows)],
            out_sems.at[stages[target], slot],
        )
        copy.start()
        pending[key] = copy

    stream_jobs(jobs, source_ref, buffer_ref, edge_ref, sems, work)
    for copy in pending.values():
        copy.wait()


def unpack(geometry, windows, specs):
    jobs = unpack_jobs(geometry, specs)
    kinds = sorted({spec[2] for spec in specs})
    stages = [kinds.index(spec[2]) for spec in specs]
    most = max(job[2] * job[3] for job in jobs)
    copies = max(len(job[4]) + len(job[5]) for job in jobs)
    edges = max([1] + [len(job[5]) for job in jobs])
    return pl.pallas_call(
        functools.partial(unpack_kernel, jobs=jobs, stages=stages),
        in_specs=[pl.BlockSpec(memory_space=pl.ANY)],
        out_specs=[pl.BlockSpec(memory_space=pl.ANY)] * len(specs),
        out_shape=[jax.ShapeDtypeStruct((s[1], s[2] * 128), BF) for s in specs],
        scratch_shapes=[
            pltpu.VMEM((2, most, 128), BF),
            pltpu.VMEM((2, edges, TILE, 128), BF),
            pltpu.VMEM((most, 128), F32),
            pltpu.SemaphoreType.DMA((2, copies)),
            pltpu.SemaphoreType.DMA((len(kinds), 2)),
        ]
        + [
            pltpu.VMEM((2, max(s[3] for s in specs if s[2] == kind), kind * 128), BF)
            for kind in kinds
        ],
        compiler_params=pltpu.CompilerParams(vmem_limit_bytes=VMEM_LIMIT),
    )(windows)


def unpack_conv_kernel(
    code_ref, source_ref, target_ref, buffer_ref, edge_ref, turn_ref, stage_ref, sems, out_sems, *,
    jobs, width
):
    first = code_ref[0] * width
    strip = first // 128
    strips = D // 128
    lead = first - strip * 128
    pending = {}

    def work(number, job, slot):
        low, rows = job[1], job[2]
        if slot in pending:
            pending.pop(slot).wait()
        turn_ref[...] = buffer_ref[slot].astype(F32)
        one = turn_ref[pl.ds(strip, rows, stride=strips), :]
        two = turn_ref[pl.ds(jnp.minimum(strip + 1, strips - 1), rows, stride=strips), :]
        pair = pltpu.roll(jnp.concatenate([one, two], axis=1), lax.rem(256 - lead, 256), 1)
        stage_ref[slot] = pair[:, :width].astype(BF)
        copy = pltpu.make_async_copy(
            stage_ref.at[slot], target_ref.at[pl.ds(low, rows)], out_sems.at[slot]
        )
        copy.start()
        pending[slot] = copy

    stream_jobs(jobs, source_ref, buffer_ref, edge_ref, sems, work)
    for copy in pending.values():
        copy.wait()


def unpack_conv(geometry, windows, code_index, rows=768):
    width = D // geometry.code_count
    depth = KERNEL * WIDTH
    jobs = unpack_jobs(geometry, [(geometry.place("conv_w"), depth, D // 128, rows)])
    copies = max(len(job[4]) + len(job[5]) for job in jobs)
    edges = max([1] + [len(job[5]) for job in jobs])
    return pl.pallas_call(
        functools.partial(unpack_conv_kernel, jobs=jobs, width=width),
        in_specs=[
            pl.BlockSpec(memory_space=pltpu.SMEM),
            pl.BlockSpec(memory_space=pl.ANY),
        ],
        out_specs=pl.BlockSpec(memory_space=pl.ANY),
        out_shape=jax.ShapeDtypeStruct((depth, width), BF),
        scratch_shapes=[
            pltpu.VMEM((2, rows * D // 128, 128), BF),
            pltpu.VMEM((2, edges, TILE, 128), BF),
            pltpu.VMEM((rows * D // 128, 128), F32),
            pltpu.VMEM((2, rows, width), BF),
            pltpu.SemaphoreType.DMA((2, copies)),
            pltpu.SemaphoreType.DMA((2,)),
        ],
        compiler_params=pltpu.CompilerParams(vmem_limit_bytes=VMEM_LIMIT),
    )(jnp.full((1,), code_index, jnp.int32), windows)


def pack_kernel(code_ref, *refs, plans):
    sources, out_ref, sems = refs[:-2], refs[-2], refs[-1]
    for code, plan in enumerate(plans):

        @pl.when(code_ref[0] == code)
        def _():
            copies = [
                pltpu.make_async_copy(
                    sources[source].at[pl.ds(begin, count)],
                    out_ref.at[slot, pl.ds(low, count)],
                    sems.at[index],
                )
                for index, (source, begin, slot, low, count) in enumerate(plan)
            ]
            for copy in copies:
                copy.start()
            for copy in copies:
                copy.wait()


def pack_plans(geometry, spans):
    plans = []
    for code in range(geometry.code_count):
        plan = []
        for slot in range(geometry.dp_count):
            begin = geometry.begins[slot * geometry.code_count + code]
            stop = begin + geometry.window
            row = begin
            while row < stop:
                place, rows, source, inner = next(
                    item for item in spans[code] if item[0] <= row < item[0] + item[1]
                )
                count = min(stop, place + rows) - row
                plan.append((source, inner + row - place, slot, row - begin, count))
                row += count
        plans.append(plan)
    return plans


def pack(geometry, code_index, sources, spans):
    plans = pack_plans(geometry, spans)
    return pl.pallas_call(
        functools.partial(pack_kernel, plans=plans),
        in_specs=[pl.BlockSpec(memory_space=pltpu.SMEM)]
        + [pl.BlockSpec(memory_space=pl.ANY)] * len(sources),
        out_specs=pl.BlockSpec(memory_space=pltpu.VMEM),
        out_shape=jax.ShapeDtypeStruct((geometry.dp_count, geometry.window, 128), BF),
        scratch_shapes=[pltpu.SemaphoreType.DMA((max(len(plan) for plan in plans),))],
        compiler_params=pltpu.CompilerParams(vmem_limit_bytes=VMEM_LIMIT),
    )(jnp.full((1,), code_index, jnp.int32), *sources)


def blocks_of_code(block):
    count = lax.axis_size("code")
    return [block] + [
        lax.ppermute(block, "code", [(i, (i + step) % count) for i in range(count)])
        for step in range(1, count)
    ]


def side_kernel(code_ref, *refs):
    blocks, out_ref = refs[:-1], refs[-1]
    count, width = len(blocks), blocks[0].shape[1]
    for code in range(count):

        @pl.when(code_ref[0] == code)
        def _():
            for source in range(count):
                out_ref[:, source * width : (source + 1) * width] = blocks[
                    (code - source) % count
                ][...]


def side_by_side(block, code_index):
    blocks = blocks_of_code(block)
    rows, width = block.shape
    return pl.pallas_call(
        side_kernel,
        in_specs=[pl.BlockSpec(memory_space=pltpu.SMEM)]
        + [pl.BlockSpec(memory_space=pltpu.VMEM)] * len(blocks),
        out_specs=pl.BlockSpec(memory_space=pltpu.VMEM),
        out_shape=jax.ShapeDtypeStruct((rows, width * len(blocks)), block.dtype),
    )(jnp.full((1,), code_index, jnp.int32), *blocks)


def sum_over(value, axis):
    count = lax.axis_size(axis)
    if count & (count - 1):
        return lax.psum(value, axis)
    bit = 1
    while bit < count:
        value = value + lax.ppermute(value, axis, [(i, i ^ bit) for i in range(count)])
        bit *= 2
    return value


def norm_forward(before, norm_gain, norm_shift):
    centred = before - jnp.mean(before, axis=-1, keepdims=True)
    inv_std = lax.rsqrt(jnp.mean(centred * centred, axis=-1, keepdims=True) + NORM_EPSILON)
    normed = centred * inv_std
    return (normed * norm_gain + norm_shift, normed, inv_std)


def norm_backward(upstream, normed, inv_std, norm_gain):
    scaled = upstream * norm_gain
    centred_grad = (
        scaled
        - jnp.mean(scaled, axis=-1, keepdims=True)
        - normed * jnp.mean(scaled * normed, axis=-1, keepdims=True)
    )
    return (
        centred_grad * inv_std,
        jnp.sum(upstream * normed, axis=0),
        jnp.sum(upstream, axis=0),
    )


def gelu(pre_act):
    return 0.5 * pre_act * (1.0 + lax.erf(pre_act * 0.7071067811865476))


def gelu_grad(pre_act):
    return (
        0.5 * (1.0 + lax.erf(pre_act * 0.7071067811865476))
        + pre_act * jnp.exp(-0.5 * pre_act * pre_act) * 0.3989422804014327
    )


def vec_part(vector, slot_index):
    return vector[slot_index * D : (slot_index + 1) * D]


def gate_maps():
    rows = (np.arange(D)[:, None] % HEAD_DIM == np.arange(HEAD_DIM)[None, :]).astype(np.float32)
    groups = np.arange(8)[:, None] // 4 == np.arange(2 * HEADS)[None, :] // HEADS
    own = np.arange(D)[:, None] // HEAD_DIM == np.arange(2 * HEADS)[None, :] % HEADS
    return rows, groups.astype(np.float32), own.astype(np.float32)


def exact_dot(left, right, dims=((1,), (0,))):
    return lax.dot_general(left, right, (dims, ((), ())), precision=HIGHEST)


def gate_columns(gate_weight):
    rows, groups, own = gate_maps()
    wide = gate_weight.astype(F32)
    sums = exact_dot(wide, jnp.asarray(groups))
    return exact_dot(jnp.asarray(rows), sums[:HEAD_DIM]) * own, sums[HEAD_DIM:]


def gate_forward(in_low, weights):
    columns, bias = weights["gate_columns"]
    high = columns.astype(BF)
    rest = (columns - high.astype(F32)).astype(BF)
    logit = dot_nn(in_low, jnp.concatenate([high, rest], axis=1))
    logit = logit[:, : 2 * HEADS] + logit[:, 2 * HEADS :] + bias
    pair = jax.nn.sigmoid(logit)
    first, second = pair[:, :HEADS], pair[:, HEADS:]
    gate_vals = first * (second * weights["gate_scale"].astype(F32) - 1.0) + 2.0
    return (gate_vals, first, second)


def gate_backward(grad_gate, first, second, in_low, weights):
    scale_vec = weights["gate_scale"].astype(F32)
    grad_scale = jnp.sum(grad_gate * first * second, axis=0)
    grad_one = grad_gate * (second * scale_vec - 1.0) * first * (1.0 - first)
    grad_two = grad_gate * first * scale_vec * second * (1.0 - second)
    both = jnp.concatenate([grad_one, grad_two], axis=1)
    rows, groups, own = gate_maps()
    high = both.astype(BF)
    rest = (both - high.astype(F32)).astype(BF)
    product = dot_tn(in_low, jnp.concatenate([high, rest], axis=1))
    product = (product[:, : 2 * HEADS] + product[:, 2 * HEADS :]) * own
    summed = exact_dot(jnp.asarray(rows), product, ((0,), (0,)))
    summed = jnp.concatenate([summed, jnp.sum(both, axis=0, keepdims=True)], axis=0)
    grad_proj = exact_dot(summed, jnp.asarray(groups), ((1,), (1,)))
    grad_heads = exact_dot(both, weights["gate_columns"][0], ((1,), (1,)))
    return (grad_heads, grad_proj, grad_scale)


def layer_forward(hidden, fill, weights, span, pick):
    vector = weights["layer_vec"].astype(F32)
    in_low = hidden.astype(BF)
    qkv_proj = dot_nn(in_low, weights["w_qkv"])
    query_low = ((qkv_proj[:, :D] + vec_part(vector, 0)) * HEAD_DIM ** (-0.5)).astype(BF)
    key_low = qkv_proj[:, D : 2 * D].astype(BF)
    value_low = (qkv_proj[:, 2 * D :] + vec_part(vector, 1)).astype(BF)
    gate_vals, first, second = gate_forward(in_low, weights)
    gate_wide = jnp.pad(jnp.transpose(gate_vals), ((0, 16 - HEADS), (0, 0)))
    attended, lse, bias = attention_forward(
        query_low, key_low, value_low, gate_wide, span, fill, pick
    )
    attn_out = dot_nn(attended, weights["w_out"]) + vec_part(vector, 2)
    mid_rows, normed_one, inv_one = norm_forward(
        DEEP_ALPHA * hidden + attn_out, vec_part(vector, 3), vec_part(vector, 4)
    )
    mid_low = mid_rows.astype(BF)
    pre_act = dot_nn(mid_low, weights["w_up"]) + vector[8 * D :]
    act_low = gelu(pre_act).astype(BF)
    ffn_out = dot_nn(act_low, weights["w_down"]) + vec_part(vector, 5)
    final_rows, normed_two, inv_two = norm_forward(
        DEEP_ALPHA * mid_rows + ffn_out, vec_part(vector, 6), vec_part(vector, 7)
    )
    kept = (in_low, query_low, key_low, value_low, gate_wide, first, second, lse, attended, bias)
    kept += (mid_low, pre_act, act_low, normed_one, inv_one, normed_two, inv_two)
    return (final_rows, kept)


def layer_backward(upstream, kept, fill, weights, span, pick):
    in_low, query_low, key_low, value_low, gate_wide, first, second, lse, attended, bias = kept[:10]
    mid_low, pre_act, act_low, normed_one, inv_one, normed_two, inv_two = kept[10:]
    vector = weights["layer_vec"].astype(F32)
    grad_res_two, grad_gain_two, grad_shift_two = norm_backward(
        upstream, normed_two, inv_two, vec_part(vector, 6)
    )
    ffn_low = grad_res_two.astype(BF)
    grad_down = weight_grad(act_low, ffn_low, 768)
    grad_pre = dot_nt(ffn_low, weights["w_down"]) * gelu_grad(pre_act)
    pre_low = grad_pre.astype(BF)
    grad_up = weight_grad(mid_low, pre_low)
    grad_mid = DEEP_ALPHA * grad_res_two + dot_nt(pre_low, weights["w_up"])
    grad_res_one, grad_gain_one, grad_shift_one = norm_backward(
        grad_mid, normed_one, inv_one, vec_part(vector, 3)
    )
    out_low = grad_res_one.astype(BF)
    grad_out = weight_grad(attended, out_low)
    grad_att = dot_nt(out_low, weights["w_out"]).astype(BF)
    parts, part_sums, grad_gate, grad_span = attention_backward(
        query_low, key_low, value_low, grad_att, gate_wide, span, fill, lse, pick, bias
    )
    grad_heads, grad_gate_proj, grad_gate_scale = gate_backward(
        jnp.transpose(grad_gate[:HEADS]), first, second, in_low, weights
    )
    proj_low = jnp.concatenate([parts[0], parts[1], parts[2]], axis=1)
    grad_qkv = weight_grad(in_low, proj_low)
    grad_hidden = DEEP_ALPHA * grad_res_one + dot_nt(proj_low, weights["w_qkv"]) + grad_heads
    grad_vec = jnp.concatenate(
        [
            part_sums[0],
            part_sums[1],
            jnp.sum(grad_res_one, axis=0),
            grad_gain_one,
            grad_shift_one,
            jnp.sum(grad_res_two, axis=0),
            grad_gain_two,
            grad_shift_two,
            jnp.sum(grad_pre, axis=0),
        ]
    )
    grad_map = {
        "w_qkv": grad_qkv,
        "w_out": grad_out,
        "w_up": grad_up,
        "w_down": grad_down,
        "layer_vec": grad_vec,
        "gate_proj": grad_gate_proj,
        "gate_scale": grad_gate_scale,
    }
    return (grad_hidden, grad_map, grad_span)


def head_pass(hidden, w_head, codebook, codes, target_codes):
    row_low = hidden.astype(BF)
    projected = dot_nn(row_low, w_head)
    inv_len = lax.rsqrt(jnp.sum(projected * projected, axis=-1, keepdims=True) + UNIT_EPSILON)
    unit_rows = projected * inv_len
    live_rows = (target_codes >= 0).astype(F32)[:, None]
    logits = LOGIT_SCALE * dot_nt(unit_rows.astype(BF), codebook)
    hits = (target_codes[:, None] == codes).astype(F32)
    top = jnp.max(logits, axis=1, keepdims=True)
    log_total = top + jnp.log(jnp.sum(jnp.exp(logits - top), axis=1, keepdims=True))
    picked = jnp.sum(logits * hits, axis=1, keepdims=True)
    loss_local = jnp.sum((log_total - picked) * live_rows)
    grad_logits = ((jnp.exp(logits - log_total) - hits) * live_rows * LOGIT_SCALE).astype(BF)
    grad_unit = dot_nn(grad_logits, codebook)
    grad_proj = (
        grad_unit - unit_rows * jnp.sum(unit_rows * grad_unit, axis=-1, keepdims=True)
    ) * inv_len
    proj_low = grad_proj.astype(BF)
    grad_head = weight_grad(row_low, proj_low)
    grad_rows = dot_nt(proj_low, w_head)
    return (loss_local, grad_rows, grad_head)


def local(
    patches,
    lengths,
    patch_masks,
    targets,
    codebook,
    params,
    first_moment,
    second_moment,
    step_count,
):
    dp_count = lax.axis_size("dp")
    code_count = lax.axis_size("code")
    code_index = lax.axis_index("code")
    shard_len = params.shape[0]
    shard_rows = shard_len // 128
    dp_index = lax.axis_index("dp")
    geometry = Geometry(dp_count, code_count, shard_rows)
    own_offset = lax.rem((dp_index * code_count + code_index) * shard_rows + geometry.phase, TILE)
    own_window = lax.dynamic_update_slice(
        jnp.zeros((geometry.window, 128), F32), params.reshape(shard_rows, 128), (own_offset, 0)
    ).astype(BF)
    windows = lax.all_gather(own_window, ("dp", "code"), axis=0, tiled=False)
    where = starts()

    def values(seg_name):
        extent = dict(layout())[seg_name]
        begin, amount = where[seg_name], math.prod(extent)
        low, high = begin // 128, -(-(begin + amount) // 128)
        found = geometry.exact(windows, low, high).reshape(-1)
        return found[begin - low * 128 : begin - low * 128 + amount].reshape(extent)

    w_patch = values("w_patch")
    glob_vec = values("glob_vec").astype(F32)
    gate_proj = values("gate_proj")
    gate_scale = values("gate_scale")
    rel_table = values("rel_table")
    w_head = values("w_head")
    layer_vec = values("layer_vec")
    conv_weight = unpack_conv(geometry, windows, code_index)
    weights = []
    for index in range(LAYERS):
        mats = unpack(
            geometry,
            windows,
            [
                (geometry.place("w_qkv", index), D, 3 * D // 128, 128),
                (geometry.place("w_out", index), D, D // 128, 384),
                (geometry.place("w_up", index), D, FF // 128, 128),
                (geometry.place("w_down", index), FF, D // 128, 512),
            ],
        )
        weights.append(
            dict(zip(("w_qkv", "w_out", "w_up", "w_down"), mats))
            | {
                "layer_vec": layer_vec[index],
                "gate_columns": gate_columns(gate_proj[index]),
                "gate_scale": gate_scale[index],
            }
        )

    places = jnp.arange(ROWS, dtype=jnp.int32)
    mask_row = jnp.pad(patch_masks[0], (0, ROWS - LONG))
    live_slot = places < jnp.minimum(lengths[0], LONG)
    visible = live_slot & (mask_row == 0)
    rank = jnp.cumsum(visible.astype(jnp.int32)) - 1
    pick = (
        visible[None, :] & (rank[None, :] == jnp.arange(SEEN, dtype=jnp.int32)[:, None])
    )
    pick_low = pick.astype(BF)
    near = jnp.sum(pick_low.reshape(SEEN, ROWS // BLOCK, BLOCK), axis=1)
    hop = jnp.sum(pick.astype(F32).reshape(SEEN, ROWS // BLOCK, BLOCK), axis=2)
    pick_seen = (pick_low, near, jnp.pad(hop, ((0, 0), (0, BLOCK - ROWS // BLOCK))))
    pick_full = pick.astype(F32)
    seen_valid = jnp.arange(SEEN, dtype=jnp.int32) < lengths[0] // 4
    seen_fill = jnp.broadcast_to(jnp.where(seen_valid, 0.0, MASK_FILL)[:, None], (SEEN, BLOCK))
    live_fill = jnp.broadcast_to(jnp.where(live_slot, 0.0, MASK_FILL)[:, None], (ROWS, BLOCK))
    live_float = live_slot.astype(F32)[:, None]
    span_table = span_onehot()
    span = dot_tn(
        jnp.pad(rel_table, ((0, 0), (0, 16 - HEADS))), jnp.asarray(span_table.T, BF)
    )

    all_codes = jnp.concatenate(blocks_of_code(codebook), axis=0)
    code_places = (
        code_index - jnp.arange(code_count, dtype=jnp.int32) + code_count
    ) % code_count * codebook.shape[0]
    code_names = (
        code_places[:, None] + jnp.arange(codebook.shape[0], dtype=jnp.int32)[None, :]
    ).reshape(1, -1)
    patch_rows = jnp.pad(patches[0], ((0, ROWS - LONG), (0, 0)))
    embedded = dot_nn(patch_rows, w_patch)
    normed_rows, normed_zero, inv_zero = norm_forward(embedded, glob_vec[0], glob_vec[1])
    start_rows = normed_rows * live_float
    conv_in = start_rows.astype(BF)
    width = D // code_count
    own_cols = code_index * width
    own_in = lax.dynamic_slice_in_dim(conv_in, own_cols, width, 1)
    half = KERNEL // 2
    conv_own = conv_call(conv_forward_kernel, own_in[:LONG], conv_weight, half, False)
    seen_own = lax.dot_general(
        pick_full, conv_own, (((1,), (0,)), ((), ())), precision=HIGHEST
    )
    seen_raw = side_by_side(seen_own, code_index)
    seen_pre = seen_raw + glob_vec[2]
    seen_start = lax.dot_general(
        pick_full, start_rows, (((1,), (0,)), ((), ())), precision=HIGHEST
    )
    seen_rows = seen_start + gelu(seen_pre)
    encoded, kept_first = layer_forward(seen_rows, seen_fill, weights[0], span, pick_seen)
    placed = lax.dot_general(
        pick_full, encoded, (((0,), (0,)), ((), ())), precision=HIGHEST
    )
    hidden = jnp.where(visible[:, None], placed, glob_vec[3])
    final, kept_second = layer_forward(hidden, live_fill, weights[1], span, None)
    target_codes = jnp.where(mask_row == 1, jnp.pad(targets[0], (0, ROWS - LONG)), -1)
    loss_local, upstream, grad_head = head_pass(final, w_head, all_codes, code_names, target_codes)

    upstream, map_second, span_second = layer_backward(
        upstream, kept_second, live_fill, weights[1], span, None
    )
    grad_mask_emb = jnp.sum(jnp.where(visible[:, None], 0.0, upstream), axis=0)
    grad_encoded = lax.dot_general(
        pick_full, upstream, (((1,), (0,)), ((), ())), precision=HIGHEST
    )
    grad_seen, map_first, span_first = layer_backward(
        grad_encoded, kept_first, seen_fill, weights[0], span, pick_seen
    )
    grad_seen = grad_seen * seen_valid[:, None].astype(F32)
    grad_conv_seen = grad_seen * gelu_grad(seen_pre)
    grad_conv = dot_tn(pick_low, grad_conv_seen.astype(BF)).astype(BF)
    grad_full = lax.dot_general(
        pick_full, grad_seen, (((0,), (0,)), ((), ())), precision=HIGHEST
    )
    own_grad = lax.dynamic_slice_in_dim(grad_conv, own_cols, width, 1)
    grad_in_own = conv_call(conv_input_kernel, own_grad[:LONG], conv_weight, half - 1, True)
    grad_conv_in = side_by_side(grad_in_own.astype(BF), code_index)
    grad_kernel, chunks = conv_weight_grad(conv_in[:LONG], grad_conv, geometry, code_index)
    grad_start = (grad_full + grad_conv_in.astype(F32)) * live_float
    grad_embedded, grad_gain_zero, grad_shift_zero = norm_backward(
        grad_start, normed_zero, inv_zero, glob_vec[0]
    )
    grad_patch = dot_tn(patch_rows, grad_embedded.astype(BF))
    grad_glob = jnp.stack(
        [grad_gain_zero, grad_shift_zero, jnp.sum(grad_conv_seen, axis=0), grad_mask_emb]
    )
    grad_rel = lax.dot_general(
        jnp.asarray(span_table),
        (span_first + span_second)[:HEADS],
        (((0,), (1,)), ((), ())),
        precision=HIGHEST,
    )
    both = (map_first, map_second)
    front = jnp.concatenate([grad_patch.reshape(-1, 128), grad_glob.reshape(-1, 128)], axis=0)
    front = jnp.pad(front, ((geometry.phase, 0), (0, 0))).astype(BF)
    sources = [front, grad_kernel]
    common = [(0, front.shape[0], 0, 0)]
    for seg_name in ("w_qkv", "w_out", "w_up", "w_down"):
        for index, layer_map in enumerate(both):
            flat = layer_map[seg_name]
            common.append((geometry.place(seg_name, index), flat.shape[0], len(sources), 0))
            sources.append(flat)
    tail_place = geometry.place("layer_vec")
    vec_rows = jnp.concatenate(
        [layer_map["layer_vec"].reshape(-1, 128) for layer_map in both], axis=0
    )
    small = [layer_map[seg_name] for seg_name in ("gate_proj", "gate_scale") for layer_map in both]
    small = jnp.concatenate([part.reshape(-1) for part in small + [grad_rel]])
    lead = small.shape[0] % 128
    small_rows = jnp.pad(small, (0, -small.shape[0] % 128)).reshape(-1, 128)
    head_rows = jnp.pad(grad_head.astype(F32), ((1, 1), (0, 0)))
    head_rows = jnp.concatenate(
        [head_rows[:-1, 128 - lead :], head_rows[1:, : 128 - lead]], axis=1
    )
    whole = small.shape[0] // 128
    tail = jnp.concatenate(
        [vec_rows, small_rows[:whole], small_rows[whole:] + head_rows[:1], head_rows[1:]], axis=0
    ).astype(BF)
    tail_rows = geometry.begins[-1] + geometry.window - tail_place
    tail = jnp.pad(tail, ((0, tail_rows - tail.shape[0]), (0, 0)))
    common.append((tail_place, tail_rows, len(sources), 0))
    sources.append(tail)
    tap_rows = WIDTH * D // 128
    spans = [
        common
        + [
            (geometry.place("conv_w") + tap * tap_rows, CHUNK * tap_rows, 1, n * CHUNK * tap_rows)
            for n, tap in enumerate(chunks[code])
        ]
        for code in range(code_count)
    ]
    own_part = pack(geometry, code_index, sources, spans)
    reduced = lax.psum_scatter(own_part, "dp", scatter_dimension=0, tiled=False).astype(F32)
    reduced = lax.dynamic_slice(reduced, (own_offset, 0), (shard_rows, 128)).reshape(shard_len)
    leader = (code_index == 0).astype(F32)
    count_local = jnp.sum((target_codes >= 0).astype(F32))
    early = jnp.concatenate(
        [
            (grad_rel * leader).reshape(-1, 128),
            jnp.full((1, 128), loss_local * leader),
            jnp.full((1, 128), count_local * leader),
        ]
    )
    early = sum_over(sum_over(jnp.pad(early, ((0, -early.shape[0] % 8), (0, 0))), "dp"), "code")
    squares_all = sum_over(sum_over(jnp.full((8, 128), jnp.sum(reduced * reduced)), "dp"), "code")
    squares_all = squares_all[0, 0]
    rel_rows = BUCKETS * HEADS // 128
    rel_all = early[:rel_rows].reshape(BUCKETS, HEADS)
    loss_all, count_all = early[rel_rows, 0], early[rel_rows + 1, 0]
    grad_norm = jnp.sqrt(squares_all) / count_all
    clip_factor = jnp.minimum(1.0, CLIP_NORM / grad_norm)
    clipped = reduced / count_all * clip_factor
    rel_grad = rel_all / count_all * clip_factor
    step_value = step_count[0].astype(F32)
    new_first = BETA_ONE * first_moment + (1.0 - BETA_ONE) * clipped
    new_second = BETA_TWO * second_moment + (1.0 - BETA_TWO) * clipped * clipped
    first_hat = new_first / (1.0 - BETA_ONE**step_value)
    second_hat = new_second / (1.0 - BETA_TWO**step_value)
    new_params = params - LEARN_RATE * (
        first_hat / (jnp.sqrt(second_hat) + ADAM_EPSILON) + WEIGHT_DECAY * params
    )
    return (
        new_params,
        new_first,
        new_second,
        new_params.astype(BF),
        loss_all / count_all,
        grad_norm,
        rel_grad,
    )


def solution(mesh):
    placed = (
        P("dp", None, None),
        P("dp"),
        P("dp", None),
        P("dp", None),
        P("code", None),
        P(("dp", "code")),
        P(("dp", "code")),
        P(("dp", "code")),
        P(),
    )
    return jax.shard_map(
        local,
        mesh=mesh,
        in_specs=placed,
        out_specs=(
            P(("dp", "code")),
            P(("dp", "code")),
            P(("dp", "code")),
            P(("dp", "code")),
            P(),
            P(),
            P(),
        ),
        check_vma=False,
    )
```

time: 1140 us -> 705 us (0.62); the launches traced: 1120 us -> 695 us
  local copies, waits for them, and re-layouts: 335 us -> 55.7 us
  blocking collectives: 96.6 us -> 0 us
  Pallas kernels: 222 us -> 178 us
  starting transfers between devices: 0.08 us -> 28.7 us
  matrix products: 89.4 us -> 76.1 us
    reshape x21 -> x10, local copies, waits for them, and re-layouts: 154 us -> 7.41 us  [the longest x3 2.09 us: local(): small = jnp.concatenate([part.reshape(-1) for part in small + [grad_rel]])]
    unnamed x3 -> x2, waiting for transfers between devices: 91.6 us -> 0.03 us
    reduce_scatter x0 -> x1, waiting for transfers between devices: none -> 69 us  [local(): lax.psum_scatter(own_part, 'dp', scatter_dimension=0, tiled=False)]
    all_gather x3 -> x0, blocking collectives: 56.7 us -> none  [the longest x1 21.9 us: local(): all_codes = lax.all_gather(codebook, 'code', axis=0, tiled=True)]
    psum x1 -> x0, blocking collectives: 40 us -> none  [local(): lax.psum((loss_local * leader, jnp.sum(reduced * reduced), count_local *...]
    slice x14 -> x13, local copies, waits for them, and re-layouts: 46.3 us -> 6.8 us  [the longest x2 1.71 us: exact(): parts.append(windows[shard, begin:begin + stop - row])]
    unnamed x435 -> x373, local copies, waits for them, and re-layouts: 42 us -> 12 us
    pallas_call x5 -> x11, Pallas kernels: 140 us -> 110 us  [the longest x2 30.5 us: unpack(): pl.pallas_call(functools.partial(unpack_kernel, jobs=jobs, stages=stages)...]
  transfers between devices with their start and end apart: 2 -> 21, of which waited for: 2 -> 7; matrix products, arithmetic and copies ran while one was open for 0% -> 5% of each run, Pallas kernels for 0% -> 13%
where the time goes in v2:
time: 705 us; the launch traced here: 695 us
  waiting for transfers between devices  285 us (40%)
  Pallas kernels  178 us (25%)
  matrix products  76.1 us (11%)
  local copies, waits for them, and re-layouts  55.7 us (8%)
  other arithmetic  46.5 us (7%)
  starting transfers between devices  28.7 us (4%)
  between operations  25.4 us (4%)
    all_gather x1, waiting for transfers between devices, local(): windows = lax.all_gather(own_window, ('dp', 'code'), axis=0, tiled=False)  209 us
    reduce_scatter x1, waiting for transfers between devices, local(): lax.psum_scatter(own_part, 'dp', scatter_dimension=0, tiled=False)  69 us
    pallas_call x9, Pallas kernels, weight_grad(): pl.pallas_call(weight_grad_kernel, grid=(depth // rows,), in_specs=[pl.Bl...  42.3 us
    pallas_call x2, Pallas kernels, unpack(): pl.pallas_call(functools.partial(unpack_kernel, jobs=jobs, stages=stages)...  30.5 us
    dot_general x13, matrix products, dot_nn(): lax.dot_general(left, right, (((1,), (0,)), ((), ())), preferred_element_...  26.7 us
    pallas_call x2, Pallas kernels, conv_call(): pl.pallas_call(kernel, grid=(steps,), in_specs=[pl.BlockSpec(padded.shape...  24.8 us
    pallas_call x2, Pallas kernels, attention_backward(): pl.pallas_call(kernel, grid=(HEADS // heads,), in_specs=[columns] * 4 + [...  24.2 us
    dot_general x10, matrix products, dot_nt(): lax.dot_general(left, right, (((1,), (1,)), ((), ())), preferred_element_...  24.1 us
  transfers between devices with their start and end apart: 21, of which 7 were waited for; matrix products, arithmetic and copies ran while one was open for 5% of the time, Pallas kernels for 13%

profile of v2, /device:TPU:0, one launch (start us, length us, event | category | flops | bytes accessed | tf_op | source)
XLA Modules:
  0.0 695.3 jit_solution(12214177501053735012)
XLA Ops:
  7.3 5.9 dynamic_update_slice.3
  14.4 4.1 collective-permute-start.4
  18.5 1.6 collective-permute-start.3
  20.1 2.3 collective-permute-start.5
  30.5 208.7 %all-gather.3.cloned.1.call-done = bf16[151552,128]{1,0:T(8,128)(2,1)} async-done(((bf16[4736,128]{1,0:T(8,128)(2,1)}), bf16[151552,128]{1,0:T(8,128)(2,1)}) %all-gather.3.cloned.1.call-update) | async-done | bytes 38797328 | tf_op jit(solution)/shard_map/all_gather | solution.py:1178
  252.0 7.7 %shard_map.306.weight_ref = bf16[6144,192]{1,0:T(8,128)(2,1)} custom-call(s32[1]{0:T(128)} %bitcast.code_ref, bf16[32,4736,128]{2,1,0:T(8,128)(2,1)} %bitcast.214), custom_call_target="tpu_custom_call" | custom-call | tf_op jit(solution)/shard_map/pallas_call | solution.py:852
  259.7 12.1 %shard_map.307 = f32[512,192]{1,0:T(8,128)} custom-call(f32[640,192]{1,0:T(8,128)} %pad_convert_fusion.3.in_ref, bf16[6144,192]{1,0:T(8,128)(2,1)} %shard_map.306.weight_ref, bf16[4,192]{1,0:T(4,128)(2,1)} %constant.197.clone.mask_ref), custom_call_target="tpu_custom_call" | custom-call | tf_op jit(solution)/shard_map/pallas_call | solution.py:243
  271.8 2.1 fusion.64.refs_0_
  275.8 3.6 collective-permute-start.2
  279.3 15.2 %shard_map.311 = (bf16[768,2304]{1,0:T(8,128)(2,1)}, bf16[768,768]{1,0:T(8,128)(2,1)}, bf16[768,3072]{1,0:T(8,128)(2,1)}, bf16[3072,768]{1,0:T(8,128)(2,1)}) custom-call(bf16[32,4736,128]{2,1,0:T(8,128)(2,1)} %bitcast.215), custom_call_target="tpu_custom_call" | custom-call | tf_op jit(solution)/shard_map/pallas_call | solution.py:796
  294.6 15.3 %shard_map.309 = (bf16[768,2304]{1,0:T(8,128)(2,1)}, bf16[768,768]{1,0:T(8,128)(2,1)}, bf16[768,3072]{1,0:T(8,128)(2,1)}, bf16[3072,768]{1,0:T(8,128)(2,1)}) custom-call(bf16[32,4736,128]{2,1,0:T(8,128)(2,1)} %bitcast.216), custom_call_target="tpu_custom_call" | custom-call | tf_op jit(solution)/shard_map/pallas_call | solution.py:796
  316.5 1.8 copy.86
  318.3 2.0 fusion.92.span_ref
  321.0 2.0 shard_map.308
  323.1 2.3 fusion.187
  326.4 2.7 fusion.193
  331.4 4.6 shard_map.310
  337.7 2.3 multiply_convert_fusion.2
  340.1 3.5 fusion.189
  346.1 2.0 fusion.194
  351.4 9.7 %shard_map.312 = (bf16[512,768]{1,0:T(8,128)(2,1)}, f32[16,512]{1,0:T(8,128)}) custom-call(bf16[512,768]{1,0:T(8,128)(2,1)} %get-tuple-element.128.q_ref, bf16[512,768]{1,0:T(8,128)(2,1)} %slice.712.k_ref, bf16[512,768]{1,0:T(8,128)(2,1)} %get-tuple-element.127.v_ref, f32[16,512]{1,0:T(8,128)} %pad.71.gate_ref, f32[16,1024]{1,0:T(8,128)} %fusion.92.span_ref, ...), custom_call_target="tpu_custom_call" | custom-call | tf_op jit(solution)/shard_map/pallas_call | solution.py:477
  361.1 2.0 fusion.191
  364.2 6.9 multiply_convert_fusion
  371.1 2.8 fusion.192
  377.3 2.0 copy.82
  379.4 1.8 multiply_reduce_fusion
  384.6 2.5 shard_map.326
  392.9 1.9 copy-done.163
  394.8 5.5 fusion.183
  400.3 3.7 multiply_reduce_fusion.2
  406.4 1.7 convolution_convert_fusion.up_ref
  408.1 3.3 shard_map.321.refs_5_
  411.3 17.1 %shard_map.313 = (bf16[3,512,768]{2,1,0:T(8,128)(2,1)}, f32[8,768]{1,0:T(8,128)}, f32[16,512]{1,0:T(8,128)}, f32[16,1024]{1,0:T(8,128)}) custom-call(bf16[512,768]{1,0:T(8,128)(2,1)} %get-tuple-element.128.q_ref, bf16[512,768]{1,0:T(8,128)(2,1)} %slice.712.k_ref, bf16[512,768]{1,0:T(8,128)(2,1)} %get-tuple-element.127.v_ref, ...), custom_call_target="tpu_custom_call" | custom-call | tf_op jit(solution)/shard_map/pallas_call | solution.py:683
  428.4 1.9 slice_bitcast_fusion.2
  431.1 2.0 fusion.173
  433.2 1.6 pad_maximum_fusion.right_ref
  435.7 2.2 select_reduce_fusion
  440.2 2.3 fusion.184
  442.6 2.4 multiply_reduce_fusion.16
  447.5 7.1 %shard_map.314 = (bf16[3,128,768]{2,1,0:T(8,128)(2,1)}, f32[8,768]{1,0:T(8,128)}, f32[16,128]{1,0:T(8,128)}, f32[16,1024]{1,0:T(8,128)}) custom-call(bf16[128,768]{1,0:T(8,128)(2,1)} %get-tuple-element.135.q_ref, bf16[128,768]{1,0:T(8,128)(2,1)} %slice.713.k_ref, bf16[128,768]{1,0:T(8,128)(2,1)} %get-tuple-element.134.v_ref, ...), custom_call_target="tpu_custom_call" | custom-call | tf_op jit(solution)/shard_map/pallas_call | solution.py:683
  455.8 2.2 convolution_add_fusion.3
  467.5 3.0 broadcast_multiply_fusion
  475.3 2.1 fusion.180
  479.1 12.8 %shard_map.315 = f32[512,192]{1,0:T(8,128)} custom-call(f32[640,192]{1,0:T(8,128)} %pad_convert_fusion.2.in_ref, bf16[6144,192]{1,0:T(8,128)(2,1)} %shard_map.306.weight_ref, bf16[4,192]{1,0:T(4,128)(2,1)} %constant.197.clone.mask_ref), custom_call_target="tpu_custom_call" | custom-call | tf_op jit(solution)/shard_map/pallas_call | solution.py:243
  493.1 1.9 collective-permute-start.6
  495.1 2.8 shard_map.320.refs_4_
  497.9 6.9 shard_map.325.refs_9_
  504.7 5.2 shard_map.324.refs_8_
  510.0 7.1 %shard_map.323.refs_7_ = bf16[18432,128]{1,0:T(8,128)(2,1)} custom-call(bf16[512,768]{1,0:T(8,128)(2,1)} %copy-done.21, bf16[512,3072]{1,0:T(8,128)(2,1)} %copy-done.20), custom_call_target="tpu_custom_call" | custom-call | tf_op jit(solution)/shard_map/pallas_call | solution.py:706
  517.1 5.1 shard_map.322.refs_6_
  522.3 5.5 shard_map.319.refs_3_
  529.3 3.9 shard_map.318.refs_2_
  538.8 21.9 %shard_map.317.refs_1_ = bf16[12096,128]{1,0:T(8,128)(2,1)} custom-call(s32[7]{0:T(128)} %fusion.152.tap_ref, f32[4,192,640]{2,1,0:T(8,128)} %bitcast.222, bf16[4,512,192]{2,1,0:T(8,128)(2,1)} %bitcast.225, f32[4,192]{1,0:T(4,128)} %constant.198.clone.mask_ref), custom_call_target="tpu_custom_call" | custom-call | tf_op jit(solution)/shard_map/pallas_call | solution.py:327
  561.6 2.3 shard_map.316
  563.9 2.1 multiply_reduce_fusion.4
  568.1 7.7 %shard_map.327 = bf16[8,4736,128]{2,1,0:T(8,128)(2,1)} custom-call(s32[1]{0:T(128)} %bitcast.code_ref, bf16[1568,128]{1,0:T(8,128)(2,1)} %fusion.42.refs_0_, bf16[12096,128]{1,0:T(8,128)(2,1)} %shard_map.317.refs_1_, bf16[13824,128]{1,0:T(8,128)(2,1)} %shard_map.318.refs_2_, bf16[13824,128]{1,0:T(8,128)(2,1)} %shard_map.319.refs_3_, ...), custom_call_target="tpu_custom_call" | custom-call | tf_op jit(solution)/shard_map/pallas_call | solution.py:913
  580.4 2.5 collective-permute-done.10
  584.3 69.0 %reduce-scatter.2.cloned.1.call-done = bf16[1,4736,128]{2,1,0:T(8,128)(2,1)} async-done(((bf16[8,4736,128]{2,1,0:T(8,128)(2,1)}), bf16[1,4736,128]{2,1,0:T(8,128)(2,1)}) %reduce-scatter.2.cloned.1.call-update) | async-done | bytes 1212432 | tf_op jit(solution)/shard_map/reduce_scatter | solution.py:1348
  653.3 2.5 fusion.5
  656.6 1.5 collective-permute-start.12
  660.4 2.4 collective-permute-start.13
  664.9 2.3 collective-permute-done.16
  670.8 2.1 collective-permute-start.18
  678.9 6.9 fusion.174
  (598 shorter events, 106.5 us)
Async XLA Ops:
  7.2 232.0 %all-gather.3.cloned.1.call-start = ((), (), s32[]{:S(2)}) async-start(), calls=%async_computation.2 | async-start | bytes 40009728 | tf_op jit(solution)/shard_map/all_gather | solution.py:1178
  7.3 7.1 %copy-start.50 = (bf16[256,256]{1,0:T(8,128)(2,1)S(1)}, bf16[256,256]{1,0:T(8,128)(2,1)}, u32[]{:S(2)}) copy-start(bf16[256,256]{1,0:T(8,128)(2,1)} %param.31) | copy-start | bytes 393220
  7.3 15.7 %copy-start.132 = (s32[1,496]{1,0:T(1,128)S(1)}, s32[1,496]{1,0:T(1,128)}, u32[]{:S(2)}) copy-start(s32[1,496]{1,0:T(1,128)} %param.29) | copy-start | bytes 5956
  7.3 17.7 %copy-start.152 = (s32[1,496]{1,0:T(1,128)S(1)}, s32[1,496]{1,0:T(1,128)}, u32[]{:S(2)}) copy-start(s32[1,496]{1,0:T(1,128)} %param.30) | copy-start | bytes 5956
  13.3 229.4 %copy-start.68 = (f32[8,24]{1,0:T(8,128)S(1)}, f32[8,24]{1,0:T(8,128)}, u32[]{:S(2)}) copy-start(f32[8,24]{1,0:T(8,128)} %constant.193.clone) | copy-start | bytes 2308
  14.3 639.0 %reduce-scatter.2.cloned.1.call-start = ((), (), s32[]{:S(2)}) async-start(), calls=%async_computation.1 | async-start | bytes 10911744 | tf_op jit(solution)/shard_map/reduce_scatter | solution.py:1348
  14.4 16.0 %collective-permute-start.4 = (bf16[256,256]{1,0:T(8,128)(2,1)S(1)}, bf16[256,256]{1,0:T(8,128)(2,1)S(1)}, u32[]{:S(2)}, u32[]{:S(2)}) collective-permute-start(bf16[256,256]{1,0:T(8,128)(2,1)S(1)} %copy-done.50), channel_id=1, source_target_pairs={{0,2},{1,3},{2,0},{3,1},{4,6},{5,7},{6,4},{7,5},{8,10},{9,11},{10,... | collective-permute-start | bytes 393224 | tf_op jit(solution)/shard_map/ppermute | solution.py:927
  18.5 11.9 %collective-permute-start.3 = (bf16[256,256]{1,0:T(8,128)(2,1)S(1)}, bf16[256,256]{1,0:T(8,128)(2,1)S(1)}, u32[]{:S(2)}, u32[]{:S(2)}) collective-permute-start(bf16[256,256]{1,0:T(8,128)(2,1)S(1)} %copy-done.50), channel_id=1, source_target_pairs={{0,1},{1,2},{2,3},{3,0},{4,5},{5,6},{6,7},{7,4},{8,9},{9,10},{10,1... | collective-permute-start | bytes 393224 | tf_op jit(solution)/shard_map/ppermute | solution.py:927
  20.1 10.4 %collective-permute-start.5 = (bf16[256,256]{1,0:T(8,128)(2,1)S(1)}, bf16[256,256]{1,0:T(8,128)(2,1)S(1)}, u32[]{:S(2)}, u32[]{:S(2)}) collective-permute-start(bf16[256,256]{1,0:T(8,128)(2,1)S(1)} %copy-done.50), channel_id=1, source_target_pairs={{0,3},{1,0},{2,1},{3,2},{4,7},{5,4},{6,5},{7,6},{8,11},{9,8},{10,9... | collective-permute-start | bytes 393224 | tf_op jit(solution)/shard_map/ppermute | solution.py:927
  23.0 248.7 %copy-start.73 = (pred[512]{0:T(512)(128)(4,1)}, pred[512]{0:T(512)(128)(4,1)S(1)}, u32[]{:S(2)}) copy-start(pred[512]{0:T(512)(128)(4,1)S(1)} %get-tuple-element.120) | copy-start | bytes 1540
  24.4 225.2 %copy-start.98 = (f32[512]{0:T(512)}, f32[512]{0:T(512)S(1)}, u32[]{:S(2)}) copy-start(f32[512]{0:T(512)S(1)} %fusion.148) | copy-start | bytes 6148
  26.5 245.3 %copy-start.52 = (s32[512]{0:T(512)}, s32[512]{0:T(512)S(1)}, u32[]{:S(2)}) copy-start(s32[512]{0:T(512)S(1)} %fusion.254) | copy-start | bytes 6148
  30.4 218.4 %copy-start.35 = (bf16[1,496,256]{2,1,0:T(8,128)(2,1)S(1)}, bf16[1,496,256]{2,1,0:T(8,128)(2,1)}, u32[]{:S(2)}) copy-start(bf16[1,496,256]{2,1,0:T(8,128)(2,1)} %param.27) | copy-start | bytes 761860
  30.5 214.6 %copy-start.37 = (bf16[1024,256]{1,0:T(8,128)(2,1)}, bf16[1024,256]{1,0:T(8,128)(2,1)S(1)}, u32[]{:S(2)}) copy-start(bf16[1024,256]{1,0:T(8,128)(2,1)S(1)} %constant_dynamic-update-slice_fusion) | copy-start | bytes 1572868
  273.8 47.2 %collective-permute-start.1 = (f32[128,192]{1,0:T(8,128)}, f32[128,192]{1,0:T(8,128)}, u32[]{:S(2)}, u32[]{:S(2)}) collective-permute-start(f32[128,192]{1,0:T(8,128)} %fusion.64.refs_0_), channel_id=1, source_target_pairs={{0,2},{1,3},{2,0},{3,1},{4,6},{5,7},{6,4},{7,5},{8,10},{9,11},{10,... | collective-permute-start | bytes 294920 | tf_op jit(solution)/shard_map/ppermute | solution.py:927
  275.3 45.7 %collective-permute-start = (f32[128,192]{1,0:T(8,128)}, f32[128,192]{1,0:T(8,128)}, u32[]{:S(2)}, u32[]{:S(2)}) collective-permute-start(f32[128,192]{1,0:T(8,128)} %fusion.64.refs_0_), channel_id=1, source_target_pairs={{0,1},{1,2},{2,3},{3,0},{4,5},{5,6},{6,7},{7,4},{8,9},{9,10},{10,1... | collective-permute-start | bytes 294920 | tf_op jit(solution)/shard_map/ppermute | solution.py:927
  275.8 45.2 %collective-permute-start.2 = (f32[128,192]{1,0:T(8,128)}, f32[128,192]{1,0:T(8,128)}, u32[]{:S(2)}, u32[]{:S(2)}) collective-permute-start(f32[128,192]{1,0:T(8,128)} %fusion.64.refs_0_), channel_id=1, source_target_pairs={{0,3},{1,0},{2,1},{3,2},{4,7},{5,4},{6,5},{7,6},{8,11},{9,8},{10,9... | collective-permute-start | bytes 294920 | tf_op jit(solution)/shard_map/ppermute | solution.py:927
  294.5 17.0 %copy-start.11 = (f32[768,64]{1,0:T(8,128)S(1)}, f32[768,64]{1,0:T(8,128)}, u32[]{:S(2)}) copy-start(f32[768,64]{1,0:T(8,128)} %constant.194.clone) | copy-start | bytes 589828
  294.5 17.0 %copy-start.31 = (f32[768,24]{0,1:T(8,128)S(1)}, f32[768,24]{0,1:T(8,128)}, u32[]{:S(2)}) copy-start(f32[768,24]{0,1:T(8,128)} %constant.195.clone) | copy-start | bytes 221188
  323.1 14.6 %slice-start = ((s8[4718592]{0:T(1024)(128)(4,1)}), s8[4194304]{0:T(1024)(128)(4,1)S(1)}, s32[]{:S(2)}) async-start(s8[4718592]{0:T(1024)(128)(4,1)} %bitcast.217), calls=%async_computation.3 | async-start | bytes 8388608
  326.4 11.3 %slice-start.1 = ((s8[4718592]{0:T(1024)(128)(4,1)}), s8[524288]{0:T(1024)(128)(4,1)S(1)}, s32[]{:S(2)}) async-start(s8[4718592]{0:T(1024)(128)(4,1)} %bitcast.217), calls=%async_computation.4 | async-start | bytes 1048576
  329.1 6.8 copy-start.14
  329.1 6.8 copy-start.111
  331.4 6.2 copy-start.83
  350.6 10.5 %copy-start.147 = (f32[768]{0:T(1024)S(1)}, f32[768]{0:T(1024)}, u32[]{:S(2)}) copy-start(f32[768]{0:T(1024)} %get-tuple-element.149) | copy-start | bytes 9220
  350.6 10.5 %copy-start.160 = (bf16[768,768]{1,0:T(8,128)(2,1)S(1)}, bf16[768,768]{1,0:T(8,128)(2,1)}, u32[]{:S(2)}) copy-start(bf16[768,768]{1,0:T(8,128)(2,1)} %get-tuple-element.35) | copy-start | bytes 3538948
  363.2 7.9 %copy-start.84 = (f32[512]{0:T(512)}, f32[512]{0:T(512)S(1)}, u32[]{:S(2)}) copy-start(f32[512]{0:T(512)S(1)} %broadcast_multiply_fusion.8) | copy-start | bytes 6148
  363.5 7.6 %copy-start.94 = (f32[512]{0:T(512)}, f32[512]{0:T(512)S(1)}, u32[]{:S(2)}) copy-start(f32[512]{0:T(512)S(1)} %add_rsqrt_fusion.2) | copy-start | bytes 6148
  363.8 7.3 %slice-start.8 = ((s8[4718592]{0:T(1024)(128)(4,1)}), s8[4194304]{0:T(1024)(128)(4,1)S(1)}, s32[]{:S(2)}) async-start(s8[4718592]{0:T(1024)(128)(4,1)} %bitcast.243), calls=%async_computation.11 | async-start | bytes 8388608
  364.1 6.9 copy-start.21
  364.2 6.9 copy-start.146
  364.2 6.9 slice-start.9
  392.8 7.5 %slice-start.6 = ((s8[4718592]{0:T(1024)(128)(4,1)}), s8[4194304]{0:T(1024)(128)(4,1)S(1)}, s32[]{:S(2)}) async-start(s8[4718592]{0:T(1024)(128)(4,1)} %bitcast.241), calls=%async_computation.9 | async-start | bytes 8388608
  392.9 7.4 %copy-start.22 = (bf16[512,768]{1,0:T(8,128)(2,1)}, bf16[512,768]{1,0:T(8,128)(2,1)S(1)}, u32[]{:S(2)}) copy-start(bf16[512,768]{1,0:T(8,128)(2,1)S(1)} %convert_element_type.280.right_ref) | copy-start | bytes 2359300
  433.2 7.0 %slice-start.4 = ((s8[4718592]{0:T(1024)(128)(4,1)}), s8[4194304]{0:T(1024)(128)(4,1)S(1)}, s32[]{:S(2)}) async-start(s8[4718592]{0:T(1024)(128)(4,1)} %bitcast.223), calls=%async_computation.7 | async-start | bytes 8388608
  446.2 9.5 %copy-start.26 = (bf16[128,768]{1,0:T(8,128)(2,1)}, bf16[128,768]{1,0:T(8,128)(2,1)S(1)}, u32[]{:S(2)}) copy-start(bf16[128,768]{1,0:T(8,128)(2,1)S(1)} %convert_element_type.286.right_ref) | copy-start | bytes 589828
  446.2 9.5 %copy-start.17 = (bf16[768,2304]{1,0:T(8,128)(2,1)S(1)}, bf16[768,2304]{1,0:T(8,128)(2,1)}, u32[]{:S(2)}) copy-start(bf16[768,2304]{1,0:T(8,128)(2,1)} %get-tuple-element.28) | copy-start | bytes 10616836
  463.3 8.0 %copy-start.7 = (f32[1537,88]{1,0:T(8,128)S(1)}, f32[1537,88]{1,0:T(8,128)}, u32[]{:S(2)}) copy-start(f32[1537,88]{1,0:T(8,128)} %slice.532) | copy-start | bytes 1623076
  463.3 8.0 %copy-start.8 = (f32[1537,40]{1,0:T(8,128)S(1)}, f32[1537,40]{1,0:T(8,128)}, u32[]{:S(2)}) copy-start(f32[1537,40]{1,0:T(8,128)} %slice.531) | copy-start | bytes 737764
  493.0 11.8 %copy-start.33 = (bf16[512,192]{1,0:T(8,128)(2,1)}, bf16[512,192]{1,0:T(8,128)(2,1)S(1)}, u32[]{:S(2)}) copy-start(bf16[512,192]{1,0:T(8,128)(2,1)S(1)} %convert_element_type.291.refs_0_) | copy-start | bytes 589828
  493.0 68.5 %collective-permute-start.8 = (bf16[512,192]{1,0:T(8,128)(2,1)S(1)}, bf16[512,192]{1,0:T(8,128)(2,1)}, u32[]{:S(2)}, u32[]{:S(2)}) collective-permute-start(bf16[512,192]{1,0:T(8,128)(2,1)S(1)} %convert_element_type.291.refs_0_), channel_id=1, source_target_pairs={{0,3},{1,0},{2,1},{3,2},{4,7},{5,4},{6,5},{7,6},{8,11},{9,8},{10,9... | collective-permute-start | bytes 589832 | tf_op jit(solution)/shard_map/ppermute | solution.py:927
  493.1 68.5 %collective-permute-start.7 = (bf16[512,192]{1,0:T(8,128)(2,1)S(1)}, bf16[512,192]{1,0:T(8,128)(2,1)}, u32[]{:S(2)}, u32[]{:S(2)}) collective-permute-start(bf16[512,192]{1,0:T(8,128)(2,1)S(1)} %convert_element_type.291.refs_0_), channel_id=1, source_target_pairs={{0,2},{1,3},{2,0},{3,1},{4,6},{5,7},{6,4},{7,5},{8,10},{9,11},{10,... | collective-permute-start | bytes 589832 | tf_op jit(solution)/shard_map/ppermute | solution.py:927
  493.1 68.4 %collective-permute-start.6 = (bf16[512,192]{1,0:T(8,128)(2,1)S(1)}, bf16[512,192]{1,0:T(8,128)(2,1)}, u32[]{:S(2)}, u32[]{:S(2)}) collective-permute-start(bf16[512,192]{1,0:T(8,128)(2,1)S(1)} %convert_element_type.291.refs_0_), channel_id=1, source_target_pairs={{0,1},{1,2},{2,3},{3,0},{4,5},{5,6},{6,7},{7,4},{8,9},{9,10},{10,1... | collective-permute-start | bytes 589832 | tf_op jit(solution)/shard_map/ppermute | solution.py:927
  529.3 6.1 copy-start.131
  529.3 6.3 copy-start.130
  529.3 6.5 copy-start.129
  529.3 6.7 copy-start.128
  529.3 6.9 copy-start.135
  529.3 7.1 %copy-start.134 = (bf16[768]{0:T(1024)(128)(2,1)S(1)}, bf16[768]{0:T(1024)(128)(2,1)}, u32[]{:S(2)}) copy-start(bf16[768]{0:T(1024)(128)(2,1)} %get-tuple-element.90) | copy-start | bytes 4612
  529.3 7.3 %copy-start.139 = (bf16[3072]{0:T(1024)(128)(2,1)S(1)}, bf16[3072]{0:T(1024)(128)(2,1)}, u32[]{:S(2)}) copy-start(bf16[3072]{0:T(1024)(128)(2,1)} %get-tuple-element.132) | copy-start | bytes 18436
  529.3 7.3 %copy-start.29 = (bf16[1536,128]{1,0:T(8,128)(2,1)S(1)}, bf16[1536,128]{1,0:T(8,128)(2,1)}, u32[]{:S(2)}) copy-start(bf16[1536,128]{1,0:T(8,128)(2,1)} %fusion.31) | copy-start | bytes 1179652
  529.3 7.3 %copy-start.149 = (bf16[1,128]{1,0:T(2,128)(2,1)S(1)}, bf16[1,128]{1,0:T(2,128)(2,1)}, u32[]{:S(2)}) copy-start(bf16[1,128]{1,0:T(2,128)(2,1)} %fusion.158) | copy-start | bytes 772
  538.8 21.9 %copy-start.42 = (f32[128,768]{1,0:T(8,128)S(1)}, f32[128,768]{1,0:T(8,128)}, u32[]{:S(2)}) copy-start(f32[128,768]{1,0:T(8,128)} %get-tuple-element.207) | copy-start | bytes 1179652
  575.8 103.0 %copy-start.6 = (f32[603008]{0:T(1024)S(1)}, f32[603008]{0:T(1024)}, u32[]{:S(2)}) copy-start(f32[603008]{0:T(1024)} %param.32) | copy-start | bytes 7236100
  577.8 1.2 collective-permute-start.9
  579.1 3.7 collective-permute-start.10
  582.9 73.7 %collective-permute-start.11 = (f32[32,128]{1,0:T(8,128)S(1)}, f32[32,128]{1,0:T(8,128)S(1)}, u32[]{:S(2)}, u32[]{:S(2)}) collective-permute-start(f32[32,128]{1,0:T(8,128)S(1)} %add.534), channel_id=1, source_target_pairs={{0,16},{4,20},{8,24},{12,28},{16,0},{20,4},{24,8},{28,12},{1,17},{... | collective-permute-start | bytes 49160 | tf_op jit(solution)/shard_map/ppermute | solution.py:963
  656.5 1.6 collective-permute-start.14
  656.6 3.8 collective-permute-start.12
  658.8 4.0 collective-permute-start.15
  660.4 9.0 %collective-permute-start.13 = (f32[32,128]{1,0:T(8,128)S(1)}, f32[32,128]{1,0:T(8,128)S(1)}, u32[]{:S(2)}, u32[]{:S(2)}) collective-permute-start(f32[32,128]{1,0:T(8,128)S(1)} %add.536), channel_id=1, source_target_pairs={{0,2},{1,3},{2,0},{3,1},{4,6},{5,7},{6,4},{7,5},{8,10},{9,11},{10,... | collective-permute-start | bytes 49160 | tf_op jit(solution)/shard_map/ppermute | solution.py:963
  663.5 3.7 collective-permute-start.16
  667.2 3.6 collective-permute-start.17
  670.8 4.6 collective-permute-start.18
  (133 other events, 377.7 us)
Sparse Core Ops, SparseCore 0:
  14.4 224.6 all-gather.2
  576.0 77.3 reduce-scatter.1

commit v3 on v2

--- a/solution.py
+++ b/solution.py
@@ -293,37 +293,50 @@
 PART = 4 * WIDTH
 
 
-def conv_chunks(geometry):
-    base, tap_rows = geometry.place("conv_w"), WIDTH * D // 128
+def owned_chunks(geometry, base, unit, count, chunk, step, slots):
     tables = []
-    for slot in range(geometry.dp_count):
-        needs = []
-        for code in range(geometry.code_count):
+    for code in range(geometry.code_count):
+        found = []
+        for slot in slots:
             begin = geometry.begins[slot * geometry.code_count + code] - base
-            low = max(begin // tap_rows, 0)
-            high = min(-(-(begin + geometry.window) // tap_rows), KERNEL)
-            needs.append((low, high))
-        count = max(-(-(high - low) // CHUNK) for low, high in needs)
-        for number in range(max(count, 0)):
-            tables.append(
-                [min(max(low, 0), KERNEL) + number * CHUNK for low, _ in needs]
-            )
-    clipped = [[min(tap, KERNEL - CHUNK) for tap in row] for row in tables]
-    return [list(column) for column in zip(*clipped)]
-
-
-def conv_weight_grad(conv_in, grad_low, geometry, code_index):
+            low = max(begin // unit, 0) // step * step
+            high = min(-(-(begin + geometry.window) // unit), count)
+            while low < high:
+                found.append(min(low, count - chunk))
+                low += chunk
+        tables.append(list(dict.fromkeys(found)))
+    most = max([1] + [len(table) for table in tables])
+    return [(table or [0]) + (table or [0])[-1:] * (most - max(len(table), 1)) for table in tables]
+
+
+def chunk_spans(chunks, base, unit, chunk, source):
+    return [
+        [(base + low * unit, chunk * unit, source, n * chunk * unit) for n, low in enumerate(table)]
+        for table in chunks
+    ]
+
+
+def chunk_table(chunks, code_index):
+    return lax.dynamic_index_in_dim(jnp.asarray(chunks, jnp.int32), code_index, 0, False)
+
+
+def conv_weight_inputs(conv_in, grad_low):
     parts = D // PART
     front = KERNEL // 2
     padded = jnp.pad(
         jnp.transpose(conv_in).astype(F32),
         ((0, 0), (front, ROWS + KERNEL - front - conv_in.shape[0])),
     ).reshape(parts, PART, ROWS + KERNEL)
-    grads = jnp.transpose(grad_low.reshape(ROWS, parts, PART), (1, 0, 2))
+    return padded, jnp.transpose(grad_low.reshape(ROWS, parts, PART), (1, 0, 2))
+
+
+def conv_weight_grad(padded, grads, geometry, code_index, slots):
+    parts = D // PART
     masks = jnp.asarray(lane_masks(PART), F32)
-    chunks = conv_chunks(geometry)
-    table = lax.dynamic_index_in_dim(jnp.asarray(chunks, jnp.int32), code_index, 0, False)
-    rows = CHUNK * WIDTH * D // 128
+    base, unit = geometry.place("conv_w"), WIDTH * D // 128
+    chunks = owned_chunks(geometry, base, unit, KERNEL, CHUNK, 1, slots)
+    table = chunk_table(chunks, code_index)
+    rows = CHUNK * unit
     out = pl.pallas_call(
         conv_weight_kernel,
         grid_spec=pltpu.PrefetchScalarGridSpec(
@@ -343,7 +356,7 @@
         out_shape=jax.ShapeDtypeStruct((len(chunks[0]) * rows, 128), BF),
         compiler_params=params_of(),
     )(table, padded, grads, masks)
-    return out, chunks
+    return out, (chunks, base, unit, CHUNK)
 
 
 BLOCK = 128
@@ -512,7 +525,8 @@
 
 def attention_backward_kernel(
     q_ref, k_ref, v_ref, up_ref, gate_ref, span_ref, fill_ref, lse_ref,
-    out_ref, sum_ref, dgate_ref, dspan_ref, prob_ref, grad_ref, turn_ref, low_ref, diag_ref,
+    dq_ref, dk_ref, dv_ref, sum_ref, dgate_ref, dspan_ref,
+    prob_ref, grad_ref, turn_ref, low_ref, diag_ref,
 ):
     step = pl.program_id(0)
     length = q_ref.shape[0]
@@ -564,9 +578,9 @@
     for side in sides:
         dspan_ref[pl.ds(step * 2 + side, 1), :] = diagonal_sums(diag_ref[side])
     grad_query = jnp.transpose(jnp.concatenate(halves, axis=0)) * HEAD_DIM ** (-0.5)
-    out_ref[0] = grad_query.astype(BF)
-    out_ref[1] = key_total.astype(BF)
-    out_ref[2] = val_total.astype(BF)
+    dq_ref[...] = grad_query.astype(BF)
+    dk_ref[...] = key_total.astype(BF)
+    dv_ref[...] = val_total.astype(BF)
     sum_ref[0:1, :] = jnp.sum(grad_query, axis=0, keepdims=True)
     sum_ref[1:2, :] = jnp.sum(val_total, axis=0, keepdims=True)
 
@@ -578,7 +592,7 @@
 
 def seen_backward_kernel(
     q_ref, k_ref, v_ref, up_ref, gate_ref, fill_ref, lse_ref, pick_ref, hop_ref, flip_ref,
-    bias_ref, out_ref, sum_ref, dgate_ref, dspan_ref, diag_ref,
+    bias_ref, dq_ref, dk_ref, dv_ref, sum_ref, dgate_ref, dspan_ref, diag_ref,
 ):
     heads, pairs = range(SEEN_HEADS), range(SEEN_HEADS // 2)
     base = pl.program_id(0) * SEEN_HEADS
@@ -640,9 +654,9 @@
         grad_query = jnp.transpose(jnp.concatenate(halves[2 * pair : 2 * pair + 2], axis=0))
         grad_query = grad_query * HEAD_DIM ** (-0.5)
         val_total = val_terms[2 * pair] + val_terms[2 * pair + 1]
-        out_ref[0, :, cols] = grad_query.astype(BF)
-        out_ref[1, :, cols] = (key_terms[2 * pair] + key_terms[2 * pair + 1]).astype(BF)
-        out_ref[2, :, cols] = val_total.astype(BF)
+        dq_ref[:, cols] = grad_query.astype(BF)
+        dk_ref[:, cols] = (key_terms[2 * pair] + key_terms[2 * pair + 1]).astype(BF)
+        dv_ref[:, cols] = val_total.astype(BF)
         sum_ref[0:1, cols] = jnp.sum(grad_query, axis=0, keepdims=True)
         sum_ref[1:2, cols] = jnp.sum(val_total, axis=0, keepdims=True)
 
@@ -652,13 +666,17 @@
     heads = 2 if pick is None else SEEN_HEADS
     columns = pl.BlockSpec((length, heads * HEAD_DIM), lambda i: (0, i))
     shapes = [
-        jax.ShapeDtypeStruct((3, length, D), BF),
+        jax.ShapeDtypeStruct((length, D), BF),
+        jax.ShapeDtypeStruct((length, D), BF),
+        jax.ShapeDtypeStruct((length, D), BF),
         jax.ShapeDtypeStruct((8, D), F32),
         jax.ShapeDtypeStruct((16, length), F32),
         jax.ShapeDtypeStruct((16, SPAN), F32),
     ]
     out_specs = [
-        pl.BlockSpec((3, length, heads * HEAD_DIM), lambda i: (0, 0, i)),
+        columns,
+        columns,
+        columns,
         pl.BlockSpec((8, heads * HEAD_DIM), lambda i: (0, i)),
         whole_spec((16, length)),
         whole_spec((16, SPAN)),
@@ -691,7 +709,7 @@
     )(*args)
 
 
-def weight_grad_kernel(left_ref, right_ref, out_ref, turn_ref):
+def weight_grad_kernel(table_ref, left_ref, right_ref, out_ref, turn_ref):
     rows = left_ref.shape[1]
     strips = right_ref.shape[1] // 128
     grad = dot_tn(left_ref[...], right_ref[...])
@@ -700,21 +718,27 @@
     out_ref[...] = turn_ref[...].astype(BF)
 
 
-def weight_grad(left, right, rows=384):
+def weight_grad(left, right, geometry, code_index, base, rows):
     length, depth = left.shape
     strips = right.shape[1] // 128
-    return pl.pallas_call(
+    slots = range(geometry.dp_count)
+    chunks = owned_chunks(geometry, base, strips, depth, rows, rows, slots)
+    out = pl.pallas_call(
         weight_grad_kernel,
-        grid=(depth // rows,),
-        in_specs=[
-            pl.BlockSpec((length, rows), lambda i: (0, i)),
-            pl.BlockSpec(right.shape, lambda i: (0, 0)),
-        ],
-        out_specs=pl.BlockSpec((rows * strips, 128), lambda i: (i, 0)),
-        out_shape=jax.ShapeDtypeStruct((depth * strips, 128), BF),
-        scratch_shapes=[pltpu.VMEM((rows * strips, 128), F32)],
+        grid_spec=pltpu.PrefetchScalarGridSpec(
+            num_scalar_prefetch=1,
+            grid=(len(chunks[0]),),
+            in_specs=[
+                pl.BlockSpec((length, rows), lambda i, t: (0, t[i])),
+                pl.BlockSpec(right.shape, lambda i, t: (0, 0)),
+            ],
+            out_specs=pl.BlockSpec((rows * strips, 128), lambda i, t: (i, 0)),
+            scratch_shapes=[pltpu.VMEM((rows * strips, 128), F32)],
+        ),
+        out_shape=jax.ShapeDtypeStruct((len(chunks[0]) * rows * strips, 128), BF),
         compiler_params=params_of(),
-    )(left, right)
+    )(chunk_table(chunks, code_index) // rows, left, right)
+    return out, (chunks, base, strips, rows)
 
 
 def unpack_jobs(geometry, specs):
@@ -869,8 +893,10 @@
     )(jnp.full((1,), code_index, jnp.int32), windows)
 
 
-def pack_kernel(code_ref, *refs, plans):
+def pack_kernel(code_ref, *refs, plans, empty):
     sources, out_ref, sems = refs[:-2], refs[-2], refs[-1]
+    for slot in range(empty):
+        out_ref[slot] = jnp.zeros_like(out_ref[slot])
     for code, plan in enumerate(plans):
 
         @pl.when(code_ref[0] == code)
@@ -889,11 +915,11 @@
                 copy.wait()
 
 
-def pack_plans(geometry, spans):
+def pack_plans(geometry, spans, slots):
     plans = []
     for code in range(geometry.code_count):
         plan = []
-        for slot in range(geometry.dp_count):
+        for slot in slots:
             begin = geometry.begins[slot * geometry.code_count + code]
             stop = begin + geometry.window
             row = begin
@@ -908,17 +934,57 @@
     return plans
 
 
-def pack(geometry, code_index, sources, spans):
-    plans = pack_plans(geometry, spans)
+def pack(geometry, code_index, sources, spans, low, high):
+    plans = pack_plans(geometry, spans, range(low, high))
     return pl.pallas_call(
-        functools.partial(pack_kernel, plans=plans),
+        functools.partial(pack_kernel, plans=plans, empty=low),
         in_specs=[pl.BlockSpec(memory_space=pltpu.SMEM)]
         + [pl.BlockSpec(memory_space=pl.ANY)] * len(sources),
         out_specs=pl.BlockSpec(memory_space=pltpu.VMEM),
-        out_shape=jax.ShapeDtypeStruct((geometry.dp_count, geometry.window, 128), BF),
+        out_shape=jax.ShapeDtypeStruct((high, geometry.window, 128), BF),
         scratch_shapes=[pltpu.SemaphoreType.DMA((max(len(plan) for plan in plans),))],
         compiler_params=pltpu.CompilerParams(vmem_limit_bytes=VMEM_LIMIT),
     )(jnp.full((1,), code_index, jnp.int32), *sources)
+
+
+def front_slots(geometry):
+    stop = geometry.place("w_qkv")
+    count = sum(
+        geometry.begins[slot * geometry.code_count + geometry.code_count - 1] + geometry.window
+        <= stop
+        for slot in range(geometry.dp_count)
+    )
+    if geometry.dp_count & (geometry.dp_count - 1) or not count:
+        return 0
+    return 1 << (count.bit_length() - 1)
+
+
+def add_low(left, right):
+    return (left.astype(F32) + right.astype(F32)).astype(BF)
+
+
+def reduce_front(held, dp_count, dp_index):
+    count = held.shape[0]
+    bit = count // 2
+    while bit:
+        mine = dp_index // bit % 2
+        keep = lax.dynamic_slice_in_dim(held, mine * bit, bit, 0)
+        give = lax.dynamic_slice_in_dim(held, (1 - mine) * bit, bit, 0)
+        held = add_low(keep, lax.ppermute(give, "dp", [(i, i ^ bit) for i in range(dp_count)]))
+        bit //= 2
+    bits = []
+    while count < dp_count:
+        bits.append(count)
+        count *= 2
+    middle = held.shape[1] // (2 * TILE) * TILE
+    halves = [held[0, :middle], held[0, middle:]]
+    for number in range(len(bits)):
+        for side, bit in enumerate((bits[number], bits[-1 - number])):
+            moved = lax.ppermute(
+                halves[side], "dp", [(i, i - bit) for i in range(dp_count) if i & bit]
+            )
+            halves[side] = add_low(halves[side], moved)
+    return jnp.concatenate(halves, axis=0)
 
 
 def blocks_of_code(block):
@@ -963,6 +1029,12 @@
         value = value + lax.ppermute(value, axis, [(i, i ^ bit) for i in range(count)])
         bit *= 2
     return value
+
+
+def sum_over_all(value):
+    count = lax.axis_size("dp") * lax.axis_size("code")
+    sent = jnp.broadcast_to(value[None], (count,) + value.shape)
+    return jnp.sum(lax.all_to_all(sent, ("dp", "code"), 0, 0), axis=0)
 
 
 def norm_forward(before, norm_gain, norm_shift):
@@ -1077,7 +1149,7 @@
     return (final_rows, kept)
 
 
-def layer_backward(upstream, kept, fill, weights, span, pick):
+def layer_backward(upstream, kept, fill, weights, span, pick, grad_of):
     in_low, query_low, key_low, value_low, gate_wide, first, second, lse, attended, bias = kept[:10]
     mid_low, pre_act, act_low, normed_one, inv_one, normed_two, inv_two = kept[10:]
     vector = weights["layer_vec"].astype(F32)
@@ -1085,25 +1157,25 @@
         upstream, normed_two, inv_two, vec_part(vector, 6)
     )
     ffn_low = grad_res_two.astype(BF)
-    grad_down = weight_grad(act_low, ffn_low, 768)
+    grad_down = grad_of("w_down", act_low, ffn_low, 512)
     grad_pre = dot_nt(ffn_low, weights["w_down"]) * gelu_grad(pre_act)
     pre_low = grad_pre.astype(BF)
-    grad_up = weight_grad(mid_low, pre_low)
+    grad_up = grad_of("w_up", mid_low, pre_low, 256)
     grad_mid = DEEP_ALPHA * grad_res_two + dot_nt(pre_low, weights["w_up"])
     grad_res_one, grad_gain_one, grad_shift_one = norm_backward(
         grad_mid, normed_one, inv_one, vec_part(vector, 3)
     )
     out_low = grad_res_one.astype(BF)
-    grad_out = weight_grad(attended, out_low)
+    grad_out = grad_of("w_out", attended, out_low, 384)
     grad_att = dot_nt(out_low, weights["w_out"]).astype(BF)
-    parts, part_sums, grad_gate, grad_span = attention_backward(
+    grad_q, grad_k, grad_v, part_sums, grad_gate, grad_span = attention_backward(
         query_low, key_low, value_low, grad_att, gate_wide, span, fill, lse, pick, bias
     )
     grad_heads, grad_gate_proj, grad_gate_scale = gate_backward(
         jnp.transpose(grad_gate[:HEADS]), first, second, in_low, weights
     )
-    proj_low = jnp.concatenate([parts[0], parts[1], parts[2]], axis=1)
-    grad_qkv = weight_grad(in_low, proj_low)
+    proj_low = jnp.concatenate([grad_q, grad_k, grad_v], axis=1)
+    grad_qkv = grad_of("w_qkv", in_low, proj_low, 256)
     grad_hidden = DEEP_ALPHA * grad_res_one + dot_nt(proj_low, weights["w_qkv"]) + grad_heads
     grad_vec = jnp.concatenate(
         [
@@ -1130,27 +1202,54 @@
     return (grad_hidden, grad_map, grad_span)
 
 
+def head_kernel(
+    in_ref, weight_ref, code_ref, name_ref, target_ref, loss_ref, rows_ref, flat_ref, low_ref
+):
+    weight, codebook, names = weight_ref[...], code_ref[...], name_ref[0:1, :]
+    loss = jnp.zeros((1, 1), F32)
+    for low in range(0, in_ref.shape[0], BLOCK):
+        rows = slice(low, low + BLOCK)
+        projected = dot_nn(in_ref[rows, :], weight)
+        inv_len = lax.rsqrt(jnp.sum(projected * projected, axis=1, keepdims=True) + UNIT_EPSILON)
+        unit_rows = projected * inv_len
+        logits = LOGIT_SCALE * dot_nt(unit_rows.astype(BF), codebook)
+        target = target_ref[rows, 0:1]
+        live = jnp.where(target >= 0, 1.0, 0.0)
+        hits = jnp.where(names == target, 1.0, 0.0)
+        top = jnp.max(logits, axis=1, keepdims=True)
+        weights = jnp.exp(logits - top)
+        total = jnp.sum(weights, axis=1, keepdims=True)
+        picked = jnp.sum(logits * hits, axis=1, keepdims=True)
+        loss += jnp.sum((top + jnp.log(total) - picked) * live, axis=0, keepdims=True)
+        grad_logits = (weights * (1.0 / total) - hits) * (live * LOGIT_SCALE)
+        grad_unit = dot_nn(grad_logits.astype(BF), codebook)
+        grad_proj = (
+            grad_unit - unit_rows * jnp.sum(unit_rows * grad_unit, axis=1, keepdims=True)
+        ) * inv_len
+        proj_low = grad_proj.astype(BF)
+        low_ref[rows, :] = proj_low
+        rows_ref[rows, :] = dot_nt(proj_low, weight)
+    loss_ref[...] = jnp.broadcast_to(loss, loss_ref.shape)
+    grad = dot_tn(in_ref[...], low_ref[...])
+    strips = PROJ // 128
+    for strip in range(strips):
+        flat_ref[pl.ds(strip, D, stride=strips), :] = grad[:, strip * 128 : (strip + 1) * 128]
+
+
 def head_pass(hidden, w_head, codebook, codes, target_codes):
-    row_low = hidden.astype(BF)
-    projected = dot_nn(row_low, w_head)
-    inv_len = lax.rsqrt(jnp.sum(projected * projected, axis=-1, keepdims=True) + UNIT_EPSILON)
-    unit_rows = projected * inv_len
-    live_rows = (target_codes >= 0).astype(F32)[:, None]
-    logits = LOGIT_SCALE * dot_nt(unit_rows.astype(BF), codebook)
-    hits = (target_codes[:, None] == codes).astype(F32)
-    top = jnp.max(logits, axis=1, keepdims=True)
-    log_total = top + jnp.log(jnp.sum(jnp.exp(logits - top), axis=1, keepdims=True))
-    picked = jnp.sum(logits * hits, axis=1, keepdims=True)
-    loss_local = jnp.sum((log_total - picked) * live_rows)
-    grad_logits = ((jnp.exp(logits - log_total) - hits) * live_rows * LOGIT_SCALE).astype(BF)
-    grad_unit = dot_nn(grad_logits, codebook)
-    grad_proj = (
-        grad_unit - unit_rows * jnp.sum(unit_rows * grad_unit, axis=-1, keepdims=True)
-    ) * inv_len
-    proj_low = grad_proj.astype(BF)
-    grad_head = weight_grad(row_low, proj_low)
-    grad_rows = dot_nt(proj_low, w_head)
-    return (loss_local, grad_rows, grad_head)
+    targets = jnp.broadcast_to(target_codes[:, None], (ROWS, 128))
+    names = jnp.broadcast_to(codes, (8, codes.shape[1]))
+    loss, grad_rows, grad_head = pl.pallas_call(
+        head_kernel,
+        out_shape=[
+            jax.ShapeDtypeStruct((8, 128), F32),
+            jax.ShapeDtypeStruct((ROWS, D), F32),
+            jax.ShapeDtypeStruct((D * PROJ // 128, 128), F32),
+        ],
+        scratch_shapes=[pltpu.VMEM((ROWS, PROJ), BF)],
+        compiler_params=pltpu.CompilerParams(vmem_limit_bytes=VMEM_LIMIT),
+    )(hidden.astype(BF), w_head, codebook, names, targets)
+    return (loss[0, 0], grad_rows, grad_head)
 
 
 def local(
@@ -1271,15 +1370,20 @@
     target_codes = jnp.where(mask_row == 1, jnp.pad(targets[0], (0, ROWS - LONG)), -1)
     loss_local, upstream, grad_head = head_pass(final, w_head, all_codes, code_names, target_codes)
 
+    def grad_maker(index):
+        return lambda seg_name, left, right, rows: weight_grad(
+            left, right, geometry, code_index, geometry.place(seg_name, index), rows
+        )
+
     upstream, map_second, span_second = layer_backward(
-        upstream, kept_second, live_fill, weights[1], span, None
+        upstream, kept_second, live_fill, weights[1], span, None, grad_maker(1)
     )
     grad_mask_emb = jnp.sum(jnp.where(visible[:, None], 0.0, upstream), axis=0)
     grad_encoded = lax.dot_general(
         pick_full, upstream, (((1,), (0,)), ((), ())), precision=HIGHEST
     )
     grad_seen, map_first, span_first = layer_backward(
-        grad_encoded, kept_first, seen_fill, weights[0], span, pick_seen
+        grad_encoded, kept_first, seen_fill, weights[0], span, pick_seen, grad_maker(0)
     )
     grad_seen = grad_seen * seen_valid[:, None].astype(F32)
     grad_conv_seen = grad_seen * gelu_grad(seen_pre)
@@ -1290,7 +1394,9 @@
     own_grad = lax.dynamic_slice_in_dim(grad_conv, own_cols, width, 1)
     grad_in_own = conv_call(conv_input_kernel, own_grad[:LONG], conv_weight, half - 1, True)
     grad_conv_in = side_by_side(grad_in_own.astype(BF), code_index)
-    grad_kernel, chunks = conv_weight_grad(conv_in[:LONG], grad_conv, geometry, code_index)
+    split = front_slots(geometry)
+    padded, grads = conv_weight_inputs(conv_in[:LONG], grad_conv)
+    rest_grad = conv_weight_grad(padded, grads, geometry, code_index, range(split, dp_count))
     grad_start = (grad_full + grad_conv_in.astype(F32)) * live_float
     grad_embedded, grad_gain_zero, grad_shift_zero = norm_backward(
         grad_start, normed_zero, inv_zero, glob_vec[0]
@@ -1305,48 +1411,6 @@
         (((0,), (1,)), ((), ())),
         precision=HIGHEST,
     )
-    both = (map_first, map_second)
-    front = jnp.concatenate([grad_patch.reshape(-1, 128), grad_glob.reshape(-1, 128)], axis=0)
-    front = jnp.pad(front, ((geometry.phase, 0), (0, 0))).astype(BF)
-    sources = [front, grad_kernel]
-    common = [(0, front.shape[0], 0, 0)]
-    for seg_name in ("w_qkv", "w_out", "w_up", "w_down"):
-        for index, layer_map in enumerate(both):
-            flat = layer_map[seg_name]
-            common.append((geometry.place(seg_name, index), flat.shape[0], len(sources), 0))
-            sources.append(flat)
-    tail_place = geometry.place("layer_vec")
-    vec_rows = jnp.concatenate(
-        [layer_map["layer_vec"].reshape(-1, 128) for layer_map in both], axis=0
-    )
-    small = [layer_map[seg_name] for seg_name in ("gate_proj", "gate_scale") for layer_map in both]
-    small = jnp.concatenate([part.reshape(-1) for part in small + [grad_rel]])
-    lead = small.shape[0] % 128
-    small_rows = jnp.pad(small, (0, -small.shape[0] % 128)).reshape(-1, 128)
-    head_rows = jnp.pad(grad_head.astype(F32), ((1, 1), (0, 0)))
-    head_rows = jnp.concatenate(
-        [head_rows[:-1, 128 - lead :], head_rows[1:, : 128 - lead]], axis=1
-    )
-    whole = small.shape[0] // 128
-    tail = jnp.concatenate(
-        [vec_rows, small_rows[:whole], small_rows[whole:] + head_rows[:1], head_rows[1:]], axis=0
-    ).astype(BF)
-    tail_rows = geometry.begins[-1] + geometry.window - tail_place
-    tail = jnp.pad(tail, ((0, tail_rows - tail.shape[0]), (0, 0)))
-    common.append((tail_place, tail_rows, len(sources), 0))
-    sources.append(tail)
-    tap_rows = WIDTH * D // 128
-    spans = [
-        common
-        + [
-            (geometry.place("conv_w") + tap * tap_rows, CHUNK * tap_rows, 1, n * CHUNK * tap_rows)
-            for n, tap in enumerate(chunks[code])
-        ]
-        for code in range(code_count)
-    ]
-    own_part = pack(geometry, code_index, sources, spans)
-    reduced = lax.psum_scatter(own_part, "dp", scatter_dimension=0, tiled=False).astype(F32)
-    reduced = lax.dynamic_slice(reduced, (own_offset, 0), (shard_rows, 128)).reshape(shard_len)
     leader = (code_index == 0).astype(F32)
     count_local = jnp.sum((target_codes >= 0).astype(F32))
     early = jnp.concatenate(
@@ -1357,7 +1421,60 @@
         ]
     )
     early = sum_over(sum_over(jnp.pad(early, ((0, -early.shape[0] % 8), (0, 0))), "dp"), "code")
-    squares_all = sum_over(sum_over(jnp.full((8, 128), jnp.sum(reduced * reduced)), "dp"), "code")
+    both = (map_first, map_second)
+    sources, spans = [], [[] for _ in range(code_count)]
+
+    def add_source(found):
+        array, (chunks, base, unit, chunk) = found
+        for code, items in enumerate(chunk_spans(chunks, base, unit, chunk, len(sources))):
+            spans[code] += items
+        sources.append(array)
+
+    for seg_name in ("w_qkv", "w_out", "w_up", "w_down"):
+        for layer_map in both:
+            add_source(layer_map[seg_name])
+    add_source(rest_grad)
+    tail_place = geometry.place("layer_vec")
+    vec_rows = jnp.concatenate(
+        [layer_map["layer_vec"].reshape(-1, 128) for layer_map in both], axis=0
+    )
+    small = [layer_map[seg_name] for seg_name in ("gate_proj", "gate_scale") for layer_map in both]
+    small = jnp.concatenate([part.reshape(-1) for part in small + [grad_rel]])
+    lead = small.shape[0] % 128
+    small_rows = jnp.pad(small, (0, -small.shape[0] % 128)).reshape(-1, 128)
+    head_rows = jnp.pad(grad_head, ((1, 1), (0, 0)))
+    head_rows = jnp.concatenate(
+        [head_rows[:-1, 128 - lead :], head_rows[1:, : 128 - lead]], axis=1
+    )
+    whole = small.shape[0] // 128
+    tail = jnp.concatenate(
+        [vec_rows, small_rows[:whole], small_rows[whole:] + head_rows[:1], head_rows[1:]], axis=0
+    ).astype(BF)
+    tail_rows = geometry.begins[-1] + geometry.window - tail_place
+    tail = jnp.pad(tail, ((0, tail_rows - tail.shape[0]), (0, 0)))
+    for items in spans:
+        items.append((tail_place, tail_rows, len(sources), 0))
+    sources.append(tail)
+    front = jnp.concatenate([grad_patch.reshape(-1, 128), grad_glob.reshape(-1, 128)], axis=0)
+    front = jnp.pad(front, ((geometry.phase, 0), (0, 0))).astype(BF)
+    if split:
+        own_part = pack(geometry, code_index, sources, spans, split, dp_count)
+        reduced = lax.psum_scatter(own_part, "dp", scatter_dimension=0, tiled=False)
+        sources, spans = [], [[] for _ in range(code_count)]
+        add_source(conv_weight_grad(padded, grads, geometry, code_index, range(split)))
+    for items in spans:
+        items.append((0, front.shape[0], len(sources), 0))
+    front, early = lax.optimization_barrier((front, early))
+    sources.append(front)
+    last_part = pack(geometry, code_index, sources, spans, 0, split or dp_count)
+    if split:
+        first = reduce_front(last_part, dp_count, dp_index)
+        reduced = jnp.where(dp_index < split, first, reduced)
+    else:
+        reduced = lax.psum_scatter(last_part, "dp", scatter_dimension=0, tiled=False)
+    reduced = lax.dynamic_slice(reduced.astype(F32), (own_offset, 0), (shard_rows, 128))
+    reduced = reduced.reshape(shard_len)
+    squares_all = sum_over_all(jnp.full((8, 128), jnp.sum(reduced * reduced)))
     squares_all = squares_all[0, 0]
     rel_rows = BUCKETS * HEADS // 128
     rel_all = early[:rel_rows].reshape(BUCKETS, HEADS)

time: 705 us -> 690 us (0.979)
  waiting for transfers between devices: 285 us -> 247 us
  other arithmetic: 46.5 us -> 57.5 us
  Pallas kernels: 178 us -> 188 us
    reduce_scatter x1, waiting for transfers between devices: 69 us -> 0.01 us  [local(): reduced = lax.psum_scatter(own_part, 'dp', scatter_dimension=0, tiled=False)]
    ppermute x0 -> x5, waiting for transfers between devices: none -> 34.9 us  [the longest x4 31.6 us: reduce_front(): lax.ppermute(halves[side], 'dp', [(i, i - bit) for i in range(dp_count) i...]
    ppermute x10 -> x5, starting transfers between devices: 13.1 us -> 4.38 us  [sum_over(): lax.ppermute(value, axis, [(i, i ^ bit) for i in range(count)])]
    pallas_call x10 -> x11, Pallas kernels: 50 us -> 56.6 us  [the longest x8 38.2 us: weight_grad(): pl.pallas_call(weight_grad_kernel, grid_spec=pltpu.PrefetchScalarGridSpec...]
    pallas_call x1 -> x2, Pallas kernels: 21.9 us -> 24.9 us  [conv_weight_grad(): pl.pallas_call(conv_weight_kernel, grid_spec=pltpu.PrefetchScalarGridSpec...]
    dot_general x13 -> x11, matrix products: 26.7 us -> 24.8 us  [dot_nn(): lax.dot_general(left, right, (((1,), (0,)), ((), ())), preferred_element_...]
    dot_general x10 -> x8, matrix products: 24.1 us -> 23 us  [dot_nt(): lax.dot_general(left, right, (((1,), (1,)), ((), ())), preferred_element_...]
  transfers between devices with their start and end apart: 21 -> 22, of which waited for: 7 -> 10; matrix products, arithmetic and copies ran while one was open for 5% -> 6% of each run, Pallas kernels for 13% -> 10%
where the time goes in v3:
time: 690 us; the launch traced here: 680 us
  waiting for transfers between devices  247 us (36%)
  Pallas kernels  188 us (27%)
  matrix products  75 us (11%)
  other arithmetic  57.5 us (8%)
  local copies, waits for them, and re-layouts  56.4 us (8%)
  starting transfers between devices  31.3 us (5%)
  between operations  24.9 us (4%)
    all_gather x1, waiting for transfers between devices, local(): windows = lax.all_gather(own_window, ('dp', 'code'), axis=0, tiled=False)  202 us
    pallas_call x8, Pallas kernels, weight_grad(): pl.pallas_call(weight_grad_kernel, grid_spec=pltpu.PrefetchScalarGridSpec...  38.2 us
    ppermute x4, waiting for transfers between devices, reduce_front(): lax.ppermute(halves[side], 'dp', [(i, i - bit) for i in range(dp_count) i...  31.6 us
    pallas_call x2, Pallas kernels, unpack(): pl.pallas_call(functools.partial(unpack_kernel, jobs=jobs, stages=stages)...  30.5 us
    pallas_call x2, Pallas kernels, conv_call(): pl.pallas_call(kernel, grid=(steps,), in_specs=[pl.BlockSpec(padded.shape...  25.1 us
    pallas_call x2, Pallas kernels, conv_weight_grad(): pl.pallas_call(conv_weight_kernel, grid_spec=pltpu.PrefetchScalarGridSpec...  24.9 us
    dot_general x11, matrix products, dot_nn(): lax.dot_general(left, right, (((1,), (0,)), ((), ())), preferred_element_...  24.8 us
    pallas_call x2, Pallas kernels, attention_backward(): pl.pallas_call(kernel, grid=(HEADS // heads,), in_specs=[columns] * 4 + [...  24.1 us
  transfers between devices with their start and end apart: 22, of which 10 were waited for; matrix products, arithmetic and copies ran while one was open for 6% of the time, Pallas kernels for 10%

profile of v3, /device:TPU:0, one launch (start us, length us, event | category | flops | bytes accessed | tf_op | source)
XLA Modules:
  0.0 679.8 jit_solution(12541484280267797351)
XLA Ops:
  7.4 5.9 dynamic_update_slice.3
  14.4 4.1 collective-permute-start.4
  20.1 2.3 collective-permute-start.5
  36.9 202.3 %all-gather.3.cloned.1.call-done = bf16[151552,128]{1,0:T(8,128)(2,1)} async-done(((bf16[4736,128]{1,0:T(8,128)(2,1)}), bf16[151552,128]{1,0:T(8,128)(2,1)}) %all-gather.3.cloned.1.call-update) | async-done | bytes 38797328 | tf_op jit(solution)/shard_map/all_gather | solution.py:1277
  252.0 7.7 %shard_map.396.weight_ref = bf16[6144,192]{1,0:T(8,128)(2,1)} custom-call(s32[1]{0:T(128)} %bitcast.code_ref, bf16[32,4736,128]{2,1,0:T(8,128)(2,1)} %bitcast.237), custom_call_target="tpu_custom_call" | custom-call | tf_op jit(solution)/shard_map/pallas_call | solution.py:876
  259.7 12.1 %shard_map.397 = f32[512,192]{1,0:T(8,128)} custom-call(f32[640,192]{1,0:T(8,128)} %pad_convert_fusion.2.in_ref, bf16[6144,192]{1,0:T(8,128)(2,1)} %shard_map.396.weight_ref, bf16[4,192]{1,0:T(4,128)(2,1)} %constant.310.clone.mask_ref), custom_call_target="tpu_custom_call" | custom-call | tf_op jit(solution)/shard_map/pallas_call | solution.py:243
  271.7 2.0 fusion.57.refs_0_
  275.7 3.6 collective-permute-start.2
  279.3 15.2 %shard_map.401 = (bf16[768,2304]{1,0:T(8,128)(2,1)}, bf16[768,768]{1,0:T(8,128)(2,1)}, bf16[768,3072]{1,0:T(8,128)(2,1)}, bf16[3072,768]{1,0:T(8,128)(2,1)}) custom-call(bf16[32,4736,128]{2,1,0:T(8,128)(2,1)} %bitcast.238), custom_call_target="tpu_custom_call" | custom-call | tf_op jit(solution)/shard_map/pallas_call | solution.py:820
  294.5 15.3 %shard_map.399 = (bf16[768,2304]{1,0:T(8,128)(2,1)}, bf16[768,768]{1,0:T(8,128)(2,1)}, bf16[768,3072]{1,0:T(8,128)(2,1)}, bf16[3072,768]{1,0:T(8,128)(2,1)}) custom-call(bf16[32,4736,128]{2,1,0:T(8,128)(2,1)} %bitcast.239), custom_call_target="tpu_custom_call" | custom-call | tf_op jit(solution)/shard_map/pallas_call | solution.py:820
  316.5 1.8 copy.78
  318.3 2.0 fusion.85.span_ref
  321.0 2.0 shard_map.398
  323.1 2.3 fusion.183
  326.4 2.7 fusion.189
  331.4 4.5 shard_map.400
  337.8 2.3 multiply_convert_fusion.2
  340.1 3.5 fusion.185
  346.2 2.0 fusion.190
  351.5 9.7 %shard_map.402 = (bf16[512,768]{1,0:T(8,128)(2,1)}, f32[16,512]{1,0:T(8,128)}) custom-call(bf16[512,768]{1,0:T(8,128)(2,1)} %get-tuple-element.144.q_ref, bf16[512,768]{1,0:T(8,128)(2,1)} %slice.697.k_ref, bf16[512,768]{1,0:T(8,128)(2,1)} %get-tuple-element.143.v_ref, f32[16,512]{1,0:T(8,128)} %pad.69.gate_ref, f32[16,1024]{1,0:T(8,128)} %fusion.85.span_ref, ...), custom_call_target="tpu_custom_call" | custom-call | tf_op jit(solution)/shard_map/pallas_call | solution.py:490
  361.1 2.4 fusion.187
  364.6 6.8 %multiply_convert_fusion = (bf16[512,3072]{1,0:T(8,128)(2,1)S(1)}, f32[512,3072]{1,0:T(8,128)}) fusion(f32[3072]{0:T(1024)S(1)} %copy-done.101, bf16[512,768]{1,0:T(8,128)(2,1)S(1)} %fusion.16.left_ref, bf16[768,3072]{1,0:T(8,128)(2,1)} %get-tuple-element.45), kind=kOutput, calls=%fused_computation.6 | convolution fusion | flops 2425356288 | bytes 14954496 | tf_op jit(solution)/shard_map/dot_general | solution.py:155
  371.5 2.8 fusion.188
  377.6 8.0 %shard_map.403 = (f32[8,128]{1,0:T(8,128)}, f32[512,768]{1,0:T(8,128)}, f32[1536,128]{1,0:T(8,128)}) custom-call(bf16[512,768]{1,0:T(8,128)(2,1)} %add_convert_fusion.1.in_ref, bf16[768,256]{1,0:T(8,128)(2,1)} %reshape.399.weight_ref, bf16[1024,256]{1,0:T(8,128)(2,1)} %pad_maximum_fusion.1.code_ref, s32[8,1024]{1,0:T(8,128)} %broadcast_in_dim.66.name_ref, ...), custom_call_target="tpu_custom_call" | custom-call | tf_op jit(solution)/shard_map/pallas_call | solution.py:1242
  385.6 2.8 multiply_reduce_fusion
  389.6 8.4 %fusion.179 = (bf16[3072]{0:T(1024)(128)(2,1)}, bf16[512,3072]{1,0:T(8,128)(2,1)S(1)}) fusion(f32[512,3072]{1,0:T(8,128)} %get-tuple-element.202, f32[3072]{0:T(1024)S(1)} %copy-done.101, bf16[512,768]{1,0:T(8,128)(2,1)S(1)} %convert_element_type.306.right_ref, bf16[3072,768]{1,0:T(8,128)(2,1)} %get-tuple-element.46), kind=kOutput, calls=%fused_computation.401 | convolution fusion | flops 2434790400 | bytes 14960640 | tf_op jit(solution)/shard_map/dot_general | solution.py:159
  398.0 3.7 multiply_reduce_fusion.1
  404.1 1.7 convolution_convert_fusion.up_ref
  405.8 17.1 %shard_map.404 = (bf16[512,768]{1,0:T(8,128)(2,1)}, bf16[512,768]{1,0:T(8,128)(2,1)}, bf16[512,768]{1,0:T(8,128)(2,1)}, f32[8,768]{1,0:T(8,128)}, f32[16,512]{1,0:T(8,128)}, /*index=5*/f32[16,1024]{1,0:T(8,128)}) custom-call(bf16[512,768]{1,0:T(8,128)(2,1)} %get-tuple-element.144.q_ref, bf16[512,768]{1,0:T(8,128)(2,1)} %slice.697.k_ref, ...), custom_call_target="tpu_custom_call" | custom-call | tf_op jit(solution)/shard_map/pallas_call | solution.py:701
  429.8 2.0 fusion.191
  431.9 2.3 select_reduce_fusion
  436.4 2.3 fusion.180
  438.8 2.4 multiply_reduce_fusion.13
  444.6 7.0 %shard_map.405 = (bf16[128,768]{1,0:T(8,128)(2,1)}, bf16[128,768]{1,0:T(8,128)(2,1)}, bf16[128,768]{1,0:T(8,128)(2,1)}, f32[8,768]{1,0:T(8,128)}, f32[16,128]{1,0:T(8,128)}, /*index=5*/f32[16,1024]{1,0:T(8,128)}) custom-call(bf16[128,768]{1,0:T(8,128)(2,1)} %get-tuple-element.152.q_ref, bf16[128,768]{1,0:T(8,128)(2,1)} %slice.698.k_ref, ...), custom_call_target="tpu_custom_call" | custom-call | tf_op jit(solution)/shard_map/pallas_call | solution.py:701
  463.5 2.9 broadcast_multiply_fusion
  468.5 6.4 shard_map.415.refs_5_
  474.9 4.9 shard_map.414.refs_4_
  479.8 5.2 shard_map.417.refs_7_
  484.9 4.1 shard_map.413.refs_3_
  489.1 5.9 shard_map.411.refs_1_
  496.5 3.4 shard_map.412.refs_2_
  500.0 2.0 fusion.176
  504.0 4.3 shard_map.416.refs_6_
  508.5 4.1 shard_map.410.refs_0_
  518.4 5.8 shard_map.418.refs_8_
  524.2 7.3 %shard_map.419 = bf16[8,4736,128]{2,1,0:T(8,128)(2,1)} custom-call(s32[1]{0:T(128)} %bitcast.code_ref, bf16[9216,128]{1,0:T(8,128)(2,1)} %shard_map.410.refs_0_, bf16[9216,128]{1,0:T(8,128)(2,1)} %shard_map.411.refs_1_, bf16[4608,128]{1,0:T(8,128)(2,1)} %shard_map.412.refs_2_, bf16[4608,128]{1,0:T(8,128)(2,1)} %shard_map.413.refs_3_, ...), custom_call_target="tpu_custom_call" | custom-call | tf_op jit(solution)/shard_map/pallas_call | solution.py:939
  541.2 2.1 collective-permute-done.11
  544.2 13.0 %shard_map.407 = f32[512,192]{1,0:T(8,128)} custom-call(f32[640,192]{1,0:T(8,128)} %pad_convert_fusion.1.in_ref, bf16[6144,192]{1,0:T(8,128)(2,1)} %shard_map.396.weight_ref, bf16[4,192]{1,0:T(4,128)(2,1)} %constant.310.clone.mask_ref), custom_call_target="tpu_custom_call" | custom-call | tf_op jit(solution)/shard_map/pallas_call | solution.py:243
  558.3 1.6 collective-permute-start.8
  559.9 1.8 collective-permute-start.7
  561.7 1.7 collective-permute-start.13
  564.3 19.1 %shard_map.406.refs_0_ = bf16[10368,128]{1,0:T(8,128)(2,1)} custom-call(s32[6]{0:T(128)} %fusion.146.tap_ref, f32[4,192,640]{2,1,0:T(8,128)} %bitcast.245, bf16[4,512,192]{2,1,0:T(8,128)(2,1)} %bitcast.248, f32[4,192]{1,0:T(4,128)} %constant.318.clone.mask_ref), custom_call_target="tpu_custom_call" | custom-call | tf_op jit(solution)/shard_map/pallas_call | solution.py:340
  584.8 2.5 shard_map.408
  587.4 2.1 multiply_reduce_fusion.3
  591.6 3.1 shard_map.409
  594.6 2.5 constant_dynamic-slice_fusion.8
  597.2 3.2 collective-permute-done.14
  600.4 1.6 add_convert_fusion
  604.7 15.0 %collective-permute-done.15 = bf16[2368,128]{1,0:T(8,128)(2,1)S(1)} collective-permute-done((bf16[2368,128]{1,0:T(8,128)(2,1)S(1)}, bf16[2368,128]{1,0:T(8,128)(2,1)S(1)}, u32[]{:S(2)}, u32[]{:S(2)}) %collective-permute-start.15) | collective-permute-done | bytes 606240 | tf_op jit(solution)/shard_map/ppermute | solution.py:983
  624.0 14.2 %collective-permute-done.16 = bf16[2368,128]{1,0:T(8,128)(2,1)S(1)} collective-permute-done((bf16[2368,128]{1,0:T(8,128)(2,1)S(1)}, bf16[2368,128]{1,0:T(8,128)(2,1)S(1)}, u32[]{:S(2)}, u32[]{:S(2)}) %collective-permute-start.16) | collective-permute-done | bytes 606240 | tf_op jit(solution)/shard_map/ppermute | solution.py:983
  640.4 4.9 fusion.5
  646.7 4.8 all-to-all-start
  654.8 5.2 all-to-all-done
  663.4 6.8 %fusion.169 = (bf16[603008]{0:T(1024)(128)(2,1)}, f32[603008]{0:T(1024)}, f32[603008]{0:T(1024)}, f32[603008]{0:T(1024)}) fusion(f32[603008]{0:T(1024)S(1)} %copy-done.3, f32[]{:T(128)} %bitcast.69, f32[]{:T(128)} %bitcast.68, f32[]{:T(128)S(6)} %min.7, f32[]{:T(128)} %bitcast.65, bf16[4711,128]{1,0:T(8,128)(2,1)} %get-tuple-element.117, f32[603008]{0:T(1024)} %param.44, ...), kind=kLoop, calls=%fused_computation.395 | loop fusion | flops 11457152 | bytes 16884240 | tf_op jit(solution)/shard_map/convert_element_type | solution.py:1498
  (550 shorter events, 120.4 us)
Async XLA Ops:
  7.2 232.0 %all-gather.3.cloned.1.call-start = ((), (), s32[]{:S(2)}) async-start(), calls=%async_computation.3 | async-start | bytes 40009728 | tf_op jit(solution)/shard_map/all_gather | solution.py:1277
  7.3 7.1 %copy-start.49 = (bf16[256,256]{1,0:T(8,128)(2,1)S(1)}, bf16[256,256]{1,0:T(8,128)(2,1)}, u32[]{:S(2)}) copy-start(bf16[256,256]{1,0:T(8,128)(2,1)} %param.41) | copy-start | bytes 393220
  7.3 15.7 %copy-start.115 = (s32[1,496]{1,0:T(1,128)S(1)}, s32[1,496]{1,0:T(1,128)}, u32[]{:S(2)}) copy-start(s32[1,496]{1,0:T(1,128)} %param.39) | copy-start | bytes 5956
  7.3 21.7 %copy-start.132 = (s32[1,496]{1,0:T(1,128)S(1)}, s32[1,496]{1,0:T(1,128)}, u32[]{:S(2)}) copy-start(s32[1,496]{1,0:T(1,128)} %param.40) | copy-start | bytes 5956
  13.3 229.4 %copy-start.64 = (f32[8,24]{1,0:T(8,128)S(1)}, f32[8,24]{1,0:T(8,128)}, u32[]{:S(2)}) copy-start(f32[8,24]{1,0:T(8,128)} %constant.306.clone) | copy-start | bytes 2308
  14.3 626.1 %reduce-scatter.2.cloned.1.call-start = ((), (), s32[]{:S(2)}) async-start(), calls=%async_computation.2 | async-start | bytes 10911744 | tf_op jit(solution)/shard_map/reduce_scatter | solution.py:1462
  14.4 21.6 %collective-permute-start.4 = (bf16[256,256]{1,0:T(8,128)(2,1)S(1)}, bf16[256,256]{1,0:T(8,128)(2,1)S(1)}, u32[]{:S(2)}, u32[]{:S(2)}) collective-permute-start(bf16[256,256]{1,0:T(8,128)(2,1)S(1)} %copy-done.49), channel_id=1, source_target_pairs={{0,2},{1,3},{2,0},{3,1},{4,6},{5,7},{6,4},{7,5},{8,10},{9,11},{10,... | collective-permute-start | bytes 393224 | tf_op jit(solution)/shard_map/ppermute | solution.py:993
  18.5 17.5 %collective-permute-start.3 = (bf16[256,256]{1,0:T(8,128)(2,1)S(1)}, bf16[256,256]{1,0:T(8,128)(2,1)S(1)}, u32[]{:S(2)}, u32[]{:S(2)}) collective-permute-start(bf16[256,256]{1,0:T(8,128)(2,1)S(1)} %copy-done.49), channel_id=1, source_target_pairs={{0,1},{1,2},{2,3},{3,0},{4,5},{5,6},{6,7},{7,4},{8,9},{9,10},{10,1... | collective-permute-start | bytes 393224 | tf_op jit(solution)/shard_map/ppermute | solution.py:993
  20.1 16.0 %collective-permute-start.5 = (bf16[256,256]{1,0:T(8,128)(2,1)S(1)}, bf16[256,256]{1,0:T(8,128)(2,1)S(1)}, u32[]{:S(2)}, u32[]{:S(2)}) collective-permute-start(bf16[256,256]{1,0:T(8,128)(2,1)S(1)} %copy-done.49), channel_id=1, source_target_pairs={{0,3},{1,0},{2,1},{3,2},{4,7},{5,4},{6,5},{7,6},{8,11},{9,8},{10,9... | collective-permute-start | bytes 393224 | tf_op jit(solution)/shard_map/ppermute | solution.py:993
  23.0 248.7 %copy-start.69 = (pred[512]{0:T(512)(128)(4,1)}, pred[512]{0:T(512)(128)(4,1)S(1)}, u32[]{:S(2)}) copy-start(pred[512]{0:T(512)(128)(4,1)S(1)} %get-tuple-element.136) | copy-start | bytes 1540
  28.5 221.2 %copy-start.81 = (f32[512]{0:T(512)}, f32[512]{0:T(512)S(1)}, u32[]{:S(2)}) copy-start(f32[512]{0:T(512)S(1)} %fusion.141) | copy-start | bytes 6148
  30.6 214.5 %copy-start.39 = (bf16[128,128]{1,0:T(8,128)(2,1)}, bf16[128,128]{1,0:T(8,128)(2,1)S(1)}, u32[]{:S(2)}) copy-start(bf16[128,128]{1,0:T(8,128)(2,1)S(1)} %fusion.72.near_ref) | copy-start | bytes 98308
  30.7 241.0 %copy-start.50 = (s32[512]{0:T(512)}, s32[512]{0:T(512)S(1)}, u32[]{:S(2)}) copy-start(s32[512]{0:T(512)S(1)} %fusion.246) | copy-start | bytes 6148
  36.9 211.9 %copy-start.30 = (bf16[1,496,256]{2,1,0:T(8,128)(2,1)S(1)}, bf16[1,496,256]{2,1,0:T(8,128)(2,1)}, u32[]{:S(2)}) copy-start(bf16[1,496,256]{2,1,0:T(8,128)(2,1)} %param.37) | copy-start | bytes 761860
  273.8 47.2 %collective-permute-start.1 = (f32[128,192]{1,0:T(8,128)}, f32[128,192]{1,0:T(8,128)}, u32[]{:S(2)}, u32[]{:S(2)}) collective-permute-start(f32[128,192]{1,0:T(8,128)} %fusion.57.refs_0_), channel_id=1, source_target_pairs={{0,2},{1,3},{2,0},{3,1},{4,6},{5,7},{6,4},{7,5},{8,10},{9,11},{10,... | collective-permute-start | bytes 294920 | tf_op jit(solution)/shard_map/ppermute | solution.py:993
  275.3 45.7 %collective-permute-start = (f32[128,192]{1,0:T(8,128)}, f32[128,192]{1,0:T(8,128)}, u32[]{:S(2)}, u32[]{:S(2)}) collective-permute-start(f32[128,192]{1,0:T(8,128)} %fusion.57.refs_0_), channel_id=1, source_target_pairs={{0,1},{1,2},{2,3},{3,0},{4,5},{5,6},{6,7},{7,4},{8,9},{9,10},{10,1... | collective-permute-start | bytes 294920 | tf_op jit(solution)/shard_map/ppermute | solution.py:993
  275.7 45.3 %collective-permute-start.2 = (f32[128,192]{1,0:T(8,128)}, f32[128,192]{1,0:T(8,128)}, u32[]{:S(2)}, u32[]{:S(2)}) collective-permute-start(f32[128,192]{1,0:T(8,128)} %fusion.57.refs_0_), channel_id=1, source_target_pairs={{0,3},{1,0},{2,1},{3,2},{4,7},{5,4},{6,5},{7,6},{8,11},{9,8},{10,9... | collective-permute-start | bytes 294920 | tf_op jit(solution)/shard_map/ppermute | solution.py:993
  294.5 17.0 %copy-start.7 = (f32[768,64]{1,0:T(8,128)S(1)}, f32[768,64]{1,0:T(8,128)}, u32[]{:S(2)}) copy-start(f32[768,64]{1,0:T(8,128)} %constant.307.clone) | copy-start | bytes 589828
  294.5 17.0 %copy-start.28 = (f32[768,24]{0,1:T(8,128)S(1)}, f32[768,24]{0,1:T(8,128)}, u32[]{:S(2)}) copy-start(f32[768,24]{0,1:T(8,128)} %constant.308.clone) | copy-start | bytes 221188
  323.1 14.6 %slice-start = ((s8[4718592]{0:T(1024)(128)(4,1)}), s8[4194304]{0:T(1024)(128)(4,1)S(1)}, s32[]{:S(2)}) async-start(s8[4718592]{0:T(1024)(128)(4,1)} %bitcast.240), calls=%async_computation.4 | async-start | bytes 8388608
  326.4 11.3 %slice-start.1 = ((s8[4718592]{0:T(1024)(128)(4,1)}), s8[524288]{0:T(1024)(128)(4,1)S(1)}, s32[]{:S(2)}) async-start(s8[4718592]{0:T(1024)(128)(4,1)} %bitcast.240), calls=%async_computation.5 | async-start | bytes 1048576
  329.1 6.8 %copy-start.10 = (bf16[768,768]{1,0:T(8,128)(2,1)S(1)}, bf16[768,768]{1,0:T(8,128)(2,1)}, u32[]{:S(2)}) copy-start(bf16[768,768]{1,0:T(8,128)(2,1)} %get-tuple-element.39) | copy-start | bytes 3538948
  329.2 6.8 copy-start.92
  344.9 111.4 %copy-start.1 = (bf16[512,768]{1,0:T(8,128)(2,1)}, bf16[512,768]{1,0:T(8,128)(2,1)S(1)}, u32[]{:S(2)}) copy-start(bf16[512,768]{1,0:T(8,128)(2,1)S(1)} %get-tuple-element.196.left_ref) | copy-start | bytes 2359300
  350.6 10.5 %copy-start.124 = (f32[768]{0:T(1024)S(1)}, f32[768]{0:T(1024)}, u32[]{:S(2)}) copy-start(f32[768]{0:T(1024)} %get-tuple-element.163) | copy-start | bytes 9220
  364.2 7.2 %slice-start.8 = ((s8[4718592]{0:T(1024)(128)(4,1)}), s8[4194304]{0:T(1024)(128)(4,1)S(1)}, s32[]{:S(2)}) async-start(s8[4718592]{0:T(1024)(128)(4,1)} %bitcast.268), calls=%async_computation.12 | async-start | bytes 8388608
  364.5 6.9 %copy-start.19 = (bf16[512,768]{1,0:T(8,128)(2,1)}, bf16[512,768]{1,0:T(8,128)(2,1)S(1)}, u32[]{:S(2)}) copy-start(bf16[512,768]{1,0:T(8,128)(2,1)S(1)} %fusion.16.left_ref) | copy-start | bytes 2359300
  364.6 6.9 %copy-start.123 = (f32[768]{0:T(1024)S(1)}, f32[768]{0:T(1024)}, u32[]{:S(2)}) copy-start(f32[768]{0:T(1024)} %get-tuple-element.160) | copy-start | bytes 9220
  364.6 6.9 %slice-start.9 = ((s8[4718592]{0:T(1024)(128)(4,1)}), s8[524288]{0:T(1024)(128)(4,1)S(1)}, s32[]{:S(2)}) async-start(s8[4718592]{0:T(1024)(128)(4,1)} %bitcast.268), calls=%async_computation.13 | async-start | bytes 1048576
  389.5 8.5 %slice-start.6 = ((s8[4718592]{0:T(1024)(128)(4,1)}), s8[4194304]{0:T(1024)(128)(4,1)S(1)}, s32[]{:S(2)}) async-start(s8[4718592]{0:T(1024)(128)(4,1)} %bitcast.266), calls=%async_computation.10 | async-start | bytes 8388608
  389.6 8.4 %copy-start.20 = (bf16[512,768]{1,0:T(8,128)(2,1)}, bf16[512,768]{1,0:T(8,128)(2,1)S(1)}, u32[]{:S(2)}) copy-start(bf16[512,768]{1,0:T(8,128)(2,1)S(1)} %convert_element_type.306.right_ref) | copy-start | bytes 2359300
  389.6 8.4 %slice-start.7 = ((s8[4718592]{0:T(1024)(128)(4,1)}), s8[524288]{0:T(1024)(128)(4,1)S(1)}, s32[]{:S(2)}) async-start(s8[4718592]{0:T(1024)(128)(4,1)} %bitcast.266), calls=%async_computation.11 | async-start | bytes 1048576
  405.8 20.5 %copy-start.21 = (f32[1536,128]{1,0:T(8,128)S(1)}, f32[1536,128]{1,0:T(8,128)}, u32[]{:S(2)}) copy-start(f32[1536,128]{1,0:T(8,128)} %get-tuple-element.65) | copy-start | bytes 2359300
  443.4 8.2 %copy-start.122 = (f32[12]{0:T(128)S(1)}, f32[12]{0:T(128)}, u32[]{:S(2)}) copy-start(f32[12]{0:T(128)} %get-tuple-element.138) | copy-start | bytes 148
  444.6 12.8 %copy-start.8 = (f32[768,64]{1,0:T(8,128)S(1)}, f32[768,64]{1,0:T(8,128)}, u32[]{:S(2)}) copy-start(f32[768,64]{1,0:T(8,128)} %constant.307.clone) | copy-start | bytes 589828
  460.5 6.2 copy-start.4
  508.4 6.5 copy-start.114
  508.4 6.7 copy-start.113
  508.4 6.9 %copy-start.112 = (bf16[768]{0:T(1024)(128)(2,1)S(1)}, bf16[768]{0:T(1024)(128)(2,1)}, u32[]{:S(2)}) copy-start(bf16[768]{0:T(1024)(128)(2,1)} %get-tuple-element.107) | copy-start | bytes 4612
  508.4 7.1 %copy-start.111 = (bf16[768]{0:T(1024)(128)(2,1)S(1)}, bf16[768]{0:T(1024)(128)(2,1)}, u32[]{:S(2)}) copy-start(bf16[768]{0:T(1024)(128)(2,1)} %get-tuple-element.122) | copy-start | bytes 4612
  508.5 7.3 %copy-start.117 = (bf16[768]{0:T(1024)(128)(2,1)S(1)}, bf16[768]{0:T(1024)(128)(2,1)}, u32[]{:S(2)}) copy-start(bf16[768]{0:T(1024)(128)(2,1)} %get-tuple-element.100) | copy-start | bytes 4612
  508.5 7.5 %copy-start.116 = (bf16[768]{0:T(1024)(128)(2,1)S(1)}, bf16[768]{0:T(1024)(128)(2,1)}, u32[]{:S(2)}) copy-start(bf16[768]{0:T(1024)(128)(2,1)} %get-tuple-element.106) | copy-start | bytes 4612
  508.5 7.7 %copy-start.119 = (bf16[3072]{0:T(1024)(128)(2,1)S(1)}, bf16[3072]{0:T(1024)(128)(2,1)}, u32[]{:S(2)}) copy-start(bf16[3072]{0:T(1024)(128)(2,1)} %get-tuple-element.145) | copy-start | bytes 18436
  508.5 7.7 %copy-start.26 = (bf16[1536,128]{1,0:T(8,128)(2,1)S(1)}, bf16[1536,128]{1,0:T(8,128)(2,1)}, u32[]{:S(2)}) copy-start(bf16[1536,128]{1,0:T(8,128)(2,1)} %fusion.26) | copy-start | bytes 1179652
  508.5 7.7 %copy-start.128 = (bf16[1,128]{1,0:T(2,128)(2,1)S(1)}, bf16[1,128]{1,0:T(2,128)(2,1)}, u32[]{:S(2)}) copy-start(bf16[1,128]{1,0:T(2,128)(2,1)} %fusion.155) | copy-start | bytes 772
  534.5 1.2 collective-permute-start.9
  535.8 3.7 collective-permute-start.10
  539.5 3.7 collective-permute-start.11
  543.3 18.4 %collective-permute-start.12 = (f32[32,128]{1,0:T(8,128)S(1)}, f32[32,128]{1,0:T(8,128)S(1)}, u32[]{:S(2)}, u32[]{:S(2)}) collective-permute-start(f32[32,128]{1,0:T(8,128)S(1)} %add.542), channel_id=1, source_target_pairs={{0,1},{1,0},{2,3},{3,2},{4,5},{5,4},{6,7},{7,6},{8,9},{9,8},{10,11... | collective-permute-start | bytes 49160 | tf_op jit(solution)/shard_map/ppermute | solution.py:1029
  544.2 19.2 %copy-start.36 = (f32[128,768]{1,0:T(8,128)S(1)}, f32[128,768]{1,0:T(8,128)}, u32[]{:S(2)}) copy-start(f32[128,768]{1,0:T(8,128)} %get-tuple-element.212) | copy-start | bytes 1179652
  557.2 7.0 %copy-start.107 = (bf16[768]{0:T(1024)(128)(2,1)S(1)}, bf16[768]{0:T(1024)(128)(2,1)}, u32[]{:S(2)}) copy-start(bf16[768]{0:T(1024)(128)(2,1)} %get-tuple-element.208) | copy-start | bytes 4612
  557.2 7.0 %copy-start.133 = (bf16[768]{0:T(1024)(128)(2,1)S(1)}, bf16[768]{0:T(1024)(128)(2,1)}, u32[]{:S(2)}) copy-start(bf16[768]{0:T(1024)(128)(2,1)} %get-tuple-element.129) | copy-start | bytes 4612
  558.3 25.1 %copy-start.29 = (bf16[512,192]{1,0:T(8,128)(2,1)}, bf16[512,192]{1,0:T(8,128)(2,1)S(1)}, u32[]{:S(2)}) copy-start(bf16[512,192]{1,0:T(8,128)(2,1)S(1)} %convert_element_type.317.refs_0_) | copy-start | bytes 589828
  558.3 25.1 %collective-permute-start.8 = (bf16[512,192]{1,0:T(8,128)(2,1)S(1)}, bf16[512,192]{1,0:T(8,128)(2,1)S(1)}, u32[]{:S(2)}, u32[]{:S(2)}) collective-permute-start(bf16[512,192]{1,0:T(8,128)(2,1)S(1)} %convert_element_type.317.refs_0_), channel_id=1, source_target_pairs={{0,3},{1,0},{2,1},{3,2},{4,7},{5,4},{6,5},{7,6},{8,11},{9,8},{10,9... | collective-permute-start | bytes 589832 | tf_op jit(solution)/shard_map/ppermute | solution.py:993
  559.9 23.5 %collective-permute-start.7 = (bf16[512,192]{1,0:T(8,128)(2,1)S(1)}, bf16[512,192]{1,0:T(8,128)(2,1)S(1)}, u32[]{:S(2)}, u32[]{:S(2)}) collective-permute-start(bf16[512,192]{1,0:T(8,128)(2,1)S(1)} %convert_element_type.317.refs_0_), channel_id=1, source_target_pairs={{0,2},{1,3},{2,0},{3,1},{4,6},{5,7},{6,4},{7,5},{8,10},{9,11},{10,... | collective-permute-start | bytes 589832 | tf_op jit(solution)/shard_map/ppermute | solution.py:993
  561.7 23.1 %collective-permute-start.6 = (bf16[512,192]{1,0:T(8,128)(2,1)S(1)}, bf16[512,192]{1,0:T(8,128)(2,1)}, u32[]{:S(2)}, u32[]{:S(2)}) collective-permute-start(bf16[512,192]{1,0:T(8,128)(2,1)S(1)} %convert_element_type.317.refs_0_), channel_id=1, source_target_pairs={{0,1},{1,2},{2,3},{3,0},{4,5},{5,6},{6,7},{7,4},{8,9},{9,10},{10,1... | collective-permute-start | bytes 589832 | tf_op jit(solution)/shard_map/ppermute | solution.py:993
  561.7 21.7 %collective-permute-start.13 = (f32[32,128]{1,0:T(8,128)S(1)}, f32[32,128]{1,0:T(8,128)S(1)}, u32[]{:S(2)}, u32[]{:S(2)}) collective-permute-start(f32[32,128]{1,0:T(8,128)S(1)} %add.543), channel_id=1, source_target_pairs={{0,2},{1,3},{2,0},{3,1},{4,6},{5,7},{6,4},{7,5},{8,10},{9,11},{10,... | collective-permute-start | bytes 49160 | tf_op jit(solution)/shard_map/ppermute | solution.py:1029
  597.2 3.2 collective-permute-start.14
  602.1 17.6 %collective-permute-start.15 = (bf16[2368,128]{1,0:T(8,128)(2,1)S(1)}, bf16[2368,128]{1,0:T(8,128)(2,1)S(1)}, u32[]{:S(2)}, u32[]{:S(2)}) collective-permute-start(bf16[2368,128]{1,0:T(8,128)(2,1)S(1)} %get-tuple-element.149), channel_id=1, source_target_pairs={{8,0},{12,4},{24,16},{28,20},{9,1},{13,5},{25,17},{29,21},{10,2},{... | collective-permute-start | bytes 1818632 | tf_op jit(solution)/shard_map/ppermute | solution.py:983
  603.4 17.6 %collective-permute-start.17 = (bf16[2368,128]{1,0:T(8,128)(2,1)S(1)}, bf16[2368,128]{1,0:T(8,128)(2,1)S(1)}, u32[]{:S(2)}, u32[]{:S(2)}) collective-permute-start(bf16[2368,128]{1,0:T(8,128)(2,1)S(1)} %get-tuple-element.150), channel_id=1, source_target_pairs={{16,0},{20,4},{24,8},{28,12},{17,1},{21,5},{25,9},{29,13},{18,2},{... | collective-permute-start | bytes 1818632 | tf_op jit(solution)/shard_map/ppermute | solution.py:983
  621.4 16.8 %collective-permute-start.16 = (bf16[2368,128]{1,0:T(8,128)(2,1)S(1)}, bf16[2368,128]{1,0:T(8,128)(2,1)S(1)}, u32[]{:S(2)}, u32[]{:S(2)}) collective-permute-start(bf16[2368,128]{1,0:T(8,128)(2,1)S(1)} %get-tuple-element.147), channel_id=1, source_target_pairs={{16,0},{20,4},{24,8},{28,12},{17,1},{21,5},{25,9},{29,13},{18,2},{... | collective-permute-start | bytes 1818632 | tf_op jit(solution)/shard_map/ppermute | solution.py:983
  622.7 16.8 %collective-permute-start.18 = (bf16[2368,128]{1,0:T(8,128)(2,1)S(1)}, bf16[2368,128]{1,0:T(8,128)(2,1)S(1)}, u32[]{:S(2)}, u32[]{:S(2)}) collective-permute-start(bf16[2368,128]{1,0:T(8,128)(2,1)S(1)} %get-tuple-element.148), channel_id=1, source_target_pairs={{8,0},{12,4},{24,16},{28,20},{9,1},{13,5},{25,17},{29,21},{10,2},{... | collective-permute-start | bytes 1818632 | tf_op jit(solution)/shard_map/ppermute | solution.py:983
  640.4 23.0 %copy-start.3 = (f32[603008]{0:T(1024)S(1)}, f32[603008]{0:T(1024)}, u32[]{:S(2)}) copy-start(f32[603008]{0:T(1024)} %param.42) | copy-start | bytes 7236100
  646.7 13.3 %all-to-all-start = ((f32[32,8,128]{2,1,0:T(8,128)}), f32[32,8,128]{2,1,0:T(8,128)S(1)}, u32[]{:S(2)}, u32[]{:S(2)}) async-start(f32[32,8,128]{2,1,0:T(8,128)} %broadcast_in_dim_broadcast_in_dim_broadcast_in_dim.3), calls=%async_computation.1 | async-start | bytes 262144 | tf_op jit(solution)/shard_map/all_to_all | solution.py:1037
  (109 other events, 343.1 us)
Sparse Core Ops, SparseCore 0:
  14.5 224.6 all-gather.2
  531.7 74.9 reduce-scatter.1

commit v4 on v3

--- a/solution.py
+++ b/solution.py
@@ -110,17 +110,6 @@
             else:
                 merged.append(item)
         return merged, edges
-
-    def exact(self, windows, low, high):
-        parts = []
-        row = low
-        while row < high:
-            shard = row // self.shard_rows
-            stop = min(high, (shard + 1) * self.shard_rows)
-            begin = self.offsets[shard] + row - shard * self.shard_rows
-            parts.append(windows[shard, begin : begin + stop - row])
-            row = stop
-        return parts[0] if len(parts) == 1 else jnp.concatenate(parts, axis=0)
 
 
 def bucket_onehot():
@@ -471,48 +460,46 @@
         out_ref[:, pair * BLOCK : (pair + 1) * BLOCK] = jnp.transpose(both).astype(BF)
 
 
-def pair_spec(length):
-    return pl.BlockSpec((length, 2 * HEAD_DIM), lambda i: (0, i))
+def head_specs(length, heads):
+    count = HEADS // heads
+    return [
+        pl.BlockSpec((length, heads * HEAD_DIM), lambda i, part=part: (0, part * count + i))
+        for part in range(3)
+    ]
 
 
 def whole_spec(shape):
     return pl.BlockSpec(shape, lambda i: (0,) * len(shape))
 
 
-def attention_forward(query, keyv, value, gate, span, fill, pick):
-    length = query.shape[0]
-    args = [query, keyv, value, gate, span, fill] + list(pick or ())
+def attention_forward(qkv, gate, span, fill, pick):
+    length = qkv.shape[0]
+    heads = 2 if pick is None else SEEN_HEADS
+    specs = head_specs(length, heads)
+    args = [qkv, qkv, qkv, gate, span, fill] + list(pick or ())
     shapes = [
         jax.ShapeDtypeStruct((length, D), BF),
         jax.ShapeDtypeStruct((16, length), F32),
     ]
+    out_specs = [specs[0], whole_spec((16, length))]
+    scratch = []
     if pick is None:
-        found = pl.pallas_call(
-            attention_forward_kernel,
-            grid=(HEADS // 2,),
-            in_specs=[pair_spec(length)] * 3 + [whole_spec(a.shape) for a in args[3:]],
-            out_specs=[pair_spec(length), whole_spec((16, length))],
-            out_shape=shapes,
-            scratch_shapes=[
-                pltpu.VMEM((2, length, length), F32),
-                pltpu.VMEM((2, length, length), BF),
-            ],
-            compiler_params=params_of(),
-        )(*args)
-        return found[0], found[1], None
-    columns = pl.BlockSpec((length, SEEN_HEADS * HEAD_DIM), lambda i: (0, i))
-    return pl.pallas_call(
-        seen_forward_kernel,
-        grid=(HEADS // SEEN_HEADS,),
-        in_specs=[columns] * 3 + [whole_spec(a.shape) for a in args[3:]],
-        out_specs=[
-            columns,
-            whole_spec((16, length)),
-            pl.BlockSpec((SEEN_HEADS * BLOCK, BLOCK), lambda i: (i, 0)),
-        ],
-        out_shape=shapes + [jax.ShapeDtypeStruct((HEADS * BLOCK, BLOCK), BF)],
+        kernel = attention_forward_kernel
+        scratch = [pltpu.VMEM((2, length, length), F32), pltpu.VMEM((2, length, length), BF)]
+    else:
+        kernel = seen_forward_kernel
+        out_specs.append(pl.BlockSpec((SEEN_HEADS * BLOCK, BLOCK), lambda i: (i, 0)))
+        shapes.append(jax.ShapeDtypeStruct((HEADS * BLOCK, BLOCK), BF))
+    found = pl.pallas_call(
+        kernel,
+        grid=(HEADS // heads,),
+        in_specs=specs + [whole_spec(a.shape) for a in args[3:]],
+        out_specs=out_specs,
+        out_shape=shapes,
+        scratch_shapes=scratch,
         compiler_params=params_of(),
     )(*args)
+    return found[0], found[1], None if pick is None else found[2]
 
 
 def diagonal_sums(turn):
@@ -525,8 +512,7 @@
 
 def attention_backward_kernel(
     q_ref, k_ref, v_ref, up_ref, gate_ref, span_ref, fill_ref, lse_ref,
-    dq_ref, dk_ref, dv_ref, sum_ref, dgate_ref, dspan_ref,
-    prob_ref, grad_ref, turn_ref, low_ref, diag_ref,
+    out_ref, sum_ref, dgate_ref, dspan_ref, prob_ref, grad_ref, turn_ref, low_ref, diag_ref,
 ):
     step = pl.program_id(0)
     length = q_ref.shape[0]
@@ -578,9 +564,9 @@
     for side in sides:
         dspan_ref[pl.ds(step * 2 + side, 1), :] = diagonal_sums(diag_ref[side])
     grad_query = jnp.transpose(jnp.concatenate(halves, axis=0)) * HEAD_DIM ** (-0.5)
-    dq_ref[...] = grad_query.astype(BF)
-    dk_ref[...] = key_total.astype(BF)
-    dv_ref[...] = val_total.astype(BF)
+    for part, value in enumerate((grad_query, key_total, val_total)):
+        begin = pl.multiple_of(part * D + step * BLOCK, BLOCK)
+        out_ref[:, pl.ds(begin, BLOCK)] = value.astype(BF)
     sum_ref[0:1, :] = jnp.sum(grad_query, axis=0, keepdims=True)
     sum_ref[1:2, :] = jnp.sum(val_total, axis=0, keepdims=True)
 
@@ -592,7 +578,7 @@
 
 def seen_backward_kernel(
     q_ref, k_ref, v_ref, up_ref, gate_ref, fill_ref, lse_ref, pick_ref, hop_ref, flip_ref,
-    bias_ref, dq_ref, dk_ref, dv_ref, sum_ref, dgate_ref, dspan_ref, diag_ref,
+    bias_ref, out_ref, sum_ref, dgate_ref, dspan_ref, diag_ref,
 ):
     heads, pairs = range(SEEN_HEADS), range(SEEN_HEADS // 2)
     base = pl.program_id(0) * SEEN_HEADS
@@ -654,35 +640,32 @@
         grad_query = jnp.transpose(jnp.concatenate(halves[2 * pair : 2 * pair + 2], axis=0))
         grad_query = grad_query * HEAD_DIM ** (-0.5)
         val_total = val_terms[2 * pair] + val_terms[2 * pair + 1]
-        dq_ref[:, cols] = grad_query.astype(BF)
-        dk_ref[:, cols] = (key_terms[2 * pair] + key_terms[2 * pair + 1]).astype(BF)
-        dv_ref[:, cols] = val_total.astype(BF)
+        key_total = key_terms[2 * pair] + key_terms[2 * pair + 1]
+        for part, value in enumerate((grad_query, key_total, val_total)):
+            begin = pl.multiple_of(part * D + base * HEAD_DIM + pair * BLOCK, BLOCK)
+            out_ref[:, pl.ds(begin, BLOCK)] = value.astype(BF)
         sum_ref[0:1, cols] = jnp.sum(grad_query, axis=0, keepdims=True)
         sum_ref[1:2, cols] = jnp.sum(val_total, axis=0, keepdims=True)
 
 
-def attention_backward(query, keyv, value, upstream, gate, span, fill, lse, pick, bias):
-    length = query.shape[0]
+def attention_backward(qkv, upstream, gate, span, fill, lse, pick, bias):
+    length = qkv.shape[0]
     heads = 2 if pick is None else SEEN_HEADS
-    columns = pl.BlockSpec((length, heads * HEAD_DIM), lambda i: (0, i))
+    specs = head_specs(length, heads)
     shapes = [
-        jax.ShapeDtypeStruct((length, D), BF),
-        jax.ShapeDtypeStruct((length, D), BF),
-        jax.ShapeDtypeStruct((length, D), BF),
+        jax.ShapeDtypeStruct((length, 3 * D), BF),
         jax.ShapeDtypeStruct((8, D), F32),
         jax.ShapeDtypeStruct((16, length), F32),
         jax.ShapeDtypeStruct((16, SPAN), F32),
     ]
     out_specs = [
-        columns,
-        columns,
-        columns,
+        whole_spec((length, 3 * D)),
         pl.BlockSpec((8, heads * HEAD_DIM), lambda i: (0, i)),
         whole_spec((16, length)),
         whole_spec((16, SPAN)),
     ]
     if pick is None:
-        args = [query, keyv, value, upstream, gate, span, fill, lse]
+        args = [qkv, qkv, qkv, upstream, gate, span, fill, lse]
         kernel, more = attention_backward_kernel, []
         scratch = [
             pltpu.VMEM((2, length, length), F32),
@@ -694,14 +677,17 @@
     else:
         turned = jnp.transpose(pick[1])
         flip = jnp.concatenate([turned, turned], axis=1)
-        args = [query, keyv, value, upstream, gate, fill, lse, pick[0], pick[2], flip, bias]
+        args = [qkv, qkv, qkv, upstream, gate, fill, lse, pick[0], pick[2], flip, bias]
         kernel = seen_backward_kernel
         more = [pl.BlockSpec((heads * BLOCK, BLOCK), lambda i: (i, 0))]
         scratch = [pltpu.VMEM((heads, BLOCK, SPAN), F32)]
     return pl.pallas_call(
         kernel,
         grid=(HEADS // heads,),
-        in_specs=[columns] * 4 + [whole_spec(a.shape) for a in args[4 : len(args) - len(more)]] + more,
+        in_specs=specs
+        + [specs[0]]
+        + [whole_spec(a.shape) for a in args[4 : len(args) - len(more)]]
+        + more,
         out_specs=out_specs,
         out_shape=shapes,
         scratch_shapes=scratch,
@@ -750,10 +736,13 @@
     return jobs
 
 
+DEPTH = 4
+
+
 def stream_jobs(jobs, source_ref, buffer_ref, edge_ref, sems, work):
     def copies(number):
         main, edges = jobs[number][4:6]
-        slot = number % 2
+        slot = number % DEPTH
         found = []
         for shard, begin, low, count in main:
             found.append(
@@ -766,15 +755,16 @@
             for index, (source, target) in enumerate(found)
         ]
 
-    for copy in copies(0):
-        copy.start()
+    for number in range(min(DEPTH - 1, len(jobs))):
+        for copy in copies(number):
+            copy.start()
     for number, job in enumerate(jobs):
-        if number + 1 < len(jobs):
-            for copy in copies(number + 1):
+        if number + DEPTH - 1 < len(jobs):
+            for copy in copies(number + DEPTH - 1):
                 copy.start()
         for copy in copies(number):
             copy.wait()
-        slot = number % 2
+        slot = number % DEPTH
         for place, (_, low) in enumerate(job[5]):
             buffer_ref[slot, low : low + TILE, :] += edge_ref[slot, place]
         work(number, job, slot)
@@ -823,14 +813,14 @@
         out_specs=[pl.BlockSpec(memory_space=pl.ANY)] * len(specs),
         out_shape=[jax.ShapeDtypeStruct((s[1], s[2] * 128), BF) for s in specs],
         scratch_shapes=[
-            pltpu.VMEM((2, most, 128), BF),
-            pltpu.VMEM((2, edges, TILE, 128), BF),
+            pltpu.VMEM((DEPTH, most, 128), BF),
+            pltpu.VMEM((DEPTH, edges, TILE, 128), BF),
             pltpu.VMEM((most, 128), F32),
-            pltpu.SemaphoreType.DMA((2, copies)),
-            pltpu.SemaphoreType.DMA((len(kinds), 2)),
+            pltpu.SemaphoreType.DMA((DEPTH, copies)),
+            pltpu.SemaphoreType.DMA((len(kinds), DEPTH)),
         ]
         + [
-            pltpu.VMEM((2, max(s[3] for s in specs if s[2] == kind), kind * 128), BF)
+            pltpu.VMEM((DEPTH, max(s[3] for s in specs if s[2] == kind), kind * 128), BF)
             for kind in kinds
         ],
         compiler_params=pltpu.CompilerParams(vmem_limit_bytes=VMEM_LIMIT),
@@ -882,15 +872,100 @@
         out_specs=pl.BlockSpec(memory_space=pl.ANY),
         out_shape=jax.ShapeDtypeStruct((depth, width), BF),
         scratch_shapes=[
-            pltpu.VMEM((2, rows * D // 128, 128), BF),
-            pltpu.VMEM((2, edges, TILE, 128), BF),
+            pltpu.VMEM((DEPTH, rows * D // 128, 128), BF),
+            pltpu.VMEM((DEPTH, edges, TILE, 128), BF),
             pltpu.VMEM((rows * D // 128, 128), F32),
-            pltpu.VMEM((2, rows, width), BF),
-            pltpu.SemaphoreType.DMA((2, copies)),
-            pltpu.SemaphoreType.DMA((2,)),
+            pltpu.VMEM((DEPTH, rows, width), BF),
+            pltpu.SemaphoreType.DMA((DEPTH, copies)),
+            pltpu.SemaphoreType.DMA((DEPTH,)),
         ],
         compiler_params=pltpu.CompilerParams(vmem_limit_bytes=VMEM_LIMIT),
     )(jnp.full((1,), code_index, jnp.int32), windows)
+
+
+def small_kernel(
+    source_ref, patch_ref, glob_ref, vec_ref, up_ref, rest_ref, head_ref,
+    buffer_ref, edge_ref, turn_ref, head_turn_ref, sems, *, jobs, phase, lead, whole
+):
+    strips = D // 128
+
+    def columns(target_ref, begin, count, kind):
+        for strip in range(strips):
+            target_ref[:, strip * 128 : (strip + 1) * 128] = turn_ref[
+                pl.ds(begin + strip, count, stride=strips), :
+            ].astype(kind)
+
+    def work(number, job, slot):
+        turn_ref[: job[2], :] = buffer_ref[slot, : job[2], :].astype(F32)
+        if number == 0:
+            columns(patch_ref, phase, PATCH_IN, BF)
+            columns(glob_ref, phase + PATCH_IN * strips, 4, F32)
+            return
+        count = vec_ref.shape[0]
+        columns(vec_ref, 0, count, F32)
+        wide = FF // 128
+        for layer in range(LAYERS):
+            begin = (layer + 1) * (count // LAYERS) * strips - wide
+            for strip in range(wide):
+                up_ref[layer : layer + 1, strip * 128 : (strip + 1) * 128] = turn_ref[
+                    begin + strip : begin + strip + 1, :
+                ]
+        begin = count * strips
+        rest_ref[...] = turn_ref[begin : begin + rest_ref.shape[0], :]
+        begin += whole
+        rows = head_turn_ref.shape[0]
+        turned = turn_ref[begin : begin + rows, :]
+        if lead:
+            lane = lax.broadcasted_iota(jnp.int32, (1, 128), 1)
+            turned = jnp.where(
+                lane < 128 - lead,
+                pltpu.roll(turned, 128 - lead, 1),
+                pltpu.roll(turn_ref[begin + 1 : begin + 1 + rows, :], 128 - lead, 1),
+            )
+        head_turn_ref[...] = turned
+        for strip in range(PROJ // 128):
+            head_ref[:, strip * 128 : (strip + 1) * 128] = head_turn_ref[
+                pl.ds(strip, D, stride=PROJ // 128), :
+            ].astype(BF)
+
+    stream_jobs(jobs, source_ref, buffer_ref, edge_ref, sems, work)
+
+
+def unpack_small(geometry, windows):
+    where = starts()
+    tail = geometry.place("layer_vec")
+    regions = [(0, geometry.place("conv_w")), (tail, geometry.begins[-1] + geometry.window)]
+    jobs = [
+        (0, 0, high - low, 1) + geometry.pieces(low, high) for low, high in regions
+    ]
+    most = max(job[2] for job in jobs)
+    copies = max(len(job[4]) + len(job[5]) for job in jobs)
+    edges = max([1] + [len(job[5]) for job in jobs])
+    slots = LAYERS * (8 + FF // D)
+    offset = where["w_head"] - where["gate_proj"]
+    rest = -(-(-(-offset // 128)) // 8) * 8
+    return pl.pallas_call(
+        functools.partial(
+            small_kernel, jobs=jobs, phase=geometry.phase, lead=offset % 128, whole=offset // 128
+        ),
+        in_specs=[pl.BlockSpec(memory_space=pl.ANY)],
+        out_shape=[
+            jax.ShapeDtypeStruct((PATCH_IN, D), BF),
+            jax.ShapeDtypeStruct((4, D), F32),
+            jax.ShapeDtypeStruct((slots, D), F32),
+            jax.ShapeDtypeStruct((LAYERS, FF), F32),
+            jax.ShapeDtypeStruct((rest, 128), F32),
+            jax.ShapeDtypeStruct((D, PROJ), BF),
+        ],
+        scratch_shapes=[
+            pltpu.VMEM((DEPTH, most, 128), BF),
+            pltpu.VMEM((DEPTH, edges, TILE, 128), BF),
+            pltpu.VMEM((most, 128), F32),
+            pltpu.VMEM((D * PROJ // 128, 128), F32),
+            pltpu.SemaphoreType.DMA((DEPTH, copies)),
+        ],
+        compiler_params=pltpu.CompilerParams(vmem_limit_bytes=VMEM_LIMIT),
+    )(windows)
 
 
 def pack_kernel(code_ref, *refs, plans, empty):
@@ -987,6 +1062,42 @@
     return jnp.concatenate(halves, axis=0)
 
 
+def tail_kernel(*refs, lead, whole):
+    vectors = refs[:-4]
+    small_ref, head_ref, out_ref, turn_ref = refs[-4:]
+    begin = 0
+    for vector_ref in vectors:
+        if len(vector_ref.shape) == 2:
+            for row in range(2):
+                for low in range(0, D, 128):
+                    turn_ref[begin : begin + 1, :] = vector_ref[row : row + 1, low : low + 128]
+                    begin += 1
+        else:
+            for low in range(0, vector_ref.shape[0], 128):
+                turn_ref[begin : begin + 1, :] = vector_ref[low : low + 128].reshape(1, 128)
+                begin += 1
+    turn_ref[begin:, :] = jnp.zeros((turn_ref.shape[0] - begin, 128), F32)
+    turn_ref[begin : begin + small_ref.shape[0], :] = small_ref[...]
+    begin += whole
+    rows = head_ref.shape[0]
+    turned = pltpu.roll(head_ref[...], lead, 1) if lead else head_ref[...]
+    lane = lax.broadcasted_iota(jnp.int32, (1, 128), 1)
+    turn_ref[begin : begin + rows, :] += jnp.where(lane >= lead, turned, 0.0)
+    turn_ref[begin + 1 : begin + 1 + rows, :] += jnp.where(lane < lead, turned, 0.0)
+    out_ref[...] = turn_ref[...].astype(BF)
+
+
+def tail_grad(vectors, small, grad_head, rows):
+    lead, whole = small.shape[0] % 128, small.shape[0] // 128
+    small = jnp.pad(small, (0, -small.shape[0] % 128)).reshape(-1, 128)
+    return pl.pallas_call(
+        functools.partial(tail_kernel, lead=lead, whole=whole),
+        out_shape=jax.ShapeDtypeStruct((rows, 128), BF),
+        scratch_shapes=[pltpu.VMEM((rows, 128), F32)],
+        compiler_params=pltpu.CompilerParams(vmem_limit_bytes=VMEM_LIMIT),
+    )(*vectors, small, grad_head)
+
+
 def blocks_of_code(block):
     count = lax.axis_size("code")
     return [block] + [
@@ -1070,7 +1181,7 @@
 
 
 def vec_part(vector, slot_index):
-    return vector[slot_index * D : (slot_index + 1) * D]
+    return vector[slot_index : slot_index + 1]
 
 
 def gate_maps():
@@ -1117,42 +1228,46 @@
     summed = exact_dot(jnp.asarray(rows), product, ((0,), (0,)))
     summed = jnp.concatenate([summed, jnp.sum(both, axis=0, keepdims=True)], axis=0)
     grad_proj = exact_dot(summed, jnp.asarray(groups), ((1,), (1,)))
-    grad_heads = exact_dot(both, weights["gate_columns"][0], ((1,), (1,)))
+    columns_high, columns_rest = split_low(weights["gate_columns"][0])
+    grad_heads = dot_nt(
+        jnp.concatenate([high, rest, high], axis=1),
+        jnp.concatenate([columns_high, columns_high, columns_rest], axis=1),
+    )
     return (grad_heads, grad_proj, grad_scale)
 
 
 def layer_forward(hidden, fill, weights, span, pick):
-    vector = weights["layer_vec"].astype(F32)
+    vector = weights["layer_vec"]
     in_low = hidden.astype(BF)
-    qkv_proj = dot_nn(in_low, weights["w_qkv"])
-    query_low = ((qkv_proj[:, :D] + vec_part(vector, 0)) * HEAD_DIM ** (-0.5)).astype(BF)
-    key_low = qkv_proj[:, D : 2 * D].astype(BF)
-    value_low = (qkv_proj[:, 2 * D :] + vec_part(vector, 1)).astype(BF)
+    shift = jnp.concatenate(
+        [vec_part(vector, 0), jnp.zeros((1, D), F32), vec_part(vector, 1)], axis=1
+    )
+    scale = np.ones((1, 3 * D), np.float32)
+    scale[:, :D] = HEAD_DIM ** (-0.5)
+    qkv_low = ((dot_nn(in_low, weights["w_qkv"]) + shift) * scale).astype(BF)
     gate_vals, first, second = gate_forward(in_low, weights)
     gate_wide = jnp.pad(jnp.transpose(gate_vals), ((0, 16 - HEADS), (0, 0)))
-    attended, lse, bias = attention_forward(
-        query_low, key_low, value_low, gate_wide, span, fill, pick
-    )
+    attended, lse, bias = attention_forward(qkv_low, gate_wide, span, fill, pick)
     attn_out = dot_nn(attended, weights["w_out"]) + vec_part(vector, 2)
     mid_rows, normed_one, inv_one = norm_forward(
         DEEP_ALPHA * hidden + attn_out, vec_part(vector, 3), vec_part(vector, 4)
     )
     mid_low = mid_rows.astype(BF)
-    pre_act = dot_nn(mid_low, weights["w_up"]) + vector[8 * D :]
+    pre_act = dot_nn(mid_low, weights["w_up"]) + weights["up_bias"]
     act_low = gelu(pre_act).astype(BF)
     ffn_out = dot_nn(act_low, weights["w_down"]) + vec_part(vector, 5)
     final_rows, normed_two, inv_two = norm_forward(
         DEEP_ALPHA * mid_rows + ffn_out, vec_part(vector, 6), vec_part(vector, 7)
     )
-    kept = (in_low, query_low, key_low, value_low, gate_wide, first, second, lse, attended, bias)
+    kept = (in_low, qkv_low, gate_wide, first, second, lse, attended, bias)
     kept += (mid_low, pre_act, act_low, normed_one, inv_one, normed_two, inv_two)
     return (final_rows, kept)
 
 
 def layer_backward(upstream, kept, fill, weights, span, pick, grad_of):
-    in_low, query_low, key_low, value_low, gate_wide, first, second, lse, attended, bias = kept[:10]
-    mid_low, pre_act, act_low, normed_one, inv_one, normed_two, inv_two = kept[10:]
-    vector = weights["layer_vec"].astype(F32)
+    in_low, qkv_low, gate_wide, first, second, lse, attended, bias = kept[:8]
+    mid_low, pre_act, act_low, normed_one, inv_one, normed_two, inv_two = kept[8:]
+    vector = weights["layer_vec"]
     grad_res_two, grad_gain_two, grad_shift_two = norm_backward(
         upstream, normed_two, inv_two, vec_part(vector, 6)
     )
@@ -1168,28 +1283,24 @@
     out_low = grad_res_one.astype(BF)
     grad_out = grad_of("w_out", attended, out_low, 384)
     grad_att = dot_nt(out_low, weights["w_out"]).astype(BF)
-    grad_q, grad_k, grad_v, part_sums, grad_gate, grad_span = attention_backward(
-        query_low, key_low, value_low, grad_att, gate_wide, span, fill, lse, pick, bias
+    proj_low, part_sums, grad_gate, grad_span = attention_backward(
+        qkv_low, grad_att, gate_wide, span, fill, lse, pick, bias
     )
     grad_heads, grad_gate_proj, grad_gate_scale = gate_backward(
         jnp.transpose(grad_gate[:HEADS]), first, second, in_low, weights
     )
-    proj_low = jnp.concatenate([grad_q, grad_k, grad_v], axis=1)
     grad_qkv = grad_of("w_qkv", in_low, proj_low, 256)
     grad_hidden = DEEP_ALPHA * grad_res_one + dot_nt(proj_low, weights["w_qkv"]) + grad_heads
-    grad_vec = jnp.concatenate(
-        [
-            part_sums[0],
-            part_sums[1],
-            jnp.sum(grad_res_one, axis=0),
-            grad_gain_one,
-            grad_shift_one,
-            jnp.sum(grad_res_two, axis=0),
-            grad_gain_two,
-            grad_shift_two,
-            jnp.sum(grad_pre, axis=0),
-        ]
-    )
+    grad_vec = [
+        part_sums,
+        jnp.sum(grad_res_one, axis=0),
+        grad_gain_one,
+        grad_shift_one,
+        jnp.sum(grad_res_two, axis=0),
+        grad_gain_two,
+        grad_shift_two,
+        jnp.sum(grad_pre, axis=0),
+    ]
     grad_map = {
         "w_qkv": grad_qkv,
         "w_out": grad_out,
@@ -1277,20 +1388,17 @@
     windows = lax.all_gather(own_window, ("dp", "code"), axis=0, tiled=False)
     where = starts()
 
+    w_patch, glob_vec, vectors, up_bias, rest, w_head = unpack_small(geometry, windows)
+    rest = rest.reshape(-1)
+
     def values(seg_name):
         extent = dict(layout())[seg_name]
-        begin, amount = where[seg_name], math.prod(extent)
-        low, high = begin // 128, -(-(begin + amount) // 128)
-        found = geometry.exact(windows, low, high).reshape(-1)
-        return found[begin - low * 128 : begin - low * 128 + amount].reshape(extent)
-
-    w_patch = values("w_patch")
-    glob_vec = values("glob_vec").astype(F32)
+        begin = where[seg_name] - where["gate_proj"]
+        return rest[begin : begin + math.prod(extent)].reshape(extent)
+
     gate_proj = values("gate_proj")
     gate_scale = values("gate_scale")
-    rel_table = values("rel_table")
-    w_head = values("w_head")
-    layer_vec = values("layer_vec")
+    rel_table = values("rel_table").astype(BF)
     conv_weight = unpack_conv(geometry, windows, code_index)
     weights = []
     for index in range(LAYERS):
@@ -1307,7 +1415,8 @@
         weights.append(
             dict(zip(("w_qkv", "w_out", "w_up", "w_down"), mats))
             | {
-                "layer_vec": layer_vec[index],
+                "layer_vec": vectors[index * (8 + FF // D) :],
+                "up_bias": up_bias[index : index + 1],
                 "gate_columns": gate_columns(gate_proj[index]),
                 "gate_scale": gate_scale[index],
             }
@@ -1344,7 +1453,7 @@
     ).reshape(1, -1)
     patch_rows = jnp.pad(patches[0], ((0, ROWS - LONG), (0, 0)))
     embedded = dot_nn(patch_rows, w_patch)
-    normed_rows, normed_zero, inv_zero = norm_forward(embedded, glob_vec[0], glob_vec[1])
+    normed_rows, normed_zero, inv_zero = norm_forward(embedded, glob_vec[0 : 1], glob_vec[1 : 2])
     start_rows = normed_rows * live_float
     conv_in = start_rows.astype(BF)
     width = D // code_count
@@ -1356,7 +1465,7 @@
         pick_full, conv_own, (((1,), (0,)), ((), ())), precision=HIGHEST
     )
     seen_raw = side_by_side(seen_own, code_index)
-    seen_pre = seen_raw + glob_vec[2]
+    seen_pre = seen_raw + glob_vec[2 : 3]
     seen_start = lax.dot_general(
         pick_full, start_rows, (((1,), (0,)), ((), ())), precision=HIGHEST
     )
@@ -1365,7 +1474,7 @@
     placed = lax.dot_general(
         pick_full, encoded, (((0,), (0,)), ((), ())), precision=HIGHEST
     )
-    hidden = jnp.where(visible[:, None], placed, glob_vec[3])
+    hidden = jnp.where(visible[:, None], placed, glob_vec[3 : 4])
     final, kept_second = layer_forward(hidden, live_fill, weights[1], span, None)
     target_codes = jnp.where(mask_row == 1, jnp.pad(targets[0], (0, ROWS - LONG)), -1)
     loss_local, upstream, grad_head = head_pass(final, w_head, all_codes, code_names, target_codes)
@@ -1399,7 +1508,7 @@
     rest_grad = conv_weight_grad(padded, grads, geometry, code_index, range(split, dp_count))
     grad_start = (grad_full + grad_conv_in.astype(F32)) * live_float
     grad_embedded, grad_gain_zero, grad_shift_zero = norm_backward(
-        grad_start, normed_zero, inv_zero, glob_vec[0]
+        grad_start, normed_zero, inv_zero, glob_vec[0 : 1]
     )
     grad_patch = dot_tn(patch_rows, grad_embedded.astype(BF))
     grad_glob = jnp.stack(
@@ -1435,23 +1544,11 @@
             add_source(layer_map[seg_name])
     add_source(rest_grad)
     tail_place = geometry.place("layer_vec")
-    vec_rows = jnp.concatenate(
-        [layer_map["layer_vec"].reshape(-1, 128) for layer_map in both], axis=0
-    )
+    vectors = [vector for layer_map in both for vector in layer_map["layer_vec"]]
     small = [layer_map[seg_name] for seg_name in ("gate_proj", "gate_scale") for layer_map in both]
     small = jnp.concatenate([part.reshape(-1) for part in small + [grad_rel]])
-    lead = small.shape[0] % 128
-    small_rows = jnp.pad(small, (0, -small.shape[0] % 128)).reshape(-1, 128)
-    head_rows = jnp.pad(grad_head, ((1, 1), (0, 0)))
-    head_rows = jnp.concatenate(
-        [head_rows[:-1, 128 - lead :], head_rows[1:, : 128 - lead]], axis=1
-    )
-    whole = small.shape[0] // 128
-    tail = jnp.concatenate(
-        [vec_rows, small_rows[:whole], small_rows[whole:] + head_rows[:1], head_rows[1:]], axis=0
-    ).astype(BF)
     tail_rows = geometry.begins[-1] + geometry.window - tail_place
-    tail = jnp.pad(tail, ((0, tail_rows - tail.shape[0]), (0, 0)))
+    tail = tail_grad(vectors, small, grad_head, tail_rows)
     for items in spans:
         items.append((tail_place, tail_rows, len(sources), 0))
     sources.append(tail)

time: 690 us -> 660 us (0.957)
  local copies, waits for them, and re-layouts: 56.4 us -> 41 us
  other arithmetic: 57.5 us -> 47.7 us
    pallas_call x2, Pallas kernels: 30.5 us -> 22.2 us  [unpack(): pl.pallas_call(functools.partial(unpack_kernel, jobs=jobs, stages=stages)...]
    convert_element_type x7 -> x0, other arithmetic: 7.62 us -> none  [the longest x2 2.52 us: gate_backward(): rest = (both - high.astype(F32)).astype(BF)]
    unnamed x324 -> x222, local copies, waits for them, and re-layouts: 13.5 us -> 6.21 us
    dot_general x8 -> x10, matrix products: 23 us -> 30.2 us  [dot_nt(): lax.dot_general(left, right, (((1,), (1,)), ((), ())), preferred_element_...]
    pallas_call x4 -> x6, Pallas kernels: 38.3 us -> 44.4 us  [the longest x2 25.1 us: attention_backward(): pl.pallas_call(kernel, grid=(HEADS // heads,), in_specs=specs + [specs[0]...]
  transfers between devices with their start and end apart: 22 -> 22, of which waited for: 10 -> 11; matrix products, arithmetic and copies ran while one was open for 6% -> 6% of each run, Pallas kernels for 10% -> 9%
where the time goes in v4:
time: 660 us; the launch traced here: 650 us
  waiting for transfers between devices  246 us (37%)
  Pallas kernels  183 us (28%)
  matrix products  76.8 us (12%)
  other arithmetic  47.7 us (7%)
  local copies, waits for them, and re-layouts  41 us (6%)
  starting transfers between devices  31.5 us (5%)
  between operations  24.5 us (4%)
    all_gather x1, waiting for transfers between devices, local(): windows = lax.all_gather(own_window, ('dp', 'code'), axis=0, tiled=False)  202 us
    pallas_call x8, Pallas kernels, weight_grad(): pl.pallas_call(weight_grad_kernel, grid_spec=pltpu.PrefetchScalarGridSpec...  37.7 us
    ppermute x4, waiting for transfers between devices, reduce_front(): lax.ppermute(halves[side], 'dp', [(i, i - bit) for i in range(dp_count) i...  31.5 us
    dot_general x10, matrix products, dot_nt(): lax.dot_general(left, right, (((1,), (1,)), ((), ())), preferred_element_...  30.2 us
    dot_general x11, matrix products, dot_nn(): lax.dot_general(left, right, (((1,), (0,)), ((), ())), preferred_element_...  28.1 us
    pallas_call x2, Pallas kernels, conv_call(): pl.pallas_call(kernel, grid=(steps,), in_specs=[pl.BlockSpec(padded.shape...  25.2 us
    pallas_call x2, Pallas kernels, attention_backward(): pl.pallas_call(kernel, grid=(HEADS // heads,), in_specs=specs + [specs[0]...  25.1 us
    pallas_call x2, Pallas kernels, conv_weight_grad(): pl.pallas_call(conv_weight_kernel, grid_spec=pltpu.PrefetchScalarGridSpec...  24.8 us
  transfers between devices with their start and end apart: 22, of which 11 were waited for; matrix products, arithmetic and copies ran while one was open for 6% of the time, Pallas kernels for 9%

profile of v4, /device:TPU:0, one launch (start us, length us, event | category | flops | bytes accessed | tf_op | source)
XLA Modules:
  0.0 650.0 jit_solution(17912840050097315360)
XLA Ops:
  7.4 5.9 dynamic_update_slice.3
  14.4 4.1 collective-permute-start.4
  20.1 2.3 collective-permute-start.5
  37.6 201.6 %all-gather.3.cloned.1.call-done = bf16[151552,128]{1,0:T(8,128)(2,1)} async-done(((bf16[4736,128]{1,0:T(8,128)(2,1)}), bf16[151552,128]{1,0:T(8,128)(2,1)}) %all-gather.3.cloned.1.call-update) | async-done | bytes 38797328 | tf_op jit(solution)/shard_map/all_gather | solution.py:1388
  239.2 2.6 shard_map.414
  251.1 5.7 shard_map.415.weight_ref
  256.8 12.1 %shard_map.416 = f32[512,192]{1,0:T(8,128)} custom-call(f32[640,192]{1,0:T(8,128)} %pad_convert_fusion.2.in_ref, bf16[6144,192]{1,0:T(8,128)(2,1)} %shard_map.415.weight_ref, bf16[4,192]{1,0:T(4,128)(2,1)} %constant.310.clone.mask_ref), custom_call_target="tpu_custom_call" | custom-call | tf_op jit(solution)/shard_map/pallas_call | solution.py:232
  268.9 2.1 fusion.54.refs_0_
  272.9 3.6 collective-permute-start.2
  276.5 11.0 %shard_map.420 = (bf16[768,2304]{1,0:T(8,128)(2,1)}, bf16[768,768]{1,0:T(8,128)(2,1)}, bf16[768,3072]{1,0:T(8,128)(2,1)}, bf16[3072,768]{1,0:T(8,128)(2,1)}) custom-call(bf16[32,4736,128]{2,1,0:T(8,128)(2,1)} %bitcast.167), custom_call_target="tpu_custom_call" | custom-call | tf_op jit(solution)/shard_map/pallas_call | solution.py:810
  287.6 11.2 %shard_map.418 = (bf16[768,2304]{1,0:T(8,128)(2,1)}, bf16[768,768]{1,0:T(8,128)(2,1)}, bf16[768,3072]{1,0:T(8,128)(2,1)}, bf16[3072,768]{1,0:T(8,128)(2,1)}) custom-call(bf16[32,4736,128]{2,1,0:T(8,128)(2,1)} %bitcast.168), custom_call_target="tpu_custom_call" | custom-call | tf_op jit(solution)/shard_map/pallas_call | solution.py:810
  306.0 1.8 copy.80
  307.8 2.0 fusion.92.span_ref
  311.9 2.0 shard_map.417
  314.0 2.3 fusion.197
  317.3 3.6 fusion.8.q_ref.k_ref.v_ref
  321.6 4.6 shard_map.419
  327.9 2.3 multiply_convert_fusion.2
  330.3 3.5 fusion.199
  336.4 3.4 fusion.6.q_ref.k_ref.v_ref
  340.7 9.7 %shard_map.421 = (bf16[512,768]{1,0:T(8,128)(2,1)}, f32[16,512]{1,0:T(8,128)}) custom-call(bf16[512,2304]{1,0:T(8,128)(2,1)} %fusion.6.q_ref.k_ref.v_ref, bf16[512,2304]{1,0:T(8,128)(2,1)} %fusion.6.q_ref.k_ref.v_ref, bf16[512,2304]{1,0:T(8,128)(2,1)} %fusion.6.q_ref.k_ref.v_ref, f32[16,512]{1,0:T(8,128)} %pad.61.gate_ref, f32[16,1024]{1,0:T(8,128)} %fusion.92.span_ref, ...), custom_call_target="tpu_custom_call" | custom-call | tf_op jit(solution)/shard_map/pallas_call | solution.py:493
  350.4 2.4 fusion.201
  353.8 6.8 %multiply_convert_fusion = (bf16[512,3072]{1,0:T(8,128)(2,1)S(1)}, f32[512,3072]{1,0:T(8,128)}) fusion(f32[3072]{0:T(1024)S(1)} %bitcast.191, bf16[512,768]{1,0:T(8,128)(2,1)S(1)} %fusion.17.left_ref, bf16[768,3072]{1,0:T(8,128)(2,1)} %get-tuple-element.52), kind=kOutput, calls=%fused_computation.6 | convolution fusion | flops 2425356288 | bytes 14954496 | tf_op jit(solution)/shard_map/dot_general | solution.py:144
  360.7 2.8 fusion.202
  366.8 7.9 %shard_map.422 = (f32[8,128]{1,0:T(8,128)}, f32[512,768]{1,0:T(8,128)}, f32[1536,128]{1,0:T(8,128)}) custom-call(bf16[512,768]{1,0:T(8,128)(2,1)} %add_convert_fusion.1.in_ref, bf16[768,256]{1,0:T(8,128)(2,1)} %get-tuple-element.54.weight_ref, bf16[1024,256]{1,0:T(8,128)(2,1)} %pad_maximum_fusion.code_ref, s32[8,1024]{1,0:T(8,128)} %broadcast_in_dim.77.name_ref, ...), custom_call_target="tpu_custom_call" | custom-call | tf_op jit(solution)/shard_map/pallas_call | solution.py:1353
  374.7 2.8 multiply_reduce_fusion
  378.7 8.4 %fusion.191 = (f32[3072]{0:T(1024)}, bf16[512,3072]{1,0:T(8,128)(2,1)S(1)}) fusion(f32[512,3072]{1,0:T(8,128)} %get-tuple-element.198, f32[3072]{0:T(1024)S(1)} %bitcast.192, bf16[512,768]{1,0:T(8,128)(2,1)S(1)} %convert_element_type.257.right_ref, bf16[3072,768]{1,0:T(8,128)(2,1)} %get-tuple-element.53), kind=kOutput, calls=%fused_computation.381 | convolution fusion | flops 2434790400 | bytes 14966784 | tf_op jit(solution)/shard_map/dot_general | solution.py:148
  387.2 3.7 multiply_reduce_fusion.1
  393.2 1.7 convolution_convert_fusion.up_ref
  395.0 18.0 %shard_map.423 = (bf16[512,2304]{1,0:T(8,128)(2,1)}, f32[8,768]{1,0:T(8,128)}, f32[16,512]{1,0:T(8,128)}, f32[16,1024]{1,0:T(8,128)}) custom-call(bf16[512,2304]{1,0:T(8,128)(2,1)} %fusion.6.q_ref.k_ref.v_ref, bf16[512,2304]{1,0:T(8,128)(2,1)} %fusion.6.q_ref.k_ref.v_ref, bf16[512,2304]{1,0:T(8,128)(2,1)} %fusion.6.q_ref.k_ref.v_ref, ...), custom_call_target="tpu_custom_call" | custom-call | tf_op jit(solution)/shard_map/pallas_call | solution.py:684
  414.5 4.7 fusion.203
  423.0 2.3 fusion.192
  425.4 2.4 multiply_reduce_fusion.13
  430.5 7.2 %shard_map.424 = (bf16[128,2304]{1,0:T(8,128)(2,1)}, f32[8,768]{1,0:T(8,128)}, f32[16,128]{1,0:T(8,128)}, f32[16,1024]{1,0:T(8,128)}) custom-call(bf16[128,2304]{1,0:T(8,128)(2,1)} %fusion.8.q_ref.k_ref.v_ref, bf16[128,2304]{1,0:T(8,128)(2,1)} %fusion.8.q_ref.k_ref.v_ref, bf16[128,2304]{1,0:T(8,128)(2,1)} %fusion.8.q_ref.k_ref.v_ref, ...), custom_call_target="tpu_custom_call" | custom-call | tf_op jit(solution)/shard_map/pallas_call | solution.py:684
  438.7 6.4 shard_map.434.refs_5_
  445.1 5.0 shard_map.433.refs_4_
  450.1 5.2 shard_map.436.refs_7_
  455.3 4.0 shard_map.432.refs_3_
  459.4 5.4 shard_map.430.refs_1_
  465.6 4.1 convolution_add_fusion.5
  470.8 2.4 broadcast_multiply_fusion
  474.1 3.4 shard_map.431.refs_2_
  480.7 4.3 shard_map.435.refs_6_
  485.0 3.9 shard_map.429.refs_0_
  489.0 5.8 shard_map.437.refs_8_
  494.7 2.4 shard_map.438.refs_9_
  497.2 7.3 %shard_map.439 = bf16[8,4736,128]{2,1,0:T(8,128)(2,1)} custom-call(s32[1]{0:T(128)} %bitcast.code_ref, bf16[9216,128]{1,0:T(8,128)(2,1)} %shard_map.429.refs_0_, bf16[9216,128]{1,0:T(8,128)(2,1)} %shard_map.430.refs_1_, bf16[4608,128]{1,0:T(8,128)(2,1)} %shard_map.431.refs_2_, bf16[4608,128]{1,0:T(8,128)(2,1)} %shard_map.432.refs_3_, ...), custom_call_target="tpu_custom_call" | custom-call | tf_op jit(solution)/shard_map/pallas_call | solution.py:1014
  514.1 2.1 collective-permute-done.11
  517.1 13.1 %shard_map.426 = f32[512,192]{1,0:T(8,128)} custom-call(f32[640,192]{1,0:T(8,128)} %pad_convert_fusion.1.in_ref, bf16[6144,192]{1,0:T(8,128)(2,1)} %shard_map.415.weight_ref, bf16[4,192]{1,0:T(4,128)(2,1)} %constant.310.clone.mask_ref), custom_call_target="tpu_custom_call" | custom-call | tf_op jit(solution)/shard_map/pallas_call | solution.py:232
  531.3 1.6 collective-permute-start.8
  532.8 1.8 collective-permute-start.7
  534.7 1.6 collective-permute-start.13
  537.2 19.0 %shard_map.425.refs_0_ = bf16[10368,128]{1,0:T(8,128)(2,1)} custom-call(s32[6]{0:T(128)} %fusion.164.tap_ref, f32[4,192,640]{2,1,0:T(8,128)} %bitcast.174, bf16[4,512,192]{2,1,0:T(8,128)(2,1)} %bitcast.177, f32[4,192]{1,0:T(4,128)} %constant.319.clone.mask_ref), custom_call_target="tpu_custom_call" | custom-call | tf_op jit(solution)/shard_map/pallas_call | solution.py:329
  557.8 2.3 shard_map.427
  560.1 2.1 multiply_reduce_fusion.3
  564.3 3.1 shard_map.428
  568.9 2.9 collective-permute-done.14
  571.7 1.6 add_convert_fusion
  576.0 15.1 %collective-permute-done.15 = bf16[2368,128]{1,0:T(8,128)(2,1)S(1)} collective-permute-done((bf16[2368,128]{1,0:T(8,128)(2,1)S(1)}, bf16[2368,128]{1,0:T(8,128)(2,1)S(1)}, u32[]{:S(2)}, u32[]{:S(2)}) %collective-permute-start.15) | collective-permute-done | bytes 606240 | tf_op jit(solution)/shard_map/ppermute | solution.py:1058
  595.6 14.0 %collective-permute-done.16 = bf16[2368,128]{1,0:T(8,128)(2,1)S(1)} collective-permute-done((bf16[2368,128]{1,0:T(8,128)(2,1)S(1)}, bf16[2368,128]{1,0:T(8,128)(2,1)S(1)}, u32[]{:S(2)}, u32[]{:S(2)}) %collective-permute-start.16) | collective-permute-done | bytes 606240 | tf_op jit(solution)/shard_map/ppermute | solution.py:1058
  611.0 4.5 fusion.9
  616.9 4.7 all-to-all-start
  624.8 5.2 all-to-all-done
  633.5 7.0 %fusion.181 = (bf16[603008]{0:T(1024)(128)(2,1)}, f32[603008]{0:T(1024)}, f32[603008]{0:T(1024)}, f32[603008]{0:T(1024)}) fusion(f32[603008]{0:T(1024)} %param.44, f32[]{:T(128)} %bitcast.43, f32[]{:T(128)} %bitcast.42, f32[]{:T(128)S(6)} %min.7, f32[]{:T(128)} %bitcast.39, bf16[4711,128]{1,0:T(8,128)(2,1)S(1)} %get-tuple-element.135, f32[603008]{0:T(1024)} %param.46, ...), kind=kLoop, calls=%fused_computation.375 | loop fusion | flops 11457152 | bytes 16884240 | tf_op jit(solution)/shard_map/convert_element_type | solution.py:1595
  (422 shorter events, 95.8 us)
Async XLA Ops:
  7.2 232.0 %all-gather.3.cloned.1.call-start = ((), (), s32[]{:S(2)}) async-start(), calls=%async_computation.3 | async-start | bytes 40009728 | tf_op jit(solution)/shard_map/all_gather | solution.py:1388
  7.3 7.1 %copy-start.37 = (bf16[256,256]{1,0:T(8,128)(2,1)S(1)}, bf16[256,256]{1,0:T(8,128)(2,1)}, u32[]{:S(2)}) copy-start(bf16[256,256]{1,0:T(8,128)(2,1)} %param.43) | copy-start | bytes 393220
  7.3 15.7 %copy-start.83 = (s32[1,496]{1,0:T(1,128)S(1)}, s32[1,496]{1,0:T(1,128)}, u32[]{:S(2)}) copy-start(s32[1,496]{1,0:T(1,128)} %param.41) | copy-start | bytes 5956
  7.3 21.8 %copy-start.95 = (s32[1,496]{1,0:T(1,128)S(1)}, s32[1,496]{1,0:T(1,128)}, u32[]{:S(2)}) copy-start(s32[1,496]{1,0:T(1,128)} %param.42) | copy-start | bytes 5956
  14.3 596.7 %reduce-scatter.2.cloned.1.call-start = ((), (), s32[]{:S(2)}) async-start(), calls=%async_computation.2 | async-start | bytes 10911744 | tf_op jit(solution)/shard_map/reduce_scatter | solution.py:1559
  14.4 22.3 %collective-permute-start.4 = (bf16[256,256]{1,0:T(8,128)(2,1)S(1)}, bf16[256,256]{1,0:T(8,128)(2,1)S(1)}, u32[]{:S(2)}, u32[]{:S(2)}) collective-permute-start(bf16[256,256]{1,0:T(8,128)(2,1)S(1)} %copy-done.37), channel_id=1, source_target_pairs={{0,2},{1,3},{2,0},{3,1},{4,6},{5,7},{6,4},{7,5},{8,10},{9,11},{10,... | collective-permute-start | bytes 393224 | tf_op jit(solution)/shard_map/ppermute | solution.py:1104
  18.5 18.2 %collective-permute-start.3 = (bf16[256,256]{1,0:T(8,128)(2,1)S(1)}, bf16[256,256]{1,0:T(8,128)(2,1)S(1)}, u32[]{:S(2)}, u32[]{:S(2)}) collective-permute-start(bf16[256,256]{1,0:T(8,128)(2,1)S(1)} %copy-done.37), channel_id=1, source_target_pairs={{0,1},{1,2},{2,3},{3,0},{4,5},{5,6},{6,7},{7,4},{8,9},{9,10},{10,1... | collective-permute-start | bytes 393224 | tf_op jit(solution)/shard_map/ppermute | solution.py:1104
  20.1 16.6 %collective-permute-start.5 = (bf16[256,256]{1,0:T(8,128)(2,1)S(1)}, bf16[256,256]{1,0:T(8,128)(2,1)S(1)}, u32[]{:S(2)}, u32[]{:S(2)}) collective-permute-start(bf16[256,256]{1,0:T(8,128)(2,1)S(1)} %copy-done.37), channel_id=1, source_target_pairs={{0,3},{1,0},{2,1},{3,2},{4,7},{5,4},{6,5},{7,6},{8,11},{9,8},{10,9... | collective-permute-start | bytes 393224 | tf_op jit(solution)/shard_map/ppermute | solution.py:1104
  23.0 245.9 %copy-start.53 = (pred[512]{0:T(512)(128)(4,1)}, pred[512]{0:T(512)(128)(4,1)S(1)}, u32[]{:S(2)}) copy-start(pred[512]{0:T(512)(128)(4,1)S(1)} %get-tuple-element.154) | copy-start | bytes 1540
  28.5 220.2 %copy-start.65 = (f32[512]{0:T(512)}, f32[512]{0:T(512)S(1)}, u32[]{:S(2)}) copy-start(f32[512]{0:T(512)S(1)} %fusion.161) | copy-start | bytes 6148
  30.7 211.1 %copy-start.31 = (bf16[128,128]{1,0:T(8,128)(2,1)}, bf16[128,128]{1,0:T(8,128)(2,1)S(1)}, u32[]{:S(2)}) copy-start(bf16[128,128]{1,0:T(8,128)(2,1)S(1)} %fusion.69.near_ref) | copy-start | bytes 98308
  30.8 238.1 %copy-start.38 = (s32[512]{0:T(512)}, s32[512]{0:T(512)S(1)}, u32[]{:S(2)}) copy-start(s32[512]{0:T(512)S(1)} %fusion.256) | copy-start | bytes 6148
  239.2 7.7 %copy-start.22 = (bf16[1,496,256]{2,1,0:T(8,128)(2,1)S(1)}, bf16[1,496,256]{2,1,0:T(8,128)(2,1)}, u32[]{:S(2)}) copy-start(bf16[1,496,256]{2,1,0:T(8,128)(2,1)} %param.39) | copy-start | bytes 761860
  271.0 40.9 %collective-permute-start.1 = (f32[128,192]{1,0:T(8,128)}, f32[128,192]{1,0:T(8,128)}, u32[]{:S(2)}, u32[]{:S(2)}) collective-permute-start(f32[128,192]{1,0:T(8,128)} %fusion.54.refs_0_), channel_id=1, source_target_pairs={{0,2},{1,3},{2,0},{3,1},{4,6},{5,7},{6,4},{7,5},{8,10},{9,11},{10,... | collective-permute-start | bytes 294920 | tf_op jit(solution)/shard_map/ppermute | solution.py:1104
  272.5 39.4 %collective-permute-start = (f32[128,192]{1,0:T(8,128)}, f32[128,192]{1,0:T(8,128)}, u32[]{:S(2)}, u32[]{:S(2)}) collective-permute-start(f32[128,192]{1,0:T(8,128)} %fusion.54.refs_0_), channel_id=1, source_target_pairs={{0,1},{1,2},{2,3},{3,0},{4,5},{5,6},{6,7},{7,4},{8,9},{9,10},{10,1... | collective-permute-start | bytes 294920 | tf_op jit(solution)/shard_map/ppermute | solution.py:1104
  272.9 39.0 %collective-permute-start.2 = (f32[128,192]{1,0:T(8,128)}, f32[128,192]{1,0:T(8,128)}, u32[]{:S(2)}, u32[]{:S(2)}) collective-permute-start(f32[128,192]{1,0:T(8,128)} %fusion.54.refs_0_), channel_id=1, source_target_pairs={{0,3},{1,0},{2,1},{3,2},{4,7},{5,4},{6,5},{7,6},{8,11},{9,8},{10,9... | collective-permute-start | bytes 294920 | tf_op jit(solution)/shard_map/ppermute | solution.py:1104
  287.5 11.2 %copy-start.64 = (f32[2,3072]{1,0:T(2,128)S(1)}, f32[2,3072]{1,0:T(2,128)}, u32[]{:S(2)}) copy-start(f32[2,3072]{1,0:T(2,128)} %get-tuple-element.47) | copy-start | bytes 73732
  287.5 11.8 %copy-start.63 = (f32[24,768]{1,0:T(8,128)S(1)}, f32[24,768]{1,0:T(8,128)}, u32[]{:S(2)}) copy-start(f32[24,768]{1,0:T(8,128)} %get-tuple-element.42) | copy-start | bytes 221188
  287.5 14.6 %copy-start.3 = (f32[768,64]{1,0:T(8,128)S(1)}, f32[768,64]{1,0:T(8,128)}, u32[]{:S(2)}) copy-start(f32[768,64]{1,0:T(8,128)} %constant.307.clone) | copy-start | bytes 589828
  287.6 14.6 %copy-start.19 = (f32[768,24]{0,1:T(8,128)S(1)}, f32[768,24]{0,1:T(8,128)}, u32[]{:S(2)}) copy-start(f32[768,24]{0,1:T(8,128)} %constant.308.clone) | copy-start | bytes 221188
  307.8 6.1 copy-start.39
  307.8 6.1 copy-start.44
  307.8 6.1 copy-start.51
  307.8 6.2 copy-start.54
  307.8 6.2 copy-start.61
  307.8 6.2 copy-start.66
  307.8 6.2 copy-start.74
  307.8 6.2 copy-start.90
  314.0 13.9 %slice-start = ((s8[4718592]{0:T(1024)(128)(4,1)}), s8[4194304]{0:T(1024)(128)(4,1)S(1)}, s32[]{:S(2)}) async-start(s8[4718592]{0:T(1024)(128)(4,1)} %bitcast.169), calls=%async_computation.4 | async-start | bytes 8388608
  317.3 10.6 %slice-start.1 = ((s8[4718592]{0:T(1024)(128)(4,1)}), s8[524288]{0:T(1024)(128)(4,1)S(1)}, s32[]{:S(2)}) async-start(s8[4718592]{0:T(1024)(128)(4,1)} %bitcast.169), calls=%async_computation.5 | async-start | bytes 1048576
  327.5 97.9 %copy-start.76 = (f32[128]{0:T(128)}, f32[128]{0:T(128)S(1)}, u32[]{:S(2)}) copy-start(f32[128]{0:T(128)S(1)} %broadcast_multiply_fusion.15) | copy-start | bytes 1540
  327.7 97.7 %copy-start.84 = (f32[128]{0:T(128)}, f32[128]{0:T(128)S(1)}, u32[]{:S(2)}) copy-start(f32[128]{0:T(128)S(1)} %add_rsqrt_fusion.4) | copy-start | bytes 1540
  335.1 84.2 %copy-start = (bf16[512,768]{1,0:T(8,128)(2,1)}, bf16[512,768]{1,0:T(8,128)(2,1)S(1)}, u32[]{:S(2)}) copy-start(bf16[512,768]{1,0:T(8,128)(2,1)S(1)} %get-tuple-element.193.left_ref) | copy-start | bytes 2359300
  340.7 9.7 %copy-start.89 = (f32[768]{0:T(1024)S(1)}, f32[768]{0:T(1024)}, u32[]{:S(2)}) copy-start(f32[768]{0:T(1024)} %get-tuple-element.117) | copy-start | bytes 9220
  353.4 7.2 %slice-start.8 = ((s8[4718592]{0:T(1024)(128)(4,1)}), s8[4194304]{0:T(1024)(128)(4,1)S(1)}, s32[]{:S(2)}) async-start(s8[4718592]{0:T(1024)(128)(4,1)} %bitcast.200), calls=%async_computation.12 | async-start | bytes 8388608
  353.8 6.9 %copy-start.9 = (bf16[512,768]{1,0:T(8,128)(2,1)}, bf16[512,768]{1,0:T(8,128)(2,1)S(1)}, u32[]{:S(2)}) copy-start(bf16[512,768]{1,0:T(8,128)(2,1)S(1)} %fusion.17.left_ref) | copy-start | bytes 2359300
  353.8 6.8 %copy-start.88 = (f32[768]{0:T(1024)S(1)}, f32[768]{0:T(1024)}, u32[]{:S(2)}) copy-start(f32[768]{0:T(1024)} %get-tuple-element.114) | copy-start | bytes 9220
  353.8 6.8 %slice-start.9 = ((s8[4718592]{0:T(1024)(128)(4,1)}), s8[524288]{0:T(1024)(128)(4,1)S(1)}, s32[]{:S(2)}) async-start(s8[4718592]{0:T(1024)(128)(4,1)} %bitcast.200), calls=%async_computation.13 | async-start | bytes 1048576
  378.6 8.5 %slice-start.6 = ((s8[4718592]{0:T(1024)(128)(4,1)}), s8[4194304]{0:T(1024)(128)(4,1)S(1)}, s32[]{:S(2)}) async-start(s8[4718592]{0:T(1024)(128)(4,1)} %bitcast.198), calls=%async_computation.10 | async-start | bytes 8388608
  378.7 8.4 %copy-start.10 = (bf16[512,768]{1,0:T(8,128)(2,1)}, bf16[512,768]{1,0:T(8,128)(2,1)S(1)}, u32[]{:S(2)}) copy-start(bf16[512,768]{1,0:T(8,128)(2,1)S(1)} %convert_element_type.257.right_ref) | copy-start | bytes 2359300
  378.7 8.4 %slice-start.7 = ((s8[4718592]{0:T(1024)(128)(4,1)}), s8[524288]{0:T(1024)(128)(4,1)S(1)}, s32[]{:S(2)}) async-start(s8[4718592]{0:T(1024)(128)(4,1)} %bitcast.198), calls=%async_computation.11 | async-start | bytes 1048576
  430.5 7.2 %copy-start.87 = (f32[12]{0:T(128)S(1)}, f32[12]{0:T(128)}, u32[]{:S(2)}) copy-start(f32[12]{0:T(128)} %get-tuple-element.178) | copy-start | bytes 148
  459.4 6.2 copy-start.15
  470.7 6.9 %copy-start.26 = (f32[128,768]{1,0:T(8,128)S(1)}, f32[128,768]{1,0:T(8,128)}, u32[]{:S(2)}) copy-start(f32[128,768]{1,0:T(8,128)} %convolution_add_fusion.5) | copy-start | bytes 1179652
  470.7 6.9 %copy-start.27 = (f32[128,768]{1,0:T(8,128)S(1)}, f32[128,768]{1,0:T(8,128)}, u32[]{:S(2)}) copy-start(f32[128,768]{1,0:T(8,128)} %shard_map.417) | copy-start | bytes 1179652
  470.7 6.8 %copy-start.36 = (bf16[768,24]{0,1:T(8,128)(2,1)S(1)}, bf16[768,24]{0,1:T(8,128)(2,1)}, u32[]{:S(2)}) copy-start(bf16[768,24]{0,1:T(8,128)(2,1)} %get-tuple-element.152) | copy-start | bytes 110596
  470.7 6.8 %copy-start.91 = (f32[768]{0:T(1024)S(1)}, f32[768]{0:T(1024)}, u32[]{:S(2)}) copy-start(f32[768]{0:T(1024)} %get-tuple-element.127) | copy-start | bytes 9220
  470.8 6.8 %copy-start.99 = (f32[128]{0:T(128)S(1)}, f32[128]{0:T(128)}, u32[]{:S(2)}) copy-start(f32[128]{0:T(128)} %compare_convert_fusion) | copy-start | bytes 1540
  507.4 1.2 collective-permute-start.9
  508.7 3.7 collective-permute-start.10
  512.4 3.7 collective-permute-start.11
  516.2 18.5 %collective-permute-start.12 = (f32[32,128]{1,0:T(8,128)S(1)}, f32[32,128]{1,0:T(8,128)S(1)}, u32[]{:S(2)}, u32[]{:S(2)}) collective-permute-start(f32[32,128]{1,0:T(8,128)S(1)} %add.551), channel_id=1, source_target_pairs={{0,1},{1,0},{2,3},{3,2},{4,5},{5,4},{6,7},{7,6},{8,9},{9,8},{10,11... | collective-permute-start | bytes 49160 | tf_op jit(solution)/shard_map/ppermute | solution.py:1140
  517.1 19.3 %copy-start.25 = (f32[128,768]{1,0:T(8,128)S(1)}, f32[128,768]{1,0:T(8,128)}, u32[]{:S(2)}) copy-start(f32[128,768]{1,0:T(8,128)} %get-tuple-element.208) | copy-start | bytes 1179652
  531.3 25.0 %copy-start.21 = (bf16[512,192]{1,0:T(8,128)(2,1)}, bf16[512,192]{1,0:T(8,128)(2,1)S(1)}, u32[]{:S(2)}) copy-start(bf16[512,192]{1,0:T(8,128)(2,1)S(1)} %convert_element_type.274.refs_0_) | copy-start | bytes 589828
  531.3 25.1 %collective-permute-start.8 = (bf16[512,192]{1,0:T(8,128)(2,1)S(1)}, bf16[512,192]{1,0:T(8,128)(2,1)S(1)}, u32[]{:S(2)}, u32[]{:S(2)}) collective-permute-start(bf16[512,192]{1,0:T(8,128)(2,1)S(1)} %convert_element_type.274.refs_0_), channel_id=1, source_target_pairs={{0,3},{1,0},{2,1},{3,2},{4,7},{5,4},{6,5},{7,6},{8,11},{9,8},{10,9... | collective-permute-start | bytes 589832 | tf_op jit(solution)/shard_map/ppermute | solution.py:1104
  532.8 23.5 %collective-permute-start.7 = (bf16[512,192]{1,0:T(8,128)(2,1)S(1)}, bf16[512,192]{1,0:T(8,128)(2,1)S(1)}, u32[]{:S(2)}, u32[]{:S(2)}) collective-permute-start(bf16[512,192]{1,0:T(8,128)(2,1)S(1)} %convert_element_type.274.refs_0_), channel_id=1, source_target_pairs={{0,2},{1,3},{2,0},{3,1},{4,6},{5,7},{6,4},{7,5},{8,10},{9,11},{10,... | collective-permute-start | bytes 589832 | tf_op jit(solution)/shard_map/ppermute | solution.py:1104
  534.7 23.1 %collective-permute-start.6 = (bf16[512,192]{1,0:T(8,128)(2,1)S(1)}, bf16[512,192]{1,0:T(8,128)(2,1)}, u32[]{:S(2)}, u32[]{:S(2)}) collective-permute-start(bf16[512,192]{1,0:T(8,128)(2,1)S(1)} %convert_element_type.274.refs_0_), channel_id=1, source_target_pairs={{0,1},{1,2},{2,3},{3,0},{4,5},{5,6},{6,7},{7,4},{8,9},{9,10},{10,1... | collective-permute-start | bytes 589832 | tf_op jit(solution)/shard_map/ppermute | solution.py:1104
  534.7 21.6 %collective-permute-start.13 = (f32[32,128]{1,0:T(8,128)S(1)}, f32[32,128]{1,0:T(8,128)S(1)}, u32[]{:S(2)}, u32[]{:S(2)}) collective-permute-start(f32[32,128]{1,0:T(8,128)S(1)} %add.552), channel_id=1, source_target_pairs={{0,2},{1,3},{2,0},{3,1},{4,6},{5,7},{6,4},{7,5},{8,10},{9,11},{10,... | collective-permute-start | bytes 49160 | tf_op jit(solution)/shard_map/ppermute | solution.py:1140
  568.8 3.0 collective-permute-start.14
  573.4 17.7 %collective-permute-start.15 = (bf16[2368,128]{1,0:T(8,128)(2,1)S(1)}, bf16[2368,128]{1,0:T(8,128)(2,1)S(1)}, u32[]{:S(2)}, u32[]{:S(2)}) collective-permute-start(bf16[2368,128]{1,0:T(8,128)(2,1)S(1)} %get-tuple-element.161), channel_id=1, source_target_pairs={{8,0},{12,4},{24,16},{28,20},{9,1},{13,5},{25,17},{29,21},{10,2},{... | collective-permute-start | bytes 1818632 | tf_op jit(solution)/shard_map/ppermute | solution.py:1058
  574.7 17.7 %collective-permute-start.17 = (bf16[2368,128]{1,0:T(8,128)(2,1)S(1)}, bf16[2368,128]{1,0:T(8,128)(2,1)S(1)}, u32[]{:S(2)}, u32[]{:S(2)}) collective-permute-start(bf16[2368,128]{1,0:T(8,128)(2,1)S(1)} %get-tuple-element.162), channel_id=1, source_target_pairs={{16,0},{20,4},{24,8},{28,12},{17,1},{21,5},{25,9},{29,13},{18,2},{... | collective-permute-start | bytes 1818632 | tf_op jit(solution)/shard_map/ppermute | solution.py:1058
  592.7 16.8 %collective-permute-start.16 = (bf16[2368,128]{1,0:T(8,128)(2,1)S(1)}, bf16[2368,128]{1,0:T(8,128)(2,1)S(1)}, u32[]{:S(2)}, u32[]{:S(2)}) collective-permute-start(bf16[2368,128]{1,0:T(8,128)(2,1)S(1)} %get-tuple-element.159), channel_id=1, source_target_pairs={{16,0},{20,4},{24,8},{28,12},{17,1},{21,5},{25,9},{29,13},{18,2},{... | collective-permute-start | bytes 1818632 | tf_op jit(solution)/shard_map/ppermute | solution.py:1058
  594.0 16.8 %collective-permute-start.18 = (bf16[2368,128]{1,0:T(8,128)(2,1)S(1)}, bf16[2368,128]{1,0:T(8,128)(2,1)S(1)}, u32[]{:S(2)}, u32[]{:S(2)}) collective-permute-start(bf16[2368,128]{1,0:T(8,128)(2,1)S(1)} %get-tuple-element.160), channel_id=1, source_target_pairs={{8,0},{12,4},{24,16},{28,20},{9,1},{13,5},{25,17},{29,21},{10,2},{... | collective-permute-start | bytes 1818632 | tf_op jit(solution)/shard_map/ppermute | solution.py:1058
  616.9 13.1 %all-to-all-start = ((f32[32,8,128]{2,1,0:T(8,128)}), f32[32,8,128]{2,1,0:T(8,128)S(1)}, u32[]{:S(2)}, u32[]{:S(2)}) async-start(f32[32,8,128]{2,1,0:T(8,128)} %broadcast_in_dim_broadcast_in_dim_broadcast_in_dim.3), calls=%async_computation.1 | async-start | bytes 262144 | tf_op jit(solution)/shard_map/all_to_all | solution.py:1148
  (68 other events, 196.2 us)
Sparse Core Ops, SparseCore 0:
  14.5 224.6 all-gather.2
  504.6 74.9 reduce-scatter.1

commit v5 on v4

--- a/solution.py
+++ b/solution.py
@@ -247,14 +247,14 @@
 CHUNK = 6
 
 
-def conv_weight_kernel(tap_ref, in_ref, grad_ref, mask_ref, out_ref, taps_ref, turn_ref):
+def conv_weight_kernel(tap_ref, in_ref, grad_ref, mask_ref, out_ref, taps_ref, turn_ref, *, chunk):
     parts = in_ref.shape[0]
     begin = tap_ref[pl.program_id(0)]
     strips = D // 128
-    rows = CHUNK * WIDTH
+    rows = chunk * WIDTH
     for part in range(parts):
         turned = pltpu.roll(in_ref[part], in_ref.shape[2] - begin, 1)
-        for tap in range(CHUNK):
+        for tap in range(chunk):
             taps_ref[part, tap * PART : (tap + 1) * PART, :] = turned[:, tap : tap + ROWS].astype(
                 BF
             )
@@ -262,7 +262,7 @@
     for part in range(parts):
         term = dot_nn(taps_ref[part], grad_ref[part])
         pieces = []
-        for tap in range(CHUNK):
+        for tap in range(chunk):
             total = None
             for group in range(mask_ref.shape[0]):
                 low = tap * PART + group * WIDTH
@@ -319,15 +319,15 @@
     return padded, jnp.transpose(grad_low.reshape(ROWS, parts, PART), (1, 0, 2))
 
 
-def conv_weight_grad(padded, grads, geometry, code_index, slots):
+def conv_weight_grad(padded, grads, geometry, code_index, slots, chunk=CHUNK):
     parts = D // PART
     masks = jnp.asarray(lane_masks(PART), F32)
     base, unit = geometry.place("conv_w"), WIDTH * D // 128
-    chunks = owned_chunks(geometry, base, unit, KERNEL, CHUNK, 1, slots)
+    chunks = owned_chunks(geometry, base, unit, KERNEL, chunk, 1, slots)
     table = chunk_table(chunks, code_index)
-    rows = CHUNK * unit
+    rows = chunk * unit
     out = pl.pallas_call(
-        conv_weight_kernel,
+        functools.partial(conv_weight_kernel, chunk=chunk),
         grid_spec=pltpu.PrefetchScalarGridSpec(
             num_scalar_prefetch=1,
             grid=(len(chunks[0]),),
@@ -338,14 +338,14 @@
             ],
             out_specs=pl.BlockSpec((rows, 128), lambda i, t: (i, 0)),
             scratch_shapes=[
-                pltpu.VMEM((parts, CHUNK * PART, ROWS), BF),
+                pltpu.VMEM((parts, chunk * PART, ROWS), BF),
                 pltpu.VMEM((rows, 128), F32),
             ],
         ),
         out_shape=jax.ShapeDtypeStruct((len(chunks[0]) * rows, 128), BF),
         compiler_params=params_of(),
     )(table, padded, grads, masks)
-    return out, (chunks, base, unit, CHUNK)
+    return out, (chunks, base, unit, chunk)
 
 
 BLOCK = 128
@@ -476,7 +476,7 @@
     length = qkv.shape[0]
     heads = 2 if pick is None else SEEN_HEADS
     specs = head_specs(length, heads)
-    args = [qkv, qkv, qkv, gate, span, fill] + list(pick or ())
+    args = [qkv, qkv, qkv, gate, span, fill] + list(pick[:3] if pick else ())
     shapes = [
         jax.ShapeDtypeStruct((length, D), BF),
         jax.ShapeDtypeStruct((16, length), F32),
@@ -675,9 +675,7 @@
             pltpu.VMEM((2, BLOCK, SPAN), F32),
         ]
     else:
-        turned = jnp.transpose(pick[1])
-        flip = jnp.concatenate([turned, turned], axis=1)
-        args = [qkv, qkv, qkv, upstream, gate, fill, lse, pick[0], pick[2], flip, bias]
+        args = [qkv, qkv, qkv, upstream, gate, fill, lse, pick[0], pick[2], pick[3], bias]
         kernel = seen_backward_kernel
         more = [pl.BlockSpec((heads * BLOCK, BLOCK), lambda i: (i, 0))]
         scratch = [pltpu.VMEM((heads, BLOCK, SPAN), F32)]
@@ -695,36 +693,103 @@
     )(*args)
 
 
-def weight_grad_kernel(table_ref, left_ref, right_ref, out_ref, turn_ref):
-    rows = left_ref.shape[1]
-    strips = right_ref.shape[1] // 128
-    grad = dot_tn(left_ref[...], right_ref[...])
-    for strip in range(strips):
-        turn_ref[pl.ds(strip, rows, stride=strips), :] = grad[:, strip * 128 : (strip + 1) * 128]
-    out_ref[...] = turn_ref[...].astype(BF)
-
-
-def weight_grad(left, right, geometry, code_index, base, rows):
-    length, depth = left.shape
-    strips = right.shape[1] // 128
+STAGES = 4
+
+
+def weight_grads_kernel(table_ref, *refs, plan):
+    count = len(plan)
+    lefts, rights, outs = refs[:count], refs[count : 2 * count], refs[2 * count : 3 * count]
+    left_bufs, right_bufs = refs[3 * count : 4 * count], refs[4 * count : 5 * count]
+    turn_ref, stage_ref, in_sems, out_sems = refs[5 * count :]
+    loads = []
+    for number in range(count):
+        loads.append(
+            [
+                pltpu.make_async_copy(source, target, in_sems.at[side, number])
+                for side, (source, target) in enumerate(
+                    ((lefts[number], left_bufs[number]), (rights[number], right_bufs[number]))
+                )
+            ]
+        )
+    for pair in loads:
+        for copy in pair:
+            copy.start()
+
+    def out_copy(number, index, slot):
+        _, _, rows, strips = plan[number]
+        size = rows * strips
+        return pltpu.make_async_copy(
+            stage_ref.at[slot, pl.ds(0, size)],
+            outs[number].at[pl.ds(pl.multiple_of(index * size, TILE), size)],
+            out_sems.at[slot],
+        )
+
+    pending = [None] * STAGES
+    for number, (offset, steps, rows, strips) in enumerate(plan):
+        for copy in loads[number]:
+            copy.wait()
+        base = number % 2 * 2
+        for slot in (base, base + 1):
+            if pending[slot] is not None:
+                pending[slot].wait()
+                pending[slot] = None
+        size = rows * strips
+
+        def body(index, carry, number=number, offset=offset, rows=rows, strips=strips, base=base):
+            size = rows * strips
+            slot = base + index % 2
+            begin = pl.multiple_of(table_ref[offset + index], 128)
+            grad = dot_tn(left_bufs[number][:, pl.ds(begin, rows)], right_bufs[number][...])
+            for strip in range(strips):
+                turn_ref[pl.ds(strip, rows, stride=strips), :] = grad[
+                    :, strip * 128 : (strip + 1) * 128
+                ]
+
+            @pl.when(index >= 2)
+            def _():
+                out_copy(number, index - 2, slot).wait()
+
+            stage_ref[slot, :size, :] = turn_ref[:size, :].astype(BF)
+            out_copy(number, index, slot).start()
+            return carry
+
+        lax.fori_loop(0, steps, body, 0)
+        for index in range(max(steps - 2, 0), steps):
+            pending[base + index % 2] = out_copy(number, index, base + index % 2)
+    for copy in pending:
+        if copy is not None:
+            copy.wait()
+
+
+def weight_grads(pairs, geometry, code_index):
     slots = range(geometry.dp_count)
-    chunks = owned_chunks(geometry, base, strips, depth, rows, rows, slots)
-    out = pl.pallas_call(
-        weight_grad_kernel,
-        grid_spec=pltpu.PrefetchScalarGridSpec(
-            num_scalar_prefetch=1,
-            grid=(len(chunks[0]),),
-            in_specs=[
-                pl.BlockSpec((length, rows), lambda i, t: (0, t[i])),
-                pl.BlockSpec(right.shape, lambda i, t: (0, 0)),
-            ],
-            out_specs=pl.BlockSpec((rows * strips, 128), lambda i, t: (i, 0)),
-            scratch_shapes=[pltpu.VMEM((rows * strips, 128), F32)],
-        ),
-        out_shape=jax.ShapeDtypeStruct((len(chunks[0]) * rows * strips, 128), BF),
-        compiler_params=params_of(),
-    )(chunk_table(chunks, code_index) // rows, left, right)
-    return out, (chunks, base, strips, rows)
+    plan, found, tables, shapes = [], [], [[] for _ in range(geometry.code_count)], []
+    for left, right, base, rows in pairs:
+        strips = right.shape[1] // 128
+        chunks = owned_chunks(geometry, base, strips, left.shape[1], rows, rows, slots)
+        plan.append((len(tables[0]), len(chunks[0]), rows, strips))
+        for table, chunk in zip(tables, chunks):
+            table += chunk
+        found.append((chunks, base, strips, rows))
+        shapes.append(jax.ShapeDtypeStruct((len(chunks[0]) * rows * strips, 128), BF))
+    most = max(rows * strips for _, _, rows, strips in plan)
+    lefts, rights = [pair[0] for pair in pairs], [pair[1] for pair in pairs]
+    anywhere = pl.BlockSpec(memory_space=pl.ANY)
+    outs = pl.pallas_call(
+        functools.partial(weight_grads_kernel, plan=plan),
+        in_specs=[pl.BlockSpec(memory_space=pltpu.SMEM)] + [anywhere] * (2 * len(pairs)),
+        out_specs=[anywhere] * len(pairs),
+        out_shape=shapes,
+        scratch_shapes=[pltpu.VMEM(a.shape, BF) for a in lefts + rights]
+        + [
+            pltpu.VMEM((most, 128), F32),
+            pltpu.VMEM((STAGES, most, 128), BF),
+            pltpu.SemaphoreType.DMA((2, len(pairs))),
+            pltpu.SemaphoreType.DMA((STAGES,)),
+        ],
+        compiler_params=pltpu.CompilerParams(vmem_limit_bytes=VMEM_LIMIT),
+    )(chunk_table(tables, code_index), *lefts, *rights)
+    return list(zip(outs, found))
 
 
 def unpack_jobs(geometry, specs):
@@ -970,6 +1035,7 @@
 
 def pack_kernel(code_ref, *refs, plans, empty):
     sources, out_ref, sems = refs[:-2], refs[-2], refs[-1]
+    turn = code_ref[1]
     for slot in range(empty):
         out_ref[slot] = jnp.zeros_like(out_ref[slot])
     for code, plan in enumerate(plans):
@@ -979,7 +1045,7 @@
             copies = [
                 pltpu.make_async_copy(
                     sources[source].at[pl.ds(begin, count)],
-                    out_ref.at[slot, pl.ds(low, count)],
+                    out_ref.at[jnp.bitwise_xor(slot, turn), pl.ds(low, count)],
                     sems.at[index],
                 )
                 for index, (source, begin, slot, low, count) in enumerate(plan)
@@ -1009,7 +1075,7 @@
     return plans
 
 
-def pack(geometry, code_index, sources, spans, low, high):
+def pack(geometry, code_index, sources, spans, low, high, turn=0):
     plans = pack_plans(geometry, spans, range(low, high))
     return pl.pallas_call(
         functools.partial(pack_kernel, plans=plans, empty=low),
@@ -1019,7 +1085,7 @@
         out_shape=jax.ShapeDtypeStruct((high, geometry.window, 128), BF),
         scratch_shapes=[pltpu.SemaphoreType.DMA((max(len(plan) for plan in plans),))],
         compiler_params=pltpu.CompilerParams(vmem_limit_bytes=VMEM_LIMIT),
-    )(jnp.full((1,), code_index, jnp.int32), *sources)
+    )(jnp.stack([code_index, jnp.int32(turn)]).astype(jnp.int32), *sources)
 
 
 def front_slots(geometry):
@@ -1038,14 +1104,12 @@
     return (left.astype(F32) + right.astype(F32)).astype(BF)
 
 
-def reduce_front(held, dp_count, dp_index):
+def reduce_front(held, dp_count):
     count = held.shape[0]
     bit = count // 2
     while bit:
-        mine = dp_index // bit % 2
-        keep = lax.dynamic_slice_in_dim(held, mine * bit, bit, 0)
-        give = lax.dynamic_slice_in_dim(held, (1 - mine) * bit, bit, 0)
-        held = add_low(keep, lax.ppermute(give, "dp", [(i, i ^ bit) for i in range(dp_count)]))
+        moved = lax.ppermute(held[bit:], "dp", [(i, i ^ bit) for i in range(dp_count)])
+        held = add_low(held[:bit], moved)
         bit //= 2
     bits = []
     while count < dp_count:
@@ -1347,9 +1411,7 @@
         flat_ref[pl.ds(strip, D, stride=strips), :] = grad[:, strip * 128 : (strip + 1) * 128]
 
 
-def head_pass(hidden, w_head, codebook, codes, target_codes):
-    targets = jnp.broadcast_to(target_codes[:, None], (ROWS, 128))
-    names = jnp.broadcast_to(codes, (8, codes.shape[1]))
+def head_pass(hidden, w_head, codebook, names, targets):
     loss, grad_rows, grad_head = pl.pallas_call(
         head_kernel,
         out_shape=[
@@ -1388,6 +1450,35 @@
     windows = lax.all_gather(own_window, ("dp", "code"), axis=0, tiled=False)
     where = starts()
 
+    places = jnp.arange(ROWS, dtype=jnp.int32)
+    mask_row = jnp.pad(patch_masks[0], (0, ROWS - LONG))
+    live_slot = places < jnp.minimum(lengths[0], LONG)
+    visible = live_slot & (mask_row == 0)
+    rank = jnp.cumsum(visible.astype(jnp.int32)) - 1
+    pick = (
+        visible[None, :] & (rank[None, :] == jnp.arange(SEEN, dtype=jnp.int32)[:, None])
+    )
+    pick_low = pick.astype(BF)
+    near = jnp.sum(pick_low.reshape(SEEN, ROWS // BLOCK, BLOCK), axis=1)
+    hop = jnp.sum(pick.astype(F32).reshape(SEEN, ROWS // BLOCK, BLOCK), axis=2)
+    flip = jnp.concatenate([jnp.transpose(near)] * 2, axis=1)
+    pick_seen = (pick_low, near, jnp.pad(hop, ((0, 0), (0, BLOCK - ROWS // BLOCK))), flip)
+    pick_full = pick.astype(F32)
+    seen_valid = jnp.arange(SEEN, dtype=jnp.int32) < lengths[0] // 4
+    seen_fill = jnp.broadcast_to(jnp.where(seen_valid, 0.0, MASK_FILL)[:, None], (SEEN, BLOCK))
+    live_fill = jnp.broadcast_to(jnp.where(live_slot, 0.0, MASK_FILL)[:, None], (ROWS, BLOCK))
+    live_float = live_slot.astype(F32)[:, None]
+    all_codes = jnp.concatenate(blocks_of_code(codebook), axis=0)
+    code_places = (
+        code_index - jnp.arange(code_count, dtype=jnp.int32) + code_count
+    ) % code_count * codebook.shape[0]
+    code_names = (
+        code_places[:, None] + jnp.arange(codebook.shape[0], dtype=jnp.int32)[None, :]
+    ).reshape(1, -1)
+    patch_rows = jnp.pad(patches[0], ((0, ROWS - LONG), (0, 0)))
+    target_codes = jnp.where(mask_row == 1, jnp.pad(targets[0], (0, ROWS - LONG)), -1)
+    target_wide = jnp.broadcast_to(target_codes[:, None], (ROWS, 128))
+    name_wide = jnp.broadcast_to(code_names, (8, code_names.shape[1]))
     w_patch, glob_vec, vectors, up_bias, rest, w_head = unpack_small(geometry, windows)
     rest = rest.reshape(-1)
 
@@ -1400,18 +1491,20 @@
     gate_scale = values("gate_scale")
     rel_table = values("rel_table").astype(BF)
     conv_weight = unpack_conv(geometry, windows, code_index)
+    specs = [
+        spec
+        for index in range(LAYERS)
+        for spec in (
+            (geometry.place("w_qkv", index), D, 3 * D // 128, 128),
+            (geometry.place("w_out", index), D, D // 128, 384),
+            (geometry.place("w_up", index), D, FF // 128, 128),
+            (geometry.place("w_down", index), FF, D // 128, 512),
+        )
+    ]
+    unpacked = unpack(geometry, windows, specs)
     weights = []
     for index in range(LAYERS):
-        mats = unpack(
-            geometry,
-            windows,
-            [
-                (geometry.place("w_qkv", index), D, 3 * D // 128, 128),
-                (geometry.place("w_out", index), D, D // 128, 384),
-                (geometry.place("w_up", index), D, FF // 128, 128),
-                (geometry.place("w_down", index), FF, D // 128, 512),
-            ],
-        )
+        mats = unpacked[4 * index : 4 * index + 4]
         weights.append(
             dict(zip(("w_qkv", "w_out", "w_up", "w_down"), mats))
             | {
@@ -1422,36 +1515,11 @@
             }
         )
 
-    places = jnp.arange(ROWS, dtype=jnp.int32)
-    mask_row = jnp.pad(patch_masks[0], (0, ROWS - LONG))
-    live_slot = places < jnp.minimum(lengths[0], LONG)
-    visible = live_slot & (mask_row == 0)
-    rank = jnp.cumsum(visible.astype(jnp.int32)) - 1
-    pick = (
-        visible[None, :] & (rank[None, :] == jnp.arange(SEEN, dtype=jnp.int32)[:, None])
-    )
-    pick_low = pick.astype(BF)
-    near = jnp.sum(pick_low.reshape(SEEN, ROWS // BLOCK, BLOCK), axis=1)
-    hop = jnp.sum(pick.astype(F32).reshape(SEEN, ROWS // BLOCK, BLOCK), axis=2)
-    pick_seen = (pick_low, near, jnp.pad(hop, ((0, 0), (0, BLOCK - ROWS // BLOCK))))
-    pick_full = pick.astype(F32)
-    seen_valid = jnp.arange(SEEN, dtype=jnp.int32) < lengths[0] // 4
-    seen_fill = jnp.broadcast_to(jnp.where(seen_valid, 0.0, MASK_FILL)[:, None], (SEEN, BLOCK))
-    live_fill = jnp.broadcast_to(jnp.where(live_slot, 0.0, MASK_FILL)[:, None], (ROWS, BLOCK))
-    live_float = live_slot.astype(F32)[:, None]
     span_table = span_onehot()
     span = dot_tn(
         jnp.pad(rel_table, ((0, 0), (0, 16 - HEADS))), jnp.asarray(span_table.T, BF)
     )
 
-    all_codes = jnp.concatenate(blocks_of_code(codebook), axis=0)
-    code_places = (
-        code_index - jnp.arange(code_count, dtype=jnp.int32) + code_count
-    ) % code_count * codebook.shape[0]
-    code_names = (
-        code_places[:, None] + jnp.arange(codebook.shape[0], dtype=jnp.int32)[None, :]
-    ).reshape(1, -1)
-    patch_rows = jnp.pad(patches[0], ((0, ROWS - LONG), (0, 0)))
     embedded = dot_nn(patch_rows, w_patch)
     normed_rows, normed_zero, inv_zero = norm_forward(embedded, glob_vec[0 : 1], glob_vec[1 : 2])
     start_rows = normed_rows * live_float
@@ -1476,12 +1544,11 @@
     )
     hidden = jnp.where(visible[:, None], placed, glob_vec[3 : 4])
     final, kept_second = layer_forward(hidden, live_fill, weights[1], span, None)
-    target_codes = jnp.where(mask_row == 1, jnp.pad(targets[0], (0, ROWS - LONG)), -1)
-    loss_local, upstream, grad_head = head_pass(final, w_head, all_codes, code_names, target_codes)
+    loss_local, upstream, grad_head = head_pass(final, w_head, all_codes, name_wide, target_wide)
 
     def grad_maker(index):
-        return lambda seg_name, left, right, rows: weight_grad(
-            left, right, geometry, code_index, geometry.place(seg_name, index), rows
+        return lambda seg_name, left, right, rows: (
+            left, right, geometry.place(seg_name, index), rows
         )
 
     upstream, map_second, span_second = layer_backward(
@@ -1505,7 +1572,9 @@
     grad_conv_in = side_by_side(grad_in_own.astype(BF), code_index)
     split = front_slots(geometry)
     padded, grads = conv_weight_inputs(conv_in[:LONG], grad_conv)
-    rest_grad = conv_weight_grad(padded, grads, geometry, code_index, range(split, dp_count))
+    rest_grad = conv_weight_grad(
+        padded, grads, geometry, code_index, range(split, dp_count), CHUNK // 2
+    )
     grad_start = (grad_full + grad_conv_in.astype(F32)) * live_float
     grad_embedded, grad_gain_zero, grad_shift_zero = norm_backward(
         grad_start, normed_zero, inv_zero, glob_vec[0 : 1]
@@ -1539,9 +1608,13 @@
             spans[code] += items
         sources.append(array)
 
-    for seg_name in ("w_qkv", "w_out", "w_up", "w_down"):
-        for layer_map in both:
-            add_source(layer_map[seg_name])
+    pairs = [
+        layer_map[seg_name]
+        for layer_map in both[::-1]
+        for seg_name in ("w_down", "w_up", "w_out", "w_qkv")
+    ]
+    for found in weight_grads(pairs, geometry, code_index):
+        add_source(found)
     add_source(rest_grad)
     tail_place = geometry.place("layer_vec")
     vectors = [vector for layer_map in both for vector in layer_map["layer_vec"]]
@@ -1559,18 +1632,19 @@
         reduced = lax.psum_scatter(own_part, "dp", scatter_dimension=0, tiled=False)
         sources, spans = [], [[] for _ in range(code_count)]
         add_source(conv_weight_grad(padded, grads, geometry, code_index, range(split)))
+    front, early = lax.optimization_barrier((front, early))
     for items in spans:
         items.append((0, front.shape[0], len(sources), 0))
-    front, early = lax.optimization_barrier((front, early))
     sources.append(front)
-    last_part = pack(geometry, code_index, sources, spans, 0, split or dp_count)
+    turn = dp_index % split if split else 0
+    last_part = pack(geometry, code_index, sources, spans, 0, split or dp_count, turn)
     if split:
-        first = reduce_front(last_part, dp_count, dp_index)
+        first = reduce_front(last_part, dp_count)
         reduced = jnp.where(dp_index < split, first, reduced)
     else:
         reduced = lax.psum_scatter(last_part, "dp", scatter_dimension=0, tiled=False)
-    reduced = lax.dynamic_slice(reduced.astype(F32), (own_offset, 0), (shard_rows, 128))
-    reduced = reduced.reshape(shard_len)
+    reduced = reduced.reshape(geometry.window, 128).astype(F32)
+    reduced = lax.dynamic_slice(reduced, (own_offset, 0), (shard_rows, 128)).reshape(shard_len)
     squares_all = sum_over_all(jnp.full((8, 128), jnp.sum(reduced * reduced)))
     squares_all = squares_all[0, 0]
     rel_rows = BUCKETS * HEADS // 128

time: 660 us -> 635 us (0.962)
  Pallas kernels: 183 us -> 161 us
    pallas_call x10 -> x3, Pallas kernels: 62.5 us -> 41.2 us  [the longest x2 23.7 us: conv_weight_grad(): pl.pallas_call(functools.partial(conv_weight_kernel, chunk=chunk), grid_s...]
    pallas_call x2 -> x1, Pallas kernels: 22.2 us -> 20.1 us  [unpack(): pl.pallas_call(functools.partial(unpack_kernel, jobs=jobs, stages=stages)...]
  transfers between devices with their start and end apart: 22 -> 22, of which waited for: 11 -> 10; matrix products, arithmetic and copies ran while one was open for 6% -> 6% of each run, Pallas kernels for 9% -> 9%
where the time goes in v5:
time: 635 us; the launch traced here: 627 us
  waiting for transfers between devices  249 us (39%)
  Pallas kernels  161 us (25%)
  matrix products  77.7 us (12%)
  other arithmetic  42.7 us (7%)
  local copies, waits for them, and re-layouts  41.4 us (7%)
  starting transfers between devices  30.9 us (5%)
  between operations  24.1 us (4%)
    all_gather x1, waiting for transfers between devices, local(): windows = lax.all_gather(own_window, ('dp', 'code'), axis=0, tiled=False)  205 us
    ppermute x4, waiting for transfers between devices, reduce_front(): lax.ppermute(halves[side], 'dp', [(i, i - bit) for i in range(dp_count) i...  31.5 us
    dot_general x10, matrix products, dot_nt(): lax.dot_general(left, right, (((1,), (1,)), ((), ())), preferred_element_...  29.9 us
    dot_general x11, matrix products, dot_nn(): lax.dot_general(left, right, (((1,), (0,)), ((), ())), preferred_element_...  27 us
    pallas_call x2, Pallas kernels, conv_call(): pl.pallas_call(kernel, grid=(steps,), in_specs=[pl.BlockSpec(padded.shape...  25.4 us
    pallas_call x2, Pallas kernels, attention_backward(): pl.pallas_call(kernel, grid=(HEADS // heads,), in_specs=specs + [specs[0]...  25 us
    pallas_call x2, Pallas kernels, conv_weight_grad(): pl.pallas_call(functools.partial(conv_weight_kernel, chunk=chunk), grid_s...  23.7 us
    pallas_call x1, Pallas kernels, unpack(): pl.pallas_call(functools.partial(unpack_kernel, jobs=jobs, stages=stages)...  20.1 us
  transfers between devices with their start and end apart: 22, of which 10 were waited for; matrix products, arithmetic and copies ran while one was open for 6% of the time, Pallas kernels for 9%

profile of v5, /device:TPU:0, one launch (start us, length us, event | category | flops | bytes accessed | tf_op | source)
XLA Modules:
  0.0 626.7 jit_solution(160670816303517984)
XLA Ops:
  7.4 5.9 dynamic_update_slice.3
  14.4 3.1 collective-permute-start.3
  17.5 2.6 collective-permute-start.4
  33.2 205.0 %all-gather.3.cloned.1.call-done = bf16[151552,128]{1,0:T(8,128)(2,1)} async-done(((bf16[4736,128]{1,0:T(8,128)(2,1)}), bf16[151552,128]{1,0:T(8,128)(2,1)}) %all-gather.3.cloned.1.call-update) | async-done | bytes 38797328 | tf_op jit(solution)/shard_map/all_gather | solution.py:1450
  238.3 2.6 shard_map.351
  240.9 5.9 shard_map.352.weight_ref
  249.7 12.1 %shard_map.353 = f32[512,192]{1,0:T(8,128)} custom-call(f32[640,192]{1,0:T(8,128)} %pad_convert_fusion.2.in_ref, bf16[6144,192]{1,0:T(8,128)(2,1)} %shard_map.352.weight_ref, bf16[4,192]{1,0:T(4,128)(2,1)} %constant.212.clone.mask_ref), custom_call_target="tpu_custom_call" | custom-call | tf_op jit(solution)/shard_map/pallas_call | solution.py:232
  261.8 2.1 fusion.54.refs_0_
  263.8 1.9 collective-permute-start.1
  265.8 3.0 collective-permute-start.2
  268.8 20.1 %shard_map.355 = (bf16[768,2304]{1,0:T(8,128)(2,1)}, bf16[768,768]{1,0:T(8,128)(2,1)}, bf16[768,3072]{1,0:T(8,128)(2,1)}, bf16[3072,768]{1,0:T(8,128)(2,1)}, bf1...) custom-call(bf16[32,4736,128]{2,1,0:T(8,128)(2,1)} %bitcast.142), custom_call_target="tpu_custom_call" | custom-call | tf_op jit(solution)/shard_map/pallas_call | solution.py:875
  297.2 1.8 copy.73
  299.1 2.0 fusion.92.span_ref
  301.1 1.4 maximum_reduce_fusion.1
  303.2 2.0 shard_map.354
  305.3 2.3 fusion.193
  308.6 3.6 fusion.8.q_ref.k_ref.v_ref
  312.9 4.5 shard_map.356
  319.3 2.3 multiply_convert_fusion.2
  321.6 3.5 fusion.195
  327.7 3.4 fusion.6.q_ref.k_ref.v_ref
  331.9 9.7 %shard_map.357 = (bf16[512,768]{1,0:T(8,128)(2,1)}, f32[16,512]{1,0:T(8,128)}) custom-call(bf16[512,2304]{1,0:T(8,128)(2,1)} %fusion.6.q_ref.k_ref.v_ref, bf16[512,2304]{1,0:T(8,128)(2,1)} %fusion.6.q_ref.k_ref.v_ref, bf16[512,2304]{1,0:T(8,128)(2,1)} %fusion.6.q_ref.k_ref.v_ref, f32[16,512]{1,0:T(8,128)} %pad.61.gate_ref, f32[16,1024]{1,0:T(8,128)} %fusion.92.span_ref, ...), custom_call_target="tpu_custom_call" | custom-call | tf_op jit(solution)/shard_map/pallas_call | solution.py:493
  341.7 2.4 fusion.197
  345.2 6.8 %multiply_convert_fusion = (bf16[512,3072]{1,0:T(8,128)(2,1)S(1)}, f32[512,3072]{1,0:T(8,128)}) fusion(f32[3072]{0:T(1024)S(1)} %bitcast.165, bf16[512,768]{1,0:T(8,128)(2,1)S(1)} %fusion.17.refs_1_, bf16[768,3072]{1,0:T(8,128)(2,1)} %get-tuple-element.60), kind=kOutput, calls=%fused_computation.6 | convolution fusion | flops 2425356288 | bytes 14954496 | tf_op jit(solution)/shard_map/dot_general | solution.py:144
  352.0 2.8 fusion.198
  358.1 7.9 %shard_map.358 = (f32[8,128]{1,0:T(8,128)}, f32[512,768]{1,0:T(8,128)}, f32[1536,128]{1,0:T(8,128)}) custom-call(bf16[512,768]{1,0:T(8,128)(2,1)} %add_convert_fusion.1.in_ref, bf16[768,256]{1,0:T(8,128)(2,1)} %get-tuple-element.62.weight_ref, bf16[1024,256]{1,0:T(8,128)(2,1)} %pad_maximum_fusion.code_ref, s32[8,1024]{1,0:T(8,128)} %broadcast_in_dim.74.name_ref, ...), custom_call_target="tpu_custom_call" | custom-call | tf_op jit(solution)/shard_map/pallas_call | solution.py:1415
  366.0 2.8 multiply_reduce_fusion
  370.1 8.7 %fusion.187 = (f32[3072]{0:T(1024)}, bf16[512,3072]{1,0:T(8,128)(2,1)S(1)}) fusion(f32[512,3072]{1,0:T(8,128)} %get-tuple-element.214, f32[3072]{0:T(1024)S(1)} %bitcast.166, bf16[512,768]{1,0:T(8,128)(2,1)S(1)} %convert_element_type.257.refs_8_, bf16[3072,768]{1,0:T(8,128)(2,1)} %get-tuple-element.61), kind=kOutput, calls=%fused_computation.350 | convolution fusion | flops 2434790400 | bytes 14966784 | tf_op jit(solution)/shard_map/dot_general | solution.py:148
  378.8 3.7 multiply_reduce_fusion.1
  384.8 1.7 convolution_convert_fusion.up_ref
  386.5 17.7 %shard_map.359 = (bf16[512,2304]{1,0:T(8,128)(2,1)}, f32[8,768]{1,0:T(8,128)}, f32[16,512]{1,0:T(8,128)}, f32[16,1024]{1,0:T(8,128)}) custom-call(bf16[512,2304]{1,0:T(8,128)(2,1)} %fusion.6.q_ref.k_ref.v_ref, bf16[512,2304]{1,0:T(8,128)(2,1)} %fusion.6.q_ref.k_ref.v_ref, bf16[512,2304]{1,0:T(8,128)(2,1)} %fusion.6.q_ref.k_ref.v_ref, ...), custom_call_target="tpu_custom_call" | custom-call | tf_op jit(solution)/shard_map/pallas_call | solution.py:682
  404.2 1.5 fusion.128
  406.5 4.7 fusion.199
  412.4 1.4 multiply_reduce_fusion.12
  414.7 2.3 fusion.188
  417.1 2.4 multiply_reduce_fusion.13
  421.9 7.2 %shard_map.360 = (bf16[128,2304]{1,0:T(8,128)(2,1)}, f32[8,768]{1,0:T(8,128)}, f32[16,128]{1,0:T(8,128)}, f32[16,1024]{1,0:T(8,128)}) custom-call(bf16[128,2304]{1,0:T(8,128)(2,1)} %fusion.8.q_ref.k_ref.v_ref, bf16[128,2304]{1,0:T(8,128)(2,1)} %fusion.8.q_ref.k_ref.v_ref, bf16[128,2304]{1,0:T(8,128)(2,1)} %fusion.8.q_ref.k_ref.v_ref, ...), custom_call_target="tpu_custom_call" | custom-call | tf_op jit(solution)/shard_map/pallas_call | solution.py:682
  431.7 2.4 convolution_add_fusion.5
  435.0 1.7 fusion.184
  443.8 2.4 broadcast_multiply_fusion
  447.2 17.6 %shard_map.365 = (bf16[9216,128]{1,0:T(8,128)(2,1)}, bf16[12288,128]{1,0:T(8,128)(2,1)}, bf16[4608,128]{1,0:T(8,128)(2,1)}, bf16[9216,128]{1,0:T(8,128)(2,1)}, b...) custom-call(s32[18]{0:T(128)} %fusion.164.table_ref, ...), custom_call_target="tpu_custom_call" | custom-call | tf_op jit(solution)/shard_map/pallas_call | solution.py:778
  464.8 4.7 shard_map.366.refs_8_
  469.5 2.4 shard_map.367.refs_9_
  471.9 8.0 %shard_map.368 = bf16[8,4736,128]{2,1,0:T(8,128)(2,1)} custom-call(s32[2]{0:T(128)} %pad_add_fusion.1.code_ref, bf16[9216,128]{1,0:T(8,128)(2,1)} %get-tuple-element.75.refs_0_, bf16[12288,128]{1,0:T(8,128)(2,1)} %get-tuple-element.76.refs_1_, bf16[4608,128]{1,0:T(8,128)(2,1)} %get-tuple-element.77.refs_2_, bf16[9216,128]{1,0:T(8,128)(2,1)} %get-tuple-element.78.refs_3_, ...), custom_call_target="tpu_custom_call" | custom-call | tf_op jit(solution)/shard_map/pallas_call | solution.py:1080
  486.0 1.9 collective-permute-done.10
  487.9 1.5 collective-permute-start.11
  489.5 2.1 collective-permute-done.11
  492.6 13.3 %shard_map.362 = f32[512,192]{1,0:T(8,128)} custom-call(f32[640,192]{1,0:T(8,128)} %pad_convert_fusion.1.in_ref, bf16[6144,192]{1,0:T(8,128)(2,1)} %shard_map.352.weight_ref, bf16[4,192]{1,0:T(4,128)(2,1)} %constant.212.clone.mask_ref), custom_call_target="tpu_custom_call" | custom-call | tf_op jit(solution)/shard_map/pallas_call | solution.py:232
  507.0 2.1 collective-permute-start.6
  509.1 1.4 collective-permute-start.7
  511.6 1.4 collective-permute-start.13
  513.8 18.9 %shard_map.361.refs_0_ = bf16[10368,128]{1,0:T(8,128)(2,1)} custom-call(s32[6]{0:T(128)} %fusion.163.tap_ref, f32[4,192,640]{2,1,0:T(8,128)} %bitcast.148, bf16[4,512,192]{2,1,0:T(8,128)(2,1)} %bitcast.151, f32[4,192]{1,0:T(4,128)} %constant.214.clone.mask_ref), custom_call_target="tpu_custom_call" | custom-call | tf_op jit(solution)/shard_map/pallas_call | solution.py:329
  534.5 2.3 shard_map.363
  536.8 2.1 multiply_reduce_fusion.3
  541.0 3.8 shard_map.364
  544.8 1.5 slice.294
  546.4 2.8 collective-permute-done.14
  552.3 15.0 %collective-permute-done.15 = bf16[2368,128]{1,0:T(8,128)(2,1)S(1)} collective-permute-done((bf16[2368,128]{1,0:T(8,128)(2,1)S(1)}, bf16[2368,128]{1,0:T(8,128)(2,1)S(1)}, u32[]{:S(2)}, u32[]{:S(2)}) %collective-permute-start.15) | collective-permute-done | bytes 606240 | tf_op jit(solution)/shard_map/ppermute | solution.py:1122
  570.2 1.5 collective-permute-start.18
  571.7 14.0 %collective-permute-done.16 = bf16[2368,128]{1,0:T(8,128)(2,1)S(1)} collective-permute-done((bf16[2368,128]{1,0:T(8,128)(2,1)S(1)}, bf16[2368,128]{1,0:T(8,128)(2,1)S(1)}, u32[]{:S(2)}, u32[]{:S(2)}) %collective-permute-start.16) | collective-permute-done | bytes 606240 | tf_op jit(solution)/shard_map/ppermute | solution.py:1122
  588.0 4.9 fusion.9
  594.2 4.7 all-to-all-start
  602.0 5.3 all-to-all-done
  610.7 6.8 %fusion.177 = (bf16[603008]{0:T(1024)(128)(2,1)}, f32[603008]{0:T(1024)}, f32[603008]{0:T(1024)}, f32[603008]{0:T(1024)}) fusion(f32[603008]{0:T(1024)S(1)} %copy-done.3, f32[]{:T(128)} %bitcast.36, f32[]{:T(128)} %bitcast.35, f32[]{:T(128)S(6)} %min.7, f32[]{:T(128)} %bitcast.32, bf16[4711,128]{1,0:T(8,128)(2,1)} %get-tuple-element.151, f32[603008]{0:T(1024)} %param.39, ...), kind=kLoop, calls=%fused_computation.344 | loop fusion | flops 11457152 | bytes 16884240 | tf_op jit(solution)/shard_map/convert_element_type | solution.py:1669
  (431 shorter events, 81.3 us)
Async XLA Ops:
  7.2 231.1 %all-gather.3.cloned.1.call-start = ((), (), s32[]{:S(2)}) async-start(), calls=%async_computation.3 | async-start | bytes 40009728 | tf_op jit(solution)/shard_map/all_gather | solution.py:1450
  7.3 7.1 %copy-start.40 = (bf16[256,256]{1,0:T(8,128)(2,1)S(1)}, bf16[256,256]{1,0:T(8,128)(2,1)}, u32[]{:S(2)}) copy-start(bf16[256,256]{1,0:T(8,128)(2,1)} %param.36) | copy-start | bytes 393220
  7.3 14.7 %copy-start.90 = (s32[1,496]{1,0:T(1,128)S(1)}, s32[1,496]{1,0:T(1,128)}, u32[]{:S(2)}) copy-start(s32[1,496]{1,0:T(1,128)} %param.34) | copy-start | bytes 5956
  7.3 18.0 %copy-start.103 = (s32[1,496]{1,0:T(1,128)S(1)}, s32[1,496]{1,0:T(1,128)}, u32[]{:S(2)}) copy-start(s32[1,496]{1,0:T(1,128)} %param.35) | copy-start | bytes 5956
  14.3 573.7 %reduce-scatter.2.cloned.1.call-start = ((), (), s32[]{:S(2)}) async-start(), calls=%async_computation.2 | async-start | bytes 10911744 | tf_op jit(solution)/shard_map/reduce_scatter | solution.py:1632
  14.4 18.0 %collective-permute-start.3 = (bf16[256,256]{1,0:T(8,128)(2,1)S(1)}, bf16[256,256]{1,0:T(8,128)(2,1)S(1)}, u32[]{:S(2)}, u32[]{:S(2)}) collective-permute-start(bf16[256,256]{1,0:T(8,128)(2,1)S(1)} %copy-done.40), channel_id=1, source_target_pairs={{0,1},{1,2},{2,3},{3,0},{4,5},{5,6},{6,7},{7,4},{8,9},{9,10},{10,1... | collective-permute-start | bytes 393224 | tf_op jit(solution)/shard_map/ppermute | solution.py:1168
  17.5 14.9 %collective-permute-start.4 = (bf16[256,256]{1,0:T(8,128)(2,1)S(1)}, bf16[256,256]{1,0:T(8,128)(2,1)S(1)}, u32[]{:S(2)}, u32[]{:S(2)}) collective-permute-start(bf16[256,256]{1,0:T(8,128)(2,1)S(1)} %copy-done.40), channel_id=1, source_target_pairs={{0,2},{1,3},{2,0},{3,1},{4,6},{5,7},{6,4},{7,5},{8,10},{9,11},{10,... | collective-permute-start | bytes 393224 | tf_op jit(solution)/shard_map/ppermute | solution.py:1168
  20.1 12.3 %collective-permute-start.5 = (bf16[256,256]{1,0:T(8,128)(2,1)S(1)}, bf16[256,256]{1,0:T(8,128)(2,1)S(1)}, u32[]{:S(2)}, u32[]{:S(2)}) collective-permute-start(bf16[256,256]{1,0:T(8,128)(2,1)S(1)} %copy-done.40), channel_id=1, source_target_pairs={{0,3},{1,0},{2,1},{3,2},{4,7},{5,4},{6,5},{7,6},{8,11},{9,8},{10,9... | collective-permute-start | bytes 393224 | tf_op jit(solution)/shard_map/ppermute | solution.py:1168
  22.1 239.7 %copy-start.55 = (pred[512]{0:T(512)(128)(4,1)}, pred[512]{0:T(512)(128)(4,1)S(1)}, u32[]{:S(2)}) copy-start(pred[512]{0:T(512)(128)(4,1)S(1)} %get-tuple-element.170) | copy-start | bytes 1540
  24.8 223.5 %copy-start.68 = (f32[512]{0:T(512)}, f32[512]{0:T(512)S(1)}, u32[]{:S(2)}) copy-start(f32[512]{0:T(512)S(1)} %fusion.161) | copy-start | bytes 6148
  27.0 213.9 %copy-start.33 = (bf16[128,128]{1,0:T(8,128)(2,1)}, bf16[128,128]{1,0:T(8,128)(2,1)S(1)}, u32[]{:S(2)}) copy-start(bf16[128,128]{1,0:T(8,128)(2,1)S(1)} %fusion.69.near_ref) | copy-start | bytes 98308
  27.1 234.7 %copy-start.41 = (s32[512]{0:T(512)}, s32[512]{0:T(512)S(1)}, u32[]{:S(2)}) copy-start(s32[512]{0:T(512)S(1)} %fusion.252) | copy-start | bytes 6148
  240.9 5.9 copy-start.25
  240.9 5.9 copy-start.29
  263.8 25.1 %copy-start.60 = (f32[40,128]{1,0:T(8,128)S(1)}, f32[40,128]{1,0:T(8,128)}, u32[]{:S(2)}) copy-start(f32[40,128]{1,0:T(8,128)} %get-tuple-element.51) | copy-start | bytes 61444
  263.8 26.1 %copy-start.50 = (f32[8,24]{1,0:T(8,128)S(1)}, f32[8,24]{1,0:T(8,128)}, u32[]{:S(2)}) copy-start(f32[8,24]{1,0:T(8,128)} %constant.208.clone) | copy-start | bytes 2308
  263.8 39.4 %collective-permute-start = (f32[128,192]{1,0:T(8,128)}, f32[128,192]{1,0:T(8,128)}, u32[]{:S(2)}, u32[]{:S(2)}) collective-permute-start(f32[128,192]{1,0:T(8,128)} %fusion.54.refs_0_), channel_id=1, source_target_pairs={{0,1},{1,2},{2,3},{3,0},{4,5},{5,6},{6,7},{7,4},{8,9},{9,10},{10,1... | collective-permute-start | bytes 294920 | tf_op jit(solution)/shard_map/ppermute | solution.py:1168
  263.8 39.4 %collective-permute-start.1 = (f32[128,192]{1,0:T(8,128)}, f32[128,192]{1,0:T(8,128)}, u32[]{:S(2)}, u32[]{:S(2)}) collective-permute-start(f32[128,192]{1,0:T(8,128)} %fusion.54.refs_0_), channel_id=1, source_target_pairs={{0,2},{1,3},{2,0},{3,1},{4,6},{5,7},{6,4},{7,5},{8,10},{9,11},{10,... | collective-permute-start | bytes 294920 | tf_op jit(solution)/shard_map/ppermute | solution.py:1168
  265.8 37.4 %collective-permute-start.2 = (f32[128,192]{1,0:T(8,128)}, f32[128,192]{1,0:T(8,128)}, u32[]{:S(2)}, u32[]{:S(2)}) collective-permute-start(f32[128,192]{1,0:T(8,128)} %fusion.54.refs_0_), channel_id=1, source_target_pairs={{0,3},{1,0},{2,1},{3,2},{4,7},{5,4},{6,5},{7,6},{8,11},{9,8},{10,9... | collective-permute-start | bytes 294920 | tf_op jit(solution)/shard_map/ppermute | solution.py:1168
  288.9 5.8 copy-start.6
  288.9 5.8 copy-start.23
  299.0 6.2 copy-start.42
  299.0 6.2 copy-start.48
  299.0 6.2 copy-start.53
  299.0 6.3 copy-start.56
  299.0 6.3 copy-start.64
  299.0 6.3 copy-start.69
  299.1 6.3 copy-start.78
  299.1 6.3 copy-start.98
  303.2 5.4 copy-start.85
  305.3 13.9 %slice-start = ((s8[4718592]{0:T(1024)(128)(4,1)}), s8[4194304]{0:T(1024)(128)(4,1)S(1)}, s32[]{:S(2)}) async-start(s8[4718592]{0:T(1024)(128)(4,1)} %bitcast.143), calls=%async_computation.4 | async-start | bytes 8388608
  308.6 10.6 %slice-start.1 = ((s8[4718592]{0:T(1024)(128)(4,1)}), s8[524288]{0:T(1024)(128)(4,1)S(1)}, s32[]{:S(2)}) async-start(s8[4718592]{0:T(1024)(128)(4,1)} %bitcast.143), calls=%async_computation.5 | async-start | bytes 1048576
  326.3 104.4 %copy-start.1 = (bf16[512,768]{1,0:T(8,128)(2,1)}, bf16[512,768]{1,0:T(8,128)(2,1)S(1)}, u32[]{:S(2)}) copy-start(bf16[512,768]{1,0:T(8,128)(2,1)S(1)} %get-tuple-element.209.refs_3_) | copy-start | bytes 2359300
  331.9 9.7 %copy-start.97 = (f32[768]{0:T(1024)S(1)}, f32[768]{0:T(1024)}, u32[]{:S(2)}) copy-start(f32[768]{0:T(1024)} %get-tuple-element.133) | copy-start | bytes 9220
  344.8 7.2 %slice-start.8 = ((s8[4718592]{0:T(1024)(128)(4,1)}), s8[4194304]{0:T(1024)(128)(4,1)S(1)}, s32[]{:S(2)}) async-start(s8[4718592]{0:T(1024)(128)(4,1)} %bitcast.174), calls=%async_computation.12 | async-start | bytes 8388608
  345.1 6.9 %copy-start.13 = (bf16[512,768]{1,0:T(8,128)(2,1)}, bf16[512,768]{1,0:T(8,128)(2,1)S(1)}, u32[]{:S(2)}) copy-start(bf16[512,768]{1,0:T(8,128)(2,1)S(1)} %fusion.17.refs_1_) | copy-start | bytes 2359300
  345.1 6.8 %copy-start.96 = (f32[768]{0:T(1024)S(1)}, f32[768]{0:T(1024)}, u32[]{:S(2)}) copy-start(f32[768]{0:T(1024)} %get-tuple-element.130) | copy-start | bytes 9220
  345.1 6.8 %slice-start.9 = ((s8[4718592]{0:T(1024)(128)(4,1)}), s8[524288]{0:T(1024)(128)(4,1)S(1)}, s32[]{:S(2)}) async-start(s8[4718592]{0:T(1024)(128)(4,1)} %bitcast.174), calls=%async_computation.13 | async-start | bytes 1048576
  370.0 8.8 %slice-start.6 = ((s8[4718592]{0:T(1024)(128)(4,1)}), s8[4194304]{0:T(1024)(128)(4,1)S(1)}, s32[]{:S(2)}) async-start(s8[4718592]{0:T(1024)(128)(4,1)} %bitcast.172), calls=%async_computation.10 | async-start | bytes 8388608
  370.1 8.7 %copy-start.14 = (bf16[512,768]{1,0:T(8,128)(2,1)}, bf16[512,768]{1,0:T(8,128)(2,1)S(1)}, u32[]{:S(2)}) copy-start(bf16[512,768]{1,0:T(8,128)(2,1)S(1)} %convert_element_type.257.refs_8_) | copy-start | bytes 2359300
  370.1 8.7 %slice-start.7 = ((s8[4718592]{0:T(1024)(128)(4,1)}), s8[524288]{0:T(1024)(128)(4,1)S(1)}, s32[]{:S(2)}) async-start(s8[4718592]{0:T(1024)(128)(4,1)} %bitcast.172), calls=%async_computation.11 | async-start | bytes 1048576
  420.7 8.5 %copy-start.20 = (bf16[128,768]{1,0:T(8,128)(2,1)}, bf16[128,768]{1,0:T(8,128)(2,1)S(1)}, u32[]{:S(2)}) copy-start(bf16[128,768]{1,0:T(8,128)(2,1)S(1)} %convert_element_type.266.refs_14_) | copy-start | bytes 589828
  421.9 7.2 %copy-start.95 = (f32[12]{0:T(128)S(1)}, f32[12]{0:T(128)}, u32[]{:S(2)}) copy-start(f32[12]{0:T(128)} %get-tuple-element.194) | copy-start | bytes 148
  421.9 9.7 %copy-start = (bf16[768,2304]{1,0:T(8,128)(2,1)S(1)}, bf16[768,2304]{1,0:T(8,128)(2,1)}, u32[]{:S(2)}) copy-start(bf16[768,2304]{1,0:T(8,128)(2,1)} %get-tuple-element.49) | copy-start | bytes 10616836
  440.2 6.3 %copy-start.100 = (f32[12]{0:T(128)S(1)}, f32[12]{0:T(128)}, u32[]{:S(2)}) copy-start(f32[12]{0:T(128)} %get-tuple-element.181) | copy-start | bytes 148
  482.9 1.2 collective-permute-start.9
  484.2 3.7 collective-permute-start.10
  487.9 3.7 collective-permute-start.11
  491.7 19.9 %collective-permute-start.12 = (f32[32,128]{1,0:T(8,128)S(1)}, f32[32,128]{1,0:T(8,128)S(1)}, u32[]{:S(2)}, u32[]{:S(2)}) collective-permute-start(f32[32,128]{1,0:T(8,128)S(1)} %add.528), channel_id=1, source_target_pairs={{0,1},{1,0},{2,3},{3,2},{4,5},{5,4},{6,7},{7,6},{8,9},{9,8},{10,11... | collective-permute-start | bytes 49160 | tf_op jit(solution)/shard_map/ppermute | solution.py:1204
  492.6 20.4 %copy-start.28 = (f32[128,768]{1,0:T(8,128)S(1)}, f32[128,768]{1,0:T(8,128)}, u32[]{:S(2)}) copy-start(f32[128,768]{1,0:T(8,128)} %get-tuple-element.224) | copy-start | bytes 1179652
  507.0 25.8 %copy-start.24 = (bf16[512,192]{1,0:T(8,128)(2,1)}, bf16[512,192]{1,0:T(8,128)(2,1)S(1)}, u32[]{:S(2)}) copy-start(bf16[512,192]{1,0:T(8,128)(2,1)S(1)} %convert_element_type.274.refs_0_) | copy-start | bytes 589828
  507.0 26.1 %collective-permute-start.6 = (bf16[512,192]{1,0:T(8,128)(2,1)S(1)}, bf16[512,192]{1,0:T(8,128)(2,1)S(1)}, u32[]{:S(2)}, u32[]{:S(2)}) collective-permute-start(bf16[512,192]{1,0:T(8,128)(2,1)S(1)} %convert_element_type.274.refs_0_), channel_id=1, source_target_pairs={{0,1},{1,2},{2,3},{3,0},{4,5},{5,6},{6,7},{7,4},{8,9},{9,10},{10,1... | collective-permute-start | bytes 589832 | tf_op jit(solution)/shard_map/ppermute | solution.py:1168
  509.1 24.0 %collective-permute-start.7 = (bf16[512,192]{1,0:T(8,128)(2,1)S(1)}, bf16[512,192]{1,0:T(8,128)(2,1)S(1)}, u32[]{:S(2)}, u32[]{:S(2)}) collective-permute-start(bf16[512,192]{1,0:T(8,128)(2,1)S(1)} %convert_element_type.274.refs_0_), channel_id=1, source_target_pairs={{0,2},{1,3},{2,0},{3,1},{4,6},{5,7},{6,4},{7,5},{8,10},{9,11},{10,... | collective-permute-start | bytes 589832 | tf_op jit(solution)/shard_map/ppermute | solution.py:1168
  510.5 24.0 %collective-permute-start.8 = (bf16[512,192]{1,0:T(8,128)(2,1)S(1)}, bf16[512,192]{1,0:T(8,128)(2,1)}, u32[]{:S(2)}, u32[]{:S(2)}) collective-permute-start(bf16[512,192]{1,0:T(8,128)(2,1)S(1)} %convert_element_type.274.refs_0_), channel_id=1, source_target_pairs={{0,3},{1,0},{2,1},{3,2},{4,7},{5,4},{6,5},{7,6},{8,11},{9,8},{10,9... | collective-permute-start | bytes 589832 | tf_op jit(solution)/shard_map/ppermute | solution.py:1168
  511.6 21.5 %collective-permute-start.13 = (f32[32,128]{1,0:T(8,128)S(1)}, f32[32,128]{1,0:T(8,128)S(1)}, u32[]{:S(2)}, u32[]{:S(2)}) collective-permute-start(f32[32,128]{1,0:T(8,128)S(1)} %add.529), channel_id=1, source_target_pairs={{0,2},{1,3},{2,0},{3,1},{4,6},{5,7},{6,4},{7,5},{8,10},{9,11},{10,... | collective-permute-start | bytes 49160 | tf_op jit(solution)/shard_map/ppermute | solution.py:1204
  513.8 19.0 %copy-start.104 = (bf16[768]{0:T(1024)(128)(2,1)S(1)}, bf16[768]{0:T(1024)(128)(2,1)}, u32[]{:S(2)}) copy-start(bf16[768]{0:T(1024)(128)(2,1)} %get-tuple-element.163) | copy-start | bytes 4612
  513.8 19.0 %copy-start.88 = (bf16[768]{0:T(1024)(128)(2,1)S(1)}, bf16[768]{0:T(1024)(128)(2,1)}, u32[]{:S(2)}) copy-start(bf16[768]{0:T(1024)(128)(2,1)} %get-tuple-element.220) | copy-start | bytes 4612
  546.3 3.0 collective-permute-start.14
  549.7 17.6 %collective-permute-start.15 = (bf16[2368,128]{1,0:T(8,128)(2,1)S(1)}, bf16[2368,128]{1,0:T(8,128)(2,1)S(1)}, u32[]{:S(2)}, u32[]{:S(2)}) collective-permute-start(bf16[2368,128]{1,0:T(8,128)(2,1)S(1)} %get-tuple-element.177), channel_id=1, source_target_pairs={{8,0},{12,4},{24,16},{28,20},{9,1},{13,5},{25,17},{29,21},{10,2},{... | collective-permute-start | bytes 1818632 | tf_op jit(solution)/shard_map/ppermute | solution.py:1122
  551.0 17.6 %collective-permute-start.17 = (bf16[2368,128]{1,0:T(8,128)(2,1)S(1)}, bf16[2368,128]{1,0:T(8,128)(2,1)S(1)}, u32[]{:S(2)}, u32[]{:S(2)}) collective-permute-start(bf16[2368,128]{1,0:T(8,128)(2,1)S(1)} %get-tuple-element.178), channel_id=1, source_target_pairs={{16,0},{20,4},{24,8},{28,12},{17,1},{21,5},{25,9},{29,13},{18,2},{... | collective-permute-start | bytes 1818632 | tf_op jit(solution)/shard_map/ppermute | solution.py:1122
  568.9 16.8 %collective-permute-start.16 = (bf16[2368,128]{1,0:T(8,128)(2,1)S(1)}, bf16[2368,128]{1,0:T(8,128)(2,1)S(1)}, u32[]{:S(2)}, u32[]{:S(2)}) collective-permute-start(bf16[2368,128]{1,0:T(8,128)(2,1)S(1)} %get-tuple-element.175), channel_id=1, source_target_pairs={{16,0},{20,4},{24,8},{28,12},{17,1},{21,5},{25,9},{29,13},{18,2},{... | collective-permute-start | bytes 1818632 | tf_op jit(solution)/shard_map/ppermute | solution.py:1122
  570.2 16.8 %collective-permute-start.18 = (bf16[2368,128]{1,0:T(8,128)(2,1)S(1)}, bf16[2368,128]{1,0:T(8,128)(2,1)S(1)}, u32[]{:S(2)}, u32[]{:S(2)}) collective-permute-start(bf16[2368,128]{1,0:T(8,128)(2,1)S(1)} %get-tuple-element.176), channel_id=1, source_target_pairs={{8,0},{12,4},{24,16},{28,20},{9,1},{13,5},{25,17},{29,21},{10,2},{... | collective-permute-start | bytes 1818632 | tf_op jit(solution)/shard_map/ppermute | solution.py:1122
  588.0 22.7 %copy-start.3 = (f32[603008]{0:T(1024)S(1)}, f32[603008]{0:T(1024)}, u32[]{:S(2)}) copy-start(f32[603008]{0:T(1024)} %param.37) | copy-start | bytes 7236100
  594.2 13.1 %all-to-all-start = ((f32[32,8,128]{2,1,0:T(8,128)}), f32[32,8,128]{2,1,0:T(8,128)S(1)}, u32[]{:S(2)}, u32[]{:S(2)}) async-start(f32[32,8,128]{2,1,0:T(8,128)} %broadcast_in_dim_broadcast_in_dim_broadcast_in_dim.3), calls=%async_computation.1 | async-start | bytes 262144 | tf_op jit(solution)/shard_map/all_to_all | solution.py:1212
  (77 other events, 201.9 us)
Sparse Core Ops, SparseCore 0:
  14.5 223.7 all-gather.2
  480.0 75.8 reduce-scatter.1

commit v6 on v5

--- a/solution.py
+++ b/solution.py
@@ -1444,8 +1444,11 @@
     dp_index = lax.axis_index("dp")
     geometry = Geometry(dp_count, code_count, shard_rows)
     own_offset = lax.rem((dp_index * code_count + code_index) * shard_rows + geometry.phase, TILE)
-    own_window = lax.dynamic_update_slice(
-        jnp.zeros((geometry.window, 128), F32), params.reshape(shard_rows, 128), (own_offset, 0)
+    spare = geometry.window - shard_rows
+    own_window = lax.dynamic_slice(
+        jnp.pad(params.reshape(shard_rows, 128), ((TILE, spare), (0, 0))),
+        (TILE - own_offset, 0),
+        (geometry.window, 128),
     ).astype(BF)
     windows = lax.all_gather(own_window, ("dp", "code"), axis=0, tiled=False)
     where = starts()

time: 635 us -> 629 us (level)
  no operation moved by 1% of the time
where the time goes in v6:
time: 629 us; the launch traced here: 620 us
  waiting for transfers between devices  249 us (40%)
  Pallas kernels  161 us (26%)
  matrix products  77.9 us (12%)
  other arithmetic  41 us (7%)
  local copies, waits for them, and re-layouts  36.1 us (6%)
  starting transfers between devices  30.8 us (5%)
  between operations  24.2 us (4%)
    all_gather x1, waiting for transfers between devices, local(): windows = lax.all_gather(own_window, ('dp', 'code'), axis=0, tiled=False)  205 us
    ppermute x4, waiting for transfers between devices, reduce_front(): lax.ppermute(halves[side], 'dp', [(i, i - bit) for i in range(dp_count) i...  31.4 us
    dot_general x10, matrix products, dot_nt(): lax.dot_general(left, right, (((1,), (1,)), ((), ())), preferred_element_...  29 us
    dot_general x11, matrix products, dot_nn(): lax.dot_general(left, right, (((1,), (0,)), ((), ())), preferred_element_...  27.2 us
    pallas_call x2, Pallas kernels, conv_call(): pl.pallas_call(kernel, grid=(steps,), in_specs=[pl.BlockSpec(padded.shape...  25.2 us
    pallas_call x2, Pallas kernels, attention_backward(): pl.pallas_call(kernel, grid=(HEADS // heads,), in_specs=specs + [specs[0]...  25 us
    pallas_call x2, Pallas kernels, conv_weight_grad(): pl.pallas_call(functools.partial(conv_weight_kernel, chunk=chunk), grid_s...  23.6 us
    pallas_call x1, Pallas kernels, unpack(): pl.pallas_call(functools.partial(unpack_kernel, jobs=jobs, stages=stages)...  20.1 us
  transfers between devices with their start and end apart: 22, of which 10 were waited for; matrix products, arithmetic and copies ran while one was open for 6% of the time, Pallas kernels for 9%

profile of v6, /device:TPU:0, one launch (start us, length us, event | category | flops | bytes accessed | tf_op | source)
XLA Modules:
  0.0 619.6 jit_solution(10647459362041900859)
XLA Ops:
  7.3 3.3 fusion.9
  10.7 3.1 collective-permute-start.3
  13.7 2.6 collective-permute-start.4
  29.5 205.1 %all-gather.3.cloned.1.call-done = bf16[151552,128]{1,0:T(8,128)(2,1)} async-done(((bf16[4736,128]{1,0:T(8,128)(2,1)}), bf16[151552,128]{1,0:T(8,128)(2,1)}) %all-gather.3.cloned.1.call-update) | async-done | bytes 38797328 | tf_op jit(solution)/shard_map/all_gather | solution.py:1453
  234.5 2.6 shard_map.351
  237.2 5.9 shard_map.352.weight_ref
  246.0 12.1 %shard_map.353 = f32[512,192]{1,0:T(8,128)} custom-call(f32[640,192]{1,0:T(8,128)} %pad_convert_fusion.2.in_ref, bf16[6144,192]{1,0:T(8,128)(2,1)} %shard_map.352.weight_ref, bf16[4,192]{1,0:T(4,128)(2,1)} %constant.215.clone.mask_ref), custom_call_target="tpu_custom_call" | custom-call | tf_op jit(solution)/shard_map/pallas_call | solution.py:232
  258.1 2.1 fusion.55.refs_0_
  260.1 1.9 collective-permute-start.1
  262.1 2.6 collective-permute-start.2
  264.7 20.1 %shard_map.355 = (bf16[768,2304]{1,0:T(8,128)(2,1)}, bf16[768,768]{1,0:T(8,128)(2,1)}, bf16[768,3072]{1,0:T(8,128)(2,1)}, bf16[3072,768]{1,0:T(8,128)(2,1)}, bf1...) custom-call(bf16[32,4736,128]{2,1,0:T(8,128)(2,1)} %bitcast.142), custom_call_target="tpu_custom_call" | custom-call | tf_op jit(solution)/shard_map/pallas_call | solution.py:875
  293.1 1.8 copy.73
  295.0 2.0 fusion.93.span_ref
  298.0 2.0 shard_map.354
  300.1 3.0 fusion.194
  304.1 3.5 fusion.8.q_ref.k_ref.v_ref
  308.3 4.5 shard_map.356
  312.9 1.5 fusion.195
  314.8 2.3 multiply_convert_fusion.2
  317.2 3.5 fusion.196
  323.2 3.4 fusion.6.q_ref.k_ref.v_ref
  327.5 9.9 %shard_map.357 = (bf16[512,768]{1,0:T(8,128)(2,1)}, f32[16,512]{1,0:T(8,128)}) custom-call(bf16[512,2304]{1,0:T(8,128)(2,1)} %fusion.6.q_ref.k_ref.v_ref, bf16[512,2304]{1,0:T(8,128)(2,1)} %fusion.6.q_ref.k_ref.v_ref, bf16[512,2304]{1,0:T(8,128)(2,1)} %fusion.6.q_ref.k_ref.v_ref, f32[16,512]{1,0:T(8,128)} %pad.66.gate_ref, f32[16,1024]{1,0:T(8,128)} %fusion.93.span_ref, ...), custom_call_target="tpu_custom_call" | custom-call | tf_op jit(solution)/shard_map/pallas_call | solution.py:493
  337.4 2.4 fusion.198
  340.8 6.8 %multiply_convert_fusion = (bf16[512,3072]{1,0:T(8,128)(2,1)S(1)}, f32[512,3072]{1,0:T(8,128)}) fusion(f32[3072]{0:T(1024)S(1)} %bitcast.165, bf16[512,768]{1,0:T(8,128)(2,1)S(1)} %fusion.18.refs_1_, bf16[768,3072]{1,0:T(8,128)(2,1)} %get-tuple-element.60), kind=kOutput, calls=%fused_computation.6 | convolution fusion | flops 2425356288 | bytes 14954496 | tf_op jit(solution)/shard_map/dot_general | solution.py:144
  347.7 2.8 fusion.199
  353.8 7.9 %shard_map.358 = (f32[8,128]{1,0:T(8,128)}, f32[512,768]{1,0:T(8,128)}, f32[1536,128]{1,0:T(8,128)}) custom-call(bf16[512,768]{1,0:T(8,128)(2,1)} %add_convert_fusion.1.in_ref, bf16[768,256]{1,0:T(8,128)(2,1)} %get-tuple-element.62.weight_ref, bf16[1024,256]{1,0:T(8,128)(2,1)} %pad_maximum_fusion.code_ref, s32[8,1024]{1,0:T(8,128)} %broadcast_in_dim.71.name_ref, ...), custom_call_target="tpu_custom_call" | custom-call | tf_op jit(solution)/shard_map/pallas_call | solution.py:1415
  361.7 2.8 multiply_reduce_fusion
  365.7 8.4 %fusion.188 = (f32[3072]{0:T(1024)}, bf16[512,3072]{1,0:T(8,128)(2,1)S(1)}) fusion(f32[512,3072]{1,0:T(8,128)} %get-tuple-element.214, f32[3072]{0:T(1024)S(1)} %bitcast.166, bf16[512,768]{1,0:T(8,128)(2,1)S(1)} %convert_element_type.259.refs_8_, bf16[3072,768]{1,0:T(8,128)(2,1)} %get-tuple-element.61), kind=kOutput, calls=%fused_computation.352 | convolution fusion | flops 2434790400 | bytes 14966784 | tf_op jit(solution)/shard_map/dot_general | solution.py:148
  374.1 3.7 multiply_reduce_fusion.1
  380.2 1.7 convolution_convert_fusion.up_ref
  381.9 17.8 %shard_map.359 = (bf16[512,2304]{1,0:T(8,128)(2,1)}, f32[8,768]{1,0:T(8,128)}, f32[16,512]{1,0:T(8,128)}, f32[16,1024]{1,0:T(8,128)}) custom-call(bf16[512,2304]{1,0:T(8,128)(2,1)} %fusion.6.q_ref.k_ref.v_ref, bf16[512,2304]{1,0:T(8,128)(2,1)} %fusion.6.q_ref.k_ref.v_ref, bf16[512,2304]{1,0:T(8,128)(2,1)} %fusion.6.q_ref.k_ref.v_ref, ...), custom_call_target="tpu_custom_call" | custom-call | tf_op jit(solution)/shard_map/pallas_call | solution.py:682
  399.6 1.5 fusion.129
  401.7 4.7 fusion.200
  407.1 1.4 multiply_reduce_fusion.12
  409.5 2.3 fusion.189
  411.8 2.4 multiply_reduce_fusion.13
  416.2 7.2 %shard_map.360 = (bf16[128,2304]{1,0:T(8,128)(2,1)}, f32[8,768]{1,0:T(8,128)}, f32[16,128]{1,0:T(8,128)}, f32[16,1024]{1,0:T(8,128)}) custom-call(bf16[128,2304]{1,0:T(8,128)(2,1)} %fusion.8.q_ref.k_ref.v_ref, bf16[128,2304]{1,0:T(8,128)(2,1)} %fusion.8.q_ref.k_ref.v_ref, bf16[128,2304]{1,0:T(8,128)(2,1)} %fusion.8.q_ref.k_ref.v_ref, ...), custom_call_target="tpu_custom_call" | custom-call | tf_op jit(solution)/shard_map/pallas_call | solution.py:682
  425.9 2.4 convolution_add_fusion.5
  429.2 1.7 fusion.185
  437.5 2.4 broadcast_multiply_fusion
  440.9 17.6 %shard_map.365 = (bf16[9216,128]{1,0:T(8,128)(2,1)}, bf16[12288,128]{1,0:T(8,128)(2,1)}, bf16[4608,128]{1,0:T(8,128)(2,1)}, bf16[9216,128]{1,0:T(8,128)(2,1)}, b...) custom-call(s32[18]{0:T(128)} %fusion.166.table_ref, ...), custom_call_target="tpu_custom_call" | custom-call | tf_op jit(solution)/shard_map/pallas_call | solution.py:778
  458.5 4.6 shard_map.366.refs_8_
  463.1 2.4 shard_map.367.refs_9_
  465.5 8.0 %shard_map.368 = bf16[8,4736,128]{2,1,0:T(8,128)(2,1)} custom-call(s32[2]{0:T(128)} %pad_add_fusion.1.code_ref, bf16[9216,128]{1,0:T(8,128)(2,1)} %get-tuple-element.75.refs_0_, bf16[12288,128]{1,0:T(8,128)(2,1)} %get-tuple-element.76.refs_1_, bf16[4608,128]{1,0:T(8,128)(2,1)} %get-tuple-element.77.refs_2_, bf16[9216,128]{1,0:T(8,128)(2,1)} %get-tuple-element.78.refs_3_, ...), custom_call_target="tpu_custom_call" | custom-call | tf_op jit(solution)/shard_map/pallas_call | solution.py:1080
  479.6 1.9 collective-permute-done.10
  481.5 1.5 collective-permute-start.11
  483.2 2.1 collective-permute-done.11
  486.2 13.2 %shard_map.362 = f32[512,192]{1,0:T(8,128)} custom-call(f32[640,192]{1,0:T(8,128)} %pad_convert_fusion.1.in_ref, bf16[6144,192]{1,0:T(8,128)(2,1)} %shard_map.352.weight_ref, bf16[4,192]{1,0:T(4,128)(2,1)} %constant.215.clone.mask_ref), custom_call_target="tpu_custom_call" | custom-call | tf_op jit(solution)/shard_map/pallas_call | solution.py:232
  500.5 2.0 collective-permute-start.6
  502.5 1.5 collective-permute-start.7
  505.0 1.5 collective-permute-start.13
  507.3 19.0 %shard_map.361.refs_0_ = bf16[10368,128]{1,0:T(8,128)(2,1)} custom-call(s32[6]{0:T(128)} %fusion.165.tap_ref, f32[4,192,640]{2,1,0:T(8,128)} %bitcast.148, bf16[4,512,192]{2,1,0:T(8,128)(2,1)} %bitcast.151, f32[4,192]{1,0:T(4,128)} %constant.217.clone.mask_ref), custom_call_target="tpu_custom_call" | custom-call | tf_op jit(solution)/shard_map/pallas_call | solution.py:329
  527.8 2.3 shard_map.363
  530.2 2.1 multiply_reduce_fusion.3
  534.3 3.8 shard_map.364
  538.1 1.5 slice.294
  539.8 2.9 collective-permute-done.14
  545.6 15.2 %collective-permute-done.15 = bf16[2368,128]{1,0:T(8,128)(2,1)S(1)} collective-permute-done((bf16[2368,128]{1,0:T(8,128)(2,1)S(1)}, bf16[2368,128]{1,0:T(8,128)(2,1)S(1)}, u32[]{:S(2)}, u32[]{:S(2)}) %collective-permute-start.15) | collective-permute-done | bytes 606240 | tf_op jit(solution)/shard_map/ppermute | solution.py:1122
  563.6 1.5 collective-permute-start.18
  565.1 14.0 %collective-permute-done.16 = bf16[2368,128]{1,0:T(8,128)(2,1)S(1)} collective-permute-done((bf16[2368,128]{1,0:T(8,128)(2,1)S(1)}, bf16[2368,128]{1,0:T(8,128)(2,1)S(1)}, u32[]{:S(2)}, u32[]{:S(2)}) %collective-permute-start.16) | collective-permute-done | bytes 606240 | tf_op jit(solution)/shard_map/ppermute | solution.py:1122
  580.6 4.5 fusion.10
  586.4 5.0 all-to-all-start
  594.6 5.2 all-to-all-done
  603.3 7.0 %fusion.178 = (bf16[603008]{0:T(1024)(128)(2,1)}, f32[603008]{0:T(1024)}, f32[603008]{0:T(1024)}, f32[603008]{0:T(1024)}) fusion(f32[603008]{0:T(1024)} %param.37, f32[]{:T(128)} %bitcast.36, f32[]{:T(128)} %bitcast.35, f32[]{:T(128)S(6)} %min.7, f32[]{:T(128)} %bitcast.32, bf16[4711,128]{1,0:T(8,128)(2,1)S(1)} %get-tuple-element.151, f32[603008]{0:T(1024)} %param.39, ...), kind=kLoop, calls=%fused_computation.346 | loop fusion | flops 11457152 | bytes 16884240 | tf_op jit(solution)/shard_map/convert_element_type | solution.py:1672
  (396 shorter events, 76.2 us)
Async XLA Ops:
  7.2 227.4 %all-gather.3.cloned.1.call-start = ((), (), s32[]{:S(2)}) async-start(), calls=%async_computation.3 | async-start | bytes 40009728 | tf_op jit(solution)/shard_map/all_gather | solution.py:1453
  7.2 11.1 %copy-start.77 = (s32[1,496]{1,0:T(1,128)S(1)}, s32[1,496]{1,0:T(1,128)}, u32[]{:S(2)}) copy-start(s32[1,496]{1,0:T(1,128)} %param.34) | copy-start | bytes 5956
  7.2 14.4 %copy-start.86 = (s32[1,496]{1,0:T(1,128)S(1)}, s32[1,496]{1,0:T(1,128)}, u32[]{:S(2)}) copy-start(s32[1,496]{1,0:T(1,128)} %param.35) | copy-start | bytes 5956
  10.6 570.0 %reduce-scatter.2.cloned.1.call-start = ((), (), s32[]{:S(2)}) async-start(), calls=%async_computation.2 | async-start | bytes 10911744 | tf_op jit(solution)/shard_map/reduce_scatter | solution.py:1635
  10.7 17.9 %collective-permute-start.3 = (bf16[256,256]{1,0:T(8,128)(2,1)S(1)}, bf16[256,256]{1,0:T(8,128)(2,1)S(1)}, u32[]{:S(2)}, u32[]{:S(2)}) collective-permute-start(bf16[256,256]{1,0:T(8,128)(2,1)S(1)} %copy-done.34), channel_id=1, source_target_pairs={{0,1},{1,2},{2,3},{3,0},{4,5},{5,6},{6,7},{7,4},{8,9},{9,10},{10,1... | collective-permute-start | bytes 393224 | tf_op jit(solution)/shard_map/ppermute | solution.py:1168
  13.7 14.9 %collective-permute-start.4 = (bf16[256,256]{1,0:T(8,128)(2,1)S(1)}, bf16[256,256]{1,0:T(8,128)(2,1)S(1)}, u32[]{:S(2)}, u32[]{:S(2)}) collective-permute-start(bf16[256,256]{1,0:T(8,128)(2,1)S(1)} %copy-done.34), channel_id=1, source_target_pairs={{0,2},{1,3},{2,0},{3,1},{4,6},{5,7},{6,4},{7,5},{8,10},{9,11},{10,... | collective-permute-start | bytes 393224 | tf_op jit(solution)/shard_map/ppermute | solution.py:1168
  16.3 12.3 %collective-permute-start.5 = (bf16[256,256]{1,0:T(8,128)(2,1)S(1)}, bf16[256,256]{1,0:T(8,128)(2,1)S(1)}, u32[]{:S(2)}, u32[]{:S(2)}) collective-permute-start(bf16[256,256]{1,0:T(8,128)(2,1)S(1)} %copy-done.34), channel_id=1, source_target_pairs={{0,3},{1,0},{2,1},{3,2},{4,7},{5,4},{6,5},{7,6},{8,11},{9,8},{10,9... | collective-permute-start | bytes 393224 | tf_op jit(solution)/shard_map/ppermute | solution.py:1168
  18.4 239.7 %copy-start.48 = (pred[512]{0:T(512)(128)(4,1)}, pred[512]{0:T(512)(128)(4,1)S(1)}, u32[]{:S(2)}) copy-start(pred[512]{0:T(512)(128)(4,1)S(1)} %get-tuple-element.170) | copy-start | bytes 1540
  21.1 223.4 %copy-start.60 = (f32[512]{0:T(512)}, f32[512]{0:T(512)S(1)}, u32[]{:S(2)}) copy-start(f32[512]{0:T(512)S(1)} %fusion.162) | copy-start | bytes 6148
  23.3 213.8 %copy-start.29 = (bf16[128,128]{1,0:T(8,128)(2,1)}, bf16[128,128]{1,0:T(8,128)(2,1)S(1)}, u32[]{:S(2)}) copy-start(bf16[128,128]{1,0:T(8,128)(2,1)S(1)} %fusion.70.near_ref) | copy-start | bytes 98308
  23.4 234.7 %copy-start.35 = (s32[512]{0:T(512)}, s32[512]{0:T(512)S(1)}, u32[]{:S(2)}) copy-start(s32[512]{0:T(512)S(1)} %fusion.253) | copy-start | bytes 6148
  237.1 5.9 copy-start.21
  237.2 5.9 copy-start.25
  260.1 24.8 %copy-start.52 = (f32[40,128]{1,0:T(8,128)S(1)}, f32[40,128]{1,0:T(8,128)}, u32[]{:S(2)}) copy-start(f32[40,128]{1,0:T(8,128)} %get-tuple-element.51) | copy-start | bytes 61444
  260.1 25.6 %copy-start.43 = (f32[8,24]{1,0:T(8,128)S(1)}, f32[8,24]{1,0:T(8,128)}, u32[]{:S(2)}) copy-start(f32[8,24]{1,0:T(8,128)} %constant.211.clone) | copy-start | bytes 2308
  260.1 37.8 %collective-permute-start = (f32[128,192]{1,0:T(8,128)}, f32[128,192]{1,0:T(8,128)}, u32[]{:S(2)}, u32[]{:S(2)}) collective-permute-start(f32[128,192]{1,0:T(8,128)} %fusion.55.refs_0_), channel_id=1, source_target_pairs={{0,1},{1,2},{2,3},{3,0},{4,5},{5,6},{6,7},{7,4},{8,9},{9,10},{10,1... | collective-permute-start | bytes 294920 | tf_op jit(solution)/shard_map/ppermute | solution.py:1168
  260.1 37.8 %collective-permute-start.1 = (f32[128,192]{1,0:T(8,128)}, f32[128,192]{1,0:T(8,128)}, u32[]{:S(2)}, u32[]{:S(2)}) collective-permute-start(f32[128,192]{1,0:T(8,128)} %fusion.55.refs_0_), channel_id=1, source_target_pairs={{0,2},{1,3},{2,0},{3,1},{4,6},{5,7},{6,4},{7,5},{8,10},{9,11},{10,... | collective-permute-start | bytes 294920 | tf_op jit(solution)/shard_map/ppermute | solution.py:1168
  262.1 35.9 %collective-permute-start.2 = (f32[128,192]{1,0:T(8,128)}, f32[128,192]{1,0:T(8,128)}, u32[]{:S(2)}, u32[]{:S(2)}) collective-permute-start(f32[128,192]{1,0:T(8,128)} %fusion.55.refs_0_), channel_id=1, source_target_pairs={{0,3},{1,0},{2,1},{3,2},{4,7},{5,4},{6,5},{7,6},{8,11},{9,8},{10,9... | collective-permute-start | bytes 294920 | tf_op jit(solution)/shard_map/ppermute | solution.py:1168
  284.8 5.1 copy-start.59
  284.8 5.7 copy-start.5
  284.9 5.7 copy-start.19
  294.9 5.1 copy-start.49
  294.9 5.1 copy-start.56
  295.0 5.1 copy-start.61
  295.0 5.1 copy-start.70
  295.0 5.1 copy-start.82
  297.9 5.3 copy-start.85
  298.0 5.4 copy-start.79
  298.0 6.1 copy-start.74
  300.1 14.7 %slice-start = ((s8[4718592]{0:T(1024)(128)(4,1)}), s8[4194304]{0:T(1024)(128)(4,1)S(1)}, s32[]{:S(2)}) async-start(s8[4718592]{0:T(1024)(128)(4,1)} %bitcast.143), calls=%async_computation.4 | async-start | bytes 8388608
  303.1 125.2 %copy-start.8 = (bf16[128,768]{1,0:T(8,128)(2,1)}, bf16[128,768]{1,0:T(8,128)(2,1)S(1)}, u32[]{:S(2)}) copy-start(bf16[128,768]{1,0:T(8,128)(2,1)S(1)} %get-tuple-element.201.refs_7_) | copy-start | bytes 589828
  304.1 10.7 %slice-start.1 = ((s8[4718592]{0:T(1024)(128)(4,1)}), s8[524288]{0:T(1024)(128)(4,1)S(1)}, s32[]{:S(2)}) async-start(s8[4718592]{0:T(1024)(128)(4,1)} %bitcast.143), calls=%async_computation.5 | async-start | bytes 1048576
  307.6 5.3 copy-start.7
  307.6 5.3 copy-start.67
  321.9 103.1 %copy-start.1 = (bf16[512,768]{1,0:T(8,128)(2,1)}, bf16[512,768]{1,0:T(8,128)(2,1)S(1)}, u32[]{:S(2)}) copy-start(bf16[512,768]{1,0:T(8,128)(2,1)S(1)} %get-tuple-element.209.refs_3_) | copy-start | bytes 2359300
  327.5 9.9 %copy-start.81 = (f32[768]{0:T(1024)S(1)}, f32[768]{0:T(1024)}, u32[]{:S(2)}) copy-start(f32[768]{0:T(1024)} %get-tuple-element.133) | copy-start | bytes 9220
  340.5 7.2 %slice-start.8 = ((s8[4718592]{0:T(1024)(128)(4,1)}), s8[4194304]{0:T(1024)(128)(4,1)S(1)}, s32[]{:S(2)}) async-start(s8[4718592]{0:T(1024)(128)(4,1)} %bitcast.174), calls=%async_computation.12 | async-start | bytes 8388608
  340.8 6.9 %copy-start.9 = (bf16[512,768]{1,0:T(8,128)(2,1)}, bf16[512,768]{1,0:T(8,128)(2,1)S(1)}, u32[]{:S(2)}) copy-start(bf16[512,768]{1,0:T(8,128)(2,1)S(1)} %fusion.18.refs_1_) | copy-start | bytes 2359300
  340.8 6.8 %copy-start.80 = (f32[768]{0:T(1024)S(1)}, f32[768]{0:T(1024)}, u32[]{:S(2)}) copy-start(f32[768]{0:T(1024)} %get-tuple-element.130) | copy-start | bytes 9220
  340.8 6.8 %slice-start.9 = ((s8[4718592]{0:T(1024)(128)(4,1)}), s8[524288]{0:T(1024)(128)(4,1)S(1)}, s32[]{:S(2)}) async-start(s8[4718592]{0:T(1024)(128)(4,1)} %bitcast.174), calls=%async_computation.13 | async-start | bytes 1048576
  365.6 8.5 %slice-start.6 = ((s8[4718592]{0:T(1024)(128)(4,1)}), s8[4194304]{0:T(1024)(128)(4,1)S(1)}, s32[]{:S(2)}) async-start(s8[4718592]{0:T(1024)(128)(4,1)} %bitcast.172), calls=%async_computation.10 | async-start | bytes 8388608
  365.7 8.4 %copy-start.10 = (bf16[512,768]{1,0:T(8,128)(2,1)}, bf16[512,768]{1,0:T(8,128)(2,1)S(1)}, u32[]{:S(2)}) copy-start(bf16[512,768]{1,0:T(8,128)(2,1)S(1)} %convert_element_type.259.refs_8_) | copy-start | bytes 2359300
  365.7 8.4 %slice-start.7 = ((s8[4718592]{0:T(1024)(128)(4,1)}), s8[524288]{0:T(1024)(128)(4,1)S(1)}, s32[]{:S(2)}) async-start(s8[4718592]{0:T(1024)(128)(4,1)} %bitcast.172), calls=%async_computation.11 | async-start | bytes 1048576
  416.2 9.7 %copy-start = (bf16[768,2304]{1,0:T(8,128)(2,1)S(1)}, bf16[768,2304]{1,0:T(8,128)(2,1)}, u32[]{:S(2)}) copy-start(bf16[768,2304]{1,0:T(8,128)(2,1)} %get-tuple-element.49) | copy-start | bytes 10616836
  434.6 5.6 copy-start.83
  476.5 1.2 collective-permute-start.9
  477.8 3.7 collective-permute-start.10
  481.5 3.7 collective-permute-start.11
  485.3 19.7 %collective-permute-start.12 = (f32[32,128]{1,0:T(8,128)S(1)}, f32[32,128]{1,0:T(8,128)S(1)}, u32[]{:S(2)}, u32[]{:S(2)}) collective-permute-start(f32[32,128]{1,0:T(8,128)S(1)} %add.533), channel_id=1, source_target_pairs={{0,1},{1,0},{2,3},{3,2},{4,5},{5,4},{6,7},{7,6},{8,9},{9,8},{10,11... | collective-permute-start | bytes 49160 | tf_op jit(solution)/shard_map/ppermute | solution.py:1204
  486.2 20.2 %copy-start.24 = (f32[128,768]{1,0:T(8,128)S(1)}, f32[128,768]{1,0:T(8,128)}, u32[]{:S(2)}) copy-start(f32[128,768]{1,0:T(8,128)} %get-tuple-element.224) | copy-start | bytes 1179652
  486.2 20.2 %copy-start.37 = (s32[512]{0:T(512)S(1)}, s32[512]{0:T(512)}, u32[]{:S(2)}) copy-start(s32[512]{0:T(512)} %copy-done.35) | copy-start | bytes 6148
  486.2 20.2 %copy-start.50 = (pred[512]{0:T(512)(128)(4,1)S(1)}, pred[512]{0:T(512)(128)(4,1)}, u32[]{:S(2)}) copy-start(pred[512]{0:T(512)(128)(4,1)} %copy-done.48) | copy-start | bytes 1540
  500.5 25.8 %copy-start.20 = (bf16[512,192]{1,0:T(8,128)(2,1)}, bf16[512,192]{1,0:T(8,128)(2,1)S(1)}, u32[]{:S(2)}) copy-start(bf16[512,192]{1,0:T(8,128)(2,1)S(1)} %convert_element_type.276.refs_0_) | copy-start | bytes 589828
  500.5 26.0 %collective-permute-start.6 = (bf16[512,192]{1,0:T(8,128)(2,1)S(1)}, bf16[512,192]{1,0:T(8,128)(2,1)S(1)}, u32[]{:S(2)}, u32[]{:S(2)}) collective-permute-start(bf16[512,192]{1,0:T(8,128)(2,1)S(1)} %convert_element_type.276.refs_0_), channel_id=1, source_target_pairs={{0,1},{1,2},{2,3},{3,0},{4,5},{5,6},{6,7},{7,4},{8,9},{9,10},{10,1... | collective-permute-start | bytes 589832 | tf_op jit(solution)/shard_map/ppermute | solution.py:1168
  502.5 23.9 %collective-permute-start.7 = (bf16[512,192]{1,0:T(8,128)(2,1)S(1)}, bf16[512,192]{1,0:T(8,128)(2,1)S(1)}, u32[]{:S(2)}, u32[]{:S(2)}) collective-permute-start(bf16[512,192]{1,0:T(8,128)(2,1)S(1)} %convert_element_type.276.refs_0_), channel_id=1, source_target_pairs={{0,2},{1,3},{2,0},{3,1},{4,6},{5,7},{6,4},{7,5},{8,10},{9,11},{10,... | collective-permute-start | bytes 589832 | tf_op jit(solution)/shard_map/ppermute | solution.py:1168
  504.0 23.8 %collective-permute-start.8 = (bf16[512,192]{1,0:T(8,128)(2,1)S(1)}, bf16[512,192]{1,0:T(8,128)(2,1)}, u32[]{:S(2)}, u32[]{:S(2)}) collective-permute-start(bf16[512,192]{1,0:T(8,128)(2,1)S(1)} %convert_element_type.276.refs_0_), channel_id=1, source_target_pairs={{0,3},{1,0},{2,1},{3,2},{4,7},{5,4},{6,5},{7,6},{8,11},{9,8},{10,9... | collective-permute-start | bytes 589832 | tf_op jit(solution)/shard_map/ppermute | solution.py:1168
  505.0 21.4 %collective-permute-start.13 = (f32[32,128]{1,0:T(8,128)S(1)}, f32[32,128]{1,0:T(8,128)S(1)}, u32[]{:S(2)}, u32[]{:S(2)}) collective-permute-start(f32[32,128]{1,0:T(8,128)S(1)} %add.534), channel_id=1, source_target_pairs={{0,2},{1,3},{2,0},{3,1},{4,6},{5,7},{6,4},{7,5},{8,10},{9,11},{10,... | collective-permute-start | bytes 49160 | tf_op jit(solution)/shard_map/ppermute | solution.py:1204
  507.3 19.0 %copy-start.87 = (bf16[768]{0:T(1024)(128)(2,1)S(1)}, bf16[768]{0:T(1024)(128)(2,1)}, u32[]{:S(2)}) copy-start(bf16[768]{0:T(1024)(128)(2,1)} %get-tuple-element.163) | copy-start | bytes 4612
  539.7 3.0 collective-permute-start.14
  543.0 17.8 %collective-permute-start.15 = (bf16[2368,128]{1,0:T(8,128)(2,1)S(1)}, bf16[2368,128]{1,0:T(8,128)(2,1)S(1)}, u32[]{:S(2)}, u32[]{:S(2)}) collective-permute-start(bf16[2368,128]{1,0:T(8,128)(2,1)S(1)} %get-tuple-element.177), channel_id=1, source_target_pairs={{8,0},{12,4},{24,16},{28,20},{9,1},{13,5},{25,17},{29,21},{10,2},{... | collective-permute-start | bytes 1818632 | tf_op jit(solution)/shard_map/ppermute | solution.py:1122
  544.3 17.6 %collective-permute-start.17 = (bf16[2368,128]{1,0:T(8,128)(2,1)S(1)}, bf16[2368,128]{1,0:T(8,128)(2,1)S(1)}, u32[]{:S(2)}, u32[]{:S(2)}) collective-permute-start(bf16[2368,128]{1,0:T(8,128)(2,1)S(1)} %get-tuple-element.178), channel_id=1, source_target_pairs={{16,0},{20,4},{24,8},{28,12},{17,1},{21,5},{25,9},{29,13},{18,2},{... | collective-permute-start | bytes 1818632 | tf_op jit(solution)/shard_map/ppermute | solution.py:1122
  562.3 16.8 %collective-permute-start.16 = (bf16[2368,128]{1,0:T(8,128)(2,1)S(1)}, bf16[2368,128]{1,0:T(8,128)(2,1)S(1)}, u32[]{:S(2)}, u32[]{:S(2)}) collective-permute-start(bf16[2368,128]{1,0:T(8,128)(2,1)S(1)} %get-tuple-element.175), channel_id=1, source_target_pairs={{16,0},{20,4},{24,8},{28,12},{17,1},{21,5},{25,9},{29,13},{18,2},{... | collective-permute-start | bytes 1818632 | tf_op jit(solution)/shard_map/ppermute | solution.py:1122
  563.6 16.8 %collective-permute-start.18 = (bf16[2368,128]{1,0:T(8,128)(2,1)S(1)}, bf16[2368,128]{1,0:T(8,128)(2,1)S(1)}, u32[]{:S(2)}, u32[]{:S(2)}) collective-permute-start(bf16[2368,128]{1,0:T(8,128)(2,1)S(1)} %get-tuple-element.176), channel_id=1, source_target_pairs={{8,0},{12,4},{24,16},{28,20},{9,1},{13,5},{25,17},{29,21},{10,2},{... | collective-permute-start | bytes 1818632 | tf_op jit(solution)/shard_map/ppermute | solution.py:1122
  586.4 13.4 %all-to-all-start = ((f32[32,8,128]{2,1,0:T(8,128)}), f32[32,8,128]{2,1,0:T(8,128)S(1)}, u32[]{:S(2)}, u32[]{:S(2)}) async-start(f32[32,8,128]{2,1,0:T(8,128)} %broadcast_in_dim_broadcast_in_dim_broadcast_in_dim.3), calls=%async_computation.1 | async-start | bytes 262144 | tf_op jit(solution)/shard_map/all_to_all | solution.py:1212
  (60 other events, 151.7 us)
Sparse Core Ops, SparseCore 0:
  11.4 223.0 all-gather.2
  473.6 75.9 reduce-scatter.1
